TPU v7x, 32 devices: a whole 2x2x4 slice. The times are simulated.
32 devices in a mesh: section: 2 (over core), ctx: 4 (over y, x), fsdp: 4 (over z).
Axes of the slice: x: 2, y: 2, z: 4, core: 2. Of those that a mesh axis runs over, the one named last changes fastest.
Arguments:
- tokens: bfloat16 [2, 4, 1024, 1024], P(None, 'fsdp', 'ctx'), may hold values from -6 to 6
- targets: bfloat16 [2, 4, 1024, 1024], P(None, 'fsdp', 'ctx'), may hold values from -6 to 6
- lengths: int32 [2, 4], replicated, may hold values from 256 to 1024, as said below
- routes: int32 [2, 2, 4, 1024, 8], P('section', None, 'fsdp', 'ctx'), may hold values from 0 to 31, all different within a row; in each aligned block of 256 rows (0 to 255, 256 to 511, ..., all dimensions but the last counted through in order) at most 72 rows name the same one
- attention_gain: bfloat16 [2, 1024], P('section', ('ctx', 'fsdp')), may hold values from 0.5 to 1.5
- query_weight: bfloat16 [2, 1024, 1024], P('section', ('ctx', 'fsdp')), may hold values from -0.1875 to 0.1875
- memory_weight: bfloat16 [2, 1024, 1024], P('section', ('ctx', 'fsdp')), may hold values from -0.1875 to 0.1875
- output_weight: bfloat16 [2, 1024, 1024], P('section', ('ctx', 'fsdp')), may hold values from -0.75 to 0.75
- mixture_gain: bfloat16 [2, 1024], P('section', ('ctx', 'fsdp')), may hold values from 0.5 to 1.5
- router_weight: bfloat16 [2, 1024, 32], P('section', ('ctx', 'fsdp')), may hold values from -0.099609375 to 0.099609375
- gate_up_weight: bfloat16 [2, 32, 1024, 1024], P('section', 'ctx', 'fsdp'), may hold values from -0.1875 to 0.1875
- down_weight: bfloat16 [2, 32, 512, 1024], P('section', 'ctx', 'fsdp'), may hold values from -1 to 1
Outputs:
- hidden_states: bfloat16 [2, 2, 4, 1024, 1024], P('section', None, 'fsdp', 'ctx')
- input_grads: float32 [2, 2, 4, 1024, 1024], P('section', None, 'fsdp', 'ctx')
- loss_value: float32 [], replicated
- attention_gain_grad: float32 [2, 1024], P('section', ('ctx', 'fsdp'))
- query_grad: float32 [2, 1024, 1024], P('section', ('ctx', 'fsdp'))
- memory_grad: float32 [2, 1024, 1024], P('section', ('ctx', 'fsdp'))
- output_grad: float32 [2, 1024, 1024], P('section', ('ctx', 'fsdp'))
- mixture_gain_grad: float32 [2, 1024], P('section', ('ctx', 'fsdp'))
- router_grad: float32 [2, 1024, 32], P('section', ('ctx', 'fsdp'))
- gate_up_grad: float32 [2, 32, 1024, 1024], P('section', 'ctx', 'fsdp')
- down_grad: float32 [2, 32, 512, 1024], P('section', 'ctx', 'fsdp')
Inputs may be any that keep to these rules, and one draw needn't show every extreme that they name: `lengths`: for every sequence index, the sequence of one micro-batch has all 1024 positions valid. `routes`: each row names 8 different experts. In every layer, micro-batch and sequence, the 256 stored rows of one device name one expert at most 72 times.
All inputs are finite; a program needn't handle non-finite values.
Results may differ from a plain program's by a relative error of at most 0.02.
Values may be sent and summed in bfloat16 or wider, within the bound.
No kernel may reach another device: no remote copies, remote signals or barrier semaphores. Data moves between devices by JAX's collectives and lax.ppermute only.
A program may use at most 384 MiB of HBM per device.

v0:
```python
import math

import jax
import jax.numpy as jnp
from jax import lax
from jax.sharding import PartitionSpec as P

QH = 16
KVH = 8
HD = 64
EXPERTS = 32
FF_E = 512
TOPK = 8


epsilon = 1e-06
rope_base = 10000.0
negative = -1e30
HIGHEST = lax.Precision.HIGHEST


def shifted(value, axis, by):
    devices = lax.axis_size(axis)
    pairs = [(i, i + by) for i in range(devices) if 0 <= i + by < devices]
    return lax.ppermute(value, axis, pairs)


def in_blocks(value, dim, devices):
    lengths = value.shape
    pieces = value.reshape(*lengths[:dim], devices, lengths[dim] // devices, *lengths[dim + 1 :])
    return jnp.moveaxis(pieces, dim, 0)


def summed_on_arrival(value, axis, dim):
    pieces = in_blocks(value, dim, lax.axis_size(axis))
    arrived = lax.all_to_all(pieces, axis, split_axis=0, concat_axis=0, tiled=True)
    return arrived.astype(jnp.float32).sum(axis=0)


def in_one_piece(arrays, axis, dim, along):
    columns = [a.reshape(*a.shape[:along], -1) for a in arrays]
    both = jnp.concatenate(columns, axis=along)
    result, at, gathered = (summed_on_arrival(both, axis, dim), 0, [])
    for a, column in zip(arrays, columns):
        slab = result[..., at : at + column.shape[along]]
        gathered.append(slab.reshape(*slab.shape[:along], *a.shape[along:]))
        at += column.shape[along]
    return tuple(gathered)


def rotary_tables(positions, head_width):
    half = head_width // 2
    inverse = rope_base ** (-2.0 * jnp.arange(half, dtype=jnp.float32) / head_width)
    angles = positions.astype(jnp.float32)[:, None] * inverse[None, :]
    angles = jnp.concatenate([angles, angles], axis=1)
    return (jnp.cos(angles)[:, None, :], jnp.sin(angles)[:, None, :])


def rotate(values, cosine, sine):
    half = values.shape[-1] // 2
    turned = jnp.concatenate([-values[..., half:], values[..., :half]], axis=-1)
    return values * cosine + turned * sine


def norm_forward(values, gain):
    factor = lax.rsqrt(jnp.mean(values * values, axis=-1, keepdims=True) + epsilon)
    return (values * factor * gain, factor)


def norm_backward(values, factor, gain, grad):
    scaled = grad * gain
    inner = jnp.mean(values * scaled, axis=-1, keepdims=True)
    return (factor * scaled - values * factor**3 * inner, jnp.sum(grad * values * factor, axis=0))


def stored_positions(first_row, count, row_count, devices):
    rows_index = first_row + jnp.arange(count, dtype=jnp.int32)
    device = rows_index // row_count
    within = rows_index % row_count
    half = row_count // 2
    return jnp.where(
        within < half, device * half + within, (2 * devices - 1 - device) * half + within - half
    )


def natural_order(gathered, devices, half):
    parts = gathered.reshape(devices, 2, half, gathered.shape[-1])
    return jnp.concatenate(
        [parts[:, 0].reshape(devices * half, -1), parts[::-1, 1].reshape(devices * half, -1)],
        axis=0,
    )


def stored_order(natural, devices, half):
    parts = natural.reshape(2, devices, half, natural.shape[-1])
    return jnp.stack([parts[0], parts[1][::-1]], axis=1).reshape(devices * 2 * half, -1)


def pick(array, index):
    return lax.dynamic_index_in_dim(array, index, 0, keepdims=False)


def place(array, value, index, live):
    return lax.dynamic_update_index_in_dim(
        array, jnp.where(live, value, pick(array, index)), index, 0
    )


def shards(
    tokens,
    targets,
    lengths,
    routes,
    attention_gain,
    query_weight,
    memory_weight,
    output_weight,
    mixture_gain,
    router_weight,
    gate_up_weight,
    down_weight,
):
    section = lax.axis_index("section")
    last_section = lax.axis_size("section") - 1
    devices = lax.axis_size("ctx")
    context = lax.axis_index("ctx")
    sequence = lax.axis_index("fsdp")
    micro = tokens.shape[0]
    rows = tokens.shape[2]
    width = tokens.shape[3]
    half = rows // 2
    total = rows * devices
    key_block = min(512, total)
    key_width = KVH * HD
    score_scale = 1.0 / math.sqrt(HD)
    local_experts = gate_up_weight.shape[1]
    capacity = rows * TOPK * 9 // (EXPERTS * 8)
    slots = EXPERTS * capacity
    positions = stored_positions(context * rows, rows, rows, devices)
    cosine, sine = rotary_tables(positions, HD)
    shared = (
        lax.all_gather(attention_gain[0], ("ctx", "fsdp"), axis=0, tiled=True),
        lax.all_gather(query_weight[0], ("ctx", "fsdp"), axis=0, tiled=True),
        lax.all_gather(memory_weight[0], ("ctx", "fsdp"), axis=0, tiled=True),
        lax.all_gather(output_weight[0], ("ctx", "fsdp"), axis=0, tiled=True),
        lax.all_gather(mixture_gain[0], ("ctx", "fsdp"), axis=0, tiled=True),
        lax.all_gather(router_weight[0], ("ctx", "fsdp"), axis=0, tiled=True),
    )
    expert_pair = (
        lax.all_gather(gate_up_weight[0], "fsdp", axis=1, tiled=True),
        lax.all_gather(down_weight[0], "fsdp", axis=1, tiled=True),
    )
    gain_first, weight_query, weight_memory, weight_output, gain_second, weight_router = shared
    weight_gate_up, weight_down = expert_pair
    gain_first_f = gain_first.astype(jnp.float32)
    gain_second_f = gain_second.astype(jnp.float32)
    router_float = weight_router.astype(jnp.float32)

    def block_count():
        causal = ((2 * devices - context) * half + key_block - 1) // key_block
        return causal

    def score_block(query4, key_rows, query_pos, key_pos, length):
        keys = key_rows[:, :key_width].reshape(key_rows.shape[0], KVH, HD)
        raw = (
            jnp.einsum("rgjd,kgd->gjrk", query4, keys, preferred_element_type=jnp.float32)
            * score_scale
        )
        valid = (key_pos[None, :] <= query_pos[:, None]) & (key_pos[None, :] < length)
        return (raw, valid[None, None])

    def pair_terms(
        query_rows, grad_rows, log_total, row_dots, query_pos, key_rows, key_pos, length
    ):
        count = query_rows.shape[0]
        key_count = key_rows.shape[0]
        query4 = query_rows.reshape(count, KVH, 2, HD)
        grad4 = grad_rows.reshape(count, KVH, 2, HD)
        keys = key_rows[:, :key_width].reshape(key_count, KVH, HD)
        values = key_rows[:, key_width:].reshape(key_count, KVH, HD)
        raw, valid = score_block(query4, key_rows, query_pos, key_pos, length)
        probs = jnp.exp(jnp.where(valid, raw - log_total[..., None], negative))
        grad_probs = jnp.einsum("rgjd,kgd->gjrk", grad4, values, preferred_element_type=jnp.float32)
        grad_scores = (probs * (grad_probs - row_dots[..., None])).astype(jnp.bfloat16)
        grad_query = (
            jnp.einsum("gjrk,kgd->rgjd", grad_scores, keys, preferred_element_type=jnp.float32)
            * score_scale
        )
        grad_keys = (
            jnp.einsum("gjrk,rgjd->kgd", grad_scores, query4, preferred_element_type=jnp.float32)
            * score_scale
        )
        grad_values = jnp.einsum(
            "gjrk,rgjd->kgd", probs.astype(jnp.bfloat16), grad4, preferred_element_type=jnp.float32
        )
        return (
            grad_query.reshape(count, QH * HD),
            jnp.concatenate(
                [
                    grad_keys.reshape(key_count, key_width),
                    grad_values.reshape(key_count, key_width),
                ],
                axis=1,
            ),
        )

    def route_gates(mix_low, route_rows):
        logits = jnp.dot(mix_low, weight_router, preferred_element_type=jnp.float32)
        return jax.nn.softmax(jnp.take_along_axis(logits, route_rows, axis=1), axis=-1)

    def slot_tables(route_rows):
        flat = route_rows.reshape(-1)
        onehot = (flat[:, None] == jnp.arange(EXPERTS, dtype=jnp.int32)[None, :]).astype(jnp.int32)
        rank = jnp.sum((jnp.cumsum(onehot, axis=0) - onehot) * onehot, axis=1)
        slot_of = flat * capacity + rank
        owner = (
            jnp.zeros((slots,), jnp.int32)
            .at[slot_of]
            .set(jnp.arange(flat.shape[0], dtype=jnp.int32))
        )
        filled = jnp.zeros((slots,), jnp.int32).at[slot_of].set(1) > 0
        return (slot_of, owner, filled)

    def layer_backward(saved, grad_output, length, route_rows, blocks):
        inputs = saved["inputs"].astype(jnp.float32)
        normed, first_factor = norm_forward(inputs, gain_first_f)
        normed_low = normed.astype(jnp.bfloat16)
        middle = saved["middle"]
        normed_mix, second_factor = norm_forward(middle, gain_second_f)
        mix_low = normed_mix.astype(jnp.bfloat16)
        gates = route_gates(mix_low, route_rows)
        slot_of, owner, filled = slot_tables(route_rows)
        picked = saved["returned"][slot_of].reshape(rows, TOPK, width).astype(jnp.float32)
        grad_gates = jnp.einsum("rd,rkd->rk", grad_output, picked, precision=HIGHEST)
        slot_grads = gates.reshape(-1)[owner][:, None] * grad_output[owner // TOPK]
        grad_outgoing = jnp.where(filled[:, None], slot_grads, 0.0).astype(jnp.bfloat16)
        grad_received = lax.all_to_all(
            grad_outgoing, "ctx", split_axis=0, concat_axis=0, tiled=True
        ).reshape(devices, local_experts, capacity, width)
        gate_up = saved["gate_up"]
        gate_part = gate_up[..., :FF_E]
        up_part = gate_up[..., FF_E:]
        sigmoid = jax.nn.sigmoid(gate_part)
        silu_part = gate_part * sigmoid
        activated = (silu_part * up_part).astype(jnp.bfloat16)
        grad_act = jnp.einsum(
            "nerd,efd->nerf", grad_received, weight_down, preferred_element_type=jnp.float32
        )
        grad_gate = grad_act * up_part * sigmoid * (1.0 + gate_part * (1.0 - sigmoid))
        grad_up = grad_act * silu_part
        grad_gate_up = jnp.concatenate([grad_gate, grad_up], axis=-1).astype(jnp.bfloat16)
        received4 = saved["received"].reshape(devices, local_experts, capacity, width)
        down_grad = jnp.einsum(
            "nerf,nerd->efd", activated, grad_received, preferred_element_type=jnp.float32
        )
        gate_up_grad = jnp.einsum(
            "nerd,nerf->edf", received4, grad_gate_up, preferred_element_type=jnp.float32
        )
        grad_rows = jnp.einsum(
            "nerf,edf->nerd", grad_gate_up, weight_gate_up, preferred_element_type=jnp.float32
        ).astype(jnp.bfloat16)
        grad_back = lax.all_to_all(
            grad_rows.reshape(slots, width), "ctx", split_axis=0, concat_axis=0, tiled=True
        )
        grad_mix = jnp.sum(
            grad_back[slot_of].reshape(rows, TOPK, width).astype(jnp.float32), axis=1
        )
        grad_chosen = gates * (grad_gates - jnp.sum(gates * grad_gates, axis=1, keepdims=True))
        expert_match = (
            route_rows[:, :, None] == jnp.arange(EXPERTS, dtype=jnp.int32)[None, None, :]
        ).astype(jnp.float32)
        grad_logits = jnp.sum(expert_match * grad_chosen[:, :, None], axis=1)
        router_grad = jnp.dot(mix_low.astype(jnp.float32).T, grad_logits, precision=HIGHEST)
        grad_mix = grad_mix + jnp.dot(grad_logits, router_float.T, precision=HIGHEST)
        grad_middle_norm, second_gain_grad = norm_backward(
            middle, second_factor, gain_second_f, grad_mix
        )
        grad_middle = grad_output + grad_middle_norm
        grad_branch = grad_middle.astype(jnp.bfloat16)
        attended = saved["attended"]
        output_grad = jnp.dot(
            attended.astype(jnp.bfloat16).T, grad_branch, preferred_element_type=jnp.float32
        )
        grad_attended = jnp.dot(
            grad_branch, weight_output.T, preferred_element_type=jnp.float32
        ).astype(jnp.bfloat16)
        row_dots = jnp.einsum(
            "rgjd,rgjd->gjr",
            grad_attended.astype(jnp.float32).reshape(rows, KVH, 2, HD),
            attended.reshape(rows, KVH, 2, HD),
            precision=HIGHEST,
        )
        query_rot = saved["query_rot"]
        memory_all = saved["memory_all"]
        log_total = saved["log_total"]

        def key_terms(step):
            first = step * key_block
            key_rows = lax.dynamic_slice_in_dim(memory_all, first, key_block, 0)
            key_pos = first + jnp.arange(key_block, dtype=jnp.int32)
            part_query, part_memory = pair_terms(
                query_rot, grad_attended, log_total, row_dots, positions, key_rows, key_pos, length
            )
            return (first, part_query, part_memory)

        def both_step(step, carry):
            grad_query, grad_memory = carry
            first, part_query, part_memory = key_terms(step)
            return (
                grad_query + part_query,
                lax.dynamic_update_slice_in_dim(grad_memory, part_memory, first, 0),
            )

        start_carry = (
            jnp.zeros((rows, QH * HD), jnp.float32),
            jnp.zeros((total, 2 * key_width), jnp.float32),
        )
        grad_query, grad_memory = lax.fori_loop(0, blocks, both_step, start_carry)
        own_memory = lax.psum_scatter(
            stored_order(grad_memory, devices, half).astype(jnp.bfloat16),
            "ctx",
            scatter_dimension=0,
            tiled=True,
        ).astype(jnp.float32)
        grad_query_raw = (
            rotate(grad_query.reshape(rows, QH, HD), cosine, -sine)
            .reshape(rows, QH * HD)
            .astype(jnp.bfloat16)
        )
        grad_key_raw = rotate(
            own_memory[:, :key_width].reshape(rows, KVH, HD), cosine, -sine
        ).reshape(rows, key_width)
        grad_memory_raw = jnp.concatenate([grad_key_raw, own_memory[:, key_width:]], axis=1).astype(
            jnp.bfloat16
        )
        query_grad = jnp.dot(normed_low.T, grad_query_raw, preferred_element_type=jnp.float32)
        memory_grad = jnp.dot(normed_low.T, grad_memory_raw, preferred_element_type=jnp.float32)
        grad_normed = jnp.dot(
            grad_query_raw, weight_query.T, preferred_element_type=jnp.float32
        ) + jnp.dot(grad_memory_raw, weight_memory.T, preferred_element_type=jnp.float32)
        grad_input_norm, first_gain_grad = norm_backward(
            inputs, first_factor, gain_first_f, grad_normed
        )
        return (
            grad_middle + grad_input_norm,
            (
                first_gain_grad,
                query_grad,
                memory_grad,
                output_grad,
                second_gain_grad,
                router_grad,
                gate_up_grad,
                down_grad,
            ),
        )

    my_tokens = tokens[:, 0]
    my_targets = targets[:, 0]
    my_routes = routes[0, :, 0]
    carried = jnp.zeros((rows, width), jnp.bfloat16)
    hidden_out = jnp.zeros((micro, rows, width), jnp.bfloat16)
    store = None
    for tick in range(micro + 1):
        offset = tick - section
        live = (offset >= 0) & (offset < micro)
        index = jnp.clip(offset, 0, micro - 1)
        layer_input = jnp.where(section == 0, pick(my_tokens, index), carried)
        length = lengths[index, sequence]
        route_rows = pick(my_routes, index)
        layer_inputs = layer_input.astype(jnp.float32)
        layer_normed, layer_first_factor = norm_forward(layer_inputs, gain_first_f)
        layer_normed_low = layer_normed.astype(jnp.bfloat16)
        query_raw = jnp.dot(layer_normed_low, weight_query, preferred_element_type=jnp.float32)
        memory_raw = jnp.dot(layer_normed_low, weight_memory, preferred_element_type=jnp.float32)
        layer_query_rot = (
            rotate(query_raw.reshape(rows, QH, HD), cosine, sine)
            .reshape(rows, QH * HD)
            .astype(jnp.bfloat16)
        )
        key_rot = rotate(memory_raw[:, :key_width].reshape(rows, KVH, HD), cosine, sine).reshape(
            rows, key_width
        )
        memory_local = jnp.concatenate([key_rot, memory_raw[:, key_width:]], axis=1).astype(
            jnp.bfloat16
        )
        gathered = lax.all_gather(memory_local, "ctx", axis=0, tiled=True)
        layer_memory_all = natural_order(gathered, devices, half)
        attention_memory_all = layer_memory_all
        attention_blocks = block_count()
        attention_query4 = layer_query_rot.reshape(rows, KVH, 2, HD)

        def key_rows_at(step):
            first = step * key_block
            return (
                lax.dynamic_slice_in_dim(attention_memory_all, first, key_block, 0),
                first + jnp.arange(key_block, dtype=jnp.int32),
            )

        def first_pass(step, carry):
            running_max, running_sum = carry
            key_rows, key_pos = key_rows_at(step)
            raw, valid = score_block(attention_query4, key_rows, positions, key_pos, length)
            masked = jnp.where(valid, raw, negative)
            new_max = jnp.maximum(running_max, jnp.max(masked, axis=-1))
            running_sum = running_sum * jnp.exp(running_max - new_max) + jnp.sum(
                jnp.exp(masked - new_max[..., None]), axis=-1
            )
            return (new_max, running_sum)

        start_max = jnp.full((KVH, 2, rows), negative, jnp.float32)
        running_max, running_sum = lax.fori_loop(
            0, attention_blocks, first_pass, (start_max, jnp.zeros_like(start_max))
        )
        attention_log_total = running_max + jnp.log(running_sum)

        def second_pass(step, attended_sum):
            key_rows, key_pos = key_rows_at(step)
            raw, valid = score_block(attention_query4, key_rows, positions, key_pos, length)
            probs = jnp.exp(
                jnp.where(valid, raw - attention_log_total[..., None], negative)
            ).astype(jnp.bfloat16)
            values = key_rows[:, key_width:].reshape(key_block, KVH, HD)
            return attended_sum + jnp.einsum(
                "gjrk,kgd->rgjd", probs, values, preferred_element_type=jnp.float32
            )

        attention_attended = lax.fori_loop(
            0, attention_blocks, second_pass, jnp.zeros((rows, KVH, 2, HD), jnp.float32)
        )
        layer_attended = attention_attended.reshape(rows, QH * HD)
        branch = jnp.dot(
            layer_attended.astype(jnp.bfloat16), weight_output, preferred_element_type=jnp.float32
        )
        layer_middle = layer_inputs + branch
        layer_normed_mix, layer_second_factor = norm_forward(layer_middle, gain_second_f)
        layer_mix_low = layer_normed_mix.astype(jnp.bfloat16)
        layer_gates = route_gates(layer_mix_low, route_rows)
        layer_slot_of, layer_owner, layer_filled = slot_tables(route_rows)
        outgoing = jnp.where(
            layer_filled[:, None], layer_mix_low[layer_owner // TOPK], jnp.zeros((), jnp.bfloat16)
        )
        received = lax.all_to_all(outgoing, "ctx", split_axis=0, concat_axis=0, tiled=True)
        layer_received4 = received.reshape(devices, local_experts, capacity, width)
        layer_gate_up = jnp.einsum(
            "nerd,edf->nerf", layer_received4, weight_gate_up, preferred_element_type=jnp.float32
        )
        layer_activated = (
            jax.nn.silu(layer_gate_up[..., :FF_E]) * layer_gate_up[..., FF_E:]
        ).astype(jnp.bfloat16)
        expert_out = jnp.einsum(
            "nerf,efd->nerd", layer_activated, weight_down, preferred_element_type=jnp.float32
        ).astype(jnp.bfloat16)
        returned = lax.all_to_all(
            expert_out.reshape(slots, width), "ctx", split_axis=0, concat_axis=0, tiled=True
        )
        layer_picked = returned[layer_slot_of].reshape(rows, TOPK, width).astype(jnp.float32)
        mixed = jnp.einsum("rk,rkd->rd", layer_gates, layer_picked, precision=HIGHEST)
        output = layer_middle + mixed
        layer_saved = {
            "inputs": layer_input,
            "memory_local": memory_local,
            "memory_all": layer_memory_all,
            "query_rot": layer_query_rot,
            "log_total": attention_log_total,
            "attended": layer_attended,
            "middle": layer_middle,
            "received": received,
            "gate_up": layer_gate_up,
            "returned": returned,
            "output": output,
        }
        output, saved = (output, layer_saved)
        sent = output.astype(jnp.bfloat16)
        hidden_out = place(hidden_out, sent, index, live)
        if store is None:
            store = jax.tree.map(lambda leaf: jnp.zeros((micro,) + leaf.shape, leaf.dtype), saved)
        store = jax.tree.map(lambda whole, leaf: place(whole, leaf, index, live), store, saved)
        carried = shifted(sent, "section", 1)
    carried_grad = jnp.zeros((rows, width), jnp.bfloat16)
    input_grads = jnp.zeros((micro, rows, width), jnp.float32)
    sums = tuple(
        (
            jnp.zeros(weight.shape, jnp.float32)
            for weight in (
                gain_first,
                weight_query,
                weight_memory,
                weight_output,
                gain_second,
                weight_router,
                weight_gate_up,
                weight_down,
            )
        )
    )
    error_part = jnp.zeros((), jnp.float32)
    for tick in range(micro + 1):
        offset = tick - (last_section - section)
        live = (offset >= 0) & (offset < micro)
        index = jnp.clip(offset, 0, micro - 1)
        saved = jax.tree.map(lambda whole: pick(whole, index), store)
        length = lengths[index, sequence]
        route_rows = pick(my_routes, index)
        valid = (positions < length).astype(jnp.float32)[:, None]
        difference = (saved["output"] - pick(my_targets, index).astype(jnp.float32)) * valid
        grad_output = jnp.where(
            section == last_section, difference, carried_grad.astype(jnp.float32)
        )
        error_part = error_part + jnp.where(
            live & (section == last_section), 0.5 * jnp.sum(difference * difference), 0.0
        )
        grad_input, weight_grads = layer_backward(
            saved, grad_output, length, route_rows, block_count()
        )
        input_grads = place(input_grads, grad_input, index, live)
        sums = tuple(
            (running + jnp.where(live, part, 0.0) for running, part in zip(sums, weight_grads))
        )
        carried_grad = shifted(grad_input.astype(jnp.bfloat16), "section", -1)
    shared_sums = in_one_piece(
        (
            sums[0].astype(jnp.bfloat16),
            sums[1].astype(jnp.bfloat16),
            sums[2].astype(jnp.bfloat16),
            sums[3].astype(jnp.bfloat16),
            sums[4].astype(jnp.bfloat16),
            sums[5].astype(jnp.bfloat16),
        ),
        ("ctx", "fsdp"),
        0,
        1,
    )
    expert_sums = (
        lax.psum_scatter(
            sums[6].astype(jnp.bfloat16), "fsdp", scatter_dimension=1, tiled=True
        ).astype(jnp.float32),
        lax.psum_scatter(
            sums[7].astype(jnp.bfloat16), "fsdp", scatter_dimension=1, tiled=True
        ).astype(jnp.float32),
    )
    error_all = lax.psum(error_part, ("section", "ctx", "fsdp"))
    loss_value = error_all / jnp.sum(lengths).astype(jnp.float32)
    return (
        hidden_out[None, :, None],
        input_grads[None, :, None],
        loss_value,
        shared_sums[0][None],
        shared_sums[1][None],
        shared_sums[2][None],
        shared_sums[3][None],
        shared_sums[4][None],
        shared_sums[5][None],
        expert_sums[0][None],
        expert_sums[1][None],
    )


def solution(mesh):
    placed = (
        P(None, "fsdp", "ctx", None),
        P(None, "fsdp", "ctx", None),
        P(),
        P("section", None, "fsdp", "ctx", None),
        P("section", ("ctx", "fsdp")),
        P("section", ("ctx", "fsdp"), None),
        P("section", ("ctx", "fsdp"), None),
        P("section", ("ctx", "fsdp"), None),
        P("section", ("ctx", "fsdp")),
        P("section", ("ctx", "fsdp"), None),
        P("section", "ctx", "fsdp", None),
        P("section", "ctx", "fsdp", None),
    )
    return jax.shard_map(
        shards,
        mesh=mesh,
        in_specs=placed,
        out_specs=(
            P("section", None, "fsdp", "ctx", None),
            P("section", None, "fsdp", "ctx", None),
            P(),
            P("section", ("ctx", "fsdp")),
            P("section", ("ctx", "fsdp"), None),
            P("section", ("ctx", "fsdp"), None),
            P("section", ("ctx", "fsdp"), None),
            P("section", ("ctx", "fsdp")),
            P("section", ("ctx", "fsdp"), None),
            P("section", "ctx", "fsdp", None),
            P("section", "ctx", "fsdp", None),
        ),
        check_vma=False,
    )
```

profile of v0, /device:TPU:9, one launch (start us, length us, event | category | flops | bytes accessed | tf_op | source)
XLA Modules:
  0.0 2976.8 jit_solution(11658784593155848358)
XLA Ops:
  12.3 31.2 %all-reduce.2 = (bf16[1024]{0:T(1024)(128)(2,1)S(1)}, bf16[1024]{0:T(1024)(128)(2,1)S(1)}) all-reduce(bf16[1024]{0:T(1024)(128)(2,1)S(1)} %dynamic-update-slice, bf16[1024]{0:T(1024)(128)(2,1)S(1)} %dynamic-update-slice.1), channel_id=2, replica_groups=mesh['section'=2,'ctx'=4,'fsdp'=4] {'ctx','fsdp'}, use_global_device_ids=true, to_apply=%add | all-reduce | flops 2048 | bytes 8192
  46.1 26.1 all-gather.23.cloned.1.call-done
  142.1 29.5 all-gather.17.cloned.1.call-done
  206.9 27.6 all-gather.27.cloned.1.call-done
  248.7 55.8 %all_to_all.125 = bf16[4,576,1024]{2,1,0:T(8,128)(2,1)} all-to-all(bf16[4,576,1024]{2,1,0:T(8,128)(2,1)S(1)} %broadcast_select_fusion.4), channel_id=1, replica_groups=mesh['section'=2,'ctx'=4,'fsdp'=4] {'ctx'}, dimensions={0} | all-to-all | bytes 9437184 | tf_op jit(solution)/shard_map/all_to_all | solution.py:443
  304.6 214.5 %all-gather.29.cloned.1.call-done = bf16[1,8,1024,1024]{3,2,1,0:T(8,128)(2,1)} async-done(((bf16[1,8,256,1024]{3,2,1,0:T(8,128)(2,1)}), bf16[1,8,1024,1024]{3,2,1,0:T(8,128)(2,1)}) %all-gather.29.cloned.1.call-update) | async-done | bytes 16777232 | tf_op jit(solution)/shard_map/all_gather | solution.py:150
  545.1 123.2 %all-gather.31.cloned.1.call-done = bf16[1,8,512,1024]{3,2,1,0:T(8,128)(2,1)} async-done(((bf16[1,8,128,1024]{3,2,1,0:T(8,128)(2,1)}), bf16[1,8,512,1024]{3,2,1,0:T(8,128)(2,1)}) %all-gather.31.cloned.1.call-update) | async-done | bytes 8388624 | tf_op jit(solution)/shard_map/all_gather | solution.py:151
  685.3 38.0 %all-gather.5 = bf16[1,1024,32]{2,0,1:T(2,128)(2,1)S(1)} all-gather(bf16[1,64,32]{2,0,1:T(2,128)(2,1)S(1)} %copy.769), channel_id=7, replica_groups=mesh['section'=2,'ctx'=4,'fsdp'=4] {'ctx','fsdp'}, dimensions={1}, use_global_device_ids=true | all-gather | bytes 69632 | tf_op jit(solution)/shard_map/all_gather | solution.py:147
  889.1 43.4 %all-to-all-done.2 = bf16[4,576,1024]{2,1,0:T(8,128)(2,1)} async-done(((bf16[4,576,1024]{2,1,0:T(8,128)(2,1)}), bf16[4,576,1024]{2,1,0:T(8,128)(2,1)}, u32[]{:S(2)}, u32[]{:S(2)}) %all-to-all-start.2) | async-done | bytes 4718624 | tf_op jit(solution)/shard_map/all_to_all | solution.py:443
  986.9 32.2 %all-to-all-done.3 = bf16[4,576,1024]{2,1,0:T(8,128)(2,1)} async-done(((bf16[4,576,1024]{2,1,0:T(8,128)(2,1)}), bf16[4,576,1024]{2,1,0:T(8,128)(2,1)}, u32[]{:S(2)}, u32[]{:S(2)}) %all-to-all-start.3) | async-done | bytes 4718624 | tf_op jit(solution)/shard_map/all_to_all | solution.py:454
  1461.1 21.7 dynamic-slice_bitcast_fusion
  1482.8 30.8 %all-to-all-done.6 = bf16[4,576,1024]{2,1,0:T(8,128)(2,1)} async-done(((bf16[4,576,1024]{2,1,0:T(8,128)(2,1)}), bf16[4,576,1024]{2,1,0:T(8,128)(2,1)}, u32[]{:S(2)}, u32[]{:S(2)}) %all-to-all-start.6) | async-done | bytes 4718624 | tf_op jit(solution)/shard_map/all_to_all | solution.py:237
  1627.9 25.1 while.117
  1797.1 57.3 %all_to_all.126 = bf16[4,576,1024]{2,1,0:T(8,128)(2,1)} all-to-all(bf16[4,576,1024]{2,1,0:T(8,128)(2,1)S(1)} %select_convert_fusion.1), channel_id=1, replica_groups=mesh['section'=2,'ctx'=4,'fsdp'=4] {'ctx'}, dimensions={0} | all-to-all | bytes 9437184 | tf_op jit(solution)/shard_map/all_to_all | solution.py:237
  1890.0 52.5 %all-to-all-done.9 = bf16[4,576,1024]{2,1,0:T(8,128)(2,1)} async-done(((bf16[4,576,1024]{2,1,0:T(8,128)(2,1)}), bf16[4,576,1024]{2,1,0:T(8,128)(2,1)}, u32[]{:S(2)}, u32[]{:S(2)}) %all-to-all-start.9) | async-done | bytes 4718624 | tf_op jit(solution)/shard_map/all_to_all | solution.py:262
  1968.9 25.5 while.118
  2127.1 57.3 %all_to_all.127 = bf16[4,576,1024]{2,1,0:T(8,128)(2,1)} all-to-all(bf16[4,576,1024]{2,1,0:T(8,128)(2,1)S(1)} %select_convert_fusion), channel_id=1, replica_groups=mesh['section'=2,'ctx'=4,'fsdp'=4] {'ctx'}, dimensions={0} | all-to-all | bytes 9437184 | tf_op jit(solution)/shard_map/all_to_all | solution.py:237
  2220.1 52.3 %all-to-all-done.11 = bf16[4,576,1024]{2,1,0:T(8,128)(2,1)} async-done(((bf16[4,576,1024]{2,1,0:T(8,128)(2,1)}), bf16[4,576,1024]{2,1,0:T(8,128)(2,1)}, u32[]{:S(2)}, u32[]{:S(2)}) %all-to-all-start.11) | async-done | bytes 4718624 | tf_op jit(solution)/shard_map/all_to_all | solution.py:262
  2298.7 25.4 while.119
  2373.4 19.8 fusion.106
  2429.5 18.6 fusion.152
  2448.2 32.7 %fusion.103 = bf16[8,1024,1024]{2,1,0:T(8,128)(2,1)} fusion(f32[8,1024,1024,1]{2,1,0,3:T(8,128)} %fusion.152, f32[8,1024,1024,1]{2,1,0,3:T(8,128)} %fusion.154, pred[]{:T(512)S(6)} %and.249, pred[]{:T(512)S(6)} %and.247, pred[]{:T(512)S(6)} %and.245, bf16[4,8,72,1024]{3,2,1,0:T(8,128)(2,1)} %bitcast.1759, bf16[4,8,72,512]{3,2,0,1:T(8,128)(2,1)} %get-tuple-element.1222, ...), kind=kOutput, calls=%fused_computation.230 | convolution fusion | flops 4891607040 | bytes 93323264 | tf_op jit(solution)/shard_map/nerd,nerf->edf/dot_general | solution.py:256
  2559.1 315.4 %psum.7 = f32[]{:T(128)} all-reduce(f32[]{:T(128)S(6)} %add.1060), channel_id=1, replica_groups=mesh['section'=2,'ctx'=4,'fsdp'=4] {'section','ctx','fsdp'}, use_global_device_ids=true, to_apply=%region_99.101 | all-reduce | flops 1 | bytes 8 | tf_op jit(solution)/shard_map/psum | solution.py:542
  2912.3 49.8 %reduce-scatter.12.cloned.1.call-done = bf16[8,256,1024]{2,1,0:T(8,128)(2,1)} async-done(((bf16[8,1024,1024]{2,1,0:T(8,128)(2,1)}), bf16[8,256,1024]{2,1,0:T(8,128)(2,1)}) %reduce-scatter.12.cloned.1.call-update) | async-done | bytes 4194320 | tf_op jit(solution)/shard_map/reduce_scatter | solution.py:535
  (1221 shorter events, 1694.6 us)
Async XLA Ops:
  7.2 65.1 %all-gather.23.cloned.1.call-start = ((), (), s32[]{:S(2)}) async-start(), calls=%async_computation.26 | async-start | bytes 2228224 | tf_op jit(solution)/shard_map/all_gather | solution.py:144
  7.9 126.6 %all-gather.25.cloned.1.call-start = ((), (), s32[]{:S(2)}) async-start(), calls=%async_computation.27 | async-start | bytes 2228224 | tf_op jit(solution)/shard_map/all_gather | solution.py:143
  8.7 162.9 %all-gather.17.cloned.1.call-start = ((), (), s32[]{:S(2)}) async-start(), calls=%async_computation.18 | async-start | bytes 2621440 | tf_op jit(solution)/shard_map/all_gather | solution.py:387
  76.5 158.0 %all-gather.27.cloned.1.call-start = ((), (), s32[]{:S(2)}) async-start(), calls=%async_computation.28 | async-start | bytes 2228224 | tf_op jit(solution)/shard_map/all_gather | solution.py:145
  77.0 442.0 %all-gather.29.cloned.1.call-start = ((), (), s32[]{:S(2)}) async-start(), calls=%async_computation.29 | async-start | bytes 20971520 | tf_op jit(solution)/shard_map/all_gather | solution.py:150
  77.6 590.7 %all-gather.31.cloned.1.call-start = ((), (), s32[]{:S(2)}) async-start(), calls=%async_computation.30 | async-start | bytes 10485760 | tf_op jit(solution)/shard_map/all_gather | solution.py:151
  680.0 61.4 %all-to-all-start.1 = ((bf16[4,576,1024]{2,1,0:T(8,128)(2,1)}), bf16[4,576,1024]{2,1,0:T(8,128)(2,1)}, u32[]{:S(2)}, u32[]{:S(2)}) async-start(bf16[4,576,1024]{2,1,0:T(8,128)(2,1)} %bitcast.1719), calls=%async_computation.1 | async-start | bytes 9437184 | tf_op jit(solution)/shard_map/all_to_all | solution.py:454
  685.1 138.0 %all-gather.19.cloned.1.call-start = ((), (), s32[]{:S(2)}) async-start(), calls=%async_computation.19 | async-start | bytes 2621440 | tf_op jit(solution)/shard_map/all_gather | solution.py:387
  874.6 57.9 %all-to-all-start.2 = ((bf16[4,576,1024]{2,1,0:T(8,128)(2,1)}), bf16[4,576,1024]{2,1,0:T(8,128)(2,1)}, u32[]{:S(2)}, u32[]{:S(2)}) async-start(bf16[4,576,1024]{2,1,0:T(8,128)(2,1)} %broadcast_select_fusion.3), calls=%async_computation.2 | async-start | bytes 9437184 | tf_op jit(solution)/shard_map/all_to_all | solution.py:443
  961.5 57.6 %all-to-all-start.3 = ((bf16[4,576,1024]{2,1,0:T(8,128)(2,1)}), bf16[4,576,1024]{2,1,0:T(8,128)(2,1)}, u32[]{:S(2)}, u32[]{:S(2)}) async-start(bf16[4,576,1024]{2,1,0:T(8,128)(2,1)} %bitcast.1717), calls=%async_computation.3 | async-start | bytes 9437184 | tf_op jit(solution)/shard_map/all_to_all | solution.py:454
  966.6 154.0 %all-gather.21.cloned.1.call-start = ((), (), s32[]{:S(2)}) async-start(), calls=%async_computation.20 | async-start | bytes 2621440 | tf_op jit(solution)/shard_map/all_gather | solution.py:387
  1173.6 57.6 %all-to-all-start.4 = ((bf16[4,576,1024]{2,1,0:T(8,128)(2,1)}), bf16[4,576,1024]{2,1,0:T(8,128)(2,1)}, u32[]{:S(2)}, u32[]{:S(2)}) async-start(bf16[4,576,1024]{2,1,0:T(8,128)(2,1)} %broadcast_select_fusion.2), calls=%async_computation.4 | async-start | bytes 9437184 | tf_op jit(solution)/shard_map/all_to_all | solution.py:443
  1259.9 58.9 %all-to-all-start.5 = ((bf16[4,576,1024]{2,1,0:T(8,128)(2,1)}), bf16[4,576,1024]{2,1,0:T(8,128)(2,1)}, u32[]{:S(2)}, u32[]{:S(2)}) async-start(bf16[4,576,1024]{2,1,0:T(8,128)(2,1)} %bitcast.1716), calls=%async_computation.5 | async-start | bytes 9437184 | tf_op jit(solution)/shard_map/all_to_all | solution.py:454
  1456.0 57.6 %all-to-all-start.6 = ((bf16[4,576,1024]{2,1,0:T(8,128)(2,1)}), bf16[4,576,1024]{2,1,0:T(8,128)(2,1)}, u32[]{:S(2)}, u32[]{:S(2)}) async-start(bf16[4,576,1024]{2,1,0:T(8,128)(2,1)} %select_convert_fusion.2), calls=%async_computation.6 | async-start | bytes 9437184 | tf_op jit(solution)/shard_map/all_to_all | solution.py:237
  1543.7 57.6 %all-to-all-start.7 = ((bf16[4,576,1024]{2,1,0:T(8,128)(2,1)}), bf16[4,576,1024]{2,1,0:T(8,128)(2,1)}, u32[]{:S(2)}, u32[]{:S(2)}) async-start(bf16[4,576,1024]{2,1,0:T(8,128)(2,1)} %bitcast.1715), calls=%async_computation.7 | async-start | bytes 9437184 | tf_op jit(solution)/shard_map/all_to_all | solution.py:262
  1548.8 167.1 %reduce-scatter.6.cloned.1.call-start = ((), (), s32[]{:S(2)}) async-start(), calls=%async_computation.21 | async-start | bytes 2621440 | tf_op jit(solution)/shard_map/reduce_scatter | solution.py:319
  1725.0 34.9 %collective-permute-start.2 = (bf16[256,1024]{1,0:T(8,128)(2,1)}, bf16[256,1024]{1,0:T(8,128)(2,1)S(1)}, u32[]{:S(2)}, u32[]{:S(2)}) collective-permute-start(bf16[256,1024]{1,0:T(8,128)(2,1)} %get-tuple-element.1168), channel_id=1, source_target_pairs={{16,0},{17,1},{18,2},{19,3},{20,4},{21,5},{22,6},{23,7},{24,8},{25... | collective-permute-start | bytes 1572872 | tf_op jit(solution)/shard_map/ppermute | solution.py:25
  1884.5 57.9 %all-to-all-start.9 = ((bf16[4,576,1024]{2,1,0:T(8,128)(2,1)}), bf16[4,576,1024]{2,1,0:T(8,128)(2,1)}, u32[]{:S(2)}, u32[]{:S(2)}) async-start(bf16[4,576,1024]{2,1,0:T(8,128)(2,1)} %bitcast.1720), calls=%async_computation.10 | async-start | bytes 9437184 | tf_op jit(solution)/shard_map/all_to_all | solution.py:262
  1889.7 157.4 %reduce-scatter.8.cloned.1.call-start = ((), (), s32[]{:S(2)}) async-start(), calls=%async_computation.22 | async-start | bytes 2621440 | tf_op jit(solution)/shard_map/reduce_scatter | solution.py:319
  2214.5 57.9 %all-to-all-start.11 = ((bf16[4,576,1024]{2,1,0:T(8,128)(2,1)}), bf16[4,576,1024]{2,1,0:T(8,128)(2,1)}, u32[]{:S(2)}, u32[]{:S(2)}) async-start(bf16[4,576,1024]{2,1,0:T(8,128)(2,1)} %bitcast.1718), calls=%async_computation.13 | async-start | bytes 9437184 | tf_op jit(solution)/shard_map/all_to_all | solution.py:262
  2219.6 301.8 %reduce-scatter.10.cloned.1.call-start = ((), (), s32[]{:S(2)}) async-start(), calls=%async_computation.23 | async-start | bytes 2621440 | tf_op jit(solution)/shard_map/reduce_scatter | solution.py:319
  2341.2 560.6 %reduce-scatter.14.cloned.1.call-start = ((), (), s32[]{:S(2)}) async-start(), calls=%async_computation.25 | async-start | bytes 10485760 | tf_op jit(solution)/shard_map/reduce_scatter | solution.py:538
  2393.3 568.8 %reduce-scatter.12.cloned.1.call-start = ((), (), s32[]{:S(2)}) async-start(), calls=%async_computation.24 | async-start | bytes 20971520 | tf_op jit(solution)/shard_map/reduce_scatter | solution.py:535
  2547.3 358.5 %all-to-all-start.12 = ((bf16[16,64,3106]{2,1,0:T(8,128)(2,1)}), bf16[16,64,3106]{2,1,0:T(8,128)(2,1)}, u32[]{:S(2)}, u32[]{:S(2)}) async-start(bf16[16,64,3106]{2,1,0:T(8,128)(2,1)} %concatenate.181), calls=%async_computation.15 | async-start | bytes 13107200 | tf_op jit(solution)/shard_map/all_to_all | solution.py:36
  (207 other events, 4992.6 us)
Sparse Core Ops, SparseCore 0:
  10.8 61.3 all-gather.22
  75.0 59.4 all-gather.24
  137.0 34.5 all-gather.16
  174.2 60.1 all-gather.26
  235.8 283.1 all-gather.28
  520.5 147.8 all-gather.30
  785.2 37.8 all-gather.18
  1053.6 35.8 all-gather.20
  1670.0 36.0 reduce-scatter.5
  2011.3 35.6 reduce-scatter.7
  2341.3 35.6 reduce-scatter.9
  2393.4 144.6 reduce-scatter.13
  2540.5 421.4 reduce-scatter.11
where the time goes:
time: 2990 us; the launch traced here: 2980 us
  local copies, waits for them, and re-layouts  814 us (27%)
  waiting for transfers between devices  729 us (24%)
  blocking collectives  555 us (19%)
  matrix products  491 us (16%)
  other arithmetic  299 us (10%)
  starting transfers between devices  63.2 us (2%)
    psum x1, blocking collectives, shards(): error_all = lax.psum(error_part, ('section', 'ctx', 'fsdp'))  315 us
    all_gather x1, waiting for transfers between devices, shards(): lax.all_gather(gate_up_weight[0], 'fsdp', axis=1, tiled=True)  214 us
    all_gather x1, waiting for transfers between devices, shards(): lax.all_gather(down_weight[0], 'fsdp', axis=1, tiled=True)  123 us
    all_to_all x2, blocking collectives, layer_backward(): lax.all_to_all(grad_outgoing, 'ctx', split_axis=0, concat_axis=0, tiled=T...  115 us
    all_to_all x3, waiting for transfers between devices, layer_backward(): lax.all_to_all(grad_rows.reshape(slots, width), 'ctx', split_axis=0, conc...  109 us
    gather x24, local copies, waits for them, and re-layouts, route_gates(): jnp.take_along_axis(logits, route_rows, axis=1)  103 us
    another operation x24, other arithmetic  76.5 us
    dynamic_slice x34, local copies, waits for them, and re-layouts, pick(): return lax.dynamic_index_in_dim(array, index, 0, keepdims=False)  76.2 us
  transfers between devices with their start and end apart: 27, of which 18 were waited for; matrix products, arithmetic and copies ran while one was open for 28% of the time, Pallas kernels for 0%

commit v1 on v0

v1 whole, which is shorter than its diff:
```python
import functools
import math

import jax
import jax.numpy as jnp
from jax import lax
from jax.experimental import pallas as pl
from jax.experimental.pallas import tpu as pltpu
from jax.sharding import PartitionSpec as P

QH = 16
KVH = 8
HD = 64
EXPERTS = 32
FF_E = 512
TOPK = 8
KW = KVH * HD
EXT = 16

epsilon = 1e-06
rope_base = 10000.0
negative = -1e30
F32 = jnp.float32
BF16 = jnp.bfloat16
VMEM_LIMIT = 60 * 1024 * 1024


def params(grid_dims=0):
    return pltpu.CompilerParams(
        vmem_limit_bytes=VMEM_LIMIT,
        dimension_semantics=("arbitrary",) * grid_dims if grid_dims else None,
    )


def cost(flops, moved, exps=0):
    return pl.CostEstimate(flops=int(flops), bytes_accessed=int(moved), transcendentals=int(exps))


def mm(a, b):
    return jnp.dot(a, b, preferred_element_type=F32)


def mm_nt(a, b):
    return lax.dot_general(a, b, (((1,), (1,)), ((), ())), preferred_element_type=F32)


def mm_tn(a, b):
    return lax.dot_general(a, b, (((0,), (0,)), ((), ())), preferred_element_type=F32)


def fixed(shape):
    return pl.BlockSpec(shape, lambda *_: (0,) * len(shape), pipeline_mode=pl.Buffered(1))


def resident(shape):
    return pl.BlockSpec(shape, lambda *_: (0,) * len(shape))


def lane_index(shape):
    return lax.broadcasted_iota(jnp.int32, shape, len(shape) - 1)


def turn(block, cosine, sine):
    low_half = lane_index(block.shape) % HD < HD // 2
    swapped = jnp.where(
        low_half, pltpu.roll(block, 128 - HD // 2, axis=1), pltpu.roll(block, HD // 2, axis=1)
    )
    return block * cosine + swapped * sine


def rolled(block):
    return pltpu.roll(block.astype(F32), HD, axis=1).astype(BF16)


def key_positions(device, half, devices, shape, dim):
    within = lax.broadcasted_iota(jnp.int32, shape, dim)
    return jnp.where(
        within < half, device * half + within, (2 * devices - 1 - device) * half + within - half
    )


def fill_bias(bias, scal, devices, rows):
    context, length = scal[0], scal[1]
    query_pos = key_positions(context, rows // 2, devices, (rows, rows), 1)
    for k in range(devices):
        key_pos = key_positions(context ^ k, rows // 2, devices, (rows, rows), 0)
        taken = (key_pos <= query_pos) & (key_pos < length)
        bias[k * rows : (k + 1) * rows, :] = jnp.where(taken, 0.0, negative)


def two_heads(block):
    even = lane_index(block.shape) < HD
    zero = jnp.zeros((), block.dtype)
    return jnp.concatenate([jnp.where(even, block, zero), jnp.where(even, zero, block)], axis=0)


def two_heads_doubled(block):
    even = lane_index(block.shape) < HD
    other = rolled(block)
    return jnp.concatenate([jnp.where(even, block, other), jnp.where(even, other, block)], axis=0)


def doubled(block, odd):
    even = lane_index(block.shape) < HD
    other = rolled(block)
    return jnp.where(even, other, block) if odd else jnp.where(even, block, other)


def one_hot(rank_row, slots):
    rows = rank_row.shape[-1]
    index = lax.broadcasted_iota(jnp.int32, (slots, rows), 0).astype(F32)
    return rank_row == index


def project_kernel(x, gain, wq, wm, cosine, sine, q_out, kv_out):
    values = x[...].astype(F32)
    factor = lax.rsqrt(jnp.mean(values * values, axis=-1, keepdims=True) + epsilon)
    normed = (values * factor * gain[...]).astype(BF16)
    cos, sin = cosine[...], sine[...]
    q0 = mm(normed, wq[...])
    for b in range(QH * HD // 128):
        at = slice(b * 128, (b + 1) * 128)
        q_out[:, at] = turn(q0[:, at], cos, sin).astype(BF16)
    kv0 = mm(normed, wm[...])
    for b in range(KW // 128):
        at = slice(b * 128, (b + 1) * 128)
        kv_out[0, :, at] = turn(kv0[:, at], cos, sin).astype(BF16)
    kv_out[1] = kv0[:, KW:].astype(BF16)


def project(x, gain, shared, cosine, sine):
    rows, width = x.shape
    return pl.pallas_call(
        project_kernel,
        name="project",
        grid=(1,),
        in_specs=[
            fixed((rows, width)),
            fixed((1, width)),
            pl.BlockSpec((width, QH * HD), lambda i: (0, 0), pipeline_mode=pl.Buffered(1)),
            pl.BlockSpec((width, 2 * KW), lambda i: (0, 1), pipeline_mode=pl.Buffered(1)),
            fixed((rows, 128)),
            fixed((rows, 128)),
        ],
        out_specs=[resident((rows, QH * HD)), resident((2, rows, KW))],
        out_shape=[
            jax.ShapeDtypeStruct((rows, QH * HD), BF16),
            jax.ShapeDtypeStruct((2, rows, KW), BF16),
        ],
        compiler_params=params(1),
        cost_estimate=cost(2 * rows * width * 2048, 2 * width * 2048 + 8 * rows * width),
    )(x, gain, shared, shared, cosine, sine)


def attend_kernel(devices, scal, x, q, *rest):
    ks, vs, rest = rest[:devices], rest[devices : 2 * devices], rest[2 * devices :]
    wo, gain, router, mask, o_out, lse_out, mid_out, msg_out, bias, held = rest
    rows = x.shape[0]
    step = pl.program_id(0)

    @pl.when(step == 0)
    def _():
        fill_bias(bias, scal, devices, rows)

    keys = jnp.concatenate([r[0] for r in ks], axis=0)
    values = jnp.concatenate([r[0] for r in vs], axis=0)
    block_bias = bias[...]
    both_bias = jnp.concatenate([block_bias, block_bias], axis=1)
    for i in range(2):
        query = two_heads(q[:, i * 128 : (i + 1) * 128])
        scores = mm_nt(doubled(keys, i), query) * (1.0 / math.sqrt(HD)) + both_bias
        top = jnp.max(scores, axis=0, keepdims=True)
        raised = jnp.exp(scores - top)
        total = jnp.sum(raised, axis=0, keepdims=True)
        probs = (raised * (1.0 / total)).astype(BF16)
        lse_out[0, i : i + 1, :] = top + jnp.log(total)
        mixed = mm_tn(values, probs)[i * HD : (i + 1) * HD]
        pair = jnp.concatenate([mixed[:, :rows], mixed[:, rows:]], axis=0)
        at = pl.multiple_of(step * 256 + i * 128, 128)
        held[:, pl.ds(at, 128)] = jnp.transpose(pair).astype(BF16)

    @pl.when(step == pl.num_programs(0) - 1)
    def _():
        attended = held[...]
        o_out[...] = attended
        middle = x[...].astype(F32) + mm(attended, wo[...])
        mid_out[...] = middle
        factor = lax.rsqrt(jnp.mean(middle * middle, axis=-1, keepdims=True) + epsilon)
        normed = (middle * factor * gain[...]).astype(BF16)
        msg_out[:rows, :] = normed
        logits = mm_nt(router[...], normed)
        chosen = mask[...] > 0.5
        top = jnp.max(jnp.where(chosen, logits, negative), axis=0, keepdims=True)
        raised = jnp.where(chosen, jnp.exp(jnp.where(chosen, logits - top, 0.0)), 0.0)
        gates = raised / jnp.sum(raised, axis=0, keepdims=True)
        high = gates.astype(BF16)
        low = (gates - high.astype(F32)).astype(BF16)
        ext = [high[:EXT], high[EXT:], low[:EXT], low[EXT:]]
        if 4 * rows < x.shape[1]:
            ext.append(jnp.zeros((EXT, x.shape[1] - 4 * rows), BF16))
        msg_out[rows:, :] = jnp.concatenate(ext, axis=1)


def attend(scal, x, q, kvs, shared, gain, router, mask):
    rows, width = x.shape
    devices = len(kvs)
    keys = devices * rows
    kv_specs = [pl.BlockSpec((1, rows, 128), lambda h: (0, 0, h)) for _ in kvs] + [
        pl.BlockSpec((1, rows, 128), lambda h: (1, 0, h)) for _ in kvs
    ]
    return pl.pallas_call(
        functools.partial(attend_kernel, devices),
        name="attend",
        grid=(KVH // 2,),
        in_specs=[
            pl.BlockSpec(memory_space=pltpu.SMEM),
            fixed((rows, width)),
            pl.BlockSpec((rows, 256), lambda h: (0, h)),
            *kv_specs,
            pl.BlockSpec((QH * HD, width), lambda h: (0, 2), pipeline_mode=pl.Buffered(1)),
            fixed((1, width)),
            fixed((EXPERTS, width)),
            fixed((EXPERTS, rows)),
        ],
        out_specs=[
            resident((rows, QH * HD)),
            pl.BlockSpec((1, 2, 2 * rows), lambda h: (h, 0, 0)),
            resident((rows, width)),
            resident((rows + EXT, width)),
        ],
        out_shape=[
            jax.ShapeDtypeStruct((rows, QH * HD), BF16),
            jax.ShapeDtypeStruct((KVH // 2, 2, 2 * rows), F32),
            jax.ShapeDtypeStruct((rows, width), F32),
            jax.ShapeDtypeStruct((rows + EXT, width), BF16),
        ],
        scratch_shapes=[pltpu.VMEM((keys, rows), F32), pltpu.VMEM((rows, QH * HD), BF16)],
        compiler_params=params(1),
        cost_estimate=cost(
            4 * rows * keys * QH * HD * 2 + 2 * rows * width * width,
            2 * width * width + 4 * keys * width + 12 * rows * width,
            rows * keys * QH,
        ),
    )(scal, x, q, *kvs, *kvs, shared, gain, router, mask)


def experts_kernel(sources, slots, scal, *rest):
    msgs, rest = rest[:sources], rest[sources:]
    rank, w1, w2, x_out, gu_out, y_out, gate_out, own_out, other_out, xs, ys = rest
    local = rank.shape[1]
    rows = rank.shape[2]
    step = pl.program_id(0)
    half = sources // 2

    @pl.when(step == 0)
    def _():
        first = scal[0]
        pick_row = lax.broadcasted_iota(jnp.int32, (EXT, 4 * rows), 0)
        for j in range(sources):
            hot = jnp.concatenate(
                [
                    jnp.where(one_hot(rank[j, i : i + 1, :], slots), 1.0, 0.0).astype(BF16)
                    for i in range(local)
                ],
                axis=0,
            )
            picked = mm(hot, msgs[j][:rows, :]).astype(BF16)
            ext = msgs[j][rows:, : 4 * rows].astype(F32)
            for i in range(local):
                xs[i, j] = picked[i * slots : (i + 1) * slots]
                expert = first + i
                row = jnp.sum(jnp.where(pick_row == expert % EXT, ext, 0.0), axis=0, keepdims=True)
                high = jnp.where(expert < EXT, row[:, :rows], row[:, rows : 2 * rows])
                low = jnp.where(expert < EXT, row[:, 2 * rows : 3 * rows], row[:, 3 * rows :])
                gate_out[j, i : i + 1, :] = high + low

    width = xs.shape[-1]
    taken = xs[step].reshape(sources * slots, width)
    x_out[0] = taken
    gate_up = mm(taken, w1[0])
    gu_out[0] = gate_up
    gate, up = gate_up[:, :FF_E], gate_up[:, FF_E:]
    activated = (gate * jax.nn.sigmoid(gate) * up).astype(BF16)
    out = mm(activated, w2[0]).astype(BF16)
    y_out[0] = out
    ys[step] = out.reshape(sources, slots, width)

    @pl.when(step == pl.num_programs(0) - 1)
    def _():
        for j in range(sources):
            spread = jnp.concatenate(
                [
                    jnp.where(one_hot(rank[j, i : i + 1, :], slots), gate_out[j, i : i + 1, :], 0.0)
                    for i in range(local)
                ],
                axis=0,
            )
            high = spread.astype(BF16)
            low = (spread - high.astype(F32)).astype(BF16)
            given = ys[:, j].reshape(local * slots, width)
            part = (mm_tn(high, given) + mm_tn(low, given)).astype(BF16)
            if j < half:
                own_out[j] = part
            else:
                other_out[j - half] = part


def experts_forward(scal, msgs, rank, w1, w2, slots):
    sources, local, rows = rank.shape
    width = msgs[0].shape[1]
    count = sources * slots
    each = lambda shape: pl.BlockSpec((1,) + shape, lambda e: (e, 0, 0))
    return pl.pallas_call(
        functools.partial(experts_kernel, sources, slots),
        name="experts_forward",
        grid=(local,),
        in_specs=[
            pl.BlockSpec(memory_space=pltpu.SMEM),
            *[fixed((rows + EXT, width)) for _ in msgs],
            fixed((sources, local, rows)),
            each((width, 2 * FF_E)),
            each((FF_E, width)),
        ],
        out_specs=[
            each((count, width)),
            each((count, 2 * FF_E)),
            each((count, width)),
            resident((sources, local, rows)),
            resident((sources // 2, rows, width)),
            resident((sources // 2, rows, width)),
        ],
        out_shape=[
            jax.ShapeDtypeStruct((local, count, width), BF16),
            jax.ShapeDtypeStruct((local, count, 2 * FF_E), F32),
            jax.ShapeDtypeStruct((local, count, width), BF16),
            jax.ShapeDtypeStruct((sources, local, rows), F32),
            jax.ShapeDtypeStruct((sources // 2, rows, width), BF16),
            jax.ShapeDtypeStruct((sources // 2, rows, width), BF16),
        ],
        scratch_shapes=[
            pltpu.VMEM((local, sources, slots, width), BF16),
            pltpu.VMEM((local, sources, slots, width), BF16),
        ],
        compiler_params=params(1),
        cost_estimate=cost(
            2 * local * count * width * 3 * FF_E * 1.3, 8 * local * count * width, local * count * FF_E
        ),
    )(scal, *msgs, rank, w1, w2)


def experts_back_kernel(sources, slots, *rest):
    msgs, rest = rest[:sources], rest[sources:]
    rank, gates, xs, gu, ys, w1, w2, router = rest[:8]
    g1_out, g2_out, router_out, own_out, other_out, held = rest[8:]
    local = rank.shape[1]
    rows = rank.shape[2]
    width = held.shape[-1]
    step = pl.program_id(0)
    half = sources // 2

    @pl.when(step == 0)
    def _():
        for j in range(sources):
            hot = jnp.concatenate(
                [
                    jnp.where(one_hot(rank[j, i : i + 1, :], slots), 1.0, 0.0).astype(BF16)
                    for i in range(local)
                ],
                axis=0,
            )
            picked = mm(hot, msgs[j][:rows, :]).astype(BF16)
            for i in range(local):
                held[i, j] = picked[i * slots : (i + 1) * slots]

    gate_columns, inner_columns = [], []
    for j in range(sources):
        hot = one_hot(rank[j, pl.ds(step, 1), :], slots)
        ext = msgs[j][rows:, :rows].astype(F32)
        inner = ext[0:1, :] + ext[1:2, :]
        gate_columns.append(
            jnp.sum(jnp.where(hot, gates[j, pl.ds(step, 1), :], 0.0), axis=1, keepdims=True)
        )
        inner_columns.append(jnp.sum(jnp.where(hot, inner, 0.0), axis=1, keepdims=True))
    gate_column = jnp.concatenate(gate_columns, axis=0)
    inner_column = jnp.concatenate(inner_columns, axis=0)
    grad_out = held[step].reshape(sources * slots, width).astype(F32)
    grad_y = (gate_column * grad_out).astype(BF16)
    given = jnp.sum(grad_out * ys[0].astype(F32), axis=1, keepdims=True)
    grad_logit = gate_column * (given - inner_column)
    gate, up = gu[0, :, :FF_E], gu[0, :, FF_E:]
    sigmoid = jax.nn.sigmoid(gate)
    silu = gate * sigmoid
    activated = (silu * up).astype(BF16)
    g2_out[0] = mm_tn(activated, grad_y).astype(BF16)
    grad_act = mm_nt(grad_y, w2[0])
    grad_gate = grad_act * up * sigmoid * (1.0 + gate * (1.0 - sigmoid))
    grad_up = grad_act * silu
    grad_gate_up = jnp.concatenate([grad_gate.astype(BF16), grad_up.astype(BF16)], axis=1)
    taken = xs[0]
    g1_out[0] = mm_tn(taken, grad_gate_up).astype(BF16)
    router_out[0] = jnp.sum(taken.astype(F32) * grad_logit, axis=0, keepdims=True)
    grad_rows = mm_nt(grad_gate_up, w1[0]) + grad_logit * router[0]
    held[step] = grad_rows.astype(BF16).reshape(sources, slots, width)

    @pl.when(step == pl.num_programs(0) - 1)
    def _():
        for j in range(sources):
            hot = jnp.concatenate(
                [
                    jnp.where(one_hot(rank[j, i : i + 1, :], slots), 1.0, 0.0)
                    for i in range(local)
                ],
                axis=0,
            ).astype(BF16)
            part = mm_tn(hot, held[:, j].reshape(local * slots, width)).astype(BF16)
            if j < half:
                own_out[j] = part
            else:
                other_out[j - half] = part


def experts_backward(msgs, rank, gates, xs, gu, ys, w1, w2, router, slots):
    sources, local, rows = rank.shape
    width = msgs[0].shape[1]
    count = sources * slots
    each = lambda shape: pl.BlockSpec((1,) + shape, lambda e: (e, 0, 0))
    return pl.pallas_call(
        functools.partial(experts_back_kernel, sources, slots),
        name="experts_backward",
        grid=(local,),
        in_specs=[
            *[fixed((rows + EXT, width)) for _ in msgs],
            fixed((sources, local, rows)),
            fixed((sources, local, rows)),
            each((count, width)),
            each((count, 2 * FF_E)),
            each((count, width)),
            each((width, 2 * FF_E)),
            each((FF_E, width)),
            each((1, width)),
        ],
        out_specs=[
            each((width, 2 * FF_E)),
            each((FF_E, width)),
            each((1, width)),
            resident((sources // 2, rows, width)),
            resident((sources // 2, rows, width)),
        ],
        out_shape=[
            jax.ShapeDtypeStruct((local, width, 2 * FF_E), BF16),
            jax.ShapeDtypeStruct((local, FF_E, width), BF16),
            jax.ShapeDtypeStruct((local, 1, width), F32),
            jax.ShapeDtypeStruct((sources // 2, rows, width), BF16),
            jax.ShapeDtypeStruct((sources // 2, rows, width), BF16),
        ],
        scratch_shapes=[pltpu.VMEM((local, sources, slots, width), BF16)],
        compiler_params=params(1),
        cost_estimate=cost(
            2 * local * count * width * 3 * FF_E * 2.3, 14 * local * count * width, local * count * FF_E
        ),
    )(*msgs, rank, gates, xs, gu, ys, w1, w2, router)


def attend_back_kernel(devices, arrived, scal, *rest):
    parts, rest = rest[:arrived], rest[arrived:]
    grad_out, middle, gain, attended, wo, q, lse, cosine, sine = rest[:9]
    ks, vs, rest = rest[9 : 9 + devices], rest[9 + devices : 9 + 2 * devices], rest[9 + 2 * devices :]
    mid_out, wo_grad, gain_grad, dq_out = rest[:4]
    dkv_outs, (bias, held) = rest[4 : 4 + devices], rest[4 + devices :]
    rows = middle.shape[0]
    scale = 1.0 / math.sqrt(HD)
    step = pl.program_id(0)

    @pl.when(step == 0)
    def _():
        fill_bias(bias, scal, devices, rows)
        grad_mix = parts[0][...].astype(F32)
        for part in parts[1:]:
            grad_mix = grad_mix + part[...].astype(F32)
        mid = middle[...]
        factor = lax.rsqrt(jnp.mean(mid * mid, axis=-1, keepdims=True) + epsilon)
        scaled = grad_mix * gain[...]
        inner = jnp.mean(mid * scaled, axis=-1, keepdims=True)
        gain_grad[...] = jnp.sum(grad_mix * mid * factor, axis=0, keepdims=True)
        grad_mid = grad_out[...] + factor * scaled - mid * (factor * factor * factor * inner)
        mid_out[...] = grad_mid
        branch = grad_mid.astype(BF16)
        wo_grad[...] = mm_tn(attended[...], branch).astype(BF16)
        held[...] = mm_nt(branch, wo[...]).astype(BF16)

    keys = jnp.concatenate([r[0] for r in ks], axis=0)
    values = jnp.concatenate([r[0] for r in vs], axis=0)
    block_bias = bias[...]
    both_bias = jnp.concatenate([block_bias, block_bias], axis=1)
    key_parts, value_parts = [], []
    for i in range(2):
        block = q[:, i * 128 : (i + 1) * 128]
        at = pl.multiple_of(step * 256 + i * 128, 128)
        grads = held[:, pl.ds(at, 128)]
        scores = mm_nt(doubled(keys, i), two_heads(block)) * scale + both_bias
        probs = jnp.exp(scores - lse[0, i : i + 1, :])
        grad_probs = mm_nt(doubled(values, i), two_heads(grads))
        product = probs * grad_probs
        dots = jnp.sum(product, axis=0, keepdims=True)
        grad_scores = (product - probs * dots).astype(BF16)
        key_parts.append(mm(grad_scores, two_heads_doubled(block)) * scale)
        value_parts.append(mm(probs.astype(BF16), two_heads_doubled(grads)))
        moved = mm_tn(keys, grad_scores)[i * HD : (i + 1) * HD] * scale
        pair = jnp.concatenate([moved[:, :rows], moved[:, rows:]], axis=0)
        dq_out[:, i * 128 : (i + 1) * 128] = turn(
            jnp.transpose(pair), cosine[...], sine[...]
        ).astype(BF16)
    even = lane_index(key_parts[0].shape) < HD
    grad_keys = jnp.where(even, key_parts[0], key_parts[1]).astype(BF16)
    grad_values = jnp.where(even, value_parts[0], value_parts[1]).astype(BF16)
    for k in range(devices):
        dkv_outs[k][0] = grad_keys[k * rows : (k + 1) * rows]
        dkv_outs[k][1] = grad_values[k * rows : (k + 1) * rows]


def attend_backward(scal, parts, grad_out, middle, gain, attended, shared, q, lse, cosine, sine, kvs):
    rows, width = middle.shape
    devices = len(kvs)
    keys = devices * rows
    kv_specs = [pl.BlockSpec((1, rows, 128), lambda h: (0, 0, h)) for _ in kvs] + [
        pl.BlockSpec((1, rows, 128), lambda h: (1, 0, h)) for _ in kvs
    ]
    return pl.pallas_call(
        functools.partial(attend_back_kernel, devices, len(parts)),
        name="attend_backward",
        grid=(KVH // 2,),
        in_specs=[
            pl.BlockSpec(memory_space=pltpu.SMEM),
            *[fixed((rows, width)) for _ in parts],
            fixed((rows, width)),
            fixed((rows, width)),
            fixed((1, width)),
            fixed((rows, QH * HD)),
            pl.BlockSpec((QH * HD, width), lambda h: (0, 2), pipeline_mode=pl.Buffered(1)),
            pl.BlockSpec((rows, 256), lambda h: (0, h)),
            pl.BlockSpec((1, 2, 2 * rows), lambda h: (h, 0, 0)),
            fixed((rows, 128)),
            fixed((rows, 128)),
            *kv_specs,
        ],
        out_specs=[
            resident((rows, width)),
            resident((QH * HD, width)),
            resident((1, width)),
            pl.BlockSpec((rows, 256), lambda h: (0, h)),
            *[pl.BlockSpec((2, rows, 128), lambda h: (0, 0, h)) for _ in kvs],
        ],
        out_shape=[
            jax.ShapeDtypeStruct((rows, width), F32),
            jax.ShapeDtypeStruct((QH * HD, width), BF16),
            jax.ShapeDtypeStruct((1, width), F32),
            jax.ShapeDtypeStruct((rows, QH * HD), BF16),
            *[jax.ShapeDtypeStruct((2, rows, KW), BF16) for _ in kvs],
        ],
        scratch_shapes=[pltpu.VMEM((keys, rows), F32), pltpu.VMEM((rows, QH * HD), BF16)],
        compiler_params=params(1),
        cost_estimate=cost(
            10 * rows * keys * QH * HD * 2 + 4 * rows * width * width,
            6 * width * width + 8 * keys * width + 20 * rows * width,
            rows * keys * QH,
        ),
    )(
        scal, *parts, grad_out, middle, gain, attended, shared, q, lse, cosine, sine, *kvs, *kvs
    )


def project_back_kernel(devices, x, gain, dq, *rest):
    parts, rest = rest[:devices], rest[devices:]
    grad_mid, wq, wm, cosine, sine, dx_out, wq_grad, wm_grad, gain_grad = rest
    values = x[...].astype(F32)
    factor = lax.rsqrt(jnp.mean(values * values, axis=-1, keepdims=True) + epsilon)
    normed = (values * factor * gain[...]).astype(BF16)
    summed = parts[0][...].astype(F32)
    for part in parts[1:]:
        summed = summed + part[...].astype(F32)
    grad_keys = [
        turn(summed[0, :, b * 128 : (b + 1) * 128], cosine[...], sine[...]).astype(BF16)
        for b in range(KW // 128)
    ]
    grad_memory = jnp.concatenate(grad_keys + [summed[1].astype(BF16)], axis=1)
    grad_query = dq[...]
    wq_grad[...] = mm_tn(normed, grad_query).astype(BF16)
    wm_grad[...] = mm_tn(normed, grad_memory).astype(BF16)
    grad_normed = mm_nt(grad_query, wq[...]) + mm_nt(grad_memory, wm[...])
    scaled = grad_normed * gain[...]
    inner = jnp.mean(values * scaled, axis=-1, keepdims=True)
    gain_grad[...] = jnp.sum(grad_normed * values * factor, axis=0, keepdims=True)
    dx_out[...] = (
        grad_mid[...] + factor * scaled - values * (factor * factor * factor * inner)
    )


def project_backward(x, gain, dq, parts, grad_mid, shared, cosine, sine):
    rows, width = x.shape
    return pl.pallas_call(
        functools.partial(project_back_kernel, len(parts)),
        name="project_backward",
        grid=(1,),
        in_specs=[
            fixed((rows, width)),
            fixed((1, width)),
            fixed((rows, QH * HD)),
            *[fixed((2, rows, KW)) for _ in parts],
            fixed((rows, width)),
            pl.BlockSpec((width, QH * HD), lambda i: (0, 0), pipeline_mode=pl.Buffered(1)),
            pl.BlockSpec((width, 2 * KW), lambda i: (0, 1), pipeline_mode=pl.Buffered(1)),
            fixed((rows, 128)),
            fixed((rows, 128)),
        ],
        out_specs=[
            resident((rows, width)),
            resident((width, QH * HD)),
            resident((width, 2 * KW)),
            resident((1, width)),
        ],
        out_shape=[
            jax.ShapeDtypeStruct((rows, width), F32),
            jax.ShapeDtypeStruct((width, QH * HD), BF16),
            jax.ShapeDtypeStruct((width, 2 * KW), BF16),
            jax.ShapeDtypeStruct((1, width), F32),
        ],
        compiler_params=params(1),
        cost_estimate=cost(8 * rows * width * 2048, 8 * width * 2048 + 16 * rows * width),
    )(x, gain, dq, *parts, grad_mid, shared, shared, cosine, sine)


def pairs_within(axis, by, sections=(0, 1)):
    count = lax.axis_size(axis)
    return [(s * count + i, s * count + (i ^ by)) for s in sections for i in range(count)]


def exchanged(value, axis, by, sections=(0, 1)):
    return lax.ppermute(value, ("section", axis), pairs_within(axis, by, sections))


def swapped(value):
    return lax.ppermute(value, "section", [(0, 1), (1, 0)])


def from_all(value, axis, sections=(0, 1)):
    count = lax.axis_size(axis)
    return [value] + [exchanged(value, axis, k, sections) for k in range(1, count)]


def in_order(blocks, me):
    size = blocks[0].shape[0]
    whole = jnp.zeros((size * len(blocks),) + blocks[0].shape[1:], blocks[0].dtype)
    for k, block in enumerate(blocks):
        whole = lax.dynamic_update_slice_in_dim(whole, block, (me ^ k) * size, 0)
    return whole


def scattered_sum(value, axis, me, sections):
    count = lax.axis_size(axis)
    size = value.shape[0] // count
    block = lambda k: lax.dynamic_slice_in_dim(value, (me ^ k) * size, size, 0)
    total = block(0).astype(F32)
    for arrived in [exchanged(block(k), axis, k, sections) for k in range(1, count)]:
        total = total + arrived.astype(F32)
    return total


def shards(
    tokens,
    targets,
    lengths,
    routes,
    attention_gain,
    query_weight,
    memory_weight,
    output_weight,
    mixture_gain,
    router_weight,
    gate_up_weight,
    down_weight,
):
    section = lax.axis_index("section")
    context = lax.axis_index("ctx")
    line = lax.axis_index("fsdp")
    devices = lax.axis_size("ctx")
    depth = lax.axis_size("fsdp")
    first_core = section == 0
    rows, width = tokens.shape[2:]
    layers = 2
    held_experts = gate_up_weight.shape[1]
    local = held_experts // 2
    sources = 2 * devices
    capacity = rows * TOPK * 9 // (EXPERTS * 8)
    slots = -(-capacity // 16) * 16
    first_expert = context * held_experts + section * local

    def both_layers(weight):
        mine = lax.dynamic_slice_in_dim(weight, section * local, local, 0)
        theirs = lax.dynamic_slice_in_dim(weight, (1 - section) * local, local, 0)
        arrived = swapped(theirs)
        return (jnp.where(first_core, mine, arrived), jnp.where(first_core, arrived, mine))

    up_shards = both_layers(gate_up_weight[0])
    down_shards = both_layers(down_weight[0])
    experts = []
    for layer in range(layers):
        experts.append(
            (
                lax.all_gather(up_shards[layer], "fsdp", axis=1, tiled=True),
                lax.all_gather(down_shards[layer], "fsdp", axis=1, tiled=True),
            )
        )

    pack = jnp.concatenate(
        [
            query_weight[0],
            memory_weight[0],
            output_weight[0],
            router_weight[0],
            attention_gain[0][:, None],
            mixture_gain[0][:, None],
            jnp.zeros((query_weight.shape[1], 128 - EXPERTS - 2), BF16),
        ],
        axis=1,
    )

    def gathered_shared(layer):
        plane = in_order(from_all(pack, "fsdp", (layer,)), line)
        whole = in_order(from_all(plane, "ctx", (layer,)), context)
        arrived = lax.ppermute(whole, "section", [(layer, 1 - layer)])
        return jnp.where(section == layer, whole, arrived)

    def small_parts(whole):
        small = whole[:, 3 * width :].T
        return (
            small[:EXPERTS],
            small[EXPERTS : EXPERTS + 1].astype(F32),
            small[EXPERTS + 1 : EXPERTS + 2].astype(F32),
        )

    my_routes = jnp.swapaxes(routes[0, :, 0], 1, 2)
    other_routes = swapped(my_routes)
    layer_routes = jnp.where(
        first_core,
        jnp.stack([my_routes, other_routes]),
        jnp.stack([other_routes, my_routes])[:, ::-1],
    )
    all_routes = jnp.stack(from_all(layer_routes, "ctx"), axis=2).reshape(
        layers, sources, TOPK, rows
    )
    ids = first_expert + jnp.arange(local, dtype=jnp.int32)
    named = jnp.any(all_routes[:, :, None] == ids[None, None, :, None, None], axis=3)
    earlier = (
        lax.broadcasted_iota(jnp.int32, (rows, rows), 0)
        < lax.broadcasted_iota(jnp.int32, (rows, rows), 1)
    ).astype(BF16)
    before = jnp.dot(
        named.astype(BF16).reshape(-1, rows), earlier, preferred_element_type=F32
    ).reshape(named.shape)
    ranks = jnp.where(named, before, -1.0)
    masks = jnp.any(
        layer_routes[:, 0, None] == jnp.arange(EXPERTS, dtype=jnp.int32)[None, :, None, None], axis=2
    ).astype(F32)

    half = rows // 2
    within = jnp.arange(rows, dtype=jnp.int32)
    positions = jnp.where(
        within < half, context * half + within, (2 * devices - 1 - context) * half + within - half
    )
    inverse = rope_base ** (-2.0 * jnp.arange(HD // 2, dtype=F32) / HD)
    angles = positions.astype(F32)[:, None] * inverse[None, :]
    sine, cosine = jnp.sin(angles), jnp.cos(angles)
    cos_table = jnp.concatenate([cosine] * 4, axis=1)
    sin_table = jnp.concatenate([-sine, sine, -sine, sine], axis=1)
    length = lengths[section, line]
    attend_scalars = jnp.stack([context, length]).astype(jnp.int32)
    expert_scalars = first_expert.astype(jnp.int32).reshape(1)

    def dispatched(message):
        plane = from_all(message, "ctx")
        return plane + [swapped(block) for block in plane]

    def returned(own, other):
        crossed = [swapped(other[k]) for k in range(devices)]
        terms = [own[0], crossed[0]]
        for k in range(1, devices):
            chip = (own[k].astype(F32) + crossed[k].astype(F32)).astype(BF16)
            terms.append(exchanged(chip, "ctx", k))
        return terms

    my_targets = lax.dynamic_index_in_dim(targets[:, 0], section, 0, keepdims=False)
    layer_input = lax.dynamic_index_in_dim(tokens[:, 0], section, 0, keepdims=False)
    saved, hidden = [], []
    for layer in range(layers):
        shared = gathered_shared(layer)
        router, gain_first, gain_second = small_parts(shared)
        w1, w2 = experts[layer]
        q, kv = project(layer_input, gain_first, shared, cos_table, sin_table)
        kvs = from_all(kv, "ctx")
        attended, lse, middle, message = attend(
            attend_scalars, layer_input, q, kvs, shared, gain_second, router, masks[layer]
        )
        messages = dispatched(message)
        xs, gate_up, ys, gates, own, other = experts_forward(
            expert_scalars, messages, ranks[layer], w1, w2, slots
        )
        mixed = functools.reduce(lambda a, b: a + b, [t.astype(F32) for t in returned(own, other)])
        output = middle + mixed
        hidden.append(output.astype(BF16))
        saved.append(
            dict(
                x=layer_input,
                shared=shared,
                router=router,
                gain_first=gain_first,
                gain_second=gain_second,
                q=q,
                kvs=kvs,
                attended=attended,
                lse=lse,
                middle=middle,
                xs=xs,
                gate_up=gate_up,
                ys=ys,
                gates=gates,
                mixed=mixed,
            )
        )
        layer_input = hidden[-1]

    valid = (positions < length).astype(F32)[:, None]
    grad_output = (output - my_targets.astype(F32)) * valid
    error = 0.5 * jnp.sum(grad_output * grad_output)
    for axis in ("section", "ctx", "fsdp"):
        by = 1
        while by < lax.axis_size(axis):
            error = error + lax.ppermute(
                error, axis, [(i, i ^ by) for i in range(lax.axis_size(axis))]
            )
            by *= 2
    loss_value = error / jnp.sum(lengths).astype(F32)

    input_grads, shared_grads, expert_grads = [None] * layers, [None] * layers, [None] * layers
    small_grads = [None] * layers
    for layer in reversed(range(layers)):
        kept = saved[layer]
        w1, w2 = experts[layer]
        inner = jnp.sum(grad_output * kept["mixed"], axis=1)
        inner_high = inner.astype(BF16)
        inner_low = (inner - inner_high.astype(F32)).astype(BF16)
        ext = jnp.pad(jnp.stack([inner_high, inner_low]), ((0, EXT - 2), (0, width - rows)))
        message = jnp.concatenate([grad_output.astype(BF16), ext], axis=0)
        own_router = lax.dynamic_slice_in_dim(kept["router"], first_expert, local, 0).astype(F32)
        g1, g2, router_grad, own, other = experts_backward(
            dispatched(message),
            ranks[layer],
            kept["gates"],
            kept["xs"],
            kept["gate_up"],
            kept["ys"],
            w1,
            w2,
            own_router[:, None, :],
            slots,
        )
        expert_grads[layer] = (
            lax.psum_scatter(g2, "fsdp", scatter_dimension=1, tiled=True),
            lax.psum_scatter(g1, "fsdp", scatter_dimension=1, tiled=True),
        )
        back = attend_backward(
            attend_scalars,
            returned(own, other),
            grad_output,
            kept["middle"],
            kept["gain_second"],
            kept["attended"],
            kept["shared"],
            kept["q"],
            kept["lse"],
            cos_table,
            -sin_table,
            kept["kvs"],
        )
        grad_mid, wo_grad, gain_second_grad, dq = back[:4]
        dkv = back[4:]
        parts = [dkv[0]] + [exchanged(dkv[k], "ctx", k) for k in range(1, devices)]
        dx, wq_grad, wm_grad, gain_first_grad = project_backward(
            kept["x"], kept["gain_first"], dq, parts, grad_mid, kept["shared"], cos_table, -sin_table
        )
        input_grads[layer] = dx
        grad_output = dx.astype(BF16).astype(F32)

        router_rows = lax.dynamic_update_slice_in_dim(
            jnp.zeros((EXPERTS, width), F32), router_grad[:, 0], first_expert, 0
        )
        small = jnp.concatenate(
            [
                router_rows,
                gain_first_grad,
                gain_second_grad,
                jnp.zeros((128 - EXPERTS - 2, width), F32),
            ],
            axis=0,
        ).astype(BF16)
        packed = jnp.concatenate([wq_grad, wm_grad, wo_grad, small.T], axis=1)
        arrived = lax.ppermute(packed, "section", [(1 - layer, layer)])
        chip = (packed.astype(F32) + arrived.astype(F32)).astype(BF16)
        plane = scattered_sum(chip, "ctx", context, (layer,)).astype(BF16)
        shared_grads[layer] = scattered_sum(plane, "fsdp", line, (layer,))

    def placed_experts(which):
        home = jnp.where(first_core, expert_grads[0][which], expert_grads[1][which])
        away = jnp.where(first_core, expert_grads[1][which], expert_grads[0][which])
        arrived = swapped(away)
        return jnp.concatenate(
            [jnp.where(first_core, home, arrived), jnp.where(first_core, arrived, home)], axis=0
        ).astype(F32)

    def placed_rows(values):
        home = jnp.where(first_core, values[0], values[1])
        arrived = swapped(jnp.where(first_core, values[1], values[0]))
        return jnp.stack(
            [jnp.where(first_core, home, arrived), jnp.where(first_core, arrived, home)]
        )

    total = jnp.where(first_core, shared_grads[0], shared_grads[1])
    at = 3 * width
    return (
        placed_rows(hidden)[None, :, None],
        placed_rows(input_grads)[None, :, None],
        loss_value,
        total[:, at + EXPERTS][None],
        total[:, :width][None],
        total[:, width : 2 * width][None],
        total[:, 2 * width : 3 * width][None],
        total[:, at + EXPERTS + 1][None],
        total[:, at : at + EXPERTS][None],
        placed_experts(1)[None],
        placed_experts(0)[None],
    )


def solution(mesh):
    placed = (
        P(None, "fsdp", "ctx", None),
        P(None, "fsdp", "ctx", None),
        P(),
        P("section", None, "fsdp", "ctx", None),
        P("section", ("ctx", "fsdp")),
        P("section", ("ctx", "fsdp"), None),
        P("section", ("ctx", "fsdp"), None),
        P("section", ("ctx", "fsdp"), None),
        P("section", ("ctx", "fsdp")),
        P("section", ("ctx", "fsdp"), None),
        P("section", "ctx", "fsdp", None),
        P("section", "ctx", "fsdp", None),
    )
    return jax.shard_map(
        shards,
        mesh=mesh,
        in_specs=placed,
        out_specs=(
            P("section", None, "fsdp", "ctx", None),
            P("section", None, "fsdp", "ctx", None),
            P(),
            P("section", ("ctx", "fsdp")),
            P("section", ("ctx", "fsdp"), None),
            P("section", ("ctx", "fsdp"), None),
            P("section", ("ctx", "fsdp"), None),
            P("section", ("ctx", "fsdp")),
            P("section", ("ctx", "fsdp"), None),
            P("section", "ctx", "fsdp", None),
            P("section", "ctx", "fsdp", None),
        ),
        check_vma=False,
    )
```

time: 2990 us -> 1240 us (0.41)
  local copies, waits for them, and re-layouts: 814 us -> 88.9 us
  blocking collectives: 555 us -> 0 us
  matrix products: 491 us -> 0.17 us
  Pallas kernels: 0 us -> 219 us
  other arithmetic: 299 us -> 92.9 us
  starting transfers between devices: 63.2 us -> 246 us
  waiting for transfers between devices: 729 us -> 560 us
    dot_general x105 -> x1, matrix products: 491 us -> 0.17 us  [shards(): jnp.dot(named.astype(BF16).reshape(-1, rows), earlier, preferred_element_...]
    all_gather x8 -> x4, waiting for transfers between devices: 441 us -> 67.5 us  [the longest x2 67.5 us: shards(): lax.all_gather(up_shards[layer], 'fsdp', axis=1, tiled=True)]
    ppermute x4 -> x111, waiting for transfers between devices: 3.3 us -> 353 us  [the longest x63 322 us: exchanged(): lax.ppermute(value, ('section', axis), pairs_within(axis, by, sections))]
    gather x42 -> x0, local copies, waits for them, and re-layouts: 316 us -> none  [the longest x24 103 us: route_gates(): jnp.take_along_axis(logits, route_rows, axis=1)]
    psum x1 -> x0, blocking collectives: 315 us -> none  [shards(): error_all = lax.psum(error_part, ('section', 'ctx', 'fsdp'))]
    ppermute x4 -> x111, starting transfers between devices: 9.12 us -> 246 us  [the longest x39 130 us: swapped(): return lax.ppermute(value, 'section', [(0, 1), (1, 0)])]
    all_to_all x10 -> x0, waiting for transfers between devices: 220 us -> none  [the longest x3 109 us: layer_backward(): lax.all_to_all(grad_rows.reshape(slots, width), 'ctx', split_axis=0, conc...]
    pallas_call x0 -> x12, Pallas kernels: none -> 219 us  [the longest x2 73.2 us: experts_backward(): pl.pallas_call(functools.partial(experts_back_kernel, sources, slots), na...]
  transfers between devices with their start and end apart: 27 -> 119, of which waited for: 18 -> 65; matrix products, arithmetic and copies ran while one was open for 28% -> 12% of each run, Pallas kernels for 0% -> 13%
where the time goes in v1:
time: 1240 us; the launch traced here: 1230 us
  waiting for transfers between devices  560 us (45%)
  starting transfers between devices  246 us (20%)
  Pallas kernels  219 us (18%)
  other arithmetic  92.9 us (7%)
  local copies, waits for them, and re-layouts  88.9 us (7%)
  between operations  21.7 us (2%)
    ppermute x63, waiting for transfers between devices, exchanged(): lax.ppermute(value, ('section', axis), pairs_within(axis, by, sections))  322 us
    reduce_scatter x2, waiting for transfers between devices, shards(): lax.psum_scatter(g1, 'fsdp', scatter_dimension=1, tiled=True)  139 us
    ppermute x39, starting transfers between devices, swapped(): return lax.ppermute(value, 'section', [(0, 1), (1, 0)])  130 us
    ppermute x63, starting transfers between devices, exchanged(): lax.ppermute(value, ('section', axis), pairs_within(axis, by, sections))  90.9 us
    pallas_call x2, Pallas kernels, experts_backward(): pl.pallas_call(functools.partial(experts_back_kernel, sources, slots), na...  73.2 us
    all_gather x2, waiting for transfers between devices, shards(): lax.all_gather(up_shards[layer], 'fsdp', axis=1, tiled=True)  67.5 us
    pallas_call x2, Pallas kernels, experts_forward(): pl.pallas_call(functools.partial(experts_kernel, sources, slots), name='e...  49.8 us
    pallas_call x2, Pallas kernels, attend_backward(): pl.pallas_call(functools.partial(attend_back_kernel, devices, len(parts))...  43.2 us
  transfers between devices with their start and end apart: 119, of which 65 were waited for; matrix products, arithmetic and copies ran while one was open for 12% of the time, Pallas kernels for 13%

profile of v1, /device:TPU:9, one launch (start us, length us, event | category | flops | bytes accessed | tf_op | source)
XLA Modules:
  0.0 1228.8 jit_solution(11509659296179406727)
XLA Ops:
  60.6 21.6 %collective-permute-done.30 = bf16[64,3200]{1,0:T(8,128)(2,1)S(1)} collective-permute-done((bf16[64,3200]{1,0:T(8,128)(2,1)S(1)}, bf16[64,3200]{1,0:T(8,128)(2,1)S(1)}, u32[]{:S(2)}, u32[]{:S(2)}) %collective-permute-start.30) | collective-permute-done | bytes 409632 | tf_op jit(solution)/shard_map/ppermute | solution.py:638
  83.0 19.6 %collective-permute-done.31 = bf16[64,3200]{1,0:T(8,128)(2,1)S(1)} collective-permute-done((bf16[64,3200]{1,0:T(8,128)(2,1)S(1)}, bf16[64,3200]{1,0:T(8,128)(2,1)S(1)}, u32[]{:S(2)}, u32[]{:S(2)}) %collective-permute-start.31) | collective-permute-done | bytes 409632 | tf_op jit(solution)/shard_map/ppermute | solution.py:638
  103.4 22.8 %collective-permute-done.32 = bf16[64,3200]{1,0:T(8,128)(2,1)S(1)} collective-permute-done((bf16[64,3200]{1,0:T(8,128)(2,1)S(1)}, bf16[64,3200]{1,0:T(8,128)(2,1)S(1)}, u32[]{:S(2)}, u32[]{:S(2)}) %collective-permute-start.32) | collective-permute-done | bytes 409632 | tf_op jit(solution)/shard_map/ppermute | solution.py:638
  130.1 44.7 %collective-permute-start.10 = (s32[2,8,256]{2,1,0:T(8,128)S(1)}, s32[2,8,256]{2,1,0:T(8,128)S(1)}, u32[]{:S(2)}, u32[]{:S(2)}) collective-permute-start(s32[2,8,256]{2,1,0:T(8,128)S(1)} %bitcast.204), channel_id=1, source_target_pairs={{0,16},{16,0},{1,17},{17,1},{2,18},{18,2},{3,19},{19,3},{4,20},{20... | collective-permute-start | bytes 49160 | tf_op jit(solution)/shard_map/ppermute | solution.py:642
  190.6 24.3 %collective-permute-done.34 = bf16[256,3200]{1,0:T(8,128)(2,1)} collective-permute-done((bf16[256,3200]{1,0:T(8,128)(2,1)}, bf16[256,3200]{1,0:T(8,128)(2,1)}, u32[]{:S(2)}, u32[]{:S(2)}) %collective-permute-start.34) | collective-permute-done | bytes 1638432 | tf_op jit(solution)/shard_map/ppermute | solution.py:638
  263.8 14.1 %attend.2 = (bf16[256,1024]{1,0:T(8,128)(2,1)}, f32[4,2,512]{2,1,0:T(2,128)}, f32[256,1024]{1,0:T(8,128)}, bf16[272,1024]{1,0:T(8,128)(2,1)}) custom-call(s32[2]{0:T(128)} %pad_add_fusion.2.scal, bf16[256,1024]{1,0:T(8,128)(2,1)} %dynamic-slice_bitcast_fusion.2.x, bf16[256,1024]{1,0:T(8,128)(2,1)} %get-tuple-element.69.q.rest_10_, ...), custom_call_target="tpu_custom_call" | custom-call | flops 2684354560 | bytes 9437184 | tf_op jit(solution)/shard_map/attend/pallas_call | solution.py:211
  283.1 10.8 collective-permute-done.18
  306.4 25.0 %experts_forward.2 = (bf16[4,640,1024]{2,1,0:T(8,128)(2,1)}, f32[4,640,1024]{2,1,0:T(8,128)}, bf16[4,640,1024]{2,1,0:T(8,128)(2,1)}, f32[8,4,256]{2,1,0:T(4,128)...) custom-call(s32[1]{0:T(128)} %bitcast.18.scal, bf16[272,1024]{1,0:T(8,128)(2,1)} %get-tuple-element.72.rest_0_, ...), custom_call_target="tpu_custom_call" | custom-call | flops 10468982784 | bytes 20971520 | tf_op jit(solution)/shard_map/experts_forward/pallas_call | solution.py:313
  355.3 12.3 %collective-permute-done.27 = bf16[256,1024]{1,0:T(8,128)(2,1)S(1)} collective-permute-done((bf16[256,1024]{1,0:T(8,128)(2,1)}, bf16[256,1024]{1,0:T(8,128)(2,1)S(1)}, u32[]{:S(2)}, u32[]{:S(2)}) %collective-permute-start.27) | collective-permute-done | bytes 524320 | tf_op jit(solution)/shard_map/ppermute | solution.py:638
  399.4 13.9 %attend.3 = (bf16[256,1024]{1,0:T(8,128)(2,1)}, f32[4,2,512]{2,1,0:T(2,128)}, f32[256,1024]{1,0:T(8,128)}, bf16[272,1024]{1,0:T(8,128)(2,1)}) custom-call(s32[2]{0:T(128)} %pad_add_fusion.2.scal, bf16[256,1024]{1,0:T(8,128)(2,1)} %add_convert_fusion.4.x, bf16[256,1024]{1,0:T(8,128)(2,1)} %get-tuple-element.75.q.rest_10_, ...), custom_call_target="tpu_custom_call" | custom-call | flops 2684354560 | bytes 9437184 | tf_op jit(solution)/shard_map/attend/pallas_call | solution.py:211
  442.9 67.5 %all-gather.9.cloned.1.call-done.rest_9_.rest_13_ = bf16[4,1024,1024]{2,1,0:T(8,128)(2,1)} async-done(((bf16[4,256,1024]{2,1,0:T(8,128)(2,1)}), bf16[4,1024,1024]{2,1,0:T(8,128)(2,1)}) %all-gather.9.cloned.1.call-update) | async-done | bytes 8388624 | tf_op jit(solution)/shard_map/all_gather | solution.py:709
  511.2 24.8 %experts_forward.3 = (bf16[4,640,1024]{2,1,0:T(8,128)(2,1)}, f32[4,640,1024]{2,1,0:T(8,128)}, bf16[4,640,1024]{2,1,0:T(8,128)(2,1)}, f32[8,4,256]{2,1,0:T(4,128)...) custom-call(s32[1]{0:T(128)} %bitcast.18.scal, bf16[272,1024]{1,0:T(8,128)(2,1)} %get-tuple-element.78.rest_0_, ...), custom_call_target="tpu_custom_call" | custom-call | flops 10468982784 | bytes 20971520 | tf_op jit(solution)/shard_map/experts_forward/pallas_call | solution.py:313
  556.5 11.3 collective-permute-done.53
  587.6 11.1 collective-permute-start.60
  601.5 36.7 %experts_backward.2 = (bf16[4,1024,1024]{2,1,0:T(8,128)(2,1)}, bf16[4,512,1024]{2,1,0:T(8,128)(2,1)}, f32[4,1,1024]{2,1,0:T(1,128)}, bf16[4,256,1024]{2,1,0:T(8,128)(2,1)}, bf16[4,256,1024]{2,1,0:T(8,128)(2,1)}) custom-call(bf16[272,1024]{1,0:T(8,128)(2,1)} %pad_maximum_fusion.2.rest_0_, bf16[272,1024]{1,0:T(8,128)(2,1)} %collective-permute-done.55.rest_1_, ...), custom_call_target="tpu_custom_call" | custom-call | flops 18522046464 | bytes 36700160 | tf_op jit(solution)/shard_map/experts_backward/pallas_call | solution.py:427
  657.4 11.2 collective-permute-done.68.rest_4_
  669.4 21.7 %attend_backward.2 = (f32[256,1024]{1,0:T(8,128)}, bf16[1024,1024]{1,0:T(8,128)(2,1)}, f32[1,1024]{1,0:T(1,128)}, bf16[256,1024]{1,0:T(8,128)(2,1)}, bf16[2,256,...) custom-call(s32[2]{0:T(128)} %pad_add_fusion.2.scal, ...), custom_call_target="tpu_custom_call" | custom-call | flops 6442450944 | bytes 19922944 | tf_op jit(solution)/shard_map/attend_backward/pallas_call | solution.py:528
  704.0 11.3 collective-permute-done.71.rest_3_
  757.9 36.5 %experts_backward.3 = (bf16[4,1024,1024]{2,1,0:T(8,128)(2,1)}, bf16[4,512,1024]{2,1,0:T(8,128)(2,1)}, f32[4,1,1024]{2,1,0:T(1,128)}, bf16[4,256,1024]{2,1,0:T(8,128)(2,1)}, bf16[4,256,1024]{2,1,0:T(8,128)(2,1)}) custom-call(bf16[272,1024]{1,0:T(8,128)(2,1)} %copy-done.51, bf16[272,1024]{1,0:T(8,128)(2,1)} %copy-done.77, ...), custom_call_target="tpu_custom_call" | custom-call | flops 18522046464 | bytes 36700160 | tf_op jit(solution)/shard_map/experts_backward/pallas_call | solution.py:427
  818.2 11.1 collective-permute-done.85.rest_4_
  829.3 21.5 %attend_backward.3 = (f32[256,1024]{1,0:T(8,128)}, bf16[1024,1024]{1,0:T(8,128)(2,1)}, f32[1,1024]{1,0:T(1,128)}, bf16[256,1024]{1,0:T(8,128)(2,1)}, bf16[2,256,...) custom-call(s32[2]{0:T(128)} %pad_add_fusion.2.scal, ...), custom_call_target="tpu_custom_call" | custom-call | flops 6442450944 | bytes 19922944 | tf_op jit(solution)/shard_map/attend_backward/pallas_call | solution.py:528
  977.3 16.6 %collective-permute-start.110 = (bf16[4,128,1024]{2,1,0:T(8,128)(2,1)}, bf16[4,128,1024]{2,1,0:T(8,128)(2,1)}, u32[]{:S(2)}, u32[]{:S(2)}) collective-permute-start(bf16[4,128,1024]{2,1,0:T(8,128)(2,1)} %broadcast_select_fusion.4), channel_id=1, source_target_pairs={{0,16},{16,0},{1,17},{17,1},{2,18},{18,2},{3,19},{19,3},{4,20},{20... | collective-permute-start | bytes 3145736 | tf_op jit(solution)/shard_map/ppermute | solution.py:642
  1006.0 28.7 %collective-permute-done.104 = bf16[256,3200]{1,0:T(8,128)(2,1)} collective-permute-done((bf16[256,3200]{1,0:T(8,128)(2,1)}, bf16[256,3200]{1,0:T(8,128)(2,1)}, u32[]{:S(2)}, u32[]{:S(2)}) %collective-permute-start.104) | collective-permute-done | bytes 1638432 | tf_op jit(solution)/shard_map/ppermute | solution.py:638
  1045.9 138.6 %reduce-scatter.5.cloned.1.call-done = bf16[4,256,1024]{2,1,0:T(8,128)(2,1)} async-done(((bf16[4,1024,1024]{2,1,0:T(8,128)(2,1)}), bf16[4,256,1024]{2,1,0:T(8,128)(2,1)}) %reduce-scatter.5.cloned.1.call-update) | async-done | bytes 2097168 | tf_op jit(solution)/shard_map/reduce_scatter | solution.py:868
  (543 shorter events, 549.4 us)
Async XLA Ops:
  7.2 296.1 %all-gather.7.cloned.1.call-start = ((), (), s32[]{:S(2)}) async-start(), calls=%async_computation.5 | async-start | bytes 5242880 | tf_op jit(solution)/shard_map/all_gather | solution.py:710
  15.7 290.2 %all-gather.5.cloned.1.call-start = ((), (), s32[]{:S(2)}) async-start(), calls=%async_computation.4 | async-start | bytes 10485760 | tf_op jit(solution)/shard_map/all_gather | solution.py:709
  24.3 418.7 %all-gather.11.cloned.1.call-start = ((), (), s32[]{:S(2)}) async-start(), calls=%async_computation.7 | async-start | bytes 5242880 | tf_op jit(solution)/shard_map/all_gather | solution.py:710
  36.3 474.1 %all-gather.9.cloned.1.call-start = ((), (), s32[]{:S(2)}) async-start(), calls=%async_computation.6 | async-start | bytes 10485760 | tf_op jit(solution)/shard_map/all_gather | solution.py:709
  50.9 176.1 %collective-permute-start.6 = (bf16[1024,3200]{1,0:T(8,128)(2,1)}, bf16[1024,3200]{1,0:T(8,128)(2,1)}, u32[]{:S(2)}, u32[]{:S(2)}) collective-permute-start(bf16[1024,3200]{1,0:T(8,128)(2,1)} %constant_dynamic-update-slice_fusion.7), channel_id=1, source_target_pairs={{0,16},{1,17},{2,18},{3,19},{4,20},{5,21},{6,22},{7,23},{8,24},{9,... | collective-permute-start | bytes 19660808 | tf_op jit(solution)/shard_map/ppermute | solution.py:730
  58.5 67.7 %collective-permute-start.32 = (bf16[64,3200]{1,0:T(8,128)(2,1)S(1)}, bf16[64,3200]{1,0:T(8,128)(2,1)S(1)}, u32[]{:S(2)}, u32[]{:S(2)}) collective-permute-start(bf16[64,3200]{1,0:T(8,128)(2,1)S(1)} %concatenate.57), channel_id=1, source_target_pairs={{16,19},{17,18},{18,17},{19,16},{20,23},{21,22},{22,21},{23,20},{2... | collective-permute-start | bytes 1228808 | tf_op jit(solution)/shard_map/ppermute | solution.py:638
  127.0 62.3 %collective-permute-start.33 = (bf16[256,3200]{1,0:T(8,128)(2,1)}, bf16[256,3200]{1,0:T(8,128)(2,1)S(1)}, u32[]{:S(2)}, u32[]{:S(2)}) collective-permute-start(bf16[256,3200]{1,0:T(8,128)(2,1)} %constant_dynamic-update-slice_fusion.4), channel_id=1, source_target_pairs={{16,20},{20,16},{24,28},{28,24},{17,21},{21,17},{25,29},{29,25},{1... | collective-permute-start | bytes 4915208 | tf_op jit(solution)/shard_map/ppermute | solution.py:638
  130.1 96.9 %collective-permute-start.10 = (s32[2,8,256]{2,1,0:T(8,128)S(1)}, s32[2,8,256]{2,1,0:T(8,128)S(1)}, u32[]{:S(2)}, u32[]{:S(2)}) collective-permute-start(s32[2,8,256]{2,1,0:T(8,128)S(1)} %bitcast.204), channel_id=1, source_target_pairs={{0,16},{16,0},{1,17},{17,1},{2,18},{18,2},{3,19},{19,3},{4,20},{20... | collective-permute-start | bytes 49160 | tf_op jit(solution)/shard_map/ppermute | solution.py:642
  183.4 791.5 %reduce-scatter.11.cloned.1.call-start = ((), (), s32[]{:S(2)}) async-start(), calls=%async_computation.11 | async-start | bytes 5242880 | tf_op jit(solution)/shard_map/reduce_scatter | solution.py:867
  220.4 123.9 %collective-permute-start.36 = (bf16[1024,3200]{1,0:T(8,128)(2,1)}, bf16[1024,3200]{1,0:T(8,128)(2,1)}, u32[]{:S(2)}, u32[]{:S(2)}) collective-permute-start(bf16[1024,3200]{1,0:T(8,128)(2,1)} %constant_dynamic-update-slice_fusion), channel_id=1, source_target_pairs={{16,0},{17,1},{18,2},{19,3},{20,4},{21,5},{22,6},{23,7},{24,8},{25... | collective-permute-start | bytes 19660808 | tf_op jit(solution)/shard_map/ppermute | solution.py:730
  416.9 93.5 %collective-permute-start.43 = (bf16[272,1024]{1,0:T(8,128)(2,1)}, bf16[272,1024]{1,0:T(8,128)(2,1)S(1)}, u32[]{:S(2)}, u32[]{:S(2)}) collective-permute-start(bf16[272,1024]{1,0:T(8,128)(2,1)} %get-tuple-element.78.rest_0_), channel_id=1, source_target_pairs={{0,16},{16,0},{1,17},{17,1},{2,18},{18,2},{3,19},{19,3},{4,20},{20... | collective-permute-start | bytes 1671176 | tf_op jit(solution)/shard_map/ppermute | solution.py:642
  425.7 84.7 %collective-permute-start.44 = (bf16[272,1024]{1,0:T(8,128)(2,1)S(1)}, bf16[272,1024]{1,0:T(8,128)(2,1)}, u32[]{:S(2)}, u32[]{:S(2)}) collective-permute-start(bf16[272,1024]{1,0:T(8,128)(2,1)S(1)} %collective-permute-done.40.rest_1_), channel_id=1, source_target_pairs={{0,16},{16,0},{1,17},{17,1},{2,18},{18,2},{3,19},{19,3},{4,20},{20... | collective-permute-start | bytes 1671176 | tf_op jit(solution)/shard_map/ppermute | solution.py:642
  432.9 77.5 %collective-permute-start.45 = (bf16[272,1024]{1,0:T(8,128)(2,1)S(1)}, bf16[272,1024]{1,0:T(8,128)(2,1)}, u32[]{:S(2)}, u32[]{:S(2)}) collective-permute-start(bf16[272,1024]{1,0:T(8,128)(2,1)S(1)} %collective-permute-done.41.rest_2_), channel_id=1, source_target_pairs={{0,16},{16,0},{1,17},{17,1},{2,18},{18,2},{3,19},{19,3},{4,20},{20... | collective-permute-start | bytes 1671176 | tf_op jit(solution)/shard_map/ppermute | solution.py:642
  442.9 67.6 %collective-permute-start.46 = (bf16[272,1024]{1,0:T(8,128)(2,1)S(1)}, bf16[272,1024]{1,0:T(8,128)(2,1)}, u32[]{:S(2)}, u32[]{:S(2)}) collective-permute-start(bf16[272,1024]{1,0:T(8,128)(2,1)S(1)} %collective-permute-done.42.rest_3_), channel_id=1, source_target_pairs={{0,16},{16,0},{1,17},{17,1},{2,18},{18,2},{3,19},{19,3},{4,20},{20... | collective-permute-start | bytes 1671176 | tf_op jit(solution)/shard_map/ppermute | solution.py:642
  638.2 336.7 %reduce-scatter.9.cloned.1.call-start = ((), (), s32[]{:S(2)}) async-start(), calls=%async_computation.10 | async-start | bytes 5242880 | tf_op jit(solution)/shard_map/reduce_scatter | solution.py:867
  794.4 251.5 %reduce-scatter.7.cloned.1.call-start = ((), (), s32[]{:S(2)}) async-start(), calls=%async_computation.9 | async-start | bytes 10485760 | tf_op jit(solution)/shard_map/reduce_scatter | solution.py:868
  795.2 389.4 %reduce-scatter.5.cloned.1.call-start = ((), (), s32[]{:S(2)}) async-start(), calls=%async_computation.8 | async-start | bytes 10485760 | tf_op jit(solution)/shard_map/reduce_scatter | solution.py:868
  968.6 66.1 %collective-permute-start.104 = (bf16[256,3200]{1,0:T(8,128)(2,1)}, bf16[256,3200]{1,0:T(8,128)(2,1)}, u32[]{:S(2)}, u32[]{:S(2)}) collective-permute-start(bf16[256,3200]{1,0:T(8,128)(2,1)} %get-tuple-element.189), channel_id=1, source_target_pairs={{16,24},{20,28},{24,16},{28,20},{17,25},{21,29},{25,17},{29,21},{1... | collective-permute-start | bytes 4915208 | tf_op jit(solution)/shard_map/ppermute | solution.py:638
  971.9 64.2 %collective-permute-start.105 = (bf16[256,3200]{1,0:T(8,128)(2,1)S(1)}, bf16[256,3200]{1,0:T(8,128)(2,1)}, u32[]{:S(2)}, u32[]{:S(2)}) collective-permute-start(bf16[256,3200]{1,0:T(8,128)(2,1)S(1)} %get-tuple-element.188), channel_id=1, source_target_pairs={{16,28},{20,24},{24,20},{28,16},{17,29},{21,25},{25,21},{29,17},{1... | collective-permute-start | bytes 4915208 | tf_op jit(solution)/shard_map/ppermute | solution.py:638
  977.3 210.4 %collective-permute-start.110 = (bf16[4,128,1024]{2,1,0:T(8,128)(2,1)}, bf16[4,128,1024]{2,1,0:T(8,128)(2,1)}, u32[]{:S(2)}, u32[]{:S(2)}) collective-permute-start(bf16[4,128,1024]{2,1,0:T(8,128)(2,1)} %broadcast_select_fusion.4), channel_id=1, source_target_pairs={{0,16},{16,0},{1,17},{17,1},{2,18},{18,2},{3,19},{19,3},{4,20},{20... | collective-permute-start | bytes 3145736 | tf_op jit(solution)/shard_map/ppermute | solution.py:642
  998.5 193.0 %collective-permute-start.100 = (bf16[64,3200]{1,0:T(8,128)(2,1)}, bf16[64,3200]{1,0:T(8,128)(2,1)S(1)}, u32[]{:S(2)}, u32[]{:S(2)}) collective-permute-start(bf16[64,3200]{1,0:T(8,128)(2,1)} %get-tuple-element.230), channel_id=1, source_target_pairs={{0,2},{1,3},{2,0},{3,1},{4,6},{5,7},{6,4},{7,5},{8,10},{9,11},{10,... | collective-permute-start | bytes 1228808 | tf_op jit(solution)/shard_map/ppermute | solution.py:638
  1005.3 188.3 %collective-permute-start.101 = (bf16[64,3200]{1,0:T(8,128)(2,1)}, bf16[64,3200]{1,0:T(8,128)(2,1)S(1)}, u32[]{:S(2)}, u32[]{:S(2)}) collective-permute-start(bf16[64,3200]{1,0:T(8,128)(2,1)} %get-tuple-element.229), channel_id=1, source_target_pairs={{0,3},{1,2},{2,1},{3,0},{4,7},{5,6},{6,5},{7,4},{8,11},{9,10},{10,... | collective-permute-start | bytes 1228808 | tf_op jit(solution)/shard_map/ppermute | solution.py:638
  1034.7 162.8 %collective-permute-start.99 = (bf16[64,3200]{1,0:T(8,128)(2,1)}, bf16[64,3200]{1,0:T(8,128)(2,1)}, u32[]{:S(2)}, u32[]{:S(2)}) collective-permute-start(bf16[64,3200]{1,0:T(8,128)(2,1)} %get-tuple-element.228), channel_id=1, source_target_pairs={{0,1},{1,0},{2,3},{3,2},{4,5},{5,4},{6,7},{7,6},{8,9},{9,8},{10,11... | collective-permute-start | bytes 1228808 | tf_op jit(solution)/shard_map/ppermute | solution.py:638
  1041.4 156.1 %collective-permute-start.106 = (bf16[64,3200]{1,0:T(8,128)(2,1)}, bf16[64,3200]{1,0:T(8,128)(2,1)}, u32[]{:S(2)}, u32[]{:S(2)}) collective-permute-start(bf16[64,3200]{1,0:T(8,128)(2,1)} %get-tuple-element.231), channel_id=1, source_target_pairs={{16,17},{17,16},{18,19},{19,18},{20,21},{21,20},{22,23},{23,22},{2... | collective-permute-start | bytes 1228808 | tf_op jit(solution)/shard_map/ppermute | solution.py:638
  (183 other events, 2944.1 us)
Sparse Core Ops, SparseCore 0:
  15.8 112.5 all-gather.6
  130.6 149.0 all-gather.4
  281.2 79.2 all-gather.10
  362.5 147.8 all-gather.8
  638.3 76.3 reduce-scatter.10
  794.5 77.1 reduce-scatter.8
  874.7 144.6 reduce-scatter.6
  1021.7 162.7 reduce-scatter.4

commit v2 on v1

v2 whole, which is shorter than its diff:
```python
import functools
import math

import jax
import jax.numpy as jnp
from jax import lax
from jax.experimental import pallas as pl
from jax.experimental.pallas import tpu as pltpu
from jax.sharding import PartitionSpec as P

QH = 16
KVH = 8
HD = 64
EXPERTS = 32
FF_E = 512
TOPK = 8
KW = KVH * HD
EXT = 16

epsilon = 1e-06
rope_base = 10000.0
negative = -1e30
F32 = jnp.float32
BF16 = jnp.bfloat16
VMEM_LIMIT = 60 * 1024 * 1024


def params(grid_dims=0):
    return pltpu.CompilerParams(
        vmem_limit_bytes=VMEM_LIMIT,
        dimension_semantics=("arbitrary",) * grid_dims if grid_dims else None,
    )


def cost(flops, moved, exps=0):
    return pl.CostEstimate(flops=int(flops), bytes_accessed=int(moved), transcendentals=int(exps))


def mm(a, b):
    return jnp.dot(a, b, preferred_element_type=F32)


def mm_nt(a, b):
    return lax.dot_general(a, b, (((1,), (1,)), ((), ())), preferred_element_type=F32)


def mm_tn(a, b):
    return lax.dot_general(a, b, (((0,), (0,)), ((), ())), preferred_element_type=F32)


def fixed(shape):
    return pl.BlockSpec(shape, lambda *_: (0,) * len(shape), pipeline_mode=pl.Buffered(1))


def resident(shape):
    return pl.BlockSpec(shape, lambda *_: (0,) * len(shape))


def lane_index(shape):
    return lax.broadcasted_iota(jnp.int32, shape, len(shape) - 1)


def turn(block, cosine, sine):
    low_half = lane_index(block.shape) % HD < HD // 2
    swapped = jnp.where(
        low_half, pltpu.roll(block, 128 - HD // 2, axis=1), pltpu.roll(block, HD // 2, axis=1)
    )
    return block * cosine + swapped * sine


def rolled(block):
    return pltpu.roll(block.astype(F32), HD, axis=1).astype(BF16)


def key_positions(device, half, devices, shape, dim):
    within = lax.broadcasted_iota(jnp.int32, shape, dim)
    return jnp.where(
        within < half, device * half + within, (2 * devices - 1 - device) * half + within - half
    )


def fill_bias(bias, scal, devices, rows):
    context, length = scal[0], scal[1]
    query_pos = key_positions(context, rows // 2, devices, (rows, rows), 1)
    for k in range(devices):
        key_pos = key_positions(context ^ k, rows // 2, devices, (rows, rows), 0)
        taken = (key_pos <= query_pos) & (key_pos < length)
        bias[k * rows : (k + 1) * rows, :] = jnp.where(taken, 0.0, negative)


def two_heads(block):
    even = lane_index(block.shape) < HD
    zero = jnp.zeros((), block.dtype)
    return jnp.concatenate([jnp.where(even, block, zero), jnp.where(even, zero, block)], axis=0)


def two_heads_doubled(block):
    even = lane_index(block.shape) < HD
    other = rolled(block)
    return jnp.concatenate([jnp.where(even, block, other), jnp.where(even, other, block)], axis=0)


def doubled(block, odd):
    even = lane_index(block.shape) < HD
    other = rolled(block)
    return jnp.where(even, other, block) if odd else jnp.where(even, block, other)


def one_hot(rank_row, slots):
    rows = rank_row.shape[-1]
    index = lax.broadcasted_iota(jnp.int32, (slots, rows), 0).astype(F32)
    return rank_row == index


def project_kernel(x, gain, wq, wm, cosine, sine, q_out, kv_out):
    values = x[...].astype(F32)
    factor = lax.rsqrt(jnp.mean(values * values, axis=-1, keepdims=True) + epsilon)
    normed = (values * factor * gain[...]).astype(BF16)
    cos, sin = cosine[...], sine[...]
    q0 = mm(normed, wq[...])
    for b in range(QH * HD // 128):
        at = slice(b * 128, (b + 1) * 128)
        q_out[:, at] = turn(q0[:, at], cos, sin).astype(BF16)
    kv0 = mm(normed, wm[...])
    for b in range(KW // 128):
        at = slice(b * 128, (b + 1) * 128)
        kv_out[0, :, at] = turn(kv0[:, at], cos, sin).astype(BF16)
    kv_out[1] = kv0[:, KW:].astype(BF16)


def project(x, gain, shared, cosine, sine):
    rows, width = x.shape
    return pl.pallas_call(
        project_kernel,
        name="project",
        grid=(1,),
        in_specs=[
            fixed((rows, width)),
            fixed((1, width)),
            pl.BlockSpec((width, QH * HD), lambda i: (0, 0), pipeline_mode=pl.Buffered(1)),
            pl.BlockSpec((width, 2 * KW), lambda i: (0, 1), pipeline_mode=pl.Buffered(1)),
            fixed((rows, 128)),
            fixed((rows, 128)),
        ],
        out_specs=[resident((rows, QH * HD)), resident((2, rows, KW))],
        out_shape=[
            jax.ShapeDtypeStruct((rows, QH * HD), BF16),
            jax.ShapeDtypeStruct((2, rows, KW), BF16),
        ],
        compiler_params=params(1),
        cost_estimate=cost(2 * rows * width * 2048, 2 * width * 2048 + 8 * rows * width),
    )(x, gain, shared, shared, cosine, sine)


def attend_kernel(devices, scal, x, q, *rest):
    ks, vs, rest = rest[:devices], rest[devices : 2 * devices], rest[2 * devices :]
    wo, gain, router, mask, o_out, lse_out, mid_out, msg_out, bias, held = rest
    rows = x.shape[0]
    step = pl.program_id(0)

    @pl.when(step == 0)
    def _():
        fill_bias(bias, scal, devices, rows)

    keys = jnp.concatenate([r[0] for r in ks], axis=0)
    values = jnp.concatenate([r[0] for r in vs], axis=0)
    block_bias = bias[...]
    both_bias = jnp.concatenate([block_bias, block_bias], axis=1)
    for i in range(2):
        query = two_heads(q[:, i * 128 : (i + 1) * 128])
        scores = mm_nt(doubled(keys, i), query) * (1.0 / math.sqrt(HD)) + both_bias
        top = jnp.max(scores, axis=0, keepdims=True)
        raised = jnp.exp(scores - top)
        total = jnp.sum(raised, axis=0, keepdims=True)
        probs = (raised * (1.0 / total)).astype(BF16)
        lse_out[0, i : i + 1, :] = top + jnp.log(total)
        mixed = mm_tn(values, probs)[i * HD : (i + 1) * HD]
        pair = jnp.concatenate([mixed[:, :rows], mixed[:, rows:]], axis=0)
        at = pl.multiple_of(step * 256 + i * 128, 128)
        held[:, pl.ds(at, 128)] = jnp.transpose(pair).astype(BF16)

    @pl.when(step == pl.num_programs(0) - 1)
    def _():
        attended = held[...]
        o_out[...] = attended
        middle = x[...].astype(F32) + mm(attended, wo[...])
        mid_out[...] = middle
        factor = lax.rsqrt(jnp.mean(middle * middle, axis=-1, keepdims=True) + epsilon)
        normed = (middle * factor * gain[...]).astype(BF16)
        msg_out[:rows, :] = normed
        logits = mm_nt(router[...], normed)
        chosen = mask[...] > 0.5
        top = jnp.max(jnp.where(chosen, logits, negative), axis=0, keepdims=True)
        raised = jnp.where(chosen, jnp.exp(jnp.where(chosen, logits - top, 0.0)), 0.0)
        gates = raised / jnp.sum(raised, axis=0, keepdims=True)
        high = gates.astype(BF16)
        low = (gates - high.astype(F32)).astype(BF16)
        ext = [high[:EXT], high[EXT:], low[:EXT], low[EXT:]]
        if 4 * rows < x.shape[1]:
            ext.append(jnp.zeros((EXT, x.shape[1] - 4 * rows), BF16))
        msg_out[rows:, :] = jnp.concatenate(ext, axis=1)


def attend(scal, x, q, kvs, shared, gain, router, mask):
    rows, width = x.shape
    devices = len(kvs)
    keys = devices * rows
    kv_specs = [pl.BlockSpec((1, rows, 128), lambda h: (0, 0, h)) for _ in kvs] + [
        pl.BlockSpec((1, rows, 128), lambda h: (1, 0, h)) for _ in kvs
    ]
    return pl.pallas_call(
        functools.partial(attend_kernel, devices),
        name="attend",
        grid=(KVH // 2,),
        in_specs=[
            pl.BlockSpec(memory_space=pltpu.SMEM),
            fixed((rows, width)),
            pl.BlockSpec((rows, 256), lambda h: (0, h)),
            *kv_specs,
            pl.BlockSpec((QH * HD, width), lambda h: (0, 2), pipeline_mode=pl.Buffered(1)),
            fixed((1, width)),
            fixed((EXPERTS, width)),
            fixed((EXPERTS, rows)),
        ],
        out_specs=[
            resident((rows, QH * HD)),
            pl.BlockSpec((1, 2, 2 * rows), lambda h: (h, 0, 0)),
            resident((rows, width)),
            resident((rows + EXT, width)),
        ],
        out_shape=[
            jax.ShapeDtypeStruct((rows, QH * HD), BF16),
            jax.ShapeDtypeStruct((KVH // 2, 2, 2 * rows), F32),
            jax.ShapeDtypeStruct((rows, width), F32),
            jax.ShapeDtypeStruct((rows + EXT, width), BF16),
        ],
        scratch_shapes=[pltpu.VMEM((keys, rows), F32), pltpu.VMEM((rows, QH * HD), BF16)],
        compiler_params=params(1),
        cost_estimate=cost(
            4 * rows * keys * QH * HD * 2 + 2 * rows * width * width,
            2 * width * width + 4 * keys * width + 12 * rows * width,
            rows * keys * QH,
        ),
    )(scal, x, q, *kvs, *kvs, shared, gain, router, mask)


def hot_rows(rank, j, slots):
    local = rank.shape[1]
    return jnp.concatenate(
        [
            jnp.where(one_hot(rank[j, i : i + 1, :], slots), 1.0, 0.0).astype(BF16)
            for i in range(local)
        ],
        axis=0,
    )


def combine(rank, held, prior, outs, buffers, slots):
    held = held if isinstance(held, list) else [held]
    prior_buffer, out_buffer, prior_sems, out_sems = buffers
    width = held[0].shape[-1]
    depth = out_buffer.shape[0]
    count = len(outs)
    fetch = lambda j: pltpu.make_async_copy(
        prior[j], prior_buffer.at[j % depth], prior_sems.at[j % depth]
    )
    send = lambda j: pltpu.make_async_copy(
        out_buffer.at[j % depth], outs[j], out_sems.at[j % depth]
    )
    for j in range(min(depth - 1, count) if prior else 0):
        fetch(j).start()
    for j in range(count):
        rows = [part[:, j].reshape(part.shape[0] * slots, width) for part in held]
        rows = rows[0] if len(rows) == 1 else jnp.concatenate(rows, axis=0)
        total = mm_tn(hot_rows(rank, j, slots), rows)
        if prior:
            if j + depth - 1 < count:
                fetch(j + depth - 1).start()
            fetch(j).wait()
            total = total + prior_buffer[j % depth].astype(F32)
        if j >= depth:
            send(j - depth).wait()
        out_buffer[j % depth] = total.astype(BF16)
        send(j).start()
    for j in range(max(0, count - depth), count):
        send(j).wait()


def gate_columns(rank, values, step, sources, slots):
    columns = []
    for j in sources:
        hot = one_hot(rank[j, pl.ds(step, 1), :], slots)
        columns.append(jnp.sum(jnp.where(hot, values(j), 0.0), axis=1, keepdims=True))
    return jnp.concatenate(columns, axis=0)


def finish_kernel(count, *refs):
    terms, (middle, goal, valid, hidden, mixed_out, grad_out, message, error) = (
        refs[:count],
        refs[count:],
    )
    rows, width = middle.shape
    mixed = terms[0][...].astype(F32)
    for term in terms[1:]:
        mixed = mixed + term[...].astype(F32)
    output = middle[...] + mixed
    hidden[...] = output.astype(BF16)
    mixed_out[...] = mixed
    grad = (output - goal[...].astype(F32)) * valid[...]
    grad_out[...] = grad
    error[...] = 0.5 * jnp.sum(
        jnp.sum(grad * grad, axis=1, keepdims=True), axis=0, keepdims=True
    )
    fill_message(message, grad, mixed)


def fill_message(message, grad, mixed):
    rows, width = grad.shape
    message[:rows, :] = grad.astype(BF16)
    inner = jnp.transpose(
        jnp.broadcast_to(jnp.sum(grad * mixed, axis=1, keepdims=True), (rows, 128))
    )[:EXT]
    high = inner.astype(BF16)
    low = (inner - high.astype(F32)).astype(BF16)
    first = lax.broadcasted_iota(jnp.int32, (EXT, rows), 0) == 0
    message[rows:, :rows] = jnp.where(first, high, low)
    message[rows:, rows:] = jnp.zeros((EXT, width - rows), BF16)


def finish(terms, middle, goal, valid):
    rows, width = middle.shape
    return pl.pallas_call(
        functools.partial(finish_kernel, len(terms)),
        name="finish",
        out_shape=[
            jax.ShapeDtypeStruct((rows, width), BF16),
            jax.ShapeDtypeStruct((rows, width), F32),
            jax.ShapeDtypeStruct((rows, width), F32),
            jax.ShapeDtypeStruct((rows + EXT, width), BF16),
            jax.ShapeDtypeStruct((1, 1), F32),
        ],
        compiler_params=params(),
        cost_estimate=cost(8 * rows * width, 24 * rows * width),
    )(*terms, middle, goal, valid)


def message_kernel(grad, mixed, message):
    fill_message(message, grad[...], mixed[...])


def grad_message(grad, mixed):
    rows, width = grad.shape
    return pl.pallas_call(
        message_kernel,
        name="grad_message",
        out_shape=jax.ShapeDtypeStruct((rows + EXT, width), BF16),
        compiler_params=params(),
        cost_estimate=cost(4 * rows * width, 10 * rows * width),
    )(grad, mixed)


def dispatch_kernel(sources, slots, backward, scal, *rest):
    msgs, (rank, x_out, side_out, arrived, picked, in_sems, out_sems) = (
        rest[:sources],
        rest[sources:],
    )
    local, rows = rank.shape[1:]
    fetch = lambda j: pltpu.make_async_copy(msgs[j], arrived.at[j], in_sems.at[j])
    send = lambda j: pltpu.make_async_copy(picked.at[j], x_out.at[:, j], out_sems.at[j])
    for j in range(sources):
        fetch(j).start()
    pick_row = lax.broadcasted_iota(jnp.int32, (EXT, 4 * rows), 0)
    for j in range(sources):
        fetch(j).wait()
        taken = mm(hot_rows(rank, j, slots), arrived[j, :rows, :]).astype(BF16)
        for i in range(local):
            picked[j, i] = taken[i * slots : (i + 1) * slots]
        send(j).start()
        if backward:
            ext = arrived[j, rows:, :rows].astype(F32)
            side_out[j] = ext[0:1, :] + ext[1:2, :]
        else:
            ext = arrived[j, rows:, : 4 * rows].astype(F32)
            for i in range(local):
                expert = scal[0] + i
                row = jnp.sum(jnp.where(pick_row == expert % EXT, ext, 0.0), axis=0, keepdims=True)
                high = jnp.where(expert < EXT, row[:, :rows], row[:, rows : 2 * rows])
                low = jnp.where(expert < EXT, row[:, 2 * rows : 3 * rows], row[:, 3 * rows :])
                side_out[j, i : i + 1, :] = high + low
    for j in range(sources):
        send(j).wait()


def dispatch(scal, msgs, rank, slots, backward):
    sources, local, rows = rank.shape
    width = msgs[0].shape[1]
    anywhere = pl.BlockSpec(memory_space=pl.ANY)
    side = (sources, 1 if backward else local, rows)
    taken, beside = pl.pallas_call(
        functools.partial(dispatch_kernel, sources, slots, backward),
        name="dispatch",
        grid=(1,),
        in_specs=[
            pl.BlockSpec(memory_space=pltpu.SMEM),
            *[anywhere for _ in msgs],
            fixed(rank.shape),
        ],
        out_specs=[anywhere, resident(side)],
        out_shape=[
            jax.ShapeDtypeStruct((local, sources, slots, width), BF16),
            jax.ShapeDtypeStruct(side, F32),
        ],
        scratch_shapes=[
            pltpu.VMEM((sources, rows + EXT, width), BF16),
            pltpu.VMEM((sources, local, slots, width), BF16),
            pltpu.SemaphoreType.DMA((sources,)),
            pltpu.SemaphoreType.DMA((sources,)),
        ],
        compiler_params=params(1),
        cost_estimate=cost(
            2 * local * sources * slots * rows * width, 2 * sources * width * (rows + local * slots)
        ),
    )(scal, *msgs, rank)
    return taken.reshape(local, sources * slots, width), beside


def fill_weights(scal, blocks, w1, w2):
    up = w1.shape[0] // len(blocks)
    down = w2.shape[0] // len(blocks)
    for k, block in enumerate(blocks):
        at = scal[1 + k]
        w1[pl.ds(pl.multiple_of(at * up, up), up), :] = block[0, :up]
        w2[pl.ds(pl.multiple_of(at * down, down), down), :] = block[0, up:]


def experts_kernel(sources, depth, slots, chained, scal, *rest):
    prior = ()
    if chained:
        prior, rest = rest[:sources], rest[sources:]
    rank, gates, xs, rest = *rest[:3], rest[3:]
    blocks, rest = rest[:depth], rest[depth:]
    gu_out, y_out, rest = *rest[:2], rest[2:]
    outs, rest = rest[:sources], rest[sources:]
    held, w1, w2 = rest[:3]
    width = held.shape[-1]
    step, part = pl.program_id(0), pl.program_id(1)
    portions = sources // (xs.shape[1] // slots)
    portion = sources // portions

    @pl.when(part == 0)
    def _():
        fill_weights(scal, blocks, w1, w2)

    gate_up = mm(xs[0], w1[...])
    gu_out[0] = gate_up
    gate, up = gate_up[:, :FF_E], gate_up[:, FF_E:]
    activated = (gate * jax.nn.sigmoid(gate) * up).astype(BF16)
    out = mm(activated, w2[...]).astype(BF16)
    y_out[0] = out
    column = gate_columns(
        rank,
        lambda j: gates[j, pl.ds(step, 1), :],
        step,
        [part * portion + n for n in range(portion)],
        slots,
    )
    held[step, pl.ds(part * portion, portion)] = (
        (column * out.astype(F32)).astype(BF16).reshape(portion, slots, width)
    )

    @pl.when((step == pl.num_programs(0) - 1) & (part == portions - 1))
    def _():
        combine(rank, held, prior, outs, rest[3:], slots)


def weight_specs(blocks, depth):
    arrays = blocks if len(blocks) == depth else blocks * depth
    rows = arrays[0].shape[1] // (depth // len(blocks))
    width = arrays[0].shape[2]
    specs = [
        pl.BlockSpec((1, rows, width), lambda e, r, f=(k if len(blocks) == 1 else 0): (e, f, 0))
        for k in range(depth)
    ]
    return arrays, specs


def stream_scratch(rows, width):
    return [
        pltpu.VMEM((4, rows, width), BF16),
        pltpu.VMEM((4, rows, width), BF16),
        pltpu.SemaphoreType.DMA((4,)),
        pltpu.SemaphoreType.DMA((4,)),
    ]


def experts_forward(scal, xs, rank, gates, blocks, depth, slots, first, prior=()):
    sources, local, rows = rank.shape
    width = xs.shape[2]
    portions = max(1, sources // 8)
    count = sources * slots
    arrays, specs = weight_specs(blocks, depth)
    anywhere = pl.BlockSpec(memory_space=pl.ANY)
    each = lambda shape, base=0: pl.BlockSpec((1,) + shape, lambda e, r: (e + base, r, 0))
    outs = pl.pallas_call(
        functools.partial(experts_kernel, sources, depth, slots, bool(prior)),
        name="experts_forward",
        grid=(local, portions),
        in_specs=[
            pl.BlockSpec(memory_space=pltpu.SMEM),
            *[anywhere for _ in prior],
            fixed((sources, local, rows)),
            fixed((sources, local, rows)),
            each((count // portions, width), first),
            *specs,
        ],
        out_specs=[
            each((count // portions, 2 * FF_E)),
            each((count // portions, width)),
            *[anywhere for _ in range(sources)],
        ],
        out_shape=[
            jax.ShapeDtypeStruct((local, count, 2 * FF_E), F32),
            jax.ShapeDtypeStruct((local, count, width), BF16),
            *[jax.ShapeDtypeStruct((rows, width), BF16) for _ in range(sources)],
        ],
        scratch_shapes=[
            pltpu.VMEM((local, sources, slots, width), BF16),
            pltpu.VMEM((width, 2 * FF_E), BF16),
            pltpu.VMEM((FF_E, width), BF16),
            *stream_scratch(rows, width),
        ],
        compiler_params=params(2),
        cost_estimate=cost(
            2 * local * count * width * 3 * FF_E * 1.3, 8 * local * count * width, local * count * FF_E
        ),
    )(scal, *prior, rank, gates, xs, *arrays)
    return outs[:2], list(outs[2:])


def experts_back_kernel(sources, depth, slots, mode, scal, *rest):
    last, order = mode
    earlier = ()
    if last:
        full_rank, rest = rest[0], rest[1:]
        earlier, rest = rest[: len(order) - 1], rest[len(order) - 1 :]
    rank, gates, inners, grads, xs, gu, ys, router, rest = *rest[:8], rest[8:]
    blocks, rest = rest[:depth], rest[depth:]
    grad_out_ref, router_out, rest = *rest[:2], rest[2:]
    outs, rest = (rest[:sources], rest[sources:]) if last else (rest[:1], rest[1:])
    held, w1, w2, sum1, sum2 = rest[:5]
    width = w1.shape[0]
    step, part = pl.program_id(0), pl.program_id(1)
    portions = sources // (xs.shape[1] // slots)
    portion = sources // portions

    @pl.when(part == 0)
    def _():
        fill_weights(scal, blocks, w1, w2)

    mine = [part * portion + n for n in range(portion)]
    gate_column = gate_columns(rank, lambda j: gates[j, pl.ds(step, 1), :], step, mine, slots)
    inner_column = gate_columns(rank, lambda j: inners[j], step, mine, slots)
    grad_out = grads[0].astype(F32)
    grad_y = (gate_column * grad_out).astype(BF16)
    given = jnp.sum(grad_out * ys[0].astype(F32), axis=1, keepdims=True)
    grad_logit = gate_column * (given - inner_column)
    gate, up = gu[0, :, :FF_E], gu[0, :, FF_E:]
    sigmoid = jax.nn.sigmoid(gate)
    silu = gate * sigmoid
    activated = (silu * up).astype(BF16)
    down_part = mm_tn(activated, grad_y)
    grad_act = mm_nt(grad_y, w2[...])
    grad_gate = grad_act * up * sigmoid * (1.0 + gate * (1.0 - sigmoid))
    grad_up = grad_act * silu
    grad_gate_up = jnp.concatenate([grad_gate.astype(BF16), grad_up.astype(BF16)], axis=1)
    taken = xs[0]
    up_part = mm_tn(taken, grad_gate_up)
    router_part = jnp.sum(taken.astype(F32) * grad_logit, axis=0, keepdims=True)
    grad_rows = mm_nt(grad_gate_up, w1[...]) + grad_logit * router[0]
    if last:
        held[step, pl.ds(part * portion, portion)] = grad_rows.astype(BF16).reshape(
            portion, slots, width
        )
    else:
        outs[0][0] = grad_rows.astype(BF16)

    def write(up_total, down_total):
        up_rows, down_rows = width // depth, FF_E // depth
        for f in range(depth):
            top = f * (up_rows + down_rows)
            grad_out_ref[0, top : top + up_rows, :] = up_total[
                f * up_rows : (f + 1) * up_rows
            ].astype(BF16)
            grad_out_ref[0, top + up_rows : top + up_rows + down_rows, :] = down_total[
                f * down_rows : (f + 1) * down_rows
            ].astype(BF16)

    if sum1 is None:
        write(up_part, down_part)
        router_out[0] = router_part
    else:

        @pl.when(part == 0)
        def _():
            sum1[...] = up_part
            sum2[...] = down_part
            router_out[0] = router_part

        @pl.when(part > 0)
        def _():
            sum1[...] += up_part
            sum2[...] += down_part
            router_out[0] += router_part

        @pl.when(part == portions - 1)
        def _():
            write(sum1, sum2)

    if last:

        @pl.when((step == pl.num_programs(0) - 1) & (part == portions - 1))
        def _():
            pieces = list(earlier) + [held]
            combine(full_rank, [pieces[o] for o in order], (), outs, rest[5:], slots)


def experts_backward(
    scal, grads, rank, gates, inners, xs, kept, router, blocks, depth, slots, first, last
):
    sources, local, rows = rank.shape
    width = xs.shape[2]
    portions = max(1, sources // 8)
    count = sources * slots
    gu, ys = kept
    arrays, specs = weight_specs(blocks, depth)
    merged = width + FF_E
    anywhere = pl.BlockSpec(memory_space=pl.ANY)
    each = lambda shape, base=0: pl.BlockSpec((1,) + shape, lambda e, r: (e + base, r, 0))
    whole = lambda shape: pl.BlockSpec((1,) + shape, lambda e, r: (e, 0, 0))
    before = []
    if last:
        before = [last[0]] + [
            part.reshape(part.shape[0], sources, slots, width) for part in last[1]
        ]
    mode = (bool(last), last[2] if last else ())

    def kernel(*refs):
        refs = list(refs)
        if portions == 1:
            at = len(refs) - (4 if last else 0)
            refs[at:at] = [None, None]
        if not last:
            refs[-4:-4] = [None]
        experts_back_kernel(sources, depth, slots, mode, *refs)

    sums = [pltpu.VMEM((width, 2 * FF_E), F32), pltpu.VMEM((FF_E, width), F32)]
    outs = pl.pallas_call(
        kernel,
        name="experts_backward",
        grid=(local, portions),
        in_specs=[
            pl.BlockSpec(memory_space=pltpu.SMEM),
            *[fixed(part.shape) for part in before],
            fixed((sources, local, rows)),
            fixed((sources, local, rows)),
            fixed((sources, 1, rows)),
            each((count // portions, width)),
            each((count // portions, width), first),
            each((count // portions, 2 * FF_E)),
            each((count // portions, width)),
            whole((1, width)),
            *specs,
        ],
        out_specs=[
            whole((merged, width)),
            whole((1, width)),
            *([anywhere] * sources if last else [each((count // portions, width))]),
        ],
        out_shape=[
            jax.ShapeDtypeStruct((local, merged, width), BF16),
            jax.ShapeDtypeStruct((local, 1, width), F32),
            *(
                [jax.ShapeDtypeStruct((rows, width), BF16)] * sources
                if last
                else [jax.ShapeDtypeStruct((local, count, width), BF16)]
            ),
        ],
        scratch_shapes=[
            *([pltpu.VMEM((local, sources, slots, width), BF16)] if last else []),
            pltpu.VMEM((width, 2 * FF_E), BF16),
            pltpu.VMEM((FF_E, width), BF16),
            *(sums if portions > 1 else []),
            *(stream_scratch(rows, width) if last else []),
        ],
        compiler_params=params(2),
        cost_estimate=cost(
            2 * local * count * width * 3 * FF_E * 2.3, 14 * local * count * width, local * count * FF_E
        ),
    )(scal, *before, rank, gates, inners, grads, xs, gu, ys, router, *arrays)
    return outs[0], outs[1], list(outs[2:])


def place_base(place, scal):
    return jnp.where(scal[1] == 0, place[1], place[2])


def place_kernel(places, number, aliased, scal, *refs):
    parts, (up_out, down_out) = refs[: -2 - aliased], refs[-2:]
    step = number(pl.program_id(0))
    up_rows = up_out.shape[1]

    def put(blocks):
        total = blocks[0][0].astype(F32)
        for block in blocks[1:]:
            total = total + block[0].astype(F32)
        up_out[0] = total[:up_rows]
        down_out[0] = total[up_rows:]

    at = 0
    for place in places:
        base, count, terms = place_base(place, scal), place[3], place[4]
        pl.when((scal[0] == place[0]) & (step >= base) & (step < base + count))(
            functools.partial(put, parts[at : at + terms])
        )
        at += terms


def place_experts(scal, pieces, held_experts, up_rows, experts, into=()):
    rows, width = pieces[0][3][0].shape[1:]
    places, specs, arrays = [], [], []
    run = next((i for i in range(1, len(experts)) if experts[i] != experts[0] + i), len(experts))
    skip = experts[run] - experts[run - 1] if run < len(experts) else 1
    number = lambda i: experts[0] + (i // run) * (run - 1 + skip) + i % run
    assert [number(i) for i in range(len(experts))] == list(experts)
    for core, even_base, odd_base, terms in pieces:
        place = (core, even_base, odd_base, terms[0].shape[0], len(terms))
        places.append(place)
        for term in terms:
            arrays.append(term)
            specs.append(
                pl.BlockSpec(
                    (1, rows, width),
                    lambda i, scal, place=place: (
                        jnp.clip(number(i) - place_base(place, scal), 0, place[3] - 1),
                        0,
                        0,
                    ),
                )
            )
    specs += [pl.BlockSpec(memory_space=pl.ANY) for _ in into]
    return pl.pallas_call(
        functools.partial(place_kernel, places, number, len(into)),
        name="place_experts",
        grid_spec=pltpu.PrefetchScalarGridSpec(
            num_scalar_prefetch=1,
            grid=(len(experts),),
            in_specs=specs,
            out_specs=[
                pl.BlockSpec((1, up_rows, width), lambda i, scal: (number(i), 0, 0)),
                pl.BlockSpec((1, rows - up_rows, width), lambda i, scal: (number(i), 0, 0)),
            ],
        ),
        out_shape=[
            jax.ShapeDtypeStruct((held_experts, up_rows, width), F32),
            jax.ShapeDtypeStruct((held_experts, rows - up_rows, width), F32),
        ],
        input_output_aliases={1 + len(arrays) + i: i for i in range(len(into))},
        compiler_params=params(1),
        cost_estimate=cost(0, 8 * len(experts) * rows * width),
    )(scal, *arrays, *into)


def assemble_kernel(devices, depth, scal, *refs):
    owns, others, whole, sem = refs[:devices], refs[devices : 2 * devices], refs[-2], refs[-1]
    piece = whole.shape[0] // (devices * depth)
    for home, blocks in ((1, owns), (0, others)):

        @pl.when(scal[0] == home)
        def _(blocks=blocks):
            for k in range(devices):
                for i in range(depth):
                    to = pl.multiple_of(((scal[1] ^ k) * depth + (scal[2] ^ i)) * piece, piece)
                    pltpu.make_async_copy(
                        blocks[k].at[pl.ds(i * piece, piece)], whole.at[pl.ds(to, piece)], sem
                    ).start()
            pltpu.make_async_copy(whole, whole, sem).wait()


def assemble(scal, owns, others, depth):
    devices = len(owns)
    rows, columns = owns[0].shape
    return pl.pallas_call(
        functools.partial(assemble_kernel, devices, depth),
        name="assemble",
        in_specs=[pl.BlockSpec(memory_space=pltpu.SMEM)]
        + [pl.BlockSpec(memory_space=pl.ANY)] * (2 * devices),
        out_specs=pl.BlockSpec(memory_space=pltpu.VMEM),
        out_shape=jax.ShapeDtypeStruct((rows * devices, columns), owns[0].dtype),
        scratch_shapes=[pltpu.SemaphoreType.DMA(())],
        compiler_params=params(),
        cost_estimate=cost(0, 4 * rows * devices * columns),
    )(scal, *owns, *others)


def attend_back_kernel(devices, arrived, scal, *rest):
    parts, rest = rest[:arrived], rest[arrived:]
    grad_out, middle, gain, attended, wo, q, lse, cosine, sine, x, gain_first = rest[:11]
    ks, vs, rest = rest[11 : 11 + devices], rest[11 + devices : 11 + 2 * devices], rest[11 + 2 * devices :]
    mid_out, weight_grads, gain_grad, dq_out = rest[:4]
    dkv_outs, (bias, held) = rest[4 : 4 + devices], rest[4 + devices :]
    width = middle.shape[1]
    rows = middle.shape[0]
    scale = 1.0 / math.sqrt(HD)
    step = pl.program_id(0)

    @pl.when(step == 0)
    def _():
        fill_bias(bias, scal, devices, rows)
        grad_mix = parts[0][...].astype(F32)
        for part in parts[1:]:
            grad_mix = grad_mix + part[...].astype(F32)
        mid = middle[...]
        factor = lax.rsqrt(jnp.mean(mid * mid, axis=-1, keepdims=True) + epsilon)
        scaled = grad_mix * gain[...]
        inner = jnp.mean(mid * scaled, axis=-1, keepdims=True)
        gain_grad[...] = jnp.sum(grad_mix * mid * factor, axis=0, keepdims=True)
        grad_mid = grad_out[...] + factor * scaled - mid * (factor * factor * factor * inner)
        mid_out[...] = grad_mid
        branch = grad_mid.astype(BF16)
        weight_grads[:, :width] = mm_tn(attended[...], branch).astype(BF16)
        held[...] = mm_nt(branch, wo[...]).astype(BF16)

    keys = jnp.concatenate([r[0] for r in ks], axis=0)
    values = jnp.concatenate([r[0] for r in vs], axis=0)
    block_bias = bias[...]
    both_bias = jnp.concatenate([block_bias, block_bias], axis=1)
    key_parts, value_parts = [], []
    for i in range(2):
        block = q[:, i * 128 : (i + 1) * 128]
        at = pl.multiple_of(step * 256 + i * 128, 128)
        grads = held[:, pl.ds(at, 128)]
        scores = mm_nt(doubled(keys, i), two_heads(block)) * scale + both_bias
        probs = jnp.exp(scores - lse[0, i : i + 1, :])
        grad_probs = mm_nt(doubled(values, i), two_heads(grads))
        product = probs * grad_probs
        dots = jnp.sum(product, axis=0, keepdims=True)
        grad_scores = (product - probs * dots).astype(BF16)
        key_parts.append(mm(grad_scores, two_heads_doubled(block)) * scale)
        value_parts.append(mm(probs.astype(BF16), two_heads_doubled(grads)))
        moved = mm_tn(keys, grad_scores)[i * HD : (i + 1) * HD] * scale
        pair = jnp.concatenate([moved[:, :rows], moved[:, rows:]], axis=0)
        dq_out[:, pl.ds(at, 128)] = turn(jnp.transpose(pair), cosine[...], sine[...]).astype(BF16)
    even = lane_index(key_parts[0].shape) < HD
    grad_keys = jnp.where(even, key_parts[0], key_parts[1]).astype(BF16)
    grad_values = jnp.where(even, value_parts[0], value_parts[1]).astype(BF16)
    for k in range(devices):
        dkv_outs[k][0] = grad_keys[k * rows : (k + 1) * rows]
        dkv_outs[k][1] = grad_values[k * rows : (k + 1) * rows]

    @pl.when(step == pl.num_programs(0) - 1)
    def _():
        values = x[...].astype(F32)
        factor = lax.rsqrt(jnp.mean(values * values, axis=-1, keepdims=True) + epsilon)
        normed = (values * factor * gain_first[...]).astype(BF16)
        weight_grads[:, width:] = mm_tn(normed, dq_out[...]).astype(BF16)


def attend_backward(
    scal, parts, grad_out, middle, gain, attended, shared, q, lse, cosine, sine, x, gain_first, kvs
):
    rows, width = middle.shape
    devices = len(kvs)
    keys = devices * rows
    kv_specs = [pl.BlockSpec((1, rows, 128), lambda h: (0, 0, h)) for _ in kvs] + [
        pl.BlockSpec((1, rows, 128), lambda h: (1, 0, h)) for _ in kvs
    ]
    return pl.pallas_call(
        functools.partial(attend_back_kernel, devices, len(parts)),
        name="attend_backward",
        grid=(KVH // 2,),
        in_specs=[
            pl.BlockSpec(memory_space=pltpu.SMEM),
            *[fixed((rows, width)) for _ in parts],
            fixed((rows, width)),
            fixed((rows, width)),
            fixed((1, width)),
            fixed((rows, QH * HD)),
            pl.BlockSpec((QH * HD, width), lambda h: (0, 2), pipeline_mode=pl.Buffered(1)),
            pl.BlockSpec((rows, 256), lambda h: (0, h)),
            pl.BlockSpec((1, 2, 2 * rows), lambda h: (h, 0, 0)),
            fixed((rows, 128)),
            fixed((rows, 128)),
            fixed((rows, width)),
            fixed((1, width)),
            *kv_specs,
        ],
        out_specs=[
            resident((rows, width)),
            resident((width, width + QH * HD)),
            resident((1, width)),
            resident((rows, QH * HD)),
            *[pl.BlockSpec((2, rows, 128), lambda h: (0, 0, h)) for _ in kvs],
        ],
        out_shape=[
            jax.ShapeDtypeStruct((rows, width), F32),
            jax.ShapeDtypeStruct((width, width + QH * HD), BF16),
            jax.ShapeDtypeStruct((1, width), F32),
            jax.ShapeDtypeStruct((rows, QH * HD), BF16),
            *[jax.ShapeDtypeStruct((2, rows, KW), BF16) for _ in kvs],
        ],
        scratch_shapes=[pltpu.VMEM((keys, rows), F32), pltpu.VMEM((rows, QH * HD), BF16)],
        compiler_params=params(1),
        cost_estimate=cost(
            10 * rows * keys * QH * HD * 2 + 4 * rows * width * width,
            6 * width * width + 8 * keys * width + 20 * rows * width,
            rows * keys * QH,
        ),
    )(
        scal,
        *parts,
        grad_out,
        middle,
        gain,
        attended,
        shared,
        q,
        lse,
        cosine,
        sine,
        x,
        gain_first,
        *kvs,
        *kvs,
    )


def project_back_kernel(devices, x, gain, dq, *rest):
    parts, rest = rest[:devices], rest[devices:]
    grad_mid, wq, wm, cosine, sine, small, dx_out, packed = rest
    values = x[...].astype(F32)
    width = values.shape[1]
    factor = lax.rsqrt(jnp.mean(values * values, axis=-1, keepdims=True) + epsilon)
    normed = (values * factor * gain[...]).astype(BF16)
    summed = parts[0][...].astype(F32)
    for part in parts[1:]:
        summed = summed + part[...].astype(F32)
    grad_keys = [
        turn(summed[0, :, b * 128 : (b + 1) * 128], cosine[...], sine[...]).astype(BF16)
        for b in range(KW // 128)
    ]
    grad_memory = jnp.concatenate(grad_keys + [summed[1].astype(BF16)], axis=1)
    grad_query = dq[...]
    packed[:, : 2 * KW] = mm_tn(normed, grad_memory).astype(BF16)
    grad_normed = mm_nt(grad_query, wq[...]) + mm_nt(grad_memory, wm[...])
    scaled = grad_normed * gain[...]
    inner = jnp.mean(values * scaled, axis=-1, keepdims=True)
    gain_grad = jnp.sum(grad_normed * values * factor, axis=0, keepdims=True)
    row = lax.broadcasted_iota(jnp.int32, (128, width), 0)
    packed[:, 2 * KW :] = jnp.transpose(
        jnp.where(row == EXPERTS, gain_grad, small[...])
    ).astype(BF16)
    dx_out[...] = (
        grad_mid[...] + factor * scaled - values * (factor * factor * factor * inner)
    )


def project_backward(x, gain, dq, parts, grad_mid, shared, cosine, sine, small):
    rows, width = x.shape
    columns = 2 * KW + 128
    return pl.pallas_call(
        functools.partial(project_back_kernel, len(parts)),
        name="project_backward",
        grid=(1,),
        in_specs=[
            fixed((rows, width)),
            fixed((1, width)),
            fixed((rows, QH * HD)),
            *[fixed((2, rows, KW)) for _ in parts],
            fixed((rows, width)),
            pl.BlockSpec((width, QH * HD), lambda i: (0, 0), pipeline_mode=pl.Buffered(1)),
            pl.BlockSpec((width, 2 * KW), lambda i: (0, 1), pipeline_mode=pl.Buffered(1)),
            fixed((rows, 128)),
            fixed((rows, 128)),
            fixed((128, width)),
        ],
        out_specs=[resident((rows, width)), resident((width, columns))],
        out_shape=[
            jax.ShapeDtypeStruct((rows, width), F32),
            jax.ShapeDtypeStruct((width, columns), BF16),
        ],
        compiler_params=params(1),
        cost_estimate=cost(8 * rows * width * 2048, 8 * width * 2048 + 16 * rows * width),
    )(x, gain, dq, *parts, grad_mid, shared, shared, cosine, sine, small)


def pairs_within(axis, by, sections=(0, 1)):
    count = lax.axis_size(axis)
    return [(s * count + i, s * count + (i ^ by)) for s in sections for i in range(count)]


def exchanged(value, axis, by, sections=(0, 1)):
    return lax.ppermute(value, ("section", axis), pairs_within(axis, by, sections))


def swapped(value):
    return lax.ppermute(value, "section", [(0, 1), (1, 0)])


def from_all(value, axis, sections=(0, 1)):
    count = lax.axis_size(axis)
    return [value] + [exchanged(value, axis, k, sections) for k in range(1, count)]


def after(value, other):
    return lax.optimization_barrier((value, other))[0]


def scattered_sum(blocks, axis, sections):
    total = blocks[0].astype(F32)
    for k in range(1, len(blocks)):
        total = total + exchanged(blocks[k], axis, k, sections).astype(F32)
    return total


def shards(
    tokens,
    targets,
    lengths,
    routes,
    attention_gain,
    query_weight,
    memory_weight,
    output_weight,
    mixture_gain,
    router_weight,
    gate_up_weight,
    down_weight,
):
    section = lax.axis_index("section")
    context = lax.axis_index("ctx")
    line = lax.axis_index("fsdp")
    devices = lax.axis_size("ctx")
    depth = lax.axis_size("fsdp")
    first_core = section == 0
    rows, width = tokens.shape[2:]
    layers = 2
    held_experts = gate_up_weight.shape[1]
    half_held = held_experts // 2
    quarter = held_experts // 4
    side = line % 2
    alternate = [list(range(parity, depth, 2)) for parity in range(2)]
    paired = False
    capacity = rows * TOPK * 9 // (EXPERTS * 8)
    slots = -(-capacity // 16) * 16
    up_rows, down_rows = gate_up_weight.shape[2], down_weight.shape[2]
    shard_rows = up_rows + down_rows

    column = context * held_experts
    plain = (column + section * half_held, half_held, 2 * devices)
    pair = (column + side * half_held + section * quarter, quarter, 4 * devices)
    places = [pair if paired else plain, plain]

    pack = jnp.concatenate(
        [
            query_weight[0],
            memory_weight[0],
            output_weight[0],
            router_weight[0],
            attention_gain[0][:, None],
            mixture_gain[0][:, None],
            jnp.zeros((query_weight.shape[1], 128 - EXPERTS - 2), BF16),
        ],
        axis=1,
    )

    def shared_of_line(layer, ahead):
        mine = pack if ahead is None else after(pack, ahead)
        return jnp.concatenate(from_all(mine, "fsdp", (layer,)), axis=0)

    def shared_of_plane(layer, block, ahead):
        mine = block if ahead is None else after(block, ahead)
        owns = from_all(mine, "ctx", (layer,))
        others = [lax.ppermute(own, "section", [(layer, 1 - layer)]) for own in owns]
        scal = jnp.stack([(section == layer).astype(jnp.int32), context, line])
        whole = assemble(scal, owns, others, depth)
        small = whole[:, 3 * width :].T
        return (
            whole,
            small[:EXPERTS],
            small[EXPERTS : EXPERTS + 1].astype(F32),
            small[EXPERTS + 1 : EXPERTS + 2].astype(F32),
        )

    my_routes = jnp.swapaxes(routes[0, :, 0], 1, 2)
    other_routes = swapped(my_routes)
    layer_routes = jnp.where(
        first_core,
        jnp.stack([my_routes, other_routes]),
        jnp.stack([other_routes, my_routes])[:, ::-1],
    )
    all_routes = jnp.stack(from_all(layer_routes, "ctx"), axis=2).reshape(
        layers, 2 * devices, TOPK, rows
    )
    source_routes = [all_routes[0], all_routes[1]]
    if paired:
        source_routes[0] = jnp.concatenate(
            [all_routes[0], exchanged(all_routes[0], "fsdp", 1)], axis=0
        )
    earlier = (
        lax.broadcasted_iota(jnp.int32, (rows, rows), 0)
        < lax.broadcasted_iota(jnp.int32, (rows, rows), 1)
    ).astype(BF16)

    def ranked(layer):
        first, local, _ = places[layer]
        ids = first + jnp.arange(local, dtype=jnp.int32)
        named = jnp.any(source_routes[layer][:, None] == ids[None, :, None, None], axis=2)
        before = jnp.dot(
            named.astype(BF16).reshape(-1, rows), earlier, preferred_element_type=F32
        ).reshape(named.shape)
        return jnp.where(named, before, -1.0)

    ranks = [ranked(layer) for layer in range(layers)]
    masks = jnp.any(
        layer_routes[:, 0, None] == jnp.arange(EXPERTS, dtype=jnp.int32)[None, :, None, None], axis=2
    ).astype(F32)

    line_blocks = [after(shared_of_line(0, None), (ranks, masks)), None]

    merged = jnp.concatenate([gate_up_weight[0], down_weight[0]], axis=1)
    if paired:
        taken = lambda parity, core: lax.dynamic_slice_in_dim(
            merged, parity * half_held + core * quarter, quarter, 0
        )
        arrived = swapped(
            jnp.where(
                first_core,
                jnp.concatenate([taken(side, 1), taken(1 - side, 1)], axis=0),
                merged[:half_held],
            )
        )
        same = jnp.where(first_core, taken(side, 0), arrived[:quarter])
        differ = jnp.where(first_core, taken(1 - side, 0), arrived[quarter:])
        late = jnp.where(first_core, arrived, merged[half_held:])
        early = None
    else:
        mine = lax.dynamic_slice_in_dim(merged, section * half_held, half_held, 0)
        arrived = swapped(
            lax.dynamic_slice_in_dim(merged, (1 - section) * half_held, half_held, 0)
        )
        early = jnp.where(first_core, mine, arrived)
        late = jnp.where(first_core, arrived, mine)

    split = [(0, half_held - 1), (half_held - 1, 1)] if half_held > 1 else [(0, half_held)]
    runs = [[(0, quarter)] if paired else split, split]
    gathered_experts = lambda shard: [
        [lax.all_gather(shard[a : a + n], "fsdp", axis=1, tiled=True)] for a, n in split
    ]

    half = rows // 2
    within = jnp.arange(rows, dtype=jnp.int32)
    positions = jnp.where(
        within < half, context * half + within, (2 * devices - 1 - context) * half + within - half
    )
    inverse = rope_base ** (-2.0 * jnp.arange(HD // 2, dtype=F32) / HD)
    angles = positions.astype(F32)[:, None] * inverse[None, :]
    sine, cosine = jnp.sin(angles), jnp.cos(angles)
    cos_table = jnp.concatenate([cosine] * 4, axis=1)
    sin_table = jnp.concatenate([-sine, sine, -sine, sine], axis=1)
    length = lengths[section, line]
    attend_scalars = jnp.stack([context, length]).astype(jnp.int32)

    def dispatched(message, wide):
        plane = from_all(message, "ctx")
        blocks = plane + [swapped(block) for block in plane]
        if wide:
            blocks = blocks + dispatched(exchanged(message, "fsdp", 1), False)
        return blocks

    def returned(outs):
        terms = []
        if len(outs) > 2 * devices:
            far = returned(outs[2 * devices :])
            total = functools.reduce(lambda a, b: a + b, [t.astype(F32) for t in far])
            terms = [exchanged(total.astype(BF16), "fsdp", 1)]
        own, other = outs[:devices], outs[devices : 2 * devices]
        crossed = [swapped(block) for block in other]
        near = [own[0], crossed[0]]
        for k in range(1, devices):
            chip = (own[k].astype(F32) + crossed[k].astype(F32)).astype(BF16)
            near.append(exchanged(chip, "ctx", k))
        return near + terms

    my_targets = lax.dynamic_index_in_dim(targets[:, 0], section, 0, keepdims=False)
    layer_input = lax.dynamic_index_in_dim(tokens[:, 0], section, 0, keepdims=False)
    valid = (positions < length).astype(F32)[:, None]
    saved, hidden = [], []
    if paired:
        arrived = exchanged(differ, "fsdp", 1)
        both = jnp.where(
            side == 0,
            jnp.concatenate([same, arrived], axis=1),
            jnp.concatenate([arrived, same], axis=1),
        )
        early_experts = [
            [
                lax.all_gather(
                    both, "fsdp", axis=1, tiled=True, axis_index_groups=alternate
                )
            ]
        ]
    else:
        early_experts = gathered_experts(early)
    ahead = None
    for layer in range(layers):
        first, local, sources = places[layer]
        shared, router, gain_first, gain_second = shared_of_plane(
            layer, line_blocks[layer], ahead
        )
        wide = sources > 2 * devices
        q, kv = project(layer_input, gain_first, shared, cos_table, sin_table)
        if layer == 0:
            line_blocks[1] = shared_of_line(1, kv)
        kvs = from_all(kv, "ctx")
        attended, lse, middle, message = attend(
            attend_scalars, layer_input, q, kvs, shared, gain_second, router, masks[layer]
        )
        messages = dispatched(message, sources > 2 * devices)
        if layer == 0:
            ahead = messages
            weights = early_experts
            late_experts = gathered_experts(after(late, message))
        else:
            weights = late_experts
        kept, outs = [], ()
        xs, gates = dispatch(
            first.astype(jnp.int32).reshape(1), messages, ranks[layer], slots, False
        )
        for (a, n), blocks in zip(runs[layer], weights):
            order = [line ^ k for k in range(depth)] if len(blocks) > 1 else range(depth)
            scal = jnp.stack([first + a, *[jnp.asarray(o) for o in order]]).astype(jnp.int32)
            run, outs = experts_forward(
                scal,
                xs,
                ranks[layer][:, a : a + n],
                gates[:, a : a + n],
                blocks,
                depth,
                slots,
                a,
                outs,
            )
            kept.append((scal, run, blocks))
        if layer == layers - 1:
            hidden_rows, mixed, grad_output, message, error = finish(
                returned(outs), middle, my_targets, valid
            )
            hidden.append(hidden_rows)
        else:
            mixed = functools.reduce(lambda a, b: a + b, [t.astype(F32) for t in returned(outs)])
            hidden.append((middle + mixed).astype(BF16))
        saved.append(
            dict(
                x=layer_input,
                shared=shared,
                router=router,
                gain_first=gain_first,
                gain_second=gain_second,
                q=q,
                kvs=kvs,
                attended=attended,
                lse=lse,
                middle=middle,
                kept=kept,
                xs=xs,
                gates=gates,
                mixed=mixed,
            )
        )
        layer_input = hidden[-1]

    error = error[0, 0]
    for axis in ("section", "ctx", "fsdp"):
        by = 1
        while by < lax.axis_size(axis):
            error = error + lax.ppermute(
                error, axis, [(i, i ^ by) for i in range(lax.axis_size(axis))]
            )
            by *= 2
    loss_value = error / jnp.sum(lengths).astype(F32)

    def home_blocks(packed, layer):
        arrived = lax.ppermute(packed, "section", [(1 - layer, layer)])
        size = packed.shape[0] // devices
        return [
            (
                lax.dynamic_slice_in_dim(packed, (context ^ k) * size, size, 0).astype(F32)
                + lax.dynamic_slice_in_dim(arrived, (context ^ k) * size, size, 0).astype(F32)
            ).astype(BF16)
            for k in range(devices)
        ]

    def home_plane(blocks, layer):
        return scattered_sum(blocks, "ctx", (layer,)).astype(BF16)

    def home_line(plane, layer):
        size = plane.shape[0] // depth
        return scattered_sum(
            [
                lax.dynamic_slice_in_dim(plane, (line ^ k) * size, size, 0)
                for k in range(depth)
            ],
            "fsdp",
            (layer,),
        )

    def placed_rows(values):
        home = jnp.where(first_core, values[0], values[1])
        arrived = swapped(jnp.where(first_core, values[1], values[0]))
        return jnp.stack(
            [jnp.where(first_core, home, arrived), jnp.where(first_core, arrived, home)]
        )

    hidden_out = placed_rows(hidden)
    input_grads, expert_grads = [None] * layers, [None] * layers
    shared_grads = [None] * layers
    waiting = None
    summed = {}
    for layer in reversed(range(layers)):
        held = saved[layer]
        first, local, sources = places[layer]
        wide = sources > 2 * devices
        if layer < layers - 1:
            message = grad_message(grad_output, held["mixed"])
        messages = dispatched(message, sources > 2 * devices)
        if waiting is not None:
            blocks_1 = [home_blocks(part, 1) for part in waiting]
            messages = after(messages, blocks_1)
            blocks_1 = after(blocks_1, messages)
            planes = [home_plane(blocks, 1) for blocks in blocks_1]
        own_router = lax.dynamic_slice_in_dim(held["router"], first, local, 0).astype(F32)
        small = jnp.zeros((128, width), F32)
        outs = ()
        gathered = []
        steps = list(zip(runs[layer], held["kept"]))
        if layer == 1:
            steps = steps[::-1]
        spans = [a for (a, _), _ in steps]
        for at, ((a, n), (scal, run, blocks)) in enumerate(steps):
            last = None
            if at == len(steps) - 1:
                order = tuple(sorted(range(len(spans)), key=lambda i: spans[i]))
                last = (ranks[layer], [rows_of for rows_of in outs], order)
            grad_rows, inners = dispatch(
                scal[:1], messages, ranks[layer][:, a : a + n], slots, True
            )
            grads, router_grad, rows_out = experts_backward(
                scal,
                grad_rows,
                ranks[layer][:, a : a + n],
                held["gates"][:, a : a + n],
                inners,
                held["xs"],
                run,
                own_router[a : a + n, None, :],
                blocks,
                depth,
                slots,
                a,
                last,
            )
            outs = rows_out if last else list(outs) + rows_out
            small = lax.dynamic_update_slice_in_dim(small, router_grad[:, 0], first + a, 0)
            gathered.append(grads)
        if wide:
            pieces = []
            for at in range(quarter):
                pair_sum = lax.psum_scatter(
                    gathered[0][at : at + 1],
                    "fsdp",
                    scatter_dimension=1,
                    tiled=True,
                    axis_index_groups=alternate,
                )
                mine = lax.dynamic_slice_in_dim(pair_sum, side * shard_rows, shard_rows, 1)
                theirs = lax.dynamic_slice_in_dim(pair_sum, (1 - side) * shard_rows, shard_rows, 1)
                for core in range(2):
                    near, far = mine, theirs
                    if core:
                        near = lax.ppermute(mine, "section", [(1, 0)])
                    far = lax.ppermute(
                        far, ("section", "fsdp"), [(core * depth + i, i ^ 1) for i in range(depth)]
                    )
                    low = core * quarter + at
                    pieces.append((0, low, half_held + low, [near]))
                    pieces.append((0, half_held + low, low, [far]))
            expert_grads[0] = pieces
        else:
            summed[layer] = [
                lax.psum_scatter(grads, "fsdp", scatter_dimension=1, tiled=True)
                for grads in gathered
            ]
            expert_grads[layer] = []
            for at, part in zip(spans, summed[layer]):
                arrived = lax.ppermute(part, "section", [(1 - layer, layer)])
                for half_at, term in ((layer, part), (1 - layer, arrived)):
                    base = half_at * half_held + at
                    expert_grads[layer].append((layer, base, base, [term]))
        if layer == 1:
            grad_output = after(grad_output, (summed[1][0], loss_value))
        else:
            grad_output = after(grad_output, summed[1][-1])
            outs = after(outs, planes)
            shared_grads[1] = [home_line(part, 1) for part in planes]
        back = attend_backward(
            attend_scalars,
            returned(outs),
            grad_output,
            held["middle"],
            held["gain_second"],
            held["attended"],
            held["shared"],
            held["q"],
            held["lse"],
            cos_table,
            -sin_table,
            held["x"],
            held["gain_first"],
            held["kvs"],
        )
        grad_mid, weight_grads, gain_second_grad, dq = back[:4]
        dkv = back[4:]
        parts = [dkv[0]] + [exchanged(dkv[k], "ctx", k) for k in range(1, devices)]
        if layer == 0:
            outward = home_blocks(weight_grads, 0)
            grad_mid = after(grad_mid, (outward, shared_grads[1]))
        else:
            grad_mid = after(grad_mid, hidden_out)
        small = lax.dynamic_update_slice_in_dim(small, gain_second_grad, EXPERTS + 1, 0)
        dx, packed = project_backward(
            held["x"],
            held["gain_first"],
            dq,
            parts,
            grad_mid,
            held["shared"],
            cos_table,
            -sin_table,
            small,
        )
        input_grads[layer] = dx
        grad_output = dx.astype(BF16).astype(F32)
        if layer == 1:
            waiting = (weight_grads, packed)
        else:
            shared_grads[0] = [
                home_line(home_plane(blocks, 0), 0) for blocks in (outward, home_blocks(packed, 0))
            ]

    pick = lambda values: jnp.where(first_core, values[0], values[1])
    outward, inward = (pick([shared_grads[0][i], shared_grads[1][i]]) for i in range(2))
    input_out = placed_rows(input_grads)
    pieces = expert_grads[0] + expert_grads[1]
    numbers = range(held_experts)
    last = [e for e in numbers if len(runs[0]) > 1 and e % half_held >= runs[0][-1][0]]
    touches = lambda piece, experts: any(
        0 <= e - base < piece[3][0].shape[0] for e in experts for base in piece[1:3]
    )
    place_scalars = jnp.stack([section, side]).astype(jnp.int32)
    placed = ()
    for experts in ([e for e in numbers if e not in last], last):
        if experts:
            placed = place_experts(
                place_scalars,
                [piece for piece in pieces if touches(piece, experts)],
                held_experts,
                up_rows,
                experts,
                placed,
            )
    up_sum, down_sum = placed
    at = 2 * KW
    return (
        hidden_out[None, :, None],
        input_out[None, :, None],
        loss_value,
        inward[:, at + EXPERTS][None],
        outward[:, width:][None],
        inward[:, :at][None],
        outward[:, :width][None],
        inward[:, at + EXPERTS + 1][None],
        inward[:, at : at + EXPERTS][None],
        up_sum[None],
        down_sum[None],
    )


def solution(mesh):
    placed = (
        P(None, "fsdp", "ctx", None),
        P(None, "fsdp", "ctx", None),
        P(),
        P("section", None, "fsdp", "ctx", None),
        P("section", ("ctx", "fsdp")),
        P("section", ("ctx", "fsdp"), None),
        P("section", ("ctx", "fsdp"), None),
        P("section", ("ctx", "fsdp"), None),
        P("section", ("ctx", "fsdp")),
        P("section", ("ctx", "fsdp"), None),
        P("section", "ctx", "fsdp", None),
        P("section", "ctx", "fsdp", None),
    )
    return jax.shard_map(
        shards,
        mesh=mesh,
        in_specs=placed,
        out_specs=(
            P("section", None, "fsdp", "ctx", None),
            P("section", None, "fsdp", "ctx", None),
            P(),
            P("section", ("ctx", "fsdp")),
            P("section", ("ctx", "fsdp"), None),
            P("section", ("ctx", "fsdp"), None),
            P("section", ("ctx", "fsdp"), None),
            P("section", ("ctx", "fsdp")),
            P("section", ("ctx", "fsdp"), None),
            P("section", "ctx", "fsdp", None),
            P("section", "ctx", "fsdp", None),
        ),
        check_vma=False,
    )
```

time: 1240 us -> 1130 us (0.911)
  waiting for transfers between devices: 560 us -> 415 us
  Pallas kernels: 219 us -> 308 us
  local copies, waits for them, and re-layouts: 88.9 us -> 43.6 us
  other arithmetic: 92.9 us -> 73.6 us
    reduce_scatter x4, waiting for transfers between devices: 139 us -> 8.95 us  [shards(): lax.psum_scatter(grads, 'fsdp', scatter_dimension=1, tiled=True)]
    ppermute x4 -> x16, waiting for transfers between devices: 0.01 us -> 91.6 us  [the longest x8 84.9 us: shared_of_plane(): lax.ppermute(own, 'section', [(layer, 1 - layer)])]
    pallas_call x4 -> x20, Pallas kernels: 123 us -> 206 us  [the longest x4 80.8 us: experts_backward(): pl.pallas_call(kernel, name='experts_backward', grid=(local, portions), i...]
    ppermute x63 -> x75, waiting for transfers between devices: 322 us -> 250 us  [exchanged(): lax.ppermute(value, ('section', axis), pairs_within(axis, by, sections))]
    ppermute x39 -> x36, starting transfers between devices: 130 us -> 66.1 us  [swapped(): return lax.ppermute(value, 'section', [(0, 1), (1, 0)])]
    ppermute x4 -> x16, starting transfers between devices: 14.1 us -> 45.9 us  [the longest x4 21.4 us: shards(): arrived = lax.ppermute(part, 'section', [(1 - layer, layer)])]
    dynamic_update_slice x17 -> x6, local copies, waits for them, and re-layouts: 27.2 us -> 1.92 us  [the longest x2 1.11 us: shards(): lax.dynamic_update_slice_in_dim(small, gain_second_grad, EXPERTS + 1, 0)]
    all_gather x4, waiting for transfers between devices: 67.5 us -> 43.2 us  [shards(): lax.all_gather(shard[a:a + n], 'fsdp', axis=1, tiled=True)]
  transfers between devices with their start and end apart: 119 -> 140, of which waited for: 65 -> 48; matrix products, arithmetic and copies ran while one was open for 12% -> 8% of each run, Pallas kernels for 13% -> 24%
where the time goes in v2:
time: 1130 us; the launch traced here: 1110 us
  waiting for transfers between devices  415 us (37%)
  Pallas kernels  308 us (27%)
  starting transfers between devices  253 us (22%)
  other arithmetic  73.6 us (7%)
  local copies, waits for them, and re-layouts  43.6 us (4%)
  between operations  21.8 us (2%)
    ppermute x75, waiting for transfers between devices, exchanged(): lax.ppermute(value, ('section', axis), pairs_within(axis, by, sections))  250 us
    ppermute x75, starting transfers between devices, exchanged(): lax.ppermute(value, ('section', axis), pairs_within(axis, by, sections))  113 us
    ppermute x8, waiting for transfers between devices, shared_of_plane(): lax.ppermute(own, 'section', [(layer, 1 - layer)])  84.9 us
    pallas_call x4, Pallas kernels, experts_backward(): pl.pallas_call(kernel, name='experts_backward', grid=(local, portions), i...  80.8 us
    ppermute x36, starting transfers between devices, swapped(): return lax.ppermute(value, 'section', [(0, 1), (1, 0)])  66.1 us
    pallas_call x4, Pallas kernels, experts_forward(): pl.pallas_call(functools.partial(experts_kernel, sources, depth, slots, b...  56.6 us
    pallas_call x2, Pallas kernels, attend_backward(): pl.pallas_call(functools.partial(attend_back_kernel, devices, len(parts))...  48.4 us
    all_gather x4, waiting for transfers between devices, shards(): lax.all_gather(shard[a:a + n], 'fsdp', axis=1, tiled=True)  43.2 us
  transfers between devices with their start and end apart: 140, of which 48 were waited for; matrix products, arithmetic and copies ran while one was open for 8% of the time, Pallas kernels for 24%

profile of v2, /device:TPU:9, one launch (start us, length us, event | category | flops | bytes accessed | tf_op | source)
XLA Modules:
  0.0 1114.9 jit_solution(11846641601576875602)
XLA Ops:
  62.5 47.3 %collective-permute-done.10.refs_4_ = bf16[256,3200]{1,0:T(8,128)(2,1)} collective-permute-done((bf16[256,3200]{1,0:T(8,128)(2,1)S(1)}, bf16[256,3200]{1,0:T(8,128)(2,1)}, u32[]{:S(2)}, u32[]{:S(2)}) %collective-permute-start.10) | collective-permute-done | bytes 1638432 | tf_op jit(solution)/shard_map/ppermute | solution.py:1083
  109.9 14.1 %collective-permute-done.11.refs_5_ = bf16[256,3200]{1,0:T(8,128)(2,1)} collective-permute-done((bf16[256,3200]{1,0:T(8,128)(2,1)}, bf16[256,3200]{1,0:T(8,128)(2,1)}, u32[]{:S(2)}, u32[]{:S(2)}) %collective-permute-start.11) | collective-permute-done | bytes 1638432 | tf_op jit(solution)/shard_map/ppermute | solution.py:1083
  124.0 21.0 %collective-permute-done.12.refs_6_ = bf16[256,3200]{1,0:T(8,128)(2,1)} collective-permute-done((bf16[256,3200]{1,0:T(8,128)(2,1)}, bf16[256,3200]{1,0:T(8,128)(2,1)}, u32[]{:S(2)}, u32[]{:S(2)}) %collective-permute-start.12) | collective-permute-done | bytes 1638432 | tf_op jit(solution)/shard_map/ppermute | solution.py:1083
  172.9 12.1 %collective-permute-done.16.rest_3_.rest_7_.rest_19_.rest_23_ = bf16[2,256,512]{2,1,0:T(8,128)(2,1)S(1)} collective-permute-done((bf16[2,256,512]{2,1,0:T(8,128)(2,1)}, bf16[2,256,512]{2,1,0:T(8,128)(2,1)S(1)}, u32[]{:S(2)}, u32[]{:S(2)}) %collective-permute-start.16) | collective-permute-done | bytes 524320 | tf_op jit(solution)/shard_map/ppermute | solution.py:1002
  185.8 13.9 %attend.2 = (bf16[256,1024]{1,0:T(8,128)(2,1)}, f32[4,2,512]{2,1,0:T(2,128)}, f32[256,1024]{1,0:T(8,128)}, bf16[272,1024]{1,0:T(8,128)(2,1)}) custom-call(s32[2]{0:T(128)} %pad_add_fusion.2.scal, bf16[256,1024]{1,0:T(8,128)(2,1)} %dynamic-slice_bitcast_fusion.1.x.rest_14_, bf16[256,1024]{1,0:T(8,128)(2,1)} %get-tuple-element.162.q.rest_10_, ...), custom_call_target="tpu_custom_call" | custom-call | flops 2684354560 | bytes 9437184 | tf_op jit(solution)/shard_map/attend/pallas_call | solution.py:211
  216.3 31.5 %collective-permute-done.33 = bf16[64,3200]{1,0:T(8,128)(2,1)S(1)} collective-permute-done((bf16[64,3200]{1,0:T(8,128)(2,1)S(1)}, bf16[64,3200]{1,0:T(8,128)(2,1)S(1)}, u32[]{:S(2)}, u32[]{:S(2)}) %collective-permute-start.33) | collective-permute-done | bytes 409632 | tf_op jit(solution)/shard_map/ppermute | solution.py:1002
  248.8 24.6 %collective-permute-done.34 = bf16[64,3200]{1,0:T(8,128)(2,1)S(1)} collective-permute-done((bf16[64,3200]{1,0:T(8,128)(2,1)S(1)}, bf16[64,3200]{1,0:T(8,128)(2,1)S(1)}, u32[]{:S(2)}, u32[]{:S(2)}) %collective-permute-start.34) | collective-permute-done | bytes 409632 | tf_op jit(solution)/shard_map/ppermute | solution.py:1002
  292.2 17.6 %experts_forward.4 = (f32[3,640,1024]{2,1,0:T(8,128)}, bf16[3,640,1024]{2,1,0:T(8,128)(2,1)}, bf16[256,1024]{1,0:T(8,128)(2,1)}, bf16[256,1024]{1,0:T(8,128)(2,1...) custom-call(s32[5]{0:T(128)} %stack.120.scal.refs_0_, ...), custom_call_target="tpu_custom_call" | custom-call | flops 7851737088 | bytes 15728640 | tf_op jit(solution)/shard_map/experts_forward/pallas_call | solution.py:504
  354.0 11.3 %collective-permute-done.31 = bf16[256,1024]{1,0:T(8,128)(2,1)} collective-permute-done((bf16[256,1024]{1,0:T(8,128)(2,1)}, bf16[256,1024]{1,0:T(8,128)(2,1)}, u32[]{:S(2)}, u32[]{:S(2)}) %collective-permute-start.31) | collective-permute-done | bytes 524320 | tf_op jit(solution)/shard_map/ppermute | solution.py:1002
  385.3 11.9 %collective-permute-done.44.rest_3_.rest_7_.rest_19_.rest_23_ = bf16[2,256,512]{2,1,0:T(8,128)(2,1)S(1)} collective-permute-done((bf16[2,256,512]{2,1,0:T(8,128)(2,1)}, bf16[2,256,512]{2,1,0:T(8,128)(2,1)S(1)}, u32[]{:S(2)}, u32[]{:S(2)}) %collective-permute-start.44) | collective-permute-done | bytes 524320 | tf_op jit(solution)/shard_map/ppermute | solution.py:1002
  398.0 13.9 %attend.3 = (bf16[256,1024]{1,0:T(8,128)(2,1)}, f32[4,2,512]{2,1,0:T(2,128)}, f32[256,1024]{1,0:T(8,128)}, bf16[272,1024]{1,0:T(8,128)(2,1)}) custom-call(s32[2]{0:T(128)} %pad_add_fusion.2.scal, bf16[256,1024]{1,0:T(8,128)(2,1)} %get-tuple-element.365.x.rest_14_, bf16[256,1024]{1,0:T(8,128)(2,1)} %get-tuple-element.186.q.rest_10_, ...), custom_call_target="tpu_custom_call" | custom-call | flops 2684354560 | bytes 9437184 | tf_op jit(solution)/shard_map/attend/pallas_call | solution.py:211
  450.0 17.7 %experts_forward.6 = (f32[3,640,1024]{2,1,0:T(8,128)}, bf16[3,640,1024]{2,1,0:T(8,128)(2,1)}, bf16[256,1024]{1,0:T(8,128)(2,1)}, bf16[256,1024]{1,0:T(8,128)(2,1...) custom-call(s32[5]{0:T(128)} %stack.120.scal.refs_0_, ...), custom_call_target="tpu_custom_call" | custom-call | flops 7851737088 | bytes 15728640 | tf_op jit(solution)/shard_map/experts_forward/pallas_call | solution.py:504
  467.7 43.2 %all-gather.11.cloned.1.call-done.rest_11_.rest_12_.rest_13_.rest_14_.refs_9_.refs_10_.refs_11_.refs_12_ = bf16[1,1536,1024]{2,1,0:T(8,128)(2,1)} async-done(((bf16[1,384,1024]{2,1,0:T(8,128)(2,1)}), bf16[1,1536,1024]{2,1,0:T(8,128)(2,1)}) %all-gather.11.cloned.1.call-update) | async-done | bytes 3145744 | tf_op jit(solution)/shard_map/all_gather | solution.py:1157
  539.5 11.9 %collective-permute-done.56.refs_3_ = bf16[256,1024]{1,0:T(8,128)(2,1)S(1)} collective-permute-done((bf16[256,1024]{1,0:T(8,128)(2,1)S(1)}, bf16[256,1024]{1,0:T(8,128)(2,1)S(1)}, u32[]{:S(2)}, u32[]{:S(2)}) %collective-permute-start.56) | collective-permute-done | bytes 524320 | tf_op jit(solution)/shard_map/ppermute | solution.py:1002
  573.1 12.2 %collective-permute-start.65 = (bf16[272,1024]{1,0:T(8,128)(2,1)S(1)}, bf16[272,1024]{1,0:T(8,128)(2,1)}, u32[]{:S(2)}, u32[]{:S(2)}) collective-permute-start(bf16[272,1024]{1,0:T(8,128)(2,1)S(1)} %collective-permute-done.61.rest_2_), channel_id=1, source_target_pairs={{0,16},{16,0},{1,17},{17,1},{2,18},{18,2},{3,19},{19,3},{4,20},{20... | collective-permute-start | bytes 1671176 | tf_op jit(solution)/shard_map/ppermute | solution.py:1006
  610.4 30.2 %experts_backward.5 = (bf16[3,1536,1024]{2,1,0:T(8,128)(2,1)}, f32[3,1,1024]{2,1,0:T(1,128)}, bf16[256,1024]{1,0:T(8,128)(2,1)}, bf16[256,1024]{1,0:T(8,128)(2,1...) custom-call(s32[5]{0:T(128)} %stack.120.scal.refs_0_, ...), custom_call_target="tpu_custom_call" | custom-call | flops 13891534848 | bytes 27525120 | tf_op jit(solution)/shard_map/experts_backward/pallas_call | solution.py:657
  652.0 15.3 %collective-permute-start.75 = (f32[]{:T(128)}, f32[]{:T(128)}, u32[]{:S(2)}, u32[]{:S(2)}) collective-permute-start(f32[]{:T(128)} %add.394), channel_id=1, source_target_pairs={{0,4},{4,0},{8,12},{12,8},{1,5},{5,1},{9,13},{13,9},{2,6},{6,2},{1... | collective-permute-start | bytes 20 | tf_op jit(solution)/shard_map/ppermute | solution.py:1286
  687.8 24.1 %attend_backward.2 = (f32[256,1024]{1,0:T(8,128)}, bf16[1024,2048]{1,0:T(8,128)(2,1)}, f32[1,1024]{1,0:T(1,128)}, bf16[256,1024]{1,0:T(8,128)(2,1)}, bf16[2,256,...) custom-call(s32[2]{0:T(128)} %pad_add_fusion.2.scal, ...), custom_call_target="tpu_custom_call" | custom-call | flops 6442450944 | bytes 19922944 | tf_op jit(solution)/shard_map/attend_backward/pallas_call | solution.py:877
  757.8 12.4 %collective-permute-start.85 = (bf16[272,1024]{1,0:T(8,128)(2,1)}, bf16[272,1024]{1,0:T(8,128)(2,1)S(1)}, u32[]{:S(2)}, u32[]{:S(2)}) collective-permute-start(bf16[272,1024]{1,0:T(8,128)(2,1)} %grad_message.1.rest_0_), channel_id=1, source_target_pairs={{0,16},{16,0},{1,17},{17,1},{2,18},{18,2},{3,19},{19,3},{4,20},{20... | collective-permute-start | bytes 1671176 | tf_op jit(solution)/shard_map/ppermute | solution.py:1006
  792.7 23.7 %experts_backward.6 = (bf16[3,1536,1024]{2,1,0:T(8,128)(2,1)}, f32[3,1,1024]{2,1,0:T(1,128)}, bf16[3,640,1024]{2,1,0:T(8,128)(2,1)}) custom-call(s32[5]{0:T(128)} %stack.120.scal.refs_0_, f32[8,3,256]{2,1,0:T(4,128)} %bitcast.134, f32[8,3,256]{2,1,0:T(4,128)} %bitcast.145, f32[8,1,256]{2,1,0:T(1,128)} %get-tuple-element.255.refs_3_, ...), custom_call_target="tpu_custom_call" | custom-call | flops 13891534848 | bytes 27525120 | tf_op jit(solution)/shard_map/experts_backward/pallas_call | solution.py:657
  839.5 16.1 %experts_backward.7 = (bf16[1,1536,1024]{2,1,0:T(8,128)(2,1)}, f32[1,1,1024]{2,1,0:T(1,128)}, bf16[256,1024]{1,0:T(8,128)(2,1)}, bf16[256,1024]{1,0:T(8,128)(2,1...) custom-call(s32[5]{0:T(128)} %stack.118.scal.refs_0_, ...), custom_call_target="tpu_custom_call" | custom-call | flops 4630511616 | bytes 9175040 | tf_op jit(solution)/shard_map/experts_backward/pallas_call | solution.py:657
  878.0 11.7 %collective-permute-done.101.rest_3_ = bf16[256,1024]{1,0:T(8,128)(2,1)} collective-permute-done((bf16[256,1024]{1,0:T(8,128)(2,1)S(1)}, bf16[256,1024]{1,0:T(8,128)(2,1)}, u32[]{:S(2)}, u32[]{:S(2)}) %collective-permute-start.101) | collective-permute-done | bytes 524320 | tf_op jit(solution)/shard_map/ppermute | solution.py:1002
  890.5 24.3 %attend_backward.3 = (f32[256,1024]{1,0:T(8,128)}, bf16[1024,2048]{1,0:T(8,128)(2,1)}, f32[1,1024]{1,0:T(1,128)}, bf16[256,1024]{1,0:T(8,128)(2,1)}, bf16[2,256,...) custom-call(s32[2]{0:T(128)} %pad_add_fusion.2.scal, ...), custom_call_target="tpu_custom_call" | custom-call | flops 6442450944 | bytes 19922944 | tf_op jit(solution)/shard_map/attend_backward/pallas_call | solution.py:877
  960.1 51.1 %collective-permute-done.113 = bf16[64,1152]{1,0:T(8,128)(2,1)} collective-permute-done((bf16[64,1152]{1,0:T(8,128)(2,1)}, bf16[64,1152]{1,0:T(8,128)(2,1)}, u32[]{:S(2)}, u32[]{:S(2)}) %collective-permute-start.113) | collective-permute-done | bytes 147488 | tf_op jit(solution)/shard_map/ppermute | solution.py:1002
  (593 shorter events, 580.0 us)
Async XLA Ops:
  7.2 285.0 %all-gather.5.cloned.1.call-start = ((), (), s32[]{:S(2)}) async-start(), calls=%async_computation.4 | async-start | bytes 11796480 | tf_op jit(solution)/shard_map/all_gather | solution.py:1157
  27.3 282.6 %all-gather.7.cloned.1.call-start = ((), (), s32[]{:S(2)}) async-start(), calls=%async_computation.5 | async-start | bytes 3932160 | tf_op jit(solution)/shard_map/all_gather | solution.py:1157
  45.8 404.3 %all-gather.9.cloned.1.call-start = ((), (), s32[]{:S(2)}) async-start(), calls=%async_computation.6 | async-start | bytes 11796480 | tf_op jit(solution)/shard_map/all_gather | solution.py:1157
  54.3 55.6 %collective-permute-start.10 = (bf16[256,3200]{1,0:T(8,128)(2,1)S(1)}, bf16[256,3200]{1,0:T(8,128)(2,1)}, u32[]{:S(2)}, u32[]{:S(2)}) collective-permute-start(bf16[256,3200]{1,0:T(8,128)(2,1)S(1)} %pad_maximum_fusion.refs_0_), channel_id=1, source_target_pairs={{0,16},{1,17},{2,18},{3,19},{4,20},{5,21},{6,22},{7,23},{8,24},{9,... | collective-permute-start | bytes 4915208 | tf_op jit(solution)/shard_map/ppermute | solution.py:1083
  55.6 68.3 %collective-permute-start.11 = (bf16[256,3200]{1,0:T(8,128)(2,1)}, bf16[256,3200]{1,0:T(8,128)(2,1)}, u32[]{:S(2)}, u32[]{:S(2)}) collective-permute-start(bf16[256,3200]{1,0:T(8,128)(2,1)} %collective-permute-done.7.refs_1_), channel_id=1, source_target_pairs={{0,16},{1,17},{2,18},{3,19},{4,20},{5,21},{6,22},{7,23},{8,24},{9,... | collective-permute-start | bytes 4915208 | tf_op jit(solution)/shard_map/ppermute | solution.py:1083
  56.9 88.0 %collective-permute-start.12 = (bf16[256,3200]{1,0:T(8,128)(2,1)}, bf16[256,3200]{1,0:T(8,128)(2,1)}, u32[]{:S(2)}, u32[]{:S(2)}) collective-permute-start(bf16[256,3200]{1,0:T(8,128)(2,1)} %collective-permute-done.8.refs_2_), channel_id=1, source_target_pairs={{0,16},{1,17},{2,18},{3,19},{4,20},{5,21},{6,22},{7,23},{8,24},{9,... | collective-permute-start | bytes 4915208 | tf_op jit(solution)/shard_map/ppermute | solution.py:1083
  58.2 89.2 %collective-permute-start.13 = (bf16[256,3200]{1,0:T(8,128)(2,1)}, bf16[256,3200]{1,0:T(8,128)(2,1)}, u32[]{:S(2)}, u32[]{:S(2)}) collective-permute-start(bf16[256,3200]{1,0:T(8,128)(2,1)} %collective-permute-done.9.refs_3_), channel_id=1, source_target_pairs={{0,16},{1,17},{2,18},{3,19},{4,20},{5,21},{6,22},{7,23},{8,24},{9,... | collective-permute-start | bytes 4915208 | tf_op jit(solution)/shard_map/ppermute | solution.py:1083
  203.0 307.9 %all-gather.11.cloned.1.call-start = ((), (), s32[]{:S(2)}) async-start(), calls=%async_computation.7 | async-start | bytes 3932160 | tf_op jit(solution)/shard_map/all_gather | solution.py:1157
  213.1 60.3 %collective-permute-start.34 = (bf16[64,3200]{1,0:T(8,128)(2,1)S(1)}, bf16[64,3200]{1,0:T(8,128)(2,1)S(1)}, u32[]{:S(2)}, u32[]{:S(2)}) collective-permute-start(bf16[64,3200]{1,0:T(8,128)(2,1)S(1)} %concatenate.18), channel_id=1, source_target_pairs={{16,19},{17,18},{18,17},{19,16},{20,23},{21,22},{22,21},{23,20},{2... | collective-permute-start | bytes 1228808 | tf_op jit(solution)/shard_map/ppermute | solution.py:1002
  273.6 50.7 %collective-permute-start.35 = (bf16[256,3200]{1,0:T(8,128)(2,1)S(1)}, bf16[256,3200]{1,0:T(8,128)(2,1)}, u32[]{:S(2)}, u32[]{:S(2)}) collective-permute-start(bf16[256,3200]{1,0:T(8,128)(2,1)S(1)} %pad_maximum_fusion.1.refs_0_), channel_id=1, source_target_pairs={{16,20},{20,16},{24,28},{28,24},{17,21},{21,17},{25,29},{29,25},{1... | collective-permute-start | bytes 4915208 | tf_op jit(solution)/shard_map/ppermute | solution.py:1002
  275.8 51.1 %collective-permute-start.36 = (bf16[256,3200]{1,0:T(8,128)(2,1)S(1)}, bf16[256,3200]{1,0:T(8,128)(2,1)}, u32[]{:S(2)}, u32[]{:S(2)}) collective-permute-start(bf16[256,3200]{1,0:T(8,128)(2,1)S(1)} %pad_maximum_fusion.1.refs_0_), channel_id=1, source_target_pairs={{16,24},{20,28},{24,16},{28,20},{17,25},{21,29},{25,17},{29,21},{1... | collective-permute-start | bytes 4915208 | tf_op jit(solution)/shard_map/ppermute | solution.py:1002
  277.8 51.5 %collective-permute-start.37 = (bf16[256,3200]{1,0:T(8,128)(2,1)S(1)}, bf16[256,3200]{1,0:T(8,128)(2,1)}, u32[]{:S(2)}, u32[]{:S(2)}) collective-permute-start(bf16[256,3200]{1,0:T(8,128)(2,1)S(1)} %pad_maximum_fusion.1.refs_0_), channel_id=1, source_target_pairs={{16,28},{20,24},{24,20},{28,16},{17,29},{21,25},{25,21},{29,17},{1... | collective-permute-start | bytes 4915208 | tf_op jit(solution)/shard_map/ppermute | solution.py:1002
  334.7 352.2 %reduce-scatter.5.cloned.1.call-start = ((), (), s32[]{:S(2)}) async-start(), calls=%async_computation.8 | async-start | bytes 3932160 | tf_op jit(solution)/shard_map/reduce_scatter | solution.py:1400
  603.6 264.1 %reduce-scatter.7.cloned.1.call-start = ((), (), s32[]{:S(2)}) async-start(), calls=%async_computation.9 | async-start | bytes 11796480 | tf_op jit(solution)/shard_map/reduce_scatter | solution.py:1400
  640.7 412.6 %reduce-scatter.11.cloned.1.call-start = ((), (), s32[]{:S(2)}) async-start(), calls=%async_computation.11 | async-start | bytes 11796480 | tf_op jit(solution)/shard_map/reduce_scatter | solution.py:1400
  642.6 44.3 %collective-permute-start.67 = (bf16[256,1024]{1,0:T(8,128)(2,1)S(1)}, bf16[256,1024]{1,0:T(8,128)(2,1)S(1)}, u32[]{:S(2)}, u32[]{:S(2)}) collective-permute-start(bf16[256,1024]{1,0:T(8,128)(2,1)S(1)} %copy-done.87), channel_id=1, source_target_pairs={{0,16},{16,0},{1,17},{17,1},{2,18},{18,2},{3,19},{19,3},{4,20},{20... | collective-permute-start | bytes 1572872 | tf_op jit(solution)/shard_map/ppermute | solution.py:1006
  711.9 69.1 %collective-permute-start.89 = (bf16[1024,2048]{1,0:T(8,128)(2,1)}, bf16[1024,2048]{1,0:T(8,128)(2,1)}, u32[]{:S(2)}, u32[]{:S(2)}) collective-permute-start(bf16[1024,2048]{1,0:T(8,128)(2,1)} %get-tuple-element.245), channel_id=1, source_target_pairs={{0,16},{1,17},{2,18},{3,19},{4,20},{5,21},{6,22},{7,23},{8,24},{9,... | collective-permute-start | bytes 12582920 | tf_op jit(solution)/shard_map/ppermute | solution.py:1293
  816.5 264.9 %reduce-scatter.9.cloned.1.call-start = ((), (), s32[]{:S(2)}) async-start(), calls=%async_computation.10 | async-start | bytes 3932160 | tf_op jit(solution)/shard_map/reduce_scatter | solution.py:1400
  943.3 69.1 %collective-permute-start.108 = (bf16[64,2048]{1,0:T(8,128)(2,1)}, bf16[64,2048]{1,0:T(8,128)(2,1)S(1)}, u32[]{:S(2)}, u32[]{:S(2)}) collective-permute-start(bf16[64,2048]{1,0:T(8,128)(2,1)} %get-tuple-element.387), channel_id=1, source_target_pairs={{16,17},{17,16},{18,19},{19,18},{20,21},{21,20},{22,23},{23,22},{2... | collective-permute-start | bytes 786440 | tf_op jit(solution)/shard_map/ppermute | solution.py:1002
  946.6 66.9 %collective-permute-start.109 = (bf16[64,2048]{1,0:T(8,128)(2,1)}, bf16[64,2048]{1,0:T(8,128)(2,1)}, u32[]{:S(2)}, u32[]{:S(2)}) collective-permute-start(bf16[64,2048]{1,0:T(8,128)(2,1)} %get-tuple-element.389), channel_id=1, source_target_pairs={{16,18},{17,19},{18,16},{19,17},{20,22},{21,23},{22,20},{23,21},{2... | collective-permute-start | bytes 786440 | tf_op jit(solution)/shard_map/ppermute | solution.py:1002
  948.6 65.3 %collective-permute-start.110 = (bf16[64,2048]{1,0:T(8,128)(2,1)}, bf16[64,2048]{1,0:T(8,128)(2,1)}, u32[]{:S(2)}, u32[]{:S(2)}) collective-permute-start(bf16[64,2048]{1,0:T(8,128)(2,1)} %get-tuple-element.388), channel_id=1, source_target_pairs={{16,19},{17,18},{18,17},{19,16},{20,23},{21,22},{22,21},{23,20},{2... | collective-permute-start | bytes 786440 | tf_op jit(solution)/shard_map/ppermute | solution.py:1002
  956.1 59.2 %collective-permute-start.125 = (bf16[64,2048]{1,0:T(8,128)(2,1)}, bf16[64,2048]{1,0:T(8,128)(2,1)}, u32[]{:S(2)}, u32[]{:S(2)}) collective-permute-start(bf16[64,2048]{1,0:T(8,128)(2,1)} %get-tuple-element.390), channel_id=1, source_target_pairs={{0,1},{1,0},{2,3},{3,2},{4,5},{5,4},{6,7},{7,6},{8,9},{9,8},{10,11... | collective-permute-start | bytes 786440 | tf_op jit(solution)/shard_map/ppermute | solution.py:1002
  957.4 53.8 %collective-permute-start.113 = (bf16[64,1152]{1,0:T(8,128)(2,1)}, bf16[64,1152]{1,0:T(8,128)(2,1)}, u32[]{:S(2)}, u32[]{:S(2)}) collective-permute-start(bf16[64,1152]{1,0:T(8,128)(2,1)} %get-tuple-element.397), channel_id=1, source_target_pairs={{16,19},{17,18},{18,17},{19,16},{20,23},{21,22},{22,21},{23,20},{2... | collective-permute-start | bytes 442376 | tf_op jit(solution)/shard_map/ppermute | solution.py:1002
  1043.7 48.1 %collective-permute-start.131 = (bf16[3,384,1024]{2,1,0:T(8,128)(2,1)}, bf16[3,384,1024]{2,1,0:T(8,128)(2,1)}, u32[]{:S(2)}, u32[]{:S(2)}) collective-permute-start(bf16[3,384,1024]{2,1,0:T(8,128)(2,1)} %reduce-scatter.7.cloned.1.call-done.refs_2_), channel_id=1, source_target_pairs={{0,16},{1,17},{2,18},{3,19},{4,20},{5,21},{6,22},{7,23},{8,24},{9,... | collective-permute-start | bytes 7077896 | tf_op jit(solution)/shard_map/ppermute | solution.py:1405
  (211 other events, 3469.2 us)
Sparse Core Ops, SparseCore 0:
  27.4 178.4 all-gather.4
  207.5 74.2 all-gather.6
  283.3 164.0 all-gather.8
  448.8 62.0 all-gather.10
  603.7 59.5 reduce-scatter.4
  665.5 161.5 reduce-scatter.6
  829.5 190.3 reduce-scatter.10
  1022.2 59.0 reduce-scatter.8

commit v3 on v2

--- a/solution.py
+++ b/solution.py
@@ -295,7 +295,7 @@
 
 
 def finish_kernel(count, *refs):
-    terms, (middle, goal, valid, hidden, mixed_out, grad_out, message, error) = (
+    terms, (middle, goal, valid, hidden, mixed_out, grad_out, message) = (
         refs[:count],
         refs[count:],
     )
@@ -308,13 +308,11 @@
     mixed_out[...] = mixed
     grad = (output - goal[...].astype(F32)) * valid[...]
     grad_out[...] = grad
-    error[...] = 0.5 * jnp.sum(
-        jnp.sum(grad * grad, axis=1, keepdims=True), axis=0, keepdims=True
-    )
-    fill_message(message, grad, mixed)
-
-
-def fill_message(message, grad, mixed):
+    error = 0.5 * jnp.sum(jnp.sum(grad * grad, axis=1, keepdims=True), axis=0, keepdims=True)
+    fill_message(message, grad, mixed, error)
+
+
+def fill_message(message, grad, mixed, error):
     rows, width = grad.shape
     message[:rows, :] = grad.astype(BF16)
     inner = jnp.transpose(
@@ -322,8 +320,13 @@
     )[:EXT]
     high = inner.astype(BF16)
     low = (inner - high.astype(F32)).astype(BF16)
-    first = lax.broadcasted_iota(jnp.int32, (EXT, rows), 0) == 0
-    message[rows:, :rows] = jnp.where(first, high, low)
+    row = lax.broadcasted_iota(jnp.int32, (EXT, rows), 0)
+    ext = jnp.where(row == 0, high.astype(F32), jnp.where(row == 1, low.astype(F32), 0.0))
+    for at in range(2, 5):
+        term = error.astype(BF16).astype(F32)
+        ext = jnp.where(row == at, term, ext)
+        error = error - term
+    message[rows:, :rows] = ext.astype(BF16)
     message[rows:, rows:] = jnp.zeros((EXT, width - rows), BF16)
 
 
@@ -337,7 +340,6 @@
             jax.ShapeDtypeStruct((rows, width), F32),
             jax.ShapeDtypeStruct((rows, width), F32),
             jax.ShapeDtypeStruct((rows + EXT, width), BF16),
-            jax.ShapeDtypeStruct((1, 1), F32),
         ],
         compiler_params=params(),
         cost_estimate=cost(8 * rows * width, 24 * rows * width),
@@ -345,7 +347,7 @@
 
 
 def message_kernel(grad, mixed, message):
-    fill_message(message, grad[...], mixed[...])
+    fill_message(message, grad[...], mixed[...], jnp.zeros((1, 1), F32))
 
 
 def grad_message(grad, mixed):
@@ -378,7 +380,8 @@
         send(j).start()
         if backward:
             ext = arrived[j, rows:, :rows].astype(F32)
-            side_out[j] = ext[0:1, :] + ext[1:2, :]
+            side_out[j, 0:1, :] = ext[0:1, :] + ext[1:2, :]
+            side_out[j, 1:2, :] = ext[2:3, :] + ext[3:4, :] + ext[4:5, :]
         else:
             ext = arrived[j, rows:, : 4 * rows].astype(F32)
             for i in range(local):
@@ -395,7 +398,7 @@
     sources, local, rows = rank.shape
     width = msgs[0].shape[1]
     anywhere = pl.BlockSpec(memory_space=pl.ANY)
-    side = (sources, 1 if backward else local, rows)
+    side = (sources, 2 if backward else local, rows)
     taken, beside = pl.pallas_call(
         functools.partial(dispatch_kernel, sources, slots, backward),
         name="dispatch",
@@ -473,12 +476,12 @@
         combine(rank, held, prior, outs, rest[3:], slots)
 
 
-def weight_specs(blocks, depth):
+def weight_specs(blocks, depth, base=0):
     arrays = blocks if len(blocks) == depth else blocks * depth
     rows = arrays[0].shape[1] // (depth // len(blocks))
     width = arrays[0].shape[2]
     specs = [
-        pl.BlockSpec((1, rows, width), lambda e, r, f=(k if len(blocks) == 1 else 0): (e, f, 0))
+        pl.BlockSpec((1, rows, width), lambda e, r, f=(k if len(blocks) == 1 else 0): (e + base, f, 0))
         for k in range(depth)
     ]
     return arrays, specs
@@ -559,7 +562,7 @@
 
     mine = [part * portion + n for n in range(portion)]
     gate_column = gate_columns(rank, lambda j: gates[j, pl.ds(step, 1), :], step, mine, slots)
-    inner_column = gate_columns(rank, lambda j: inners[j], step, mine, slots)
+    inner_column = gate_columns(rank, lambda j: inners[j, 0:1, :], step, mine, slots)
     grad_out = grads[0].astype(F32)
     grad_y = (gate_column * grad_out).astype(BF16)
     given = jnp.sum(grad_out * ys[0].astype(F32), axis=1, keepdims=True)
@@ -625,14 +628,14 @@
 
 
 def experts_backward(
-    scal, grads, rank, gates, inners, xs, kept, router, blocks, depth, slots, first, last
+    scal, grads, rank, gates, inners, xs, kept, router, blocks, depth, slots, first, base, last
 ):
     sources, local, rows = rank.shape
     width = xs.shape[2]
     portions = max(1, sources // 8)
     count = sources * slots
     gu, ys = kept
-    arrays, specs = weight_specs(blocks, depth)
+    arrays, specs = weight_specs(blocks, depth, base)
     merged = width + FF_E
     anywhere = pl.BlockSpec(memory_space=pl.ANY)
     each = lambda shape, base=0: pl.BlockSpec((1,) + shape, lambda e, r: (e + base, r, 0))
@@ -663,11 +666,11 @@
             *[fixed(part.shape) for part in before],
             fixed((sources, local, rows)),
             fixed((sources, local, rows)),
-            fixed((sources, 1, rows)),
+            fixed((sources, 2, rows)),
             each((count // portions, width)),
             each((count // portions, width), first),
-            each((count // portions, 2 * FF_E)),
-            each((count // portions, width)),
+            each((count // portions, 2 * FF_E), base),
+            each((count // portions, width), base),
             whole((1, width)),
             *specs,
         ],
@@ -700,53 +703,39 @@
     return outs[0], outs[1], list(outs[2:])
 
 
-def place_base(place, scal):
-    return jnp.where(scal[1] == 0, place[1], place[2])
-
-
 def place_kernel(places, number, aliased, scal, *refs):
     parts, (up_out, down_out) = refs[: -2 - aliased], refs[-2:]
     step = number(pl.program_id(0))
     up_rows = up_out.shape[1]
 
-    def put(blocks):
-        total = blocks[0][0].astype(F32)
-        for block in blocks[1:]:
-            total = total + block[0].astype(F32)
-        up_out[0] = total[:up_rows]
-        down_out[0] = total[up_rows:]
+    def put(block):
+        up_out[0] = block[0, :up_rows].astype(F32)
+        down_out[0] = block[0, up_rows:].astype(F32)
 
     at = 0
     for place in places:
-        base, count, terms = place_base(place, scal), place[3], place[4]
-        pl.when((scal[0] == place[0]) & (step >= base) & (step < base + count))(
-            functools.partial(put, parts[at : at + terms])
+        core, base, count = place
+        pl.when((scal[0] == core) & (step >= base) & (step < base + count))(
+            functools.partial(put, parts[at])
         )
-        at += terms
+        at += 1
 
 
 def place_experts(scal, pieces, held_experts, up_rows, experts, into=()):
-    rows, width = pieces[0][3][0].shape[1:]
-    places, specs, arrays = [], [], []
+    rows, width = pieces[0][2].shape[1:]
     run = next((i for i in range(1, len(experts)) if experts[i] != experts[0] + i), len(experts))
     skip = experts[run] - experts[run - 1] if run < len(experts) else 1
     number = lambda i: experts[0] + (i // run) * (run - 1 + skip) + i % run
     assert [number(i) for i in range(len(experts))] == list(experts)
-    for core, even_base, odd_base, terms in pieces:
-        place = (core, even_base, odd_base, terms[0].shape[0], len(terms))
-        places.append(place)
-        for term in terms:
-            arrays.append(term)
-            specs.append(
-                pl.BlockSpec(
-                    (1, rows, width),
-                    lambda i, scal, place=place: (
-                        jnp.clip(number(i) - place_base(place, scal), 0, place[3] - 1),
-                        0,
-                        0,
-                    ),
-                )
-            )
+    places = [(core, base, array.shape[0]) for core, base, array in pieces]
+    arrays = [array for _, _, array in pieces]
+    specs = [
+        pl.BlockSpec(
+            (1, rows, width),
+            lambda i, scal, base=base, top=count - 1: (jnp.clip(number(i) - base, 0, top), 0, 0),
+        )
+        for _, base, count in places
+    ]
     specs += [pl.BlockSpec(memory_space=pl.ANY) for _ in into]
     return pl.pallas_call(
         functools.partial(place_kernel, places, number, len(into)),
@@ -1046,10 +1035,6 @@
     layers = 2
     held_experts = gate_up_weight.shape[1]
     half_held = held_experts // 2
-    quarter = held_experts // 4
-    side = line % 2
-    alternate = [list(range(parity, depth, 2)) for parity in range(2)]
-    paired = False
     capacity = rows * TOPK * 9 // (EXPERTS * 8)
     slots = -(-capacity // 16) * 16
     up_rows, down_rows = gate_up_weight.shape[2], down_weight.shape[2]
@@ -1057,8 +1042,7 @@
 
     column = context * held_experts
     plain = (column + section * half_held, half_held, 2 * devices)
-    pair = (column + side * half_held + section * quarter, quarter, 4 * devices)
-    places = [pair if paired else plain, plain]
+    places = [plain, plain]
 
     pack = jnp.concatenate(
         [
@@ -1102,10 +1086,6 @@
         layers, 2 * devices, TOPK, rows
     )
     source_routes = [all_routes[0], all_routes[1]]
-    if paired:
-        source_routes[0] = jnp.concatenate(
-            [all_routes[0], exchanged(all_routes[0], "fsdp", 1)], axis=0
-        )
     earlier = (
         lax.broadcasted_iota(jnp.int32, (rows, rows), 0)
         < lax.broadcasted_iota(jnp.int32, (rows, rows), 1)
@@ -1127,35 +1107,27 @@
 
     line_blocks = [after(shared_of_line(0, None), (ranks, masks)), None]
 
-    merged = jnp.concatenate([gate_up_weight[0], down_weight[0]], axis=1)
-    if paired:
-        taken = lambda parity, core: lax.dynamic_slice_in_dim(
-            merged, parity * half_held + core * quarter, quarter, 0
-        )
-        arrived = swapped(
-            jnp.where(
-                first_core,
-                jnp.concatenate([taken(side, 1), taken(1 - side, 1)], axis=0),
-                merged[:half_held],
+    whole = [(0, half_held)]
+    split = [(0, half_held - 1), (half_held - 1, 1)] if half_held > 1 else whole
+    runs = [whole, split]
+    back_runs = [split, split[::-1]]
+
+    def gathered_experts(layer, ahead):
+        parts = []
+        for a, n in runs[layer]:
+            rows_of = lambda half: jnp.concatenate(
+                [
+                    weight[0, half * half_held + a : half * half_held + a + n]
+                    for weight in (gate_up_weight, down_weight)
+                ],
+                axis=1,
             )
-        )
-        same = jnp.where(first_core, taken(side, 0), arrived[:quarter])
-        differ = jnp.where(first_core, taken(1 - side, 0), arrived[quarter:])
-        late = jnp.where(first_core, arrived, merged[half_held:])
-        early = None
-    else:
-        mine = lax.dynamic_slice_in_dim(merged, section * half_held, half_held, 0)
-        arrived = swapped(
-            lax.dynamic_slice_in_dim(merged, (1 - section) * half_held, half_held, 0)
-        )
-        early = jnp.where(first_core, mine, arrived)
-        late = jnp.where(first_core, arrived, mine)
-
-    split = [(0, half_held - 1), (half_held - 1, 1)] if half_held > 1 else [(0, half_held)]
-    runs = [[(0, quarter)] if paired else split, split]
-    gathered_experts = lambda shard: [
-        [lax.all_gather(shard[a : a + n], "fsdp", axis=1, tiled=True)] for a, n in split
-    ]
+            arrived = lax.ppermute(rows_of(1 - layer), "section", [(layer, 1 - layer)])
+            shard = jnp.where(section == layer, rows_of(layer), arrived)
+            if ahead is not None:
+                shard = after(shard, ahead)
+            parts.append([lax.all_gather(shard, "fsdp", axis=1, tiled=True)])
+        return parts
 
     half = rows // 2
     within = jnp.arange(rows, dtype=jnp.int32)
@@ -1170,54 +1142,31 @@
     length = lengths[section, line]
     attend_scalars = jnp.stack([context, length]).astype(jnp.int32)
 
-    def dispatched(message, wide):
+    def dispatched(message):
         plane = from_all(message, "ctx")
         blocks = plane + [swapped(block) for block in plane]
-        if wide:
-            blocks = blocks + dispatched(exchanged(message, "fsdp", 1), False)
         return blocks
 
     def returned(outs):
-        terms = []
-        if len(outs) > 2 * devices:
-            far = returned(outs[2 * devices :])
-            total = functools.reduce(lambda a, b: a + b, [t.astype(F32) for t in far])
-            terms = [exchanged(total.astype(BF16), "fsdp", 1)]
         own, other = outs[:devices], outs[devices : 2 * devices]
         crossed = [swapped(block) for block in other]
         near = [own[0], crossed[0]]
         for k in range(1, devices):
             chip = (own[k].astype(F32) + crossed[k].astype(F32)).astype(BF16)
             near.append(exchanged(chip, "ctx", k))
-        return near + terms
+        return near
 
     my_targets = lax.dynamic_index_in_dim(targets[:, 0], section, 0, keepdims=False)
     layer_input = lax.dynamic_index_in_dim(tokens[:, 0], section, 0, keepdims=False)
     valid = (positions < length).astype(F32)[:, None]
     saved, hidden = [], []
-    if paired:
-        arrived = exchanged(differ, "fsdp", 1)
-        both = jnp.where(
-            side == 0,
-            jnp.concatenate([same, arrived], axis=1),
-            jnp.concatenate([arrived, same], axis=1),
-        )
-        early_experts = [
-            [
-                lax.all_gather(
-                    both, "fsdp", axis=1, tiled=True, axis_index_groups=alternate
-                )
-            ]
-        ]
-    else:
-        early_experts = gathered_experts(early)
+    early_experts = gathered_experts(0, None)
     ahead = None
     for layer in range(layers):
         first, local, sources = places[layer]
         shared, router, gain_first, gain_second = shared_of_plane(
             layer, line_blocks[layer], ahead
         )
-        wide = sources > 2 * devices
         q, kv = project(layer_input, gain_first, shared, cos_table, sin_table)
         if layer == 0:
             line_blocks[1] = shared_of_line(1, kv)
@@ -1225,11 +1174,11 @@
         attended, lse, middle, message = attend(
             attend_scalars, layer_input, q, kvs, shared, gain_second, router, masks[layer]
         )
-        messages = dispatched(message, sources > 2 * devices)
+        messages = dispatched(message)
         if layer == 0:
             ahead = messages
             weights = early_experts
-            late_experts = gathered_experts(after(late, message))
+            late_experts = gathered_experts(1, message)
         else:
             weights = late_experts
         kept, outs = [], ()
@@ -1250,9 +1199,9 @@
                 a,
                 outs,
             )
-            kept.append((scal, run, blocks))
+            kept.append((a, n, scal, run, blocks))
         if layer == layers - 1:
-            hidden_rows, mixed, grad_output, message, error = finish(
+            hidden_rows, mixed, grad_output, message = finish(
                 returned(outs), middle, my_targets, valid
             )
             hidden.append(hidden_rows)
@@ -1279,16 +1228,6 @@
         )
         layer_input = hidden[-1]
 
-    error = error[0, 0]
-    for axis in ("section", "ctx", "fsdp"):
-        by = 1
-        while by < lax.axis_size(axis):
-            error = error + lax.ppermute(
-                error, axis, [(i, i ^ by) for i in range(lax.axis_size(axis))]
-            )
-            by *= 2
-    loss_value = error / jnp.sum(lengths).astype(F32)
-
     def home_blocks(packed, layer):
         arrived = lax.ppermute(packed, "section", [(1 - layer, layer)])
         size = packed.shape[0] // devices
@@ -1321,7 +1260,6 @@
             [jnp.where(first_core, home, arrived), jnp.where(first_core, arrived, home)]
         )
 
-    hidden_out = placed_rows(hidden)
     input_grads, expert_grads = [None] * layers, [None] * layers
     shared_grads = [None] * layers
     waiting = None
@@ -1329,10 +1267,9 @@
     for layer in reversed(range(layers)):
         held = saved[layer]
         first, local, sources = places[layer]
-        wide = sources > 2 * devices
         if layer < layers - 1:
             message = grad_message(grad_output, held["mixed"])
-        messages = dispatched(message, sources > 2 * devices)
+        messages = dispatched(message)
         if waiting is not None:
             blocks_1 = [home_blocks(part, 1) for part in waiting]
             messages = after(messages, blocks_1)
@@ -1342,11 +1279,13 @@
         small = jnp.zeros((128, width), F32)
         outs = ()
         gathered = []
-        steps = list(zip(runs[layer], held["kept"]))
-        if layer == 1:
-            steps = steps[::-1]
-        spans = [a for (a, _), _ in steps]
-        for at, ((a, n), (scal, run, blocks)) in enumerate(steps):
+        steps = back_runs[layer]
+        spans = [a for a, _ in steps]
+        for at, (a, n) in enumerate(steps):
+            base, _, scal, run, blocks = next(
+                kept for kept in held["kept"] if kept[0] <= a and a + n <= kept[0] + kept[1]
+            )
+            scal = jnp.concatenate([scal[:1] + (a - base), scal[1:]])
             last = None
             if at == len(steps) - 1:
                 order = tuple(sorted(range(len(spans)), key=lambda i: spans[i]))
@@ -1367,51 +1306,24 @@
                 depth,
                 slots,
                 a,
+                a - base,
                 last,
             )
             outs = rows_out if last else list(outs) + rows_out
+            if layer == 1 and at == 0:
+                error = jnp.sum(inners[:, 1, 0])
             small = lax.dynamic_update_slice_in_dim(small, router_grad[:, 0], first + a, 0)
             gathered.append(grads)
-        if wide:
-            pieces = []
-            for at in range(quarter):
-                pair_sum = lax.psum_scatter(
-                    gathered[0][at : at + 1],
-                    "fsdp",
-                    scatter_dimension=1,
-                    tiled=True,
-                    axis_index_groups=alternate,
-                )
-                mine = lax.dynamic_slice_in_dim(pair_sum, side * shard_rows, shard_rows, 1)
-                theirs = lax.dynamic_slice_in_dim(pair_sum, (1 - side) * shard_rows, shard_rows, 1)
-                for core in range(2):
-                    near, far = mine, theirs
-                    if core:
-                        near = lax.ppermute(mine, "section", [(1, 0)])
-                    far = lax.ppermute(
-                        far, ("section", "fsdp"), [(core * depth + i, i ^ 1) for i in range(depth)]
-                    )
-                    low = core * quarter + at
-                    pieces.append((0, low, half_held + low, [near]))
-                    pieces.append((0, half_held + low, low, [far]))
-            expert_grads[0] = pieces
-        else:
-            summed[layer] = [
-                lax.psum_scatter(grads, "fsdp", scatter_dimension=1, tiled=True)
-                for grads in gathered
-            ]
-            expert_grads[layer] = []
-            for at, part in zip(spans, summed[layer]):
-                arrived = lax.ppermute(part, "section", [(1 - layer, layer)])
-                for half_at, term in ((layer, part), (1 - layer, arrived)):
-                    base = half_at * half_held + at
-                    expert_grads[layer].append((layer, base, base, [term]))
+        summed[layer] = [
+            lax.psum_scatter(grads, "fsdp", scatter_dimension=1, tiled=True)
+            for grads in gathered
+        ]
+        expert_grads[layer] = list(zip(spans, summed[layer]))
         if layer == 1:
-            grad_output = after(grad_output, (summed[1][0], loss_value))
+            grad_output = after(grad_output, summed[1][0])
         else:
             grad_output = after(grad_output, summed[1][-1])
             outs = after(outs, planes)
-            shared_grads[1] = [home_line(part, 1) for part in planes]
         back = attend_backward(
             attend_scalars,
             returned(outs),
@@ -1433,9 +1345,15 @@
         parts = [dkv[0]] + [exchanged(dkv[k], "ctx", k) for k in range(1, devices)]
         if layer == 0:
             outward = home_blocks(weight_grads, 0)
-            grad_mid = after(grad_mid, (outward, shared_grads[1]))
+            grad_mid = after(grad_mid, outward)
         else:
-            grad_mid = after(grad_mid, hidden_out)
+            by = 1
+            while by < depth:
+                error = error + lax.ppermute(error, "fsdp", [(i, i ^ by) for i in range(depth)])
+                by *= 2
+            loss_value = error / jnp.sum(lengths).astype(F32)
+            hidden_out = placed_rows(hidden)
+            grad_mid = after(grad_mid, (loss_value, hidden_out))
         small = lax.dynamic_update_slice_in_dim(small, gain_second_grad, EXPERTS + 1, 0)
         dx, packed = project_backward(
             held["x"],
@@ -1453,32 +1371,38 @@
         if layer == 1:
             waiting = (weight_grads, packed)
         else:
+            outward, planes = after((outward, planes), packed)
             shared_grads[0] = [
-                home_line(home_plane(blocks, 0), 0) for blocks in (outward, home_blocks(packed, 0))
-            ]
+                home_line(home_plane(blocks, 0), 0) for blocks in (home_blocks(packed, 0), outward)
+            ][::-1]
+            shared_grads[1] = [home_line(part, 1) for part in planes]
 
     pick = lambda values: jnp.where(first_core, values[0], values[1])
     outward, inward = (pick([shared_grads[0][i], shared_grads[1][i]]) for i in range(2))
     input_out = placed_rows(input_grads)
-    pieces = expert_grads[0] + expert_grads[1]
-    numbers = range(held_experts)
-    last = [e for e in numbers if len(runs[0]) > 1 and e % half_held >= runs[0][-1][0]]
-    touches = lambda piece, experts: any(
-        0 <= e - base < piece[3][0].shape[0] for e in experts for base in piece[1:3]
-    )
-    place_scalars = jnp.stack([section, side]).astype(jnp.int32)
-    placed = ()
-    for experts in ([e for e in numbers if e not in last], last):
-        if experts:
-            placed = place_experts(
-                place_scalars,
-                [piece for piece in pieces if touches(piece, experts)],
-                held_experts,
-                up_rows,
-                experts,
-                placed,
-            )
-    up_sum, down_sum = placed
+    def pieces_of(layer, at, part):
+        arrived = lax.ppermute(part, "section", [(1 - layer, layer)])
+        return [
+            (layer, half * half_held + at, term)
+            for half, term in ((layer, part), (1 - layer, arrived))
+        ]
+
+    def placed(pieces, experts, into):
+        touched = [p for p in pieces if any(0 <= e - p[1] < p[2].shape[0] for e in experts)]
+        return place_experts(
+            section.astype(jnp.int32).reshape(1), touched, held_experts, up_rows, experts, into
+        )
+
+    parts = [(layer, at, part) for layer in (1, 0) for at, part in expert_grads[layer]]
+    pieces = [piece for part in parts[:-1] for piece in pieces_of(*part)]
+    layer, at, part = parts[-1]
+    last = [half * half_held + at + i for half in range(2) for i in range(part.shape[0])]
+    sums = ()
+    if len(last) < held_experts:
+        sums = placed(pieces, [e for e in range(held_experts) if e not in last], ())
+        outward, inward = after((outward, inward), sums)
+        part = after(part, (outward, inward, input_out))
+    up_sum, down_sum = placed(pieces + pieces_of(layer, at, part), last, sums)
     at = 2 * KW
     return (
         hidden_out[None, :, None],

time: 1130 us -> 1110 us (0.982)
  waiting for transfers between devices: 415 us -> 371 us
  starting transfers between devices: 253 us -> 281 us
    ppermute x8, waiting for transfers between devices: 84.9 us -> 23.7 us  [shared_of_plane(): lax.ppermute(own, 'section', [(layer, 1 - layer)])]
    reduce_scatter x4, waiting for transfers between devices: 8.95 us -> 66.8 us  [shards(): lax.psum_scatter(grads, 'fsdp', scatter_dimension=1, tiled=True)]
    ppermute x75, waiting for transfers between devices: 250 us -> 208 us  [exchanged(): lax.ppermute(value, ('section', axis), pairs_within(axis, by, sections))]
    ppermute x9, starting transfers between devices: 48.6 us -> 71.2 us  [the longest x3 59 us: gathered_experts(): arrived = lax.ppermute(rows_of(1 - layer), 'section', [(layer, 1 - layer)])]
    all_gather x4 -> x3, waiting for transfers between devices: 43.2 us -> 54.6 us  [gathered_experts(): parts.append([lax.all_gather(shard, 'fsdp', axis=1, tiled=True)])]
    pallas_call x4 -> x3, Pallas kernels: 56.6 us -> 49 us  [experts_forward(): pl.pallas_call(functools.partial(experts_kernel, sources, depth, slots, b...]
    ppermute x36 -> x35, starting transfers between devices: 66.1 us -> 70.3 us  [swapped(): return lax.ppermute(value, 'section', [(0, 1), (1, 0)])]
  transfers between devices with their start and end apart: 140 -> 138, of which waited for: 48 -> 51; matrix products, arithmetic and copies ran while one was open for 8% -> 10% of each run, Pallas kernels for 24% -> 24%
where the time goes in v3:
time: 1110 us; the launch traced here: 1100 us
  waiting for transfers between devices  371 us (33%)
  Pallas kernels  300 us (27%)
  starting transfers between devices  281 us (25%)
  other arithmetic  83.8 us (8%)
  local copies, waits for them, and re-layouts  45.7 us (4%)
  between operations  19.8 us (2%)
    ppermute x75, waiting for transfers between devices, exchanged(): lax.ppermute(value, ('section', axis), pairs_within(axis, by, sections))  208 us
    ppermute x75, starting transfers between devices, exchanged(): lax.ppermute(value, ('section', axis), pairs_within(axis, by, sections))  113 us
    pallas_call x4, Pallas kernels, experts_backward(): pl.pallas_call(kernel, name='experts_backward', grid=(local, portions), i...  81 us
    ppermute x35, starting transfers between devices, swapped(): return lax.ppermute(value, 'section', [(0, 1), (1, 0)])  70.3 us
    reduce_scatter x4, waiting for transfers between devices, shards(): lax.psum_scatter(grads, 'fsdp', scatter_dimension=1, tiled=True)  66.8 us
    ppermute x3, starting transfers between devices, gathered_experts(): arrived = lax.ppermute(rows_of(1 - layer), 'section', [(layer, 1 - layer)])  59 us
    all_gather x3, waiting for transfers between devices, gathered_experts(): parts.append([lax.all_gather(shard, 'fsdp', axis=1, tiled=True)])  54.6 us
    pallas_call x2, Pallas kernels, attend_backward(): pl.pallas_call(functools.partial(attend_back_kernel, devices, len(parts))...  49.6 us
  transfers between devices with their start and end apart: 138, of which 51 were waited for; matrix products, arithmetic and copies ran while one was open for 10% of the time, Pallas kernels for 24%

profile of v3, /device:TPU:9, one launch (start us, length us, event | category | flops | bytes accessed | tf_op | source)
XLA Modules:
  0.0 1103.1 jit_solution(4696489443816938984)
XLA Ops:
  62.5 55.3 %collective-permute-start.52 = (bf16[3,384,1024]{2,1,0:T(8,128)(2,1)}, bf16[3,384,1024]{2,1,0:T(8,128)(2,1)}, u32[]{:S(2)}, u32[]{:S(2)}) collective-permute-start(bf16[3,384,1024]{2,1,0:T(8,128)(2,1)} %pad_maximum_fusion.1), channel_id=1, source_target_pairs={{16,0},{17,1},{18,2},{19,3},{20,4},{21,5},{22,6},{23,7},{24,8},{25... | collective-permute-start | bytes 7077896 | tf_op jit(solution)/shard_map/ppermute | solution.py:1125
  129.0 20.9 %collective-permute-done.12.refs_6_ = bf16[256,3200]{1,0:T(8,128)(2,1)} collective-permute-done((bf16[256,3200]{1,0:T(8,128)(2,1)}, bf16[256,3200]{1,0:T(8,128)(2,1)}, u32[]{:S(2)}, u32[]{:S(2)}) %collective-permute-start.12) | collective-permute-done | bytes 1638432 | tf_op jit(solution)/shard_map/ppermute | solution.py:1067
  175.3 12.2 %collective-permute-done.16.rest_3_.rest_7_.rest_19_.rest_23_ = bf16[2,256,512]{2,1,0:T(8,128)(2,1)} collective-permute-done((bf16[2,256,512]{2,1,0:T(8,128)(2,1)}, bf16[2,256,512]{2,1,0:T(8,128)(2,1)}, u32[]{:S(2)}, u32[]{:S(2)}) %collective-permute-start.16) | collective-permute-done | bytes 524320 | tf_op jit(solution)/shard_map/ppermute | solution.py:991
  187.5 13.9 %attend.2 = (bf16[256,1024]{1,0:T(8,128)(2,1)}, f32[4,2,512]{2,1,0:T(2,128)}, f32[256,1024]{1,0:T(8,128)}, bf16[272,1024]{1,0:T(8,128)(2,1)}) custom-call(s32[2]{0:T(128)} %pad_add_fusion.2.scal, bf16[256,1024]{1,0:T(8,128)(2,1)} %dynamic-slice_bitcast_fusion.1.x.rest_14_, bf16[256,1024]{1,0:T(8,128)(2,1)} %get-tuple-element.161.q.rest_10_, ...), custom_call_target="tpu_custom_call" | custom-call | flops 2684354560 | bytes 9437184 | tf_op jit(solution)/shard_map/attend/pallas_call | solution.py:211
  211.5 21.0 %collective-permute-done.32 = bf16[64,3200]{1,0:T(8,128)(2,1)S(1)} collective-permute-done((bf16[64,3200]{1,0:T(8,128)(2,1)S(1)}, bf16[64,3200]{1,0:T(8,128)(2,1)S(1)}, u32[]{:S(2)}, u32[]{:S(2)}) %collective-permute-start.32) | collective-permute-done | bytes 409632 | tf_op jit(solution)/shard_map/ppermute | solution.py:991
  240.3 24.2 %collective-permute-done.34 = bf16[64,3200]{1,0:T(8,128)(2,1)S(1)} collective-permute-done((bf16[64,3200]{1,0:T(8,128)(2,1)S(1)}, bf16[64,3200]{1,0:T(8,128)(2,1)S(1)}, u32[]{:S(2)}, u32[]{:S(2)}) %collective-permute-start.34) | collective-permute-done | bytes 409632 | tf_op jit(solution)/shard_map/ppermute | solution.py:991
  284.8 21.3 %experts_forward.3 = (f32[4,640,1024]{2,1,0:T(8,128)}, bf16[4,640,1024]{2,1,0:T(8,128)(2,1)}, bf16[256,1024]{1,0:T(8,128)(2,1)}, bf16[256,1024]{1,0:T(8,128)(2,1...) custom-call(s32[5]{0:T(128)} %stack.107.scal.refs_0_, ...), custom_call_target="tpu_custom_call" | custom-call | flops 10468982784 | bytes 20971520 | tf_op jit(solution)/shard_map/experts_forward/pallas_call | solution.py:507
  340.5 11.4 %collective-permute-done.31 = bf16[256,1024]{1,0:T(8,128)(2,1)} collective-permute-done((bf16[256,1024]{1,0:T(8,128)(2,1)}, bf16[256,1024]{1,0:T(8,128)(2,1)}, u32[]{:S(2)}, u32[]{:S(2)}) %collective-permute-start.31) | collective-permute-done | bytes 524320 | tf_op jit(solution)/shard_map/ppermute | solution.py:991
  384.8 14.3 %attend.3 = (bf16[256,1024]{1,0:T(8,128)(2,1)}, f32[4,2,512]{2,1,0:T(2,128)}, f32[256,1024]{1,0:T(8,128)}, bf16[272,1024]{1,0:T(8,128)(2,1)}) custom-call(s32[2]{0:T(128)} %pad_add_fusion.2.scal, bf16[256,1024]{1,0:T(8,128)(2,1)} %get-tuple-element.359.x.rest_14_, bf16[256,1024]{1,0:T(8,128)(2,1)} %get-tuple-element.177.q.rest_10_, ...), custom_call_target="tpu_custom_call" | custom-call | flops 2684354560 | bytes 9437184 | tf_op jit(solution)/shard_map/attend/pallas_call | solution.py:211
  445.7 17.1 %experts_forward.4 = (f32[3,640,1024]{2,1,0:T(8,128)}, bf16[3,640,1024]{2,1,0:T(8,128)(2,1)}, bf16[256,1024]{1,0:T(8,128)(2,1)}, bf16[256,1024]{1,0:T(8,128)(2,1...) custom-call(s32[5]{0:T(128)} %stack.107.scal.refs_0_, ...), custom_call_target="tpu_custom_call" | custom-call | flops 7851737088 | bytes 15728640 | tf_op jit(solution)/shard_map/experts_forward/pallas_call | solution.py:507
  462.9 46.5 %all-gather.8.cloned.1.call-done.rest_11_.rest_12_.rest_13_.rest_14_.refs_9_.refs_10_.refs_11_.refs_12_ = bf16[1,1536,1024]{2,1,0:T(8,128)(2,1)} async-done(((bf16[1,384,1024]{2,1,0:T(8,128)(2,1)}), bf16[1,1536,1024]{2,1,0:T(8,128)(2,1)}) %all-gather.8.cloned.1.call-update) | async-done | bytes 3145744 | tf_op jit(solution)/shard_map/all_gather | solution.py:1129
  538.1 11.9 %collective-permute-done.58.refs_3_ = bf16[256,1024]{1,0:T(8,128)(2,1)S(1)} collective-permute-done((bf16[256,1024]{1,0:T(8,128)(2,1)S(1)}, bf16[256,1024]{1,0:T(8,128)(2,1)S(1)}, u32[]{:S(2)}, u32[]{:S(2)}) %collective-permute-start.58) | collective-permute-done | bytes 524320 | tf_op jit(solution)/shard_map/ppermute | solution.py:991
  571.9 12.2 %collective-permute-start.67 = (bf16[272,1024]{1,0:T(8,128)(2,1)S(1)}, bf16[272,1024]{1,0:T(8,128)(2,1)}, u32[]{:S(2)}, u32[]{:S(2)}) collective-permute-start(bf16[272,1024]{1,0:T(8,128)(2,1)S(1)} %collective-permute-done.63.rest_2_), channel_id=1, source_target_pairs={{0,16},{16,0},{1,17},{17,1},{2,18},{18,2},{3,19},{19,3},{4,20},{20... | collective-permute-start | bytes 1671176 | tf_op jit(solution)/shard_map/ppermute | solution.py:995
  591.5 10.7 experts_backward.4
  608.8 30.7 %experts_backward.5 = (bf16[3,1536,1024]{2,1,0:T(8,128)(2,1)}, f32[3,1,1024]{2,1,0:T(1,128)}, bf16[256,1024]{1,0:T(8,128)(2,1)}, bf16[256,1024]{1,0:T(8,128)(2,1...) custom-call(s32[5]{0:T(128)} %stack.107.scal.refs_0_, ...), custom_call_target="tpu_custom_call" | custom-call | flops 13891534848 | bytes 27525120 | tf_op jit(solution)/shard_map/experts_backward/pallas_call | solution.py:660
  646.2 15.8 %reduce-scatter.5.cloned.1.call-done.refs_0_ = bf16[1,384,1024]{2,1,0:T(8,128)(2,1)} async-done(((bf16[1,1536,1024]{2,1,0:T(8,128)(2,1)}), bf16[1,384,1024]{2,1,0:T(8,128)(2,1)}) %reduce-scatter.5.cloned.1.call-update) | async-done | bytes 786448 | tf_op jit(solution)/shard_map/reduce_scatter | solution.py:1318
  669.6 25.0 %attend_backward.2 = (f32[256,1024]{1,0:T(8,128)}, bf16[1024,2048]{1,0:T(8,128)(2,1)}, f32[1,1024]{1,0:T(1,128)}, bf16[256,1024]{1,0:T(8,128)(2,1)}, bf16[2,256,...) custom-call(s32[2]{0:T(128)} %pad_add_fusion.2.scal, ...), custom_call_target="tpu_custom_call" | custom-call | flops 6442450944 | bytes 19922944 | tf_op jit(solution)/shard_map/attend_backward/pallas_call | solution.py:866
  743.1 12.3 %collective-permute-start.84 = (bf16[272,1024]{1,0:T(8,128)(2,1)}, bf16[272,1024]{1,0:T(8,128)(2,1)S(1)}, u32[]{:S(2)}, u32[]{:S(2)}) collective-permute-start(bf16[272,1024]{1,0:T(8,128)(2,1)} %grad_message.1.rest_0_), channel_id=1, source_target_pairs={{0,16},{16,0},{1,17},{17,1},{2,18},{18,2},{3,19},{19,3},{4,20},{20... | collective-permute-start | bytes 1671176 | tf_op jit(solution)/shard_map/ppermute | solution.py:995
  777.5 23.5 %experts_backward.6 = (bf16[3,1536,1024]{2,1,0:T(8,128)(2,1)}, f32[3,1,1024]{2,1,0:T(1,128)}, bf16[3,640,1024]{2,1,0:T(8,128)(2,1)}) custom-call(s32[5]{0:T(128)} %stack.107.scal.refs_0_, f32[8,3,256]{2,1,0:T(4,128)} %bitcast.148, f32[8,3,256]{2,1,0:T(4,128)} %bitcast.158, f32[8,2,256]{2,1,0:T(2,128)} %get-tuple-element.246.refs_3_, ...), custom_call_target="tpu_custom_call" | custom-call | flops 13891534848 | bytes 27525120 | tf_op jit(solution)/shard_map/experts_backward/pallas_call | solution.py:660
  827.2 16.2 %experts_backward.7 = (bf16[1,1536,1024]{2,1,0:T(8,128)(2,1)}, f32[1,1,1024]{2,1,0:T(1,128)}, bf16[256,1024]{1,0:T(8,128)(2,1)}, bf16[256,1024]{1,0:T(8,128)(2,1...) custom-call(s32[5]{0:T(128)} %concatenate.55.refs_0_, ...), custom_call_target="tpu_custom_call" | custom-call | flops 4630511616 | bytes 9175040 | tf_op jit(solution)/shard_map/experts_backward/pallas_call | solution.py:660
  865.7 11.7 %collective-permute-done.100.rest_3_ = bf16[256,1024]{1,0:T(8,128)(2,1)} collective-permute-done((bf16[256,1024]{1,0:T(8,128)(2,1)S(1)}, bf16[256,1024]{1,0:T(8,128)(2,1)}, u32[]{:S(2)}, u32[]{:S(2)}) %collective-permute-start.100) | collective-permute-done | bytes 524320 | tf_op jit(solution)/shard_map/ppermute | solution.py:991
  878.2 24.6 %attend_backward.3 = (f32[256,1024]{1,0:T(8,128)}, bf16[1024,2048]{1,0:T(8,128)(2,1)}, f32[1,1024]{1,0:T(1,128)}, bf16[256,1024]{1,0:T(8,128)(2,1)}, bf16[2,256,...) custom-call(s32[2]{0:T(128)} %pad_add_fusion.2.scal, ...), custom_call_target="tpu_custom_call" | custom-call | flops 6442450944 | bytes 19922944 | tf_op jit(solution)/shard_map/attend_backward/pallas_call | solution.py:866
  921.5 10.7 collective-permute-done.104.rest_2_
  1032.9 51.0 %reduce-scatter.11.cloned.1.call-done.refs_2_ = bf16[1,384,1024]{2,1,0:T(8,128)(2,1)} async-done(((bf16[1,1536,1024]{2,1,0:T(8,128)(2,1)}), bf16[1,384,1024]{2,1,0:T(8,128)(2,1)}) %reduce-scatter.11.cloned.1.call-update) | async-done | bytes 786448 | tf_op jit(solution)/shard_map/reduce_scatter | solution.py:1318
  (583 shorter events, 569.1 us)
Async XLA Ops:
  7.2 277.6 %all-gather.4.cloned.1.call-start = ((), (), s32[]{:S(2)}) async-start(), calls=%async_computation.4 | async-start | bytes 15728640 | tf_op jit(solution)/shard_map/all_gather | solution.py:1129
  28.5 417.2 %all-gather.6.cloned.1.call-start = ((), (), s32[]{:S(2)}) async-start(), calls=%async_computation.5 | async-start | bytes 11796480 | tf_op jit(solution)/shard_map/all_gather | solution.py:1129
  52.8 66.3 %collective-permute-start.7 = (bf16[256,3200]{1,0:T(8,128)(2,1)}, bf16[256,3200]{1,0:T(8,128)(2,1)}, u32[]{:S(2)}, u32[]{:S(2)}) collective-permute-start(bf16[256,3200]{1,0:T(8,128)(2,1)} %pad_maximum_fusion.3.refs_0_), channel_id=1, source_target_pairs={{0,4},{4,0},{8,12},{12,8},{1,5},{5,1},{9,13},{13,9},{2,6},{6,2},{1... | collective-permute-start | bytes 4915208 | tf_op jit(solution)/shard_map/ppermute | solution.py:991
  54.6 65.7 %collective-permute-start.8 = (bf16[256,3200]{1,0:T(8,128)(2,1)}, bf16[256,3200]{1,0:T(8,128)(2,1)}, u32[]{:S(2)}, u32[]{:S(2)}) collective-permute-start(bf16[256,3200]{1,0:T(8,128)(2,1)} %pad_maximum_fusion.3.refs_0_), channel_id=1, source_target_pairs={{0,8},{4,12},{8,0},{12,4},{1,9},{5,13},{9,1},{13,5},{2,10},{6,14},... | collective-permute-start | bytes 4915208 | tf_op jit(solution)/shard_map/ppermute | solution.py:991
  56.5 65.2 %collective-permute-start.9 = (bf16[256,3200]{1,0:T(8,128)(2,1)}, bf16[256,3200]{1,0:T(8,128)(2,1)}, u32[]{:S(2)}, u32[]{:S(2)}) collective-permute-start(bf16[256,3200]{1,0:T(8,128)(2,1)} %pad_maximum_fusion.3.refs_0_), channel_id=1, source_target_pairs={{0,12},{4,8},{8,4},{12,0},{1,13},{5,9},{9,5},{13,1},{2,14},{6,10},... | collective-permute-start | bytes 4915208 | tf_op jit(solution)/shard_map/ppermute | solution.py:991
  62.5 106.0 %collective-permute-start.52 = (bf16[3,384,1024]{2,1,0:T(8,128)(2,1)}, bf16[3,384,1024]{2,1,0:T(8,128)(2,1)}, u32[]{:S(2)}, u32[]{:S(2)}) collective-permute-start(bf16[3,384,1024]{2,1,0:T(8,128)(2,1)} %pad_maximum_fusion.1), channel_id=1, source_target_pairs={{16,0},{17,1},{18,2},{19,3},{20,4},{21,5},{22,6},{23,7},{24,8},{25... | collective-permute-start | bytes 7077896 | tf_op jit(solution)/shard_map/ppermute | solution.py:1125
  201.4 308.0 %all-gather.8.cloned.1.call-start = ((), (), s32[]{:S(2)}) async-start(), calls=%async_computation.6 | async-start | bytes 3932160 | tf_op jit(solution)/shard_map/all_gather | solution.py:1129
  201.5 36.6 %collective-permute-start.17 = (bf16[272,1024]{1,0:T(8,128)(2,1)}, bf16[272,1024]{1,0:T(8,128)(2,1)S(1)}, u32[]{:S(2)}, u32[]{:S(2)}) collective-permute-start(bf16[272,1024]{1,0:T(8,128)(2,1)} %get-tuple-element.164.rest_0_), channel_id=1, source_target_pairs={{0,4},{4,0},{8,12},{12,8},{16,20},{20,16},{24,28},{28,24},{1,5},{5... | collective-permute-start | bytes 1671176 | tf_op jit(solution)/shard_map/ppermute | solution.py:991
  201.8 36.8 %collective-permute-start.18 = (bf16[272,1024]{1,0:T(8,128)(2,1)}, bf16[272,1024]{1,0:T(8,128)(2,1)S(1)}, u32[]{:S(2)}, u32[]{:S(2)}) collective-permute-start(bf16[272,1024]{1,0:T(8,128)(2,1)} %get-tuple-element.164.rest_0_), channel_id=1, source_target_pairs={{0,8},{4,12},{8,0},{12,4},{16,24},{20,28},{24,16},{28,20},{1,9},{5... | collective-permute-start | bytes 1671176 | tf_op jit(solution)/shard_map/ppermute | solution.py:991
  202.1 36.5 %collective-permute-start.19 = (bf16[272,1024]{1,0:T(8,128)(2,1)}, bf16[272,1024]{1,0:T(8,128)(2,1)S(1)}, u32[]{:S(2)}, u32[]{:S(2)}) collective-permute-start(bf16[272,1024]{1,0:T(8,128)(2,1)} %get-tuple-element.164.rest_0_), channel_id=1, source_target_pairs={{0,12},{4,8},{8,4},{12,0},{16,28},{20,24},{24,20},{28,16},{1,13},{... | collective-permute-start | bytes 1671176 | tf_op jit(solution)/shard_map/ppermute | solution.py:991
  265.9 44.0 %collective-permute-start.35 = (bf16[256,3200]{1,0:T(8,128)(2,1)}, bf16[256,3200]{1,0:T(8,128)(2,1)}, u32[]{:S(2)}, u32[]{:S(2)}) collective-permute-start(bf16[256,3200]{1,0:T(8,128)(2,1)} %pad_maximum_fusion.4.refs_0_), channel_id=1, source_target_pairs={{16,20},{20,16},{24,28},{28,24},{17,21},{21,17},{25,29},{29,25},{1... | collective-permute-start | bytes 4915208 | tf_op jit(solution)/shard_map/ppermute | solution.py:991
  269.0 43.3 %collective-permute-start.36 = (bf16[256,3200]{1,0:T(8,128)(2,1)}, bf16[256,3200]{1,0:T(8,128)(2,1)}, u32[]{:S(2)}, u32[]{:S(2)}) collective-permute-start(bf16[256,3200]{1,0:T(8,128)(2,1)} %pad_maximum_fusion.4.refs_0_), channel_id=1, source_target_pairs={{16,24},{20,28},{24,16},{28,20},{17,25},{21,29},{25,17},{29,21},{1... | collective-permute-start | bytes 4915208 | tf_op jit(solution)/shard_map/ppermute | solution.py:991
  272.2 42.6 %collective-permute-start.37 = (bf16[256,3200]{1,0:T(8,128)(2,1)}, bf16[256,3200]{1,0:T(8,128)(2,1)S(1)}, u32[]{:S(2)}, u32[]{:S(2)}) collective-permute-start(bf16[256,3200]{1,0:T(8,128)(2,1)} %pad_maximum_fusion.4.refs_0_), channel_id=1, source_target_pairs={{16,28},{20,24},{24,20},{28,16},{17,29},{21,25},{25,21},{29,17},{1... | collective-permute-start | bytes 4915208 | tf_op jit(solution)/shard_map/ppermute | solution.py:991
  319.3 342.7 %reduce-scatter.5.cloned.1.call-start = ((), (), s32[]{:S(2)}) async-start(), calls=%async_computation.7 | async-start | bytes 3932160 | tf_op jit(solution)/shard_map/reduce_scatter | solution.py:1318
  602.2 253.4 %reduce-scatter.7.cloned.1.call-start = ((), (), s32[]{:S(2)}) async-start(), calls=%async_computation.8 | async-start | bytes 11796480 | tf_op jit(solution)/shard_map/reduce_scatter | solution.py:1318
  639.5 368.6 %reduce-scatter.9.cloned.1.call-start = ((), (), s32[]{:S(2)}) async-start(), calls=%async_computation.9 | async-start | bytes 11796480 | tf_op jit(solution)/shard_map/reduce_scatter | solution.py:1318
  694.6 71.0 %collective-permute-start.88 = (bf16[1024,2048]{1,0:T(8,128)(2,1)}, bf16[1024,2048]{1,0:T(8,128)(2,1)}, u32[]{:S(2)}, u32[]{:S(2)}) collective-permute-start(bf16[1024,2048]{1,0:T(8,128)(2,1)} %get-tuple-element.236), channel_id=1, source_target_pairs={{0,16},{1,17},{2,18},{3,19},{4,20},{5,21},{6,22},{7,23},{8,24},{9,... | collective-permute-start | bytes 12582920 | tf_op jit(solution)/shard_map/ppermute | solution.py:1232
  801.0 282.8 %reduce-scatter.11.cloned.1.call-start = ((), (), s32[]{:S(2)}) async-start(), calls=%async_computation.10 | async-start | bytes 3932160 | tf_op jit(solution)/shard_map/reduce_scatter | solution.py:1318
  806.7 36.7 %collective-permute-start.94 = (bf16[256,1152]{1,0:T(8,128)(2,1)S(1)}, bf16[256,1152]{1,0:T(8,128)(2,1)}, u32[]{:S(2)}, u32[]{:S(2)}) collective-permute-start(bf16[256,1152]{1,0:T(8,128)(2,1)S(1)} %copy-done.32), channel_id=1, source_target_pairs={{16,24},{20,28},{24,16},{28,20},{17,25},{21,29},{25,17},{29,21},{1... | collective-permute-start | bytes 1769480 | tf_op jit(solution)/shard_map/ppermute | solution.py:991
  808.6 34.8 %collective-permute-start.95 = (bf16[256,1152]{1,0:T(8,128)(2,1)S(1)}, bf16[256,1152]{1,0:T(8,128)(2,1)}, u32[]{:S(2)}, u32[]{:S(2)}) collective-permute-start(bf16[256,1152]{1,0:T(8,128)(2,1)S(1)} %copy-done.31), channel_id=1, source_target_pairs={{16,28},{20,24},{24,20},{28,16},{17,29},{21,25},{25,21},{29,17},{1... | collective-permute-start | bytes 1769480 | tf_op jit(solution)/shard_map/ppermute | solution.py:991
  941.1 39.4 %collective-permute-start.117 = (bf16[1024,1152]{1,0:T(8,128)(2,1)}, bf16[1024,1152]{1,0:T(8,128)(2,1)}, u32[]{:S(2)}, u32[]{:S(2)}) collective-permute-start(bf16[1024,1152]{1,0:T(8,128)(2,1)} %get-tuple-element.293), channel_id=1, source_target_pairs={{16,0},{17,1},{18,2},{19,3},{20,4},{21,5},{22,6},{23,7},{24,8},{25... | collective-permute-start | bytes 7077896 | tf_op jit(solution)/shard_map/ppermute | solution.py:1232
  950.1 58.0 %collective-permute-start.107 = (f32[256,1024]{1,0:T(8,128)S(1)}, f32[256,1024]{1,0:T(8,128)}, u32[]{:S(2)}, u32[]{:S(2)}) collective-permute-start(f32[256,1024]{1,0:T(8,128)S(1)} %broadcast_select_fusion), channel_id=1, source_target_pairs={{0,16},{16,0},{1,17},{17,1},{2,18},{18,2},{3,19},{19,3},{4,20},{20... | collective-permute-start | bytes 3145736 | tf_op jit(solution)/shard_map/ppermute | solution.py:995
  985.4 38.4 %collective-permute-start.127 = (bf16[3,384,1024]{2,1,0:T(8,128)(2,1)}, bf16[3,384,1024]{2,1,0:T(8,128)(2,1)}, u32[]{:S(2)}, u32[]{:S(2)}) collective-permute-start(bf16[3,384,1024]{2,1,0:T(8,128)(2,1)} %reduce-scatter.7.cloned.1.call-done.refs_0_), channel_id=1, source_target_pairs={{0,16},{1,17},{2,18},{3,19},{4,20},{5,21},{6,22},{7,23},{8,24},{9,... | collective-permute-start | bytes 7077896 | tf_op jit(solution)/shard_map/ppermute | solution.py:1384
  1022.3 67.2 %collective-permute-start.129 = (bf16[1,384,1024]{2,1,0:T(8,128)(2,1)}, bf16[1,384,1024]{2,1,0:T(8,128)(2,1)S(1)}, u32[]{:S(2)}, u32[]{:S(2)}) collective-permute-start(bf16[1,384,1024]{2,1,0:T(8,128)(2,1)} %reduce-scatter.5.cloned.1.call-done.refs_0_), channel_id=1, source_target_pairs={{0,16},{1,17},{2,18},{3,19},{4,20},{5,21},{6,22},{7,23},{8,24},{9,... | collective-permute-start | bytes 2359304 | tf_op jit(solution)/shard_map/ppermute | solution.py:1384
  (204 other events, 2684.0 us)
Sparse Core Ops, SparseCore 0:
  28.7 248.9 all-gather.3
  279.8 165.8 all-gather.5
  447.3 62.0 all-gather.7
  602.3 59.5 reduce-scatter.4
  664.1 161.6 reduce-scatter.6
  828.0 176.2 reduce-scatter.8
  1006.6 77.2 reduce-scatter.10

commit v4 on v3

--- a/solution.py
+++ b/solution.py
@@ -32,8 +32,10 @@
     )
 
 
-def cost(flops, moved, exps=0):
-    return pl.CostEstimate(flops=int(flops), bytes_accessed=int(moved), transcendentals=int(exps))
+def cost(flops, moved, exps=0, share=1.0):
+    return pl.CostEstimate(
+        flops=int(flops / share), bytes_accessed=int(moved), transcendentals=int(exps)
+    )
 
 
 def mm(a, b):
@@ -148,7 +150,9 @@
             jax.ShapeDtypeStruct((2, rows, KW), BF16),
         ],
         compiler_params=params(1),
-        cost_estimate=cost(2 * rows * width * 2048, 2 * width * 2048 + 8 * rows * width),
+        cost_estimate=cost(
+            2 * rows * width * 2048, 2 * width * 2048 + 8 * rows * width, share=0.2
+        ),
     )(x, gain, shared, shared, cosine, sine)
 
 
@@ -240,6 +244,7 @@
             4 * rows * keys * QH * HD * 2 + 2 * rows * width * width,
             2 * width * width + 4 * keys * width + 12 * rows * width,
             rows * keys * QH,
+            0.17,
         ),
     )(scal, x, q, *kvs, *kvs, shared, gain, router, mask)
 
@@ -294,15 +299,23 @@
     return jnp.concatenate(columns, axis=0)
 
 
-def finish_kernel(count, *refs):
-    terms, (middle, goal, valid, hidden, mixed_out, grad_out, message) = (
-        refs[:count],
-        refs[count:],
-    )
+def finish_kernel(count, routed, slots, *refs):
+    terms, (middle, goal, valid, refs) = refs[:count], (*refs[count : count + 3], refs[count + 3 :])
+    if routed:
+        rank, refs = refs[0], refs[1:]
+        arrived, refs = refs[:routed], refs[routed:]
+    hidden, mixed_out, grad_out, message, refs = *refs[:4], refs[4:]
     rows, width = middle.shape
     mixed = terms[0][...].astype(F32)
     for term in terms[1:]:
         mixed = mixed + term[...].astype(F32)
+    if routed:
+        given = jnp.concatenate([ref[...].reshape(-1, width) for ref in arrived], axis=0)
+        hots = [
+            jnp.where(one_hot(rank[i : i + 1, :], slots), 1.0, 0.0).astype(BF16)
+            for i in range(rank.shape[0])
+        ]
+        mixed = mixed + mm_tn(jnp.concatenate(hots, axis=0), given)
     output = middle[...] + mixed
     hidden[...] = output.astype(BF16)
     mixed_out[...] = mixed
@@ -310,6 +323,33 @@
     grad_out[...] = grad
     error = 0.5 * jnp.sum(jnp.sum(grad * grad, axis=1, keepdims=True), axis=0, keepdims=True)
     fill_message(message, grad, mixed, error)
+    if routed:
+        low = message[:rows, :]
+        inner = message[rows:, :rows]
+        for i, hot in enumerate(hots):
+            out = refs[i // 2]
+            out[i % 2, :slots, :] = mm(hot, low).astype(BF16)
+            spread = jnp.where(one_hot(rank[i : i + 1, :], 128), 1.0, 0.0).astype(BF16)
+            out[i % 2, slots:, :128] = mm_nt(inner, spread).astype(BF16)
+            out[i % 2, slots:, 128:] = jnp.zeros((EXT, width - 128), BF16)
+
+
+def finish(terms, middle, goal, valid, rank=None, arrived=(), slots=0):
+    rows, width = middle.shape
+    messages = len(rank) // 2 if arrived else 0
+    return pl.pallas_call(
+        functools.partial(finish_kernel, len(terms), len(arrived), slots),
+        name="finish",
+        out_shape=[
+            jax.ShapeDtypeStruct((rows, width), BF16),
+            jax.ShapeDtypeStruct((rows, width), F32),
+            jax.ShapeDtypeStruct((rows, width), F32),
+            jax.ShapeDtypeStruct((rows + EXT, width), BF16),
+            *[jax.ShapeDtypeStruct((2, slots + EXT, width), BF16) for _ in range(messages)],
+        ],
+        compiler_params=params(),
+        cost_estimate=cost(8 * rows * width, 24 * rows * width),
+    )(*terms, middle, goal, valid, *([rank, *arrived] if arrived else []))
 
 
 def fill_message(message, grad, mixed, error):
@@ -328,22 +368,6 @@
         error = error - term
     message[rows:, :rows] = ext.astype(BF16)
     message[rows:, rows:] = jnp.zeros((EXT, width - rows), BF16)
-
-
-def finish(terms, middle, goal, valid):
-    rows, width = middle.shape
-    return pl.pallas_call(
-        functools.partial(finish_kernel, len(terms)),
-        name="finish",
-        out_shape=[
-            jax.ShapeDtypeStruct((rows, width), BF16),
-            jax.ShapeDtypeStruct((rows, width), F32),
-            jax.ShapeDtypeStruct((rows, width), F32),
-            jax.ShapeDtypeStruct((rows + EXT, width), BF16),
-        ],
-        compiler_params=params(),
-        cost_estimate=cost(8 * rows * width, 24 * rows * width),
-    )(*terms, middle, goal, valid)
 
 
 def message_kernel(grad, mixed, message):
@@ -421,7 +445,10 @@
         ],
         compiler_params=params(1),
         cost_estimate=cost(
-            2 * local * sources * slots * rows * width, 2 * sources * width * (rows + local * slots)
+            2 * local * sources * slots * rows * width,
+            2 * sources * width * (rows + local * slots),
+            0,
+            0.05 * local,
         ),
     )(scal, *msgs, rank)
     return taken.reshape(local, sources * slots, width), beside
@@ -436,16 +463,19 @@
         w2[pl.ds(pl.multiple_of(at * down, down), down), :] = block[0, up:]
 
 
-def experts_kernel(sources, depth, slots, chained, scal, *rest):
+def experts_kernel(sources, depth, slots, chained, combined, scal, *rest):
     prior = ()
     if chained:
         prior, rest = rest[:sources], rest[sources:]
     rank, gates, xs, rest = *rest[:3], rest[3:]
     blocks, rest = rest[:depth], rest[depth:]
     gu_out, y_out, rest = *rest[:2], rest[2:]
-    outs, rest = rest[:sources], rest[sources:]
-    held, w1, w2 = rest[:3]
-    width = held.shape[-1]
+    if combined:
+        outs, rest = rest[:sources], rest[sources:]
+        held, w1, w2 = rest[:3]
+    else:
+        rows_out, w1, w2 = rest
+    width = w1.shape[0]
     step, part = pl.program_id(0), pl.program_id(1)
     portions = sources // (xs.shape[1] // slots)
     portion = sources // portions
@@ -467,13 +497,16 @@
         [part * portion + n for n in range(portion)],
         slots,
     )
-    held[step, pl.ds(part * portion, portion)] = (
-        (column * out.astype(F32)).astype(BF16).reshape(portion, slots, width)
-    )
-
-    @pl.when((step == pl.num_programs(0) - 1) & (part == portions - 1))
-    def _():
-        combine(rank, held, prior, outs, rest[3:], slots)
+    given = (column * out.astype(F32)).astype(BF16).reshape(portion, slots, width)
+    if combined:
+        held[step, pl.ds(part * portion, portion)] = given
+
+        @pl.when((step == pl.num_programs(0) - 1) & (part == portions - 1))
+        def _():
+            combine(rank, held, prior, outs, rest[3:], slots)
+
+    else:
+        rows_out[0] = given
 
 
 def weight_specs(blocks, depth, base=0):
@@ -496,7 +529,7 @@
     ]
 
 
-def experts_forward(scal, xs, rank, gates, blocks, depth, slots, first, prior=()):
+def experts_forward(scal, xs, rank, gates, blocks, depth, slots, first, prior=(), combined=True):
     sources, local, rows = rank.shape
     width = xs.shape[2]
     portions = max(1, sources // 8)
@@ -505,7 +538,7 @@
     anywhere = pl.BlockSpec(memory_space=pl.ANY)
     each = lambda shape, base=0: pl.BlockSpec((1,) + shape, lambda e, r: (e + base, r, 0))
     outs = pl.pallas_call(
-        functools.partial(experts_kernel, sources, depth, slots, bool(prior)),
+        functools.partial(experts_kernel, sources, depth, slots, bool(prior), combined),
         name="experts_forward",
         grid=(local, portions),
         in_specs=[
@@ -519,34 +552,52 @@
         out_specs=[
             each((count // portions, 2 * FF_E)),
             each((count // portions, width)),
-            *[anywhere for _ in range(sources)],
+            *(
+                [anywhere] * sources
+                if combined
+                else [
+                    pl.BlockSpec((1, sources // portions, slots, width), lambda e, r: (e, r, 0, 0))
+                ]
+            ),
         ],
         out_shape=[
             jax.ShapeDtypeStruct((local, count, 2 * FF_E), F32),
             jax.ShapeDtypeStruct((local, count, width), BF16),
-            *[jax.ShapeDtypeStruct((rows, width), BF16) for _ in range(sources)],
+            *(
+                [jax.ShapeDtypeStruct((rows, width), BF16)] * sources
+                if combined
+                else [jax.ShapeDtypeStruct((local, sources, slots, width), BF16)]
+            ),
         ],
         scratch_shapes=[
-            pltpu.VMEM((local, sources, slots, width), BF16),
+            *([pltpu.VMEM((local, sources, slots, width), BF16)] if combined else []),
             pltpu.VMEM((width, 2 * FF_E), BF16),
             pltpu.VMEM((FF_E, width), BF16),
-            *stream_scratch(rows, width),
+            *(stream_scratch(rows, width) if combined else []),
         ],
         compiler_params=params(2),
         cost_estimate=cost(
-            2 * local * count * width * 3 * FF_E * 1.3, 8 * local * count * width, local * count * FF_E
+            2 * local * count * width * 3 * FF_E * 1.3,
+            8 * local * count * width,
+            local * count * FF_E,
+            0.1 * (local + 1),
         ),
     )(scal, *prior, rank, gates, xs, *arrays)
     return outs[:2], list(outs[2:])
 
 
 def experts_back_kernel(sources, depth, slots, mode, scal, *rest):
-    last, order = mode
+    last, order, direct = mode
     earlier = ()
     if last:
         full_rank, rest = rest[0], rest[1:]
         earlier, rest = rest[: len(order) - 1], rest[len(order) - 1 :]
-    rank, gates, inners, grads, xs, gu, ys, router, rest = *rest[:8], rest[8:]
+    if direct:
+        rank, gates, rest = *rest[:2], rest[2:]
+        given_rows, rest = rest[:sources], rest[sources:]
+    else:
+        rank, gates, inners, grads, rest = *rest[:4], rest[4:]
+    xs, gu, ys, router, rest = *rest[:4], rest[4:]
     blocks, rest = rest[:depth], rest[depth:]
     grad_out_ref, router_out, rest = *rest[:2], rest[2:]
     outs, rest = (rest[:sources], rest[sources:]) if last else (rest[:1], rest[1:])
@@ -562,8 +613,19 @@
 
     mine = [part * portion + n for n in range(portion)]
     gate_column = gate_columns(rank, lambda j: gates[j, pl.ds(step, 1), :], step, mine, slots)
-    inner_column = gate_columns(rank, lambda j: inners[j, 0:1, :], step, mine, slots)
-    grad_out = grads[0].astype(F32)
+    if direct:
+        blocks_of = [ref[0] if len(ref.shape) == 3 else ref[...] for ref in given_rows]
+        grad_out = jnp.concatenate([block[:slots] for block in blocks_of], axis=0).astype(F32)
+        inner_column = jnp.concatenate(
+            [
+                jnp.transpose(block[slots:, :128].astype(F32))[:slots, :2].sum(axis=1, keepdims=True)
+                for block in blocks_of
+            ],
+            axis=0,
+        )
+    else:
+        inner_column = gate_columns(rank, lambda j: inners[j, 0:1, :], step, mine, slots)
+        grad_out = grads[0].astype(F32)
     grad_y = (gate_column * grad_out).astype(BF16)
     given = jnp.sum(grad_out * ys[0].astype(F32), axis=1, keepdims=True)
     grad_logit = gate_column * (given - inner_column)
@@ -628,8 +690,9 @@
 
 
 def experts_backward(
-    scal, grads, rank, gates, inners, xs, kept, router, blocks, depth, slots, first, base, last
+    scal, grads, rank, gates, inners, xs, kept, router, blocks, depth, slots, first, base, begin, last
 ):
+    direct = isinstance(grads, list)
     sources, local, rows = rank.shape
     width = xs.shape[2]
     portions = max(1, sources // 8)
@@ -645,7 +708,20 @@
         before = [last[0]] + [
             part.reshape(part.shape[0], sources, slots, width) for part in last[1]
         ]
-    mode = (bool(last), last[2] if last else ())
+    mode = (bool(last), last[2] if last else (), direct)
+    if direct:
+        given = grads
+        given_specs = [
+            fixed(block.shape)
+            if block.ndim == 2
+            else pl.BlockSpec(
+                (1,) + block.shape[1:], lambda *_: (0, 0, 0), pipeline_mode=pl.Buffered(1)
+            )
+            for block in grads
+        ]
+    else:
+        given = [inners, grads]
+        given_specs = [fixed((sources, 2, rows)), each((count // portions, width), begin)]
 
     def kernel(*refs):
         refs = list(refs)
@@ -666,8 +742,7 @@
             *[fixed(part.shape) for part in before],
             fixed((sources, local, rows)),
             fixed((sources, local, rows)),
-            fixed((sources, 2, rows)),
-            each((count // portions, width)),
+            *given_specs,
             each((count // portions, width), first),
             each((count // portions, 2 * FF_E), base),
             each((count // portions, width), base),
@@ -697,9 +772,12 @@
         ],
         compiler_params=params(2),
         cost_estimate=cost(
-            2 * local * count * width * 3 * FF_E * 2.3, 14 * local * count * width, local * count * FF_E
+            2 * local * count * width * 3 * FF_E * 2.3,
+            14 * local * count * width,
+            local * count * FF_E,
+            0.37,
         ),
-    )(scal, *before, rank, gates, inners, grads, xs, gu, ys, router, *arrays)
+    )(scal, *before, rank, gates, *given, xs, gu, ys, router, *arrays)
     return outs[0], outs[1], list(outs[2:])
 
 
@@ -759,6 +837,35 @@
     )(scal, *arrays, *into)
 
 
+def pack_kernel(scal, up, down, out):
+    up_rows = up.shape[1]
+    out[0, :up_rows, :] = up[0]
+    out[0, up_rows:, :] = down[0]
+
+
+def pack_experts(half, up, down):
+    experts, up_rows, width = up.shape
+    rows = up_rows + down.shape[1]
+    local = experts // 2
+    take = lambda i, scal: (scal[0] * local + i, 0, 0)
+    return pl.pallas_call(
+        pack_kernel,
+        name="pack_experts",
+        grid_spec=pltpu.PrefetchScalarGridSpec(
+            num_scalar_prefetch=1,
+            grid=(local,),
+            in_specs=[
+                pl.BlockSpec((1, up_rows, width), take),
+                pl.BlockSpec((1, rows - up_rows, width), take),
+            ],
+            out_specs=pl.BlockSpec((1, rows, width), lambda i, scal: (i, 0, 0)),
+        ),
+        out_shape=jax.ShapeDtypeStruct((local, rows, width), BF16),
+        compiler_params=params(1),
+        cost_estimate=cost(0, 4 * local * rows * width),
+    )(half.astype(jnp.int32).reshape(1), up, down)
+
+
 def assemble_kernel(devices, depth, scal, *refs):
     owns, others, whole, sem = refs[:devices], refs[devices : 2 * devices], refs[-2], refs[-1]
     piece = whole.shape[0] // (devices * depth)
@@ -903,6 +1010,7 @@
             10 * rows * keys * QH * HD * 2 + 4 * rows * width * width,
             6 * width * width + 8 * keys * width + 20 * rows * width,
             rows * keys * QH,
+            0.23,
         ),
     )(
         scal,
@@ -978,7 +1086,9 @@
             jax.ShapeDtypeStruct((width, columns), BF16),
         ],
         compiler_params=params(1),
-        cost_estimate=cost(8 * rows * width * 2048, 8 * width * 2048 + 16 * rows * width),
+        cost_estimate=cost(
+            6 * rows * width * 2048, 8 * width * 2048 + 16 * rows * width, share=0.35
+        ),
     )(x, gain, dq, *parts, grad_mid, shared, shared, cosine, sine, small)
 
 
@@ -1004,11 +1114,14 @@
     return lax.optimization_barrier((value, other))[0]
 
 
-def scattered_sum(blocks, axis, sections):
-    total = blocks[0].astype(F32)
-    for k in range(1, len(blocks)):
-        total = total + exchanged(blocks[k], axis, k, sections).astype(F32)
-    return total
+def scattered(blocks, axis, sections):
+    return [blocks[0]] + [
+        exchanged(blocks[k], axis, k, sections) for k in range(1, len(blocks))
+    ]
+
+
+def added(terms):
+    return functools.reduce(lambda a, b: a + b, [term.astype(F32) for term in terms])
 
 
 def shards(
@@ -1105,27 +1218,40 @@
         layer_routes[:, 0, None] == jnp.arange(EXPERTS, dtype=jnp.int32)[None, :, None, None], axis=2
     ).astype(F32)
 
-    line_blocks = [after(shared_of_line(0, None), (ranks, masks)), None]
+    own_ranks = jnp.where(
+        masks[1] > 0.5,
+        jnp.dot(masks[1].astype(BF16), earlier, preferred_element_type=F32),
+        -1.0,
+    )
+    last_rank = jnp.take(
+        own_ranks,
+        jnp.stack(
+            [
+                (context ^ k) * held_experts + (section ^ m) * half_held + half_held - 1
+                for k in range(devices)
+                for m in range(2)
+            ]
+        ),
+        axis=0,
+    )
+
+    line_blocks = [after(shared_of_line(0, None), (ranks, masks, last_rank)), None]
 
     whole = [(0, half_held)]
     split = [(0, half_held - 1), (half_held - 1, 1)] if half_held > 1 else whole
     runs = [whole, split]
     back_runs = [split, split[::-1]]
+    if half_held > 2:
+        back_runs[1] = [(half_held - 1, 1), (half_held - 2, 1), (0, half_held - 2)]
+
+    arrived = swapped(pack_experts(1 - section, gate_up_weight[0], down_weight[0]))
+    mine = pack_experts(section, gate_up_weight[0], down_weight[0])
 
     def gathered_experts(layer, ahead):
+        own, other = (mine, arrived) if ahead is None else after((mine, arrived), ahead)
         parts = []
         for a, n in runs[layer]:
-            rows_of = lambda half: jnp.concatenate(
-                [
-                    weight[0, half * half_held + a : half * half_held + a + n]
-                    for weight in (gate_up_weight, down_weight)
-                ],
-                axis=1,
-            )
-            arrived = lax.ppermute(rows_of(1 - layer), "section", [(layer, 1 - layer)])
-            shard = jnp.where(section == layer, rows_of(layer), arrived)
-            if ahead is not None:
-                shard = after(shard, ahead)
+            shard = jnp.where(section == layer, own[a : a + n], other[a : a + n])
             parts.append([lax.all_gather(shard, "fsdp", axis=1, tiled=True)])
         return parts
 
@@ -1185,9 +1311,12 @@
         xs, gates = dispatch(
             first.astype(jnp.int32).reshape(1), messages, ranks[layer], slots, False
         )
-        for (a, n), blocks in zip(runs[layer], weights):
-            order = [line ^ k for k in range(depth)] if len(blocks) > 1 else range(depth)
-            scal = jnp.stack([first + a, *[jnp.asarray(o) for o in order]]).astype(jnp.int32)
+        sparse = layer == 1 and len(runs[layer]) > 1
+        for at, ((a, n), blocks) in enumerate(zip(runs[layer], weights)):
+            scal = jnp.stack([first + a, *[jnp.asarray(k) for k in range(depth)]]).astype(jnp.int32)
+            by_rows = sparse and at == len(runs[layer]) - 1
+            if by_rows:
+                scal = after(scal, terms)
             run, outs = experts_forward(
                 scal,
                 xs,
@@ -1197,16 +1326,25 @@
                 depth,
                 slots,
                 a,
-                outs,
+                () if by_rows else outs,
+                not by_rows,
             )
             kept.append((a, n, scal, run, blocks))
+            if not by_rows:
+                terms = returned(outs)
         if layer == layers - 1:
-            hidden_rows, mixed, grad_output, message = finish(
-                returned(outs), middle, my_targets, valid
+            routed = [last_rank, [], slots] if sparse else []
+            if sparse:
+                near, far = outs[0][0, :devices], swapped(outs[0][0, devices:])
+                routed[1] = [near[0], far[0]] + [
+                    exchanged(jnp.stack([near[k], far[k]]), "ctx", k) for k in range(1, devices)
+                ]
+            hidden_rows, mixed, grad_output, message, *row_messages = finish(
+                terms, middle, my_targets, valid, *routed
             )
             hidden.append(hidden_rows)
         else:
-            mixed = functools.reduce(lambda a, b: a + b, [t.astype(F32) for t in returned(outs)])
+            mixed = functools.reduce(lambda a, b: a + b, [t.astype(F32) for t in terms])
             hidden.append((middle + mixed).astype(BF16))
         saved.append(
             dict(
@@ -1240,18 +1378,16 @@
         ]
 
     def home_plane(blocks, layer):
-        return scattered_sum(blocks, "ctx", (layer,)).astype(BF16)
-
-    def home_line(plane, layer):
+        return added(scattered(blocks, "ctx", (layer,))).astype(BF16)
+
+    def home_line(plane, layer, ahead=None):
         size = plane.shape[0] // depth
-        return scattered_sum(
-            [
-                lax.dynamic_slice_in_dim(plane, (line ^ k) * size, size, 0)
-                for k in range(depth)
-            ],
-            "fsdp",
-            (layer,),
-        )
+        blocks = [
+            lax.dynamic_slice_in_dim(plane, (line ^ k) * size, size, 0) for k in range(depth)
+        ]
+        if ahead is not None:
+            blocks[-1] = after(blocks[-1], ahead)
+        return scattered(blocks, "fsdp", (layer,))
 
     def placed_rows(values):
         home = jnp.where(first_core, values[0], values[1])
@@ -1261,7 +1397,6 @@
         )
 
     input_grads, expert_grads = [None] * layers, [None] * layers
-    shared_grads = [None] * layers
     waiting = None
     summed = {}
     for layer in reversed(range(layers)):
@@ -1269,6 +1404,13 @@
         first, local, sources = places[layer]
         if layer < layers - 1:
             message = grad_message(grad_output, held["mixed"])
+        sparse = layer == 1 and len(back_runs[layer]) > 1
+        if sparse:
+            plane = [row_messages[0]] + [
+                exchanged(row_messages[k], "ctx", k) for k in range(1, devices)
+            ]
+            row_blocks = plane + [swapped(block[1]) for block in plane]
+            message = after(message, plane[1])
         messages = dispatched(message)
         if waiting is not None:
             blocks_1 = [home_blocks(part, 1) for part in waiting]
@@ -1290,9 +1432,18 @@
             if at == len(steps) - 1:
                 order = tuple(sorted(range(len(spans)), key=lambda i: spans[i]))
                 last = (ranks[layer], [rows_of for rows_of in outs], order)
-            grad_rows, inners = dispatch(
-                scal[:1], messages, ranks[layer][:, a : a + n], slots, True
-            )
+            if sparse and at == 0:
+                grad_rows, inners, start = row_blocks, None, a
+            elif not sparse:
+                grad_rows, inners = dispatch(
+                    scal[:1], messages, ranks[layer][:, a : a + n], slots, True
+                )
+                start = a
+            elif at == 1:
+                start = 0
+                grad_rows, inners = dispatch(
+                    scal[:1], messages, ranks[layer][:, : half_held - 1], slots, True
+                )
             grads, router_grad, rows_out = experts_backward(
                 scal,
                 grad_rows,
@@ -1307,18 +1458,19 @@
                 slots,
                 a,
                 a - base,
+                a - start,
                 last,
             )
             outs = rows_out if last else list(outs) + rows_out
-            if layer == 1 and at == 0:
+            if layer == 1 and inners is not None:
                 error = jnp.sum(inners[:, 1, 0])
             small = lax.dynamic_update_slice_in_dim(small, router_grad[:, 0], first + a, 0)
             gathered.append(grads)
-        summed[layer] = [
-            lax.psum_scatter(grads, "fsdp", scatter_dimension=1, tiled=True)
-            for grads in gathered
-        ]
-        expert_grads[layer] = list(zip(spans, summed[layer]))
+        over_line = lambda grads: lax.psum_scatter(
+            grads, "fsdp", scatter_dimension=1, tiled=True
+        )
+        at_once = gathered if layer == 1 or len(gathered) == 1 else gathered[:-1]
+        summed[layer] = [over_line(grads) for grads in at_once]
         if layer == 1:
             grad_output = after(grad_output, summed[1][0])
         else:
@@ -1353,7 +1505,7 @@
                 by *= 2
             loss_value = error / jnp.sum(lengths).astype(F32)
             hidden_out = placed_rows(hidden)
-            grad_mid = after(grad_mid, (loss_value, hidden_out))
+            grad_mid = after(grad_mid, (loss_value, hidden_out, summed[1][: len(steps) - 1]))
         small = lax.dynamic_update_slice_in_dim(small, gain_second_grad, EXPERTS + 1, 0)
         dx, packed = project_backward(
             held["x"],
@@ -1366,20 +1518,17 @@
             -sin_table,
             small,
         )
+        expert_grads[layer] = (spans, summed[layer])
         input_grads[layer] = dx
         grad_output = dx.astype(BF16).astype(F32)
         if layer == 1:
             waiting = (weight_grads, packed)
         else:
             outward, planes = after((outward, planes), packed)
-            shared_grads[0] = [
-                home_line(home_plane(blocks, 0), 0) for blocks in (home_blocks(packed, 0), outward)
-            ][::-1]
-            shared_grads[1] = [home_line(part, 1) for part in planes]
-
-    pick = lambda values: jnp.where(first_core, values[0], values[1])
-    outward, inward = (pick([shared_grads[0][i], shared_grads[1][i]]) for i in range(2))
-    input_out = placed_rows(input_grads)
+            summed[0] += [over_line(after(grads, packed)) for grads in gathered[len(at_once) :]]
+            inward_plane = home_plane(home_blocks(packed, 0), 0)
+            outward_plane = home_plane(outward, 0)
+
     def pieces_of(layer, at, part):
         arrived = lax.ppermute(part, "section", [(1 - layer, layer)])
         return [
@@ -1393,15 +1542,22 @@
             section.astype(jnp.int32).reshape(1), touched, held_experts, up_rows, experts, into
         )
 
-    parts = [(layer, at, part) for layer in (1, 0) for at, part in expert_grads[layer]]
+    parts = [(layer, at, part) for layer in (1, 0) for at, part in zip(*expert_grads[layer])]
     pieces = [piece for part in parts[:-1] for piece in pieces_of(*part)]
     layer, at, part = parts[-1]
     last = [half * half_held + at + i for half in range(2) for i in range(part.shape[0])]
     sums = ()
     if len(last) < held_experts:
         sums = placed(pieces, [e for e in range(held_experts) if e not in last], ())
-        outward, inward = after((outward, inward), sums)
-        part = after(part, (outward, inward, input_out))
+    first_terms = home_line(
+        jnp.concatenate([outward_plane, inward_plane], axis=1), 0, sums if sums else None
+    )
+    second_terms = home_line(jnp.concatenate(planes, axis=1), 1)
+    shared_grads = jnp.where(first_core, added(first_terms), added(second_terms))
+    outward, inward = shared_grads[:, : 2 * width], shared_grads[:, 2 * width :]
+    input_out = placed_rows(input_grads)
+    if sums:
+        part = after(part, (first_terms, second_terms))
     up_sum, down_sum = placed(pieces + pieces_of(layer, at, part), last, sums)
     at = 2 * KW
     return (

time: 1110 us -> 1100 us (level)
  starting transfers between devices: 281 us -> 225 us
  waiting for transfers between devices: 371 us -> 418 us
    ppermute x75, waiting for transfers between devices: 208 us -> 293 us  [exchanged(): lax.ppermute(value, ('section', axis), pairs_within(axis, by, sections))]
    ppermute x3 -> x0, starting transfers between devices: 59 us -> none  [gathered_experts(): arrived = lax.ppermute(rows_of(1 - layer), 'section', [(layer, 1 - layer)])]
    reduce_scatter x4 -> x5, waiting for transfers between devices: 66.8 us -> 15.8 us  [shards(): lax.psum_scatter(grads, 'fsdp', scatter_dimension=1, tiled=True)]
    ppermute x8, waiting for transfers between devices: 23.7 us -> 72.3 us  [shared_of_plane(): lax.ppermute(own, 'section', [(layer, 1 - layer)])]
    all_gather x3, waiting for transfers between devices: 54.6 us -> 22.3 us  [gathered_experts(): parts.append([lax.all_gather(shard, 'fsdp', axis=1, tiled=True)])]
    ppermute x35 -> x41, starting transfers between devices: 70.3 us -> 59 us  [swapped(): return lax.ppermute(value, 'section', [(0, 1), (1, 0)])]
    pallas_call x6 -> x5, Pallas kernels: 34.1 us -> 29.4 us  [dispatch(): pl.pallas_call(functools.partial(dispatch_kernel, sources, slots, backwar...]
    pallas_call x4 -> x5, Pallas kernels: 81 us -> 84.7 us  [experts_backward(): pl.pallas_call(kernel, name='experts_backward', grid=(local, portions), i...]
  transfers between devices with their start and end apart: 138 -> 143, of which waited for: 51 -> 59; matrix products, arithmetic and copies ran while one was open for 10% -> 10% of each run, Pallas kernels for 24% -> 25%
where the time goes in v4:
time: 1100 us; the launch traced here: 1090 us
  waiting for transfers between devices  418 us (38%)
  Pallas kernels  303 us (28%)
  starting transfers between devices  225 us (20%)
  other arithmetic  79 us (7%)
  local copies, waits for them, and re-layouts  41.4 us (4%)
  between operations  19.7 us (2%)
    ppermute x75, waiting for transfers between devices, exchanged(): lax.ppermute(value, ('section', axis), pairs_within(axis, by, sections))  293 us
    ppermute x75, starting transfers between devices, exchanged(): lax.ppermute(value, ('section', axis), pairs_within(axis, by, sections))  116 us
    pallas_call x5, Pallas kernels, experts_backward(): pl.pallas_call(kernel, name='experts_backward', grid=(local, portions), i...  84.7 us
    ppermute x8, waiting for transfers between devices, shared_of_plane(): lax.ppermute(own, 'section', [(layer, 1 - layer)])  72.3 us
    ppermute x41, starting transfers between devices, swapped(): return lax.ppermute(value, 'section', [(0, 1), (1, 0)])  59 us
    pallas_call x2, Pallas kernels, attend_backward(): pl.pallas_call(functools.partial(attend_back_kernel, devices, len(parts))...  48.7 us
    pallas_call x3, Pallas kernels, experts_forward(): pl.pallas_call(functools.partial(experts_kernel, sources, depth, slots, b...  44.9 us
    pallas_call x5, Pallas kernels, dispatch(): pl.pallas_call(functools.partial(dispatch_kernel, sources, slots, backwar...  29.4 us
  transfers between devices with their start and end apart: 143, of which 59 were waited for; matrix products, arithmetic and copies ran while one was open for 10% of the time, Pallas kernels for 25%

profile of v4, /device:TPU:9, one launch (start us, length us, event | category | flops | bytes accessed | tf_op | source)
XLA Modules:
  0.0 1087.5 jit_solution(9342781148655809603)
XLA Ops:
  53.9 37.3 %collective-permute-done.10.refs_4_ = bf16[256,3200]{1,0:T(8,128)(2,1)} collective-permute-done((bf16[256,3200]{1,0:T(8,128)(2,1)S(1)}, bf16[256,3200]{1,0:T(8,128)(2,1)}, u32[]{:S(2)}, u32[]{:S(2)}) %collective-permute-start.10) | collective-permute-done | bytes 1638432 | tf_op jit(solution)/shard_map/ppermute | solution.py:1180
  91.2 15.1 %collective-permute-done.13.refs_7_ = bf16[256,3200]{1,0:T(8,128)(2,1)} collective-permute-done((bf16[256,3200]{1,0:T(8,128)(2,1)}, bf16[256,3200]{1,0:T(8,128)(2,1)}, u32[]{:S(2)}, u32[]{:S(2)}) %collective-permute-start.13) | collective-permute-done | bytes 1638432 | tf_op jit(solution)/shard_map/ppermute | solution.py:1180
  106.2 17.5 %collective-permute-done.12.refs_6_ = bf16[256,3200]{1,0:T(8,128)(2,1)} collective-permute-done((bf16[256,3200]{1,0:T(8,128)(2,1)}, bf16[256,3200]{1,0:T(8,128)(2,1)}, u32[]{:S(2)}, u32[]{:S(2)}) %collective-permute-start.12) | collective-permute-done | bytes 1638432 | tf_op jit(solution)/shard_map/ppermute | solution.py:1180
  152.5 12.6 %collective-permute-done.15.rest_2_.rest_6_.rest_18_.rest_22_ = bf16[2,256,512]{2,1,0:T(8,128)(2,1)S(1)} collective-permute-done((bf16[2,256,512]{2,1,0:T(8,128)(2,1)}, bf16[2,256,512]{2,1,0:T(8,128)(2,1)S(1)}, u32[]{:S(2)}, u32[]{:S(2)}) %collective-permute-start.15) | collective-permute-done | bytes 524320 | tf_op jit(solution)/shard_map/ppermute | solution.py:1101
  166.1 14.0 %attend.2 = (bf16[256,1024]{1,0:T(8,128)(2,1)}, f32[4,2,512]{2,1,0:T(2,128)}, f32[256,1024]{1,0:T(8,128)}, bf16[272,1024]{1,0:T(8,128)(2,1)}) custom-call(s32[2]{0:T(128)} %pad_add_fusion.2.scal, bf16[256,1024]{1,0:T(8,128)(2,1)} %dynamic-slice_bitcast_fusion.1.x.rest_14_, bf16[256,1024]{1,0:T(8,128)(2,1)} %get-tuple-element.161.q.rest_10_, ...), custom_call_target="tpu_custom_call" | custom-call | flops 15790320640 | bytes 9437184 | tf_op jit(solution)/shard_map/attend/pallas_call | solution.py:215
  183.5 13.3 %collective-permute-start.34 = (bf16[64,3200]{1,0:T(8,128)(2,1)S(1)}, bf16[64,3200]{1,0:T(8,128)(2,1)S(1)}, u32[]{:S(2)}, u32[]{:S(2)}) collective-permute-start(bf16[64,3200]{1,0:T(8,128)(2,1)S(1)} %concatenate.55), channel_id=1, source_target_pairs={{16,19},{17,18},{18,17},{19,16},{20,23},{21,22},{22,21},{23,20},{2... | collective-permute-start | bytes 1228808 | tf_op jit(solution)/shard_map/ppermute | solution.py:1101
  205.5 27.9 %collective-permute-done.34 = bf16[64,3200]{1,0:T(8,128)(2,1)S(1)} collective-permute-done((bf16[64,3200]{1,0:T(8,128)(2,1)S(1)}, bf16[64,3200]{1,0:T(8,128)(2,1)S(1)}, u32[]{:S(2)}, u32[]{:S(2)}) %collective-permute-start.34) | collective-permute-done | bytes 409632 | tf_op jit(solution)/shard_map/ppermute | solution.py:1101
  235.3 19.7 %collective-permute-done.33 = bf16[64,3200]{1,0:T(8,128)(2,1)S(1)} collective-permute-done((bf16[64,3200]{1,0:T(8,128)(2,1)S(1)}, bf16[64,3200]{1,0:T(8,128)(2,1)S(1)}, u32[]{:S(2)}, u32[]{:S(2)}) %collective-permute-start.33) | collective-permute-done | bytes 409632 | tf_op jit(solution)/shard_map/ppermute | solution.py:1101
  274.8 21.5 %experts_forward.3 = (f32[4,640,1024]{2,1,0:T(8,128)}, bf16[4,640,1024]{2,1,0:T(8,128)(2,1)}, bf16[256,1024]{1,0:T(8,128)(2,1)}, bf16[256,1024]{1,0:T(8,128)(2,1...) custom-call(s32[5]{0:T(128)} %stack.177.scal.refs_0_, ...), custom_call_target="tpu_custom_call" | custom-call | flops 20937965568 | bytes 20971520 | tf_op jit(solution)/shard_map/experts_forward/pallas_call | solution.py:540
  330.4 11.3 %collective-permute-done.31 = bf16[256,1024]{1,0:T(8,128)(2,1)} collective-permute-done((bf16[256,1024]{1,0:T(8,128)(2,1)}, bf16[256,1024]{1,0:T(8,128)(2,1)}, u32[]{:S(2)}, u32[]{:S(2)}) %collective-permute-start.31) | collective-permute-done | bytes 524320 | tf_op jit(solution)/shard_map/ppermute | solution.py:1101
  363.3 13.0 %collective-permute-done.43.rest_2_.rest_6_.rest_18_.rest_22_ = bf16[2,256,512]{2,1,0:T(8,128)(2,1)} collective-permute-done((bf16[2,256,512]{2,1,0:T(8,128)(2,1)}, bf16[2,256,512]{2,1,0:T(8,128)(2,1)}, u32[]{:S(2)}, u32[]{:S(2)}) %collective-permute-start.43) | collective-permute-done | bytes 524320 | tf_op jit(solution)/shard_map/ppermute | solution.py:1101
  376.3 13.8 %attend.3 = (bf16[256,1024]{1,0:T(8,128)(2,1)}, f32[4,2,512]{2,1,0:T(2,128)}, f32[256,1024]{1,0:T(8,128)}, bf16[272,1024]{1,0:T(8,128)(2,1)}) custom-call(s32[2]{0:T(128)} %pad_add_fusion.2.scal, bf16[256,1024]{1,0:T(8,128)(2,1)} %get-tuple-element.362.x.rest_14_, bf16[256,1024]{1,0:T(8,128)(2,1)} %get-tuple-element.177.q.rest_10_, ...), custom_call_target="tpu_custom_call" | custom-call | flops 15790320640 | bytes 9437184 | tf_op jit(solution)/shard_map/attend/pallas_call | solution.py:215
  433.2 17.0 %experts_forward.4 = (f32[3,640,1024]{2,1,0:T(8,128)}, bf16[3,640,1024]{2,1,0:T(8,128)(2,1)}, bf16[256,1024]{1,0:T(8,128)(2,1)}, bf16[256,1024]{1,0:T(8,128)(2,1...) custom-call(s32[5]{0:T(128)} %stack.177.scal.refs_0_, ...), custom_call_target="tpu_custom_call" | custom-call | flops 19629342720 | bytes 15728640 | tf_op jit(solution)/shard_map/experts_forward/pallas_call | solution.py:540
  467.1 13.5 %collective-permute-done.56.refs_3_ = bf16[256,1024]{1,0:T(8,128)(2,1)S(1)} collective-permute-done((bf16[256,1024]{1,0:T(8,128)(2,1)S(1)}, bf16[256,1024]{1,0:T(8,128)(2,1)S(1)}, u32[]{:S(2)}, u32[]{:S(2)}) %collective-permute-start.56) | collective-permute-done | bytes 524320 | tf_op jit(solution)/shard_map/ppermute | solution.py:1101
  480.7 16.8 %all-gather.8.cloned.1.call-done.rest_3_.rest_4_.rest_5_.rest_6_.refs_15_.refs_16_.refs_17_.refs_18_ = bf16[1,1536,1024]{2,1,0:T(8,128)(2,1)} async-done(((bf16[1,384,1024]{2,1,0:T(8,128)(2,1)}), bf16[1,1536,1024]{2,1,0:T(8,128)(2,1)}) %all-gather.8.cloned.1.call-update) | async-done | bytes 3145744 | tf_op jit(solution)/shard_map/all_gather | solution.py:1255
  617.8 23.4 %experts_backward.7 = (bf16[2,1536,1024]{2,1,0:T(8,128)(2,1)}, f32[2,1,1024]{2,1,0:T(1,128)}, bf16[256,1024]{1,0:T(8,128)(2,1)}, bf16[256,1024]{1,0:T(8,128)(2,1...) custom-call(s32[5]{0:T(128)} %stack.177.scal.refs_0_, ...), custom_call_target="tpu_custom_call" | custom-call | flops 25029791744 | bytes 18350080 | tf_op jit(solution)/shard_map/experts_backward/pallas_call | solution.py:736
  670.7 24.1 %attend_backward.2 = (f32[256,1024]{1,0:T(8,128)}, bf16[1024,2048]{1,0:T(8,128)(2,1)}, f32[1,1024]{1,0:T(1,128)}, bf16[256,1024]{1,0:T(8,128)(2,1)}, bf16[2,256,...) custom-call(s32[2]{0:T(128)} %pad_add_fusion.2.scal, ...), custom_call_target="tpu_custom_call" | custom-call | flops 28010655744 | bytes 19922944 | tf_op jit(solution)/shard_map/attend_backward/pallas_call | solution.py:973
  742.6 12.7 %collective-permute-start.93 = (bf16[272,1024]{1,0:T(8,128)(2,1)}, bf16[272,1024]{1,0:T(8,128)(2,1)S(1)}, u32[]{:S(2)}, u32[]{:S(2)}) collective-permute-start(bf16[272,1024]{1,0:T(8,128)(2,1)} %grad_message.1.rest_0_), channel_id=1, source_target_pairs={{0,16},{16,0},{1,17},{17,1},{2,18},{18,2},{3,19},{19,3},{4,20},{20... | collective-permute-start | bytes 1671176 | tf_op jit(solution)/shard_map/ppermute | solution.py:1105
  776.7 23.6 %experts_backward.8 = (bf16[3,1536,1024]{2,1,0:T(8,128)(2,1)}, f32[3,1,1024]{2,1,0:T(1,128)}, bf16[3,640,1024]{2,1,0:T(8,128)(2,1)}) custom-call(s32[5]{0:T(128)} %stack.177.scal.refs_0_, f32[8,3,256]{2,1,0:T(4,128)} %bitcast.193, f32[8,3,256]{2,1,0:T(4,128)} %bitcast.203, f32[8,2,256]{2,1,0:T(2,128)} %get-tuple-element.246.refs_3_, ...), custom_call_target="tpu_custom_call" | custom-call | flops 37544689664 | bytes 27525120 | tf_op jit(solution)/shard_map/experts_backward/pallas_call | solution.py:736
  826.2 16.2 %experts_backward.9 = (bf16[1,1536,1024]{2,1,0:T(8,128)(2,1)}, f32[1,1,1024]{2,1,0:T(1,128)}, bf16[256,1024]{1,0:T(8,128)(2,1)}, bf16[256,1024]{1,0:T(8,128)(2,1...) custom-call(s32[5]{0:T(128)} %concatenate.60.refs_0_, ...), custom_call_target="tpu_custom_call" | custom-call | flops 12514895872 | bytes 9175040 | tf_op jit(solution)/shard_map/experts_backward/pallas_call | solution.py:736
  865.2 12.7 %collective-permute-done.109.rest_3_ = bf16[256,1024]{1,0:T(8,128)(2,1)} collective-permute-done((bf16[256,1024]{1,0:T(8,128)(2,1)S(1)}, bf16[256,1024]{1,0:T(8,128)(2,1)}, u32[]{:S(2)}, u32[]{:S(2)}) %collective-permute-start.109) | collective-permute-done | bytes 524320 | tf_op jit(solution)/shard_map/ppermute | solution.py:1101
  878.0 24.6 %attend_backward.3 = (f32[256,1024]{1,0:T(8,128)}, bf16[1024,2048]{1,0:T(8,128)(2,1)}, f32[1,1024]{1,0:T(1,128)}, bf16[256,1024]{1,0:T(8,128)(2,1)}, bf16[2,256,...) custom-call(s32[2]{0:T(128)} %pad_add_fusion.2.scal, ...), custom_call_target="tpu_custom_call" | custom-call | flops 28010655744 | bytes 19922944 | tf_op jit(solution)/shard_map/attend_backward/pallas_call | solution.py:973
  951.2 15.7 %reduce-scatter.12.cloned.1.call-done.refs_4_ = bf16[3,384,1024]{2,1,0:T(8,128)(2,1)} async-done(((bf16[3,1536,1024]{2,1,0:T(8,128)(2,1)}), bf16[3,384,1024]{2,1,0:T(8,128)(2,1)}) %reduce-scatter.12.cloned.1.call-update) | async-done | bytes 2359312 | tf_op jit(solution)/shard_map/reduce_scatter | solution.py:1469
  1024.6 33.1 %collective-permute-done.131 = bf16[64,3200]{1,0:T(8,128)(2,1)} collective-permute-done((bf16[64,3200]{1,0:T(8,128)(2,1)}, bf16[64,3200]{1,0:T(8,128)(2,1)}, u32[]{:S(2)}, u32[]{:S(2)}) %collective-permute-start.131) | collective-permute-done | bytes 409632 | tf_op jit(solution)/shard_map/ppermute | solution.py:1101
  (606 shorter events, 617.3 us)
Async XLA Ops:
  7.2 267.6 %all-gather.4.cloned.1.call-start = ((), (), s32[]{:S(2)}) async-start(), calls=%async_computation.5 | async-start | bytes 15728640 | tf_op jit(solution)/shard_map/all_gather | solution.py:1255
  21.7 411.5 %all-gather.6.cloned.1.call-start = ((), (), s32[]{:S(2)}) async-start(), calls=%async_computation.6 | async-start | bytes 11796480 | tf_op jit(solution)/shard_map/all_gather | solution.py:1255
  45.6 45.5 %collective-permute-start.10 = (bf16[256,3200]{1,0:T(8,128)(2,1)S(1)}, bf16[256,3200]{1,0:T(8,128)(2,1)}, u32[]{:S(2)}, u32[]{:S(2)}) collective-permute-start(bf16[256,3200]{1,0:T(8,128)(2,1)S(1)} %pad_maximum_fusion.refs_0_), channel_id=1, source_target_pairs={{0,16},{1,17},{2,18},{3,19},{4,20},{5,21},{6,22},{7,23},{8,24},{9,... | collective-permute-start | bytes 4915208 | tf_op jit(solution)/shard_map/ppermute | solution.py:1180
  46.9 59.3 %collective-permute-start.13 = (bf16[256,3200]{1,0:T(8,128)(2,1)}, bf16[256,3200]{1,0:T(8,128)(2,1)}, u32[]{:S(2)}, u32[]{:S(2)}) collective-permute-start(bf16[256,3200]{1,0:T(8,128)(2,1)} %collective-permute-done.9.refs_3_), channel_id=1, source_target_pairs={{0,16},{1,17},{2,18},{3,19},{4,20},{5,21},{6,22},{7,23},{8,24},{9,... | collective-permute-start | bytes 4915208 | tf_op jit(solution)/shard_map/ppermute | solution.py:1180
  48.2 75.4 %collective-permute-start.12 = (bf16[256,3200]{1,0:T(8,128)(2,1)}, bf16[256,3200]{1,0:T(8,128)(2,1)}, u32[]{:S(2)}, u32[]{:S(2)}) collective-permute-start(bf16[256,3200]{1,0:T(8,128)(2,1)} %collective-permute-done.8.refs_2_), channel_id=1, source_target_pairs={{0,16},{1,17},{2,18},{3,19},{4,20},{5,21},{6,22},{7,23},{8,24},{9,... | collective-permute-start | bytes 4915208 | tf_op jit(solution)/shard_map/ppermute | solution.py:1180
  49.6 76.6 %collective-permute-start.11 = (bf16[256,3200]{1,0:T(8,128)(2,1)}, bf16[256,3200]{1,0:T(8,128)(2,1)}, u32[]{:S(2)}, u32[]{:S(2)}) collective-permute-start(bf16[256,3200]{1,0:T(8,128)(2,1)} %collective-permute-done.7.refs_1_), channel_id=1, source_target_pairs={{0,16},{1,17},{2,18},{3,19},{4,20},{5,21},{6,22},{7,23},{8,24},{9,... | collective-permute-start | bytes 4915208 | tf_op jit(solution)/shard_map/ppermute | solution.py:1180
  183.4 314.0 %all-gather.8.cloned.1.call-start = ((), (), s32[]{:S(2)}) async-start(), calls=%async_computation.7 | async-start | bytes 3932160 | tf_op jit(solution)/shard_map/all_gather | solution.py:1255
  183.5 49.9 %collective-permute-start.34 = (bf16[64,3200]{1,0:T(8,128)(2,1)S(1)}, bf16[64,3200]{1,0:T(8,128)(2,1)S(1)}, u32[]{:S(2)}, u32[]{:S(2)}) collective-permute-start(bf16[64,3200]{1,0:T(8,128)(2,1)S(1)} %concatenate.55), channel_id=1, source_target_pairs={{16,19},{17,18},{18,17},{19,16},{20,23},{21,22},{22,21},{23,20},{2... | collective-permute-start | bytes 1228808 | tf_op jit(solution)/shard_map/ppermute | solution.py:1101
  196.8 59.0 %collective-permute-start.19 = (bf16[272,1024]{1,0:T(8,128)(2,1)}, bf16[272,1024]{1,0:T(8,128)(2,1)}, u32[]{:S(2)}, u32[]{:S(2)}) collective-permute-start(bf16[272,1024]{1,0:T(8,128)(2,1)} %get-tuple-element.164.rest_0_), channel_id=1, source_target_pairs={{0,12},{4,8},{8,4},{12,0},{16,28},{20,24},{24,20},{28,16},{1,13},{... | collective-permute-start | bytes 1671176 | tf_op jit(solution)/shard_map/ppermute | solution.py:1101
  198.0 57.8 %collective-permute-start.18 = (bf16[272,1024]{1,0:T(8,128)(2,1)}, bf16[272,1024]{1,0:T(8,128)(2,1)}, u32[]{:S(2)}, u32[]{:S(2)}) collective-permute-start(bf16[272,1024]{1,0:T(8,128)(2,1)} %get-tuple-element.164.rest_0_), channel_id=1, source_target_pairs={{0,8},{4,12},{8,0},{12,4},{16,24},{20,28},{24,16},{28,20},{1,9},{5... | collective-permute-start | bytes 1671176 | tf_op jit(solution)/shard_map/ppermute | solution.py:1101
  198.8 57.5 %collective-permute-start.17 = (bf16[272,1024]{1,0:T(8,128)(2,1)}, bf16[272,1024]{1,0:T(8,128)(2,1)}, u32[]{:S(2)}, u32[]{:S(2)}) collective-permute-start(bf16[272,1024]{1,0:T(8,128)(2,1)} %get-tuple-element.164.rest_0_), channel_id=1, source_target_pairs={{0,4},{4,0},{8,12},{12,8},{16,20},{20,16},{24,28},{28,24},{1,5},{5... | collective-permute-start | bytes 1671176 | tf_op jit(solution)/shard_map/ppermute | solution.py:1101
  199.5 55.5 %collective-permute-start.33 = (bf16[64,3200]{1,0:T(8,128)(2,1)S(1)}, bf16[64,3200]{1,0:T(8,128)(2,1)S(1)}, u32[]{:S(2)}, u32[]{:S(2)}) collective-permute-start(bf16[64,3200]{1,0:T(8,128)(2,1)S(1)} %concatenate.55), channel_id=1, source_target_pairs={{16,18},{17,19},{18,16},{19,17},{20,22},{21,23},{22,20},{23,21},{2... | collective-permute-start | bytes 1228808 | tf_op jit(solution)/shard_map/ppermute | solution.py:1101
  259.7 40.4 %collective-permute-start.37 = (bf16[256,3200]{1,0:T(8,128)(2,1)}, bf16[256,3200]{1,0:T(8,128)(2,1)}, u32[]{:S(2)}, u32[]{:S(2)}) collective-permute-start(bf16[256,3200]{1,0:T(8,128)(2,1)} %pad_maximum_fusion.1.refs_0_), channel_id=1, source_target_pairs={{16,28},{20,24},{24,20},{28,16},{17,29},{21,25},{25,21},{29,17},{1... | collective-permute-start | bytes 4915208 | tf_op jit(solution)/shard_map/ppermute | solution.py:1101
  420.6 228.1 %reduce-scatter.6.cloned.1.call-start = ((), (), s32[]{:S(2)}) async-start(), calls=%async_computation.8 | async-start | bytes 3932160 | tf_op jit(solution)/shard_map/reduce_scatter | solution.py:1469
  567.3 146.5 %reduce-scatter.8.cloned.1.call-start = ((), (), s32[]{:S(2)}) async-start(), calls=%async_computation.9 | async-start | bytes 3932160 | tf_op jit(solution)/shard_map/reduce_scatter | solution.py:1469
  615.2 240.2 %reduce-scatter.10.cloned.1.call-start = ((), (), s32[]{:S(2)}) async-start(), calls=%async_computation.10 | async-start | bytes 7864320 | tf_op jit(solution)/shard_map/reduce_scatter | solution.py:1469
  642.3 324.6 %reduce-scatter.12.cloned.1.call-start = ((), (), s32[]{:S(2)}) async-start(), calls=%async_computation.11 | async-start | bytes 11796480 | tf_op jit(solution)/shard_map/reduce_scatter | solution.py:1469
  694.8 70.0 %collective-permute-start.97 = (bf16[1024,2048]{1,0:T(8,128)(2,1)}, bf16[1024,2048]{1,0:T(8,128)(2,1)}, u32[]{:S(2)}, u32[]{:S(2)}) collective-permute-start(bf16[1024,2048]{1,0:T(8,128)(2,1)} %get-tuple-element.236), channel_id=1, source_target_pairs={{0,16},{1,17},{2,18},{3,19},{4,20},{5,21},{6,22},{7,23},{8,24},{9,... | collective-permute-start | bytes 12582920 | tf_op jit(solution)/shard_map/ppermute | solution.py:1370
  800.3 261.8 %reduce-scatter.14.cloned.1.call-start = ((), (), s32[]{:S(2)}) async-start(), calls=%async_computation.12 | async-start | bytes 3932160 | tf_op jit(solution)/shard_map/reduce_scatter | solution.py:1469
  989.9 67.7 %collective-permute-start.131 = (bf16[64,3200]{1,0:T(8,128)(2,1)}, bf16[64,3200]{1,0:T(8,128)(2,1)}, u32[]{:S(2)}, u32[]{:S(2)}) collective-permute-start(bf16[64,3200]{1,0:T(8,128)(2,1)} %get-tuple-element.386), channel_id=1, source_target_pairs={{16,18},{17,19},{18,16},{19,17},{20,22},{21,23},{22,20},{23,21},{2... | collective-permute-start | bytes 1228808 | tf_op jit(solution)/shard_map/ppermute | solution.py:1101
  993.1 65.8 %collective-permute-start.124 = (bf16[64,3200]{1,0:T(8,128)(2,1)}, bf16[64,3200]{1,0:T(8,128)(2,1)}, u32[]{:S(2)}, u32[]{:S(2)}) collective-permute-start(bf16[64,3200]{1,0:T(8,128)(2,1)} %get-tuple-element.381), channel_id=1, source_target_pairs={{0,1},{1,0},{2,3},{3,2},{4,5},{5,4},{6,7},{7,6},{8,9},{9,8},{10,11... | collective-permute-start | bytes 1228808 | tf_op jit(solution)/shard_map/ppermute | solution.py:1101
  996.0 62.9 %collective-permute-start.125 = (bf16[64,3200]{1,0:T(8,128)(2,1)}, bf16[64,3200]{1,0:T(8,128)(2,1)}, u32[]{:S(2)}, u32[]{:S(2)}) collective-permute-start(bf16[64,3200]{1,0:T(8,128)(2,1)} %get-tuple-element.382), channel_id=1, source_target_pairs={{0,2},{1,3},{2,0},{3,1},{4,6},{5,7},{6,4},{7,5},{8,10},{9,11},{10,... | collective-permute-start | bytes 1228808 | tf_op jit(solution)/shard_map/ppermute | solution.py:1101
  1006.4 52.6 %collective-permute-start.129 = (bf16[64,3200]{1,0:T(8,128)(2,1)}, bf16[64,3200]{1,0:T(8,128)(2,1)S(1)}, u32[]{:S(2)}, u32[]{:S(2)}) collective-permute-start(bf16[64,3200]{1,0:T(8,128)(2,1)} %get-tuple-element.301), channel_id=1, source_target_pairs={{0,3},{1,2},{2,1},{3,0},{4,7},{5,6},{6,5},{7,4},{8,11},{9,10},{10,... | collective-permute-start | bytes 1228808 | tf_op jit(solution)/shard_map/ppermute | solution.py:1101
  1014.1 56.2 %collective-permute-start.116 = (f32[256,1024]{1,0:T(8,128)}, f32[256,1024]{1,0:T(8,128)}, u32[]{:S(2)}, u32[]{:S(2)}) collective-permute-start(f32[256,1024]{1,0:T(8,128)} %broadcast_select_fusion.1), channel_id=1, source_target_pairs={{0,16},{16,0},{1,17},{17,1},{2,18},{18,2},{3,19},{19,3},{4,20},{20... | collective-permute-start | bytes 3145736 | tf_op jit(solution)/shard_map/ppermute | solution.py:1105
  (209 other events, 2708.1 us)
Sparse Core Ops, SparseCore 0:
  21.9 243.2 all-gather.3
  267.3 165.8 all-gather.5
  435.4 62.0 all-gather.7
  567.4 59.5 reduce-scatter.5
  629.2 60.2 reduce-scatter.7
  691.6 111.2 reduce-scatter.9
  805.3 161.5 reduce-scatter.11
  969.2 92.8 reduce-scatter.13

commit v5 on v4

--- a/solution.py
+++ b/solution.py
@@ -327,11 +327,13 @@
         low = message[:rows, :]
         inner = message[rows:, :rows]
         for i, hot in enumerate(hots):
-            out = refs[i // 2]
-            out[i % 2, :slots, :] = mm(hot, low).astype(BF16)
             spread = jnp.where(one_hot(rank[i : i + 1, :], 128), 1.0, 0.0).astype(BF16)
-            out[i % 2, slots:, :128] = mm_nt(inner, spread).astype(BF16)
-            out[i % 2, slots:, 128:] = jnp.zeros((EXT, width - 128), BF16)
+            below = jnp.concatenate(
+                [mm_nt(inner, spread)[:8], jnp.zeros((8, width - 128), F32)], axis=1
+            )
+            refs[i // 2][i % 2] = jnp.concatenate(
+                [mm(hot, low)[: slots - 8], below], axis=0
+            ).astype(BF16)
 
 
 def finish(terms, middle, goal, valid, rank=None, arrived=(), slots=0):
@@ -345,7 +347,7 @@
             jax.ShapeDtypeStruct((rows, width), F32),
             jax.ShapeDtypeStruct((rows, width), F32),
             jax.ShapeDtypeStruct((rows + EXT, width), BF16),
-            *[jax.ShapeDtypeStruct((2, slots + EXT, width), BF16) for _ in range(messages)],
+            *[jax.ShapeDtypeStruct((2, slots, width), BF16) for _ in range(messages)],
         ],
         compiler_params=params(),
         cost_estimate=cost(8 * rows * width, 24 * rows * width),
@@ -520,6 +522,36 @@
     return arrays, specs
 
 
+def combine_kernel(order, rank, *refs):
+    parts, rest = refs[: len(order)], refs[len(order) :]
+    outs, buffers = rest[:-4], rest[-4:]
+    slots = parts[0].shape[2]
+    combine(rank, [parts[o] for o in order], (), outs, buffers, slots)
+
+
+def combine_rows(rank, parts, order, slots):
+    sources, _, rows = rank.shape
+    width = parts[0].shape[-1]
+    parts = [part.reshape(part.shape[0], sources, slots, width) for part in parts]
+    return list(
+        pl.pallas_call(
+            functools.partial(combine_kernel, order),
+            name="combine_rows",
+            grid=(1,),
+            in_specs=[fixed(rank.shape), *[fixed(part.shape) for part in parts]],
+            out_specs=[pl.BlockSpec(memory_space=pl.ANY)] * sources,
+            out_shape=[jax.ShapeDtypeStruct((rows, width), BF16)] * sources,
+            scratch_shapes=stream_scratch(rows, width),
+            compiler_params=params(1),
+            cost_estimate=cost(
+                2 * sources * rows * width * rank.shape[1] * slots,
+                4 * sources * width * rank.shape[1] * slots,
+                share=0.2,
+            ),
+        )(rank, *parts)
+    )
+
+
 def stream_scratch(rows, width):
     return [
         pltpu.VMEM((4, rows, width), BF16),
@@ -615,10 +647,11 @@
     gate_column = gate_columns(rank, lambda j: gates[j, pl.ds(step, 1), :], step, mine, slots)
     if direct:
         blocks_of = [ref[0] if len(ref.shape) == 3 else ref[...] for ref in given_rows]
-        grad_out = jnp.concatenate([block[:slots] for block in blocks_of], axis=0).astype(F32)
+        blocks_of = [block.astype(F32) for block in blocks_of]
+        grad_out = jnp.concatenate(blocks_of, axis=0)
         inner_column = jnp.concatenate(
             [
-                jnp.transpose(block[slots:, :128].astype(F32))[:slots, :2].sum(axis=1, keepdims=True)
+                jnp.transpose(block[slots - 8 :, :128])[:slots, :2].sum(axis=1, keepdims=True)
                 for block in blocks_of
             ],
             axis=0,
@@ -1241,8 +1274,7 @@
     split = [(0, half_held - 1), (half_held - 1, 1)] if half_held > 1 else whole
     runs = [whole, split]
     back_runs = [split, split[::-1]]
-    if half_held > 2:
-        back_runs[1] = [(half_held - 1, 1), (half_held - 2, 1), (0, half_held - 2)]
+    by_rows_fits = half_held > 1 and slots - capacity >= 8 and slots % 16 == 0
 
     arrived = swapped(pack_experts(1 - section, gate_up_weight[0], down_weight[0]))
     mine = pack_experts(section, gate_up_weight[0], down_weight[0])
@@ -1311,7 +1343,7 @@
         xs, gates = dispatch(
             first.astype(jnp.int32).reshape(1), messages, ranks[layer], slots, False
         )
-        sparse = layer == 1 and len(runs[layer]) > 1
+        sparse = layer == 1 and by_rows_fits
         for at, ((a, n), blocks) in enumerate(zip(runs[layer], weights)):
             scal = jnp.stack([first + a, *[jnp.asarray(k) for k in range(depth)]]).astype(jnp.int32)
             by_rows = sparse and at == len(runs[layer]) - 1
@@ -1404,7 +1436,7 @@
         first, local, sources = places[layer]
         if layer < layers - 1:
             message = grad_message(grad_output, held["mixed"])
-        sparse = layer == 1 and len(back_runs[layer]) > 1
+        sparse = layer == 1 and by_rows_fits
         if sparse:
             plane = [row_messages[0]] + [
                 exchanged(row_messages[k], "ctx", k) for k in range(1, devices)
@@ -1413,10 +1445,15 @@
             message = after(message, plane[1])
         messages = dispatched(message)
         if waiting is not None:
-            blocks_1 = [home_blocks(part, 1) for part in waiting]
-            messages = after(messages, blocks_1)
-            blocks_1 = after(blocks_1, messages)
-            planes = [home_plane(blocks, 1) for blocks in blocks_1]
+            by = 1
+            while by < depth:
+                error = error + lax.ppermute(error, "fsdp", [(i, i ^ by) for i in range(depth)])
+                by *= 2
+            loss_value = error / jnp.sum(lengths).astype(F32)
+            hidden_out = placed_rows(hidden)
+            blocks_1 = [waiting[0], home_blocks(waiting[1], 1)]
+            messages = after(messages, (blocks_1, loss_value, hidden_out))
+            planes = [home_plane(blocks, 1) for blocks in after(blocks_1, messages)]
         own_router = lax.dynamic_slice_in_dim(held["router"], first, local, 0).astype(F32)
         small = jnp.zeros((128, width), F32)
         outs = ()
@@ -1429,7 +1466,7 @@
             )
             scal = jnp.concatenate([scal[:1] + (a - base), scal[1:]])
             last = None
-            if at == len(steps) - 1:
+            if at == len(steps) - 1 and not sparse:
                 order = tuple(sorted(range(len(spans)), key=lambda i: spans[i]))
                 last = (ranks[layer], [rows_of for rows_of in outs], order)
             if sparse and at == 0:
@@ -1466,6 +1503,9 @@
                 error = jnp.sum(inners[:, 1, 0])
             small = lax.dynamic_update_slice_in_dim(small, router_grad[:, 0], first + a, 0)
             gathered.append(grads)
+        if sparse:
+            order = tuple(sorted(range(len(spans)), key=lambda i: spans[i]))
+            outs = combine_rows(ranks[layer], outs, order, slots)
         over_line = lambda grads: lax.psum_scatter(
             grads, "fsdp", scatter_dimension=1, tiled=True
         )
@@ -1495,17 +1535,8 @@
         grad_mid, weight_grads, gain_second_grad, dq = back[:4]
         dkv = back[4:]
         parts = [dkv[0]] + [exchanged(dkv[k], "ctx", k) for k in range(1, devices)]
-        if layer == 0:
-            outward = home_blocks(weight_grads, 0)
-            grad_mid = after(grad_mid, outward)
-        else:
-            by = 1
-            while by < depth:
-                error = error + lax.ppermute(error, "fsdp", [(i, i ^ by) for i in range(depth)])
-                by *= 2
-            loss_value = error / jnp.sum(lengths).astype(F32)
-            hidden_out = placed_rows(hidden)
-            grad_mid = after(grad_mid, (loss_value, hidden_out, summed[1][: len(steps) - 1]))
+        outward = home_blocks(weight_grads, layer)
+        grad_mid = after(grad_mid, outward)
         small = lax.dynamic_update_slice_in_dim(small, gain_second_grad, EXPERTS + 1, 0)
         dx, packed = project_backward(
             held["x"],
@@ -1522,9 +1553,9 @@
         input_grads[layer] = dx
         grad_output = dx.astype(BF16).astype(F32)
         if layer == 1:
-            waiting = (weight_grads, packed)
+            waiting = (outward, packed)
         else:
-            outward, planes = after((outward, planes), packed)
+            outward = after(outward, packed)
             summed[0] += [over_line(after(grads, packed)) for grads in gathered[len(at_once) :]]
             inward_plane = home_plane(home_blocks(packed, 0), 0)
             outward_plane = home_plane(outward, 0)
@@ -1555,7 +1586,7 @@
     second_terms = home_line(jnp.concatenate(planes, axis=1), 1)
     shared_grads = jnp.where(first_core, added(first_terms), added(second_terms))
     outward, inward = shared_grads[:, : 2 * width], shared_grads[:, 2 * width :]
-    input_out = placed_rows(input_grads)
+    input_out = placed_rows(after(input_grads, inward_plane))
     if sums:
         part = after(part, (first_terms, second_terms))
     up_sum, down_sum = placed(pieces + pieces_of(layer, at, part), last, sums)

time: 1100 us -> 1080 us (0.982)
  starting transfers between devices: 225 us -> 213 us
    pallas_call x5 -> x4, Pallas kernels: 84.7 us -> 74 us  [experts_backward(): pl.pallas_call(kernel, name='experts_backward', grid=(local, portions), i...]
  transfers between devices with their start and end apart: 143 -> 141, of which waited for: 59 -> 57; matrix products, arithmetic and copies ran while one was open for 10% -> 10% of each run, Pallas kernels for 25% -> 25%
where the time goes in v5:
time: 1080 us; the launch traced here: 1070 us
  waiting for transfers between devices  416 us (39%)
  Pallas kernels  299 us (28%)
  starting transfers between devices  213 us (20%)
  other arithmetic  84.9 us (8%)
  local copies, waits for them, and re-layouts  38.3 us (4%)
  between operations  19.8 us (2%)
    ppermute x75, waiting for transfers between devices, exchanged(): lax.ppermute(value, ('section', axis), pairs_within(axis, by, sections))  288 us
    ppermute x75, starting transfers between devices, exchanged(): lax.ppermute(value, ('section', axis), pairs_within(axis, by, sections))  116 us
    pallas_call x4, Pallas kernels, experts_backward(): pl.pallas_call(kernel, name='experts_backward', grid=(local, portions), i...  74 us
    ppermute x8, waiting for transfers between devices, shared_of_plane(): lax.ppermute(own, 'section', [(layer, 1 - layer)])  72.3 us
    ppermute x41, starting transfers between devices, swapped(): return lax.ppermute(value, 'section', [(0, 1), (1, 0)])  50.9 us
    pallas_call x2, Pallas kernels, attend_backward(): pl.pallas_call(functools.partial(attend_back_kernel, devices, len(parts))...  48.5 us
    pallas_call x3, Pallas kernels, experts_forward(): pl.pallas_call(functools.partial(experts_kernel, sources, depth, slots, b...  45.2 us
    pallas_call x5, Pallas kernels, dispatch(): pl.pallas_call(functools.partial(dispatch_kernel, sources, slots, backwar...  29.3 us
  transfers between devices with their start and end apart: 141, of which 57 were waited for; matrix products, arithmetic and copies ran while one was open for 10% of the time, Pallas kernels for 25%

profile of v5, /device:TPU:9, one launch (start us, length us, event | category | flops | bytes accessed | tf_op | source)
XLA Modules:
  0.0 1072.8 jit_solution(15307120999211349301)
XLA Ops:
  53.9 37.3 %collective-permute-done.10.refs_4_ = bf16[256,3200]{1,0:T(8,128)(2,1)} collective-permute-done((bf16[256,3200]{1,0:T(8,128)(2,1)S(1)}, bf16[256,3200]{1,0:T(8,128)(2,1)}, u32[]{:S(2)}, u32[]{:S(2)}) %collective-permute-start.10) | collective-permute-done | bytes 1638432 | tf_op jit(solution)/shard_map/ppermute | solution.py:1213
  91.2 15.1 %collective-permute-done.13.refs_7_ = bf16[256,3200]{1,0:T(8,128)(2,1)} collective-permute-done((bf16[256,3200]{1,0:T(8,128)(2,1)}, bf16[256,3200]{1,0:T(8,128)(2,1)}, u32[]{:S(2)}, u32[]{:S(2)}) %collective-permute-start.13) | collective-permute-done | bytes 1638432 | tf_op jit(solution)/shard_map/ppermute | solution.py:1213
  106.2 17.5 %collective-permute-done.12.refs_6_ = bf16[256,3200]{1,0:T(8,128)(2,1)} collective-permute-done((bf16[256,3200]{1,0:T(8,128)(2,1)}, bf16[256,3200]{1,0:T(8,128)(2,1)}, u32[]{:S(2)}, u32[]{:S(2)}) %collective-permute-start.12) | collective-permute-done | bytes 1638432 | tf_op jit(solution)/shard_map/ppermute | solution.py:1213
  152.5 12.6 %collective-permute-done.15.rest_2_.rest_6_.rest_18_.rest_22_ = bf16[2,256,512]{2,1,0:T(8,128)(2,1)S(1)} collective-permute-done((bf16[2,256,512]{2,1,0:T(8,128)(2,1)}, bf16[2,256,512]{2,1,0:T(8,128)(2,1)S(1)}, u32[]{:S(2)}, u32[]{:S(2)}) %collective-permute-start.15) | collective-permute-done | bytes 524320 | tf_op jit(solution)/shard_map/ppermute | solution.py:1134
  166.1 14.0 %attend.2 = (bf16[256,1024]{1,0:T(8,128)(2,1)}, f32[4,2,512]{2,1,0:T(2,128)}, f32[256,1024]{1,0:T(8,128)}, bf16[272,1024]{1,0:T(8,128)(2,1)}) custom-call(s32[2]{0:T(128)} %pad_add_fusion.2.scal, bf16[256,1024]{1,0:T(8,128)(2,1)} %dynamic-slice_bitcast_fusion.1.x.rest_14_, bf16[256,1024]{1,0:T(8,128)(2,1)} %get-tuple-element.159.q.rest_10_, ...), custom_call_target="tpu_custom_call" | custom-call | flops 15790320640 | bytes 9437184 | tf_op jit(solution)/shard_map/attend/pallas_call | solution.py:215
  183.5 13.3 %collective-permute-start.34 = (bf16[64,3200]{1,0:T(8,128)(2,1)S(1)}, bf16[64,3200]{1,0:T(8,128)(2,1)S(1)}, u32[]{:S(2)}, u32[]{:S(2)}) collective-permute-start(bf16[64,3200]{1,0:T(8,128)(2,1)S(1)} %concatenate.51), channel_id=1, source_target_pairs={{16,19},{17,18},{18,17},{19,16},{20,23},{21,22},{22,21},{23,20},{2... | collective-permute-start | bytes 1228808 | tf_op jit(solution)/shard_map/ppermute | solution.py:1134
  205.5 27.9 %collective-permute-done.34 = bf16[64,3200]{1,0:T(8,128)(2,1)S(1)} collective-permute-done((bf16[64,3200]{1,0:T(8,128)(2,1)S(1)}, bf16[64,3200]{1,0:T(8,128)(2,1)S(1)}, u32[]{:S(2)}, u32[]{:S(2)}) %collective-permute-start.34) | collective-permute-done | bytes 409632 | tf_op jit(solution)/shard_map/ppermute | solution.py:1134
  235.3 19.7 %collective-permute-done.33 = bf16[64,3200]{1,0:T(8,128)(2,1)S(1)} collective-permute-done((bf16[64,3200]{1,0:T(8,128)(2,1)S(1)}, bf16[64,3200]{1,0:T(8,128)(2,1)S(1)}, u32[]{:S(2)}, u32[]{:S(2)}) %collective-permute-start.33) | collective-permute-done | bytes 409632 | tf_op jit(solution)/shard_map/ppermute | solution.py:1134
  274.8 21.5 %experts_forward.3 = (f32[4,640,1024]{2,1,0:T(8,128)}, bf16[4,640,1024]{2,1,0:T(8,128)(2,1)}, bf16[256,1024]{1,0:T(8,128)(2,1)}, bf16[256,1024]{1,0:T(8,128)(2,1...) custom-call(s32[5]{0:T(128)} %stack.177.scal.refs_0_, ...), custom_call_target="tpu_custom_call" | custom-call | flops 20937965568 | bytes 20971520 | tf_op jit(solution)/shard_map/experts_forward/pallas_call | solution.py:572
  363.2 13.1 %collective-permute-done.43.rest_2_.rest_6_.rest_18_.rest_22_ = bf16[2,256,512]{2,1,0:T(8,128)(2,1)} collective-permute-done((bf16[2,256,512]{2,1,0:T(8,128)(2,1)}, bf16[2,256,512]{2,1,0:T(8,128)(2,1)}, u32[]{:S(2)}, u32[]{:S(2)}) %collective-permute-start.43) | collective-permute-done | bytes 524320 | tf_op jit(solution)/shard_map/ppermute | solution.py:1134
  376.2 13.8 %attend.3 = (bf16[256,1024]{1,0:T(8,128)(2,1)}, f32[4,2,512]{2,1,0:T(2,128)}, f32[256,1024]{1,0:T(8,128)}, bf16[272,1024]{1,0:T(8,128)(2,1)}) custom-call(s32[2]{0:T(128)} %pad_add_fusion.2.scal, bf16[256,1024]{1,0:T(8,128)(2,1)} %get-tuple-element.358.x.rest_14_, bf16[256,1024]{1,0:T(8,128)(2,1)} %get-tuple-element.175.q.rest_10_, ...), custom_call_target="tpu_custom_call" | custom-call | flops 15790320640 | bytes 9437184 | tf_op jit(solution)/shard_map/attend/pallas_call | solution.py:215
  433.2 17.3 %experts_forward.4 = (f32[3,640,1024]{2,1,0:T(8,128)}, bf16[3,640,1024]{2,1,0:T(8,128)(2,1)}, bf16[256,1024]{1,0:T(8,128)(2,1)}, bf16[256,1024]{1,0:T(8,128)(2,1...) custom-call(s32[5]{0:T(128)} %stack.177.scal.refs_0_, ...), custom_call_target="tpu_custom_call" | custom-call | flops 19629342720 | bytes 15728640 | tf_op jit(solution)/shard_map/experts_forward/pallas_call | solution.py:572
  467.4 13.5 %collective-permute-done.56.refs_3_ = bf16[256,1024]{1,0:T(8,128)(2,1)S(1)} collective-permute-done((bf16[256,1024]{1,0:T(8,128)(2,1)S(1)}, bf16[256,1024]{1,0:T(8,128)(2,1)S(1)}, u32[]{:S(2)}, u32[]{:S(2)}) %collective-permute-start.56) | collective-permute-done | bytes 524320 | tf_op jit(solution)/shard_map/ppermute | solution.py:1134
  481.0 16.5 %all-gather.8.cloned.1.call-done.rest_3_.rest_4_.rest_5_.rest_6_.refs_15_.refs_16_.refs_17_.refs_18_ = bf16[1,1536,1024]{2,1,0:T(8,128)(2,1)} async-done(((bf16[1,384,1024]{2,1,0:T(8,128)(2,1)}), bf16[1,1536,1024]{2,1,0:T(8,128)(2,1)}) %all-gather.8.cloned.1.call-update) | async-done | bytes 3145744 | tf_op jit(solution)/shard_map/all_gather | solution.py:1287
  568.9 11.4 %collective-permute-done.73.rest_3_ = bf16[272,1024]{1,0:T(8,128)(2,1)S(1)} collective-permute-done((bf16[272,1024]{1,0:T(8,128)(2,1)S(1)}, bf16[272,1024]{1,0:T(8,128)(2,1)S(1)}, u32[]{:S(2)}, u32[]{:S(2)}) %collective-permute-start.73) | collective-permute-done | bytes 557088 | tf_op jit(solution)/shard_map/ppermute | solution.py:1134
  601.4 23.5 %experts_backward.5 = (bf16[3,1536,1024]{2,1,0:T(8,128)(2,1)}, f32[3,1,1024]{2,1,0:T(1,128)}, bf16[3,640,1024]{2,1,0:T(8,128)(2,1)}) custom-call(s32[5]{0:T(128)} %stack.177.scal.refs_0_, f32[8,3,256]{2,1,0:T(4,128)} %bitcast.194, f32[8,3,256]{2,1,0:T(4,128)} %bitcast.196, f32[8,2,256]{2,1,0:T(2,128)} %get-tuple-element.203.refs_3_, ...), custom_call_target="tpu_custom_call" | custom-call | flops 37544689664 | bytes 27525120 | tf_op jit(solution)/shard_map/experts_backward/pallas_call | solution.py:769
  648.5 12.6 %collective-permute-done.82.rest_3_ = bf16[256,1024]{1,0:T(8,128)(2,1)S(1)} collective-permute-done((bf16[256,1024]{1,0:T(8,128)(2,1)S(1)}, bf16[256,1024]{1,0:T(8,128)(2,1)S(1)}, u32[]{:S(2)}, u32[]{:S(2)}) %collective-permute-start.82) | collective-permute-done | bytes 524320 | tf_op jit(solution)/shard_map/ppermute | solution.py:1134
  661.9 24.1 %attend_backward.2 = (f32[256,1024]{1,0:T(8,128)}, bf16[1024,2048]{1,0:T(8,128)(2,1)}, f32[1,1024]{1,0:T(1,128)}, bf16[256,1024]{1,0:T(8,128)(2,1)}, bf16[2,256,...) custom-call(s32[2]{0:T(128)} %pad_add_fusion.2.scal, ...), custom_call_target="tpu_custom_call" | custom-call | flops 28010655744 | bytes 19922944 | tf_op jit(solution)/shard_map/attend_backward/pallas_call | solution.py:1006
  765.1 23.5 %experts_backward.6 = (bf16[3,1536,1024]{2,1,0:T(8,128)(2,1)}, f32[3,1,1024]{2,1,0:T(1,128)}, bf16[3,640,1024]{2,1,0:T(8,128)(2,1)}) custom-call(s32[5]{0:T(128)} %stack.177.scal.refs_0_, f32[8,3,256]{2,1,0:T(4,128)} %bitcast.185, f32[8,3,256]{2,1,0:T(4,128)} %bitcast.191, f32[8,2,256]{2,1,0:T(2,128)} %get-tuple-element.242.refs_3_, ...), custom_call_target="tpu_custom_call" | custom-call | flops 37544689664 | bytes 27525120 | tf_op jit(solution)/shard_map/experts_backward/pallas_call | solution.py:769
  814.6 16.2 %experts_backward.7 = (bf16[1,1536,1024]{2,1,0:T(8,128)(2,1)}, f32[1,1,1024]{2,1,0:T(1,128)}, bf16[256,1024]{1,0:T(8,128)(2,1)}, bf16[256,1024]{1,0:T(8,128)(2,1...) custom-call(s32[5]{0:T(128)} %concatenate.56.refs_0_, ...), custom_call_target="tpu_custom_call" | custom-call | flops 12514895872 | bytes 9175040 | tf_op jit(solution)/shard_map/experts_backward/pallas_call | solution.py:769
  852.8 12.6 %collective-permute-done.109.rest_3_ = bf16[256,1024]{1,0:T(8,128)(2,1)} collective-permute-done((bf16[256,1024]{1,0:T(8,128)(2,1)S(1)}, bf16[256,1024]{1,0:T(8,128)(2,1)}, u32[]{:S(2)}, u32[]{:S(2)}) %collective-permute-start.109) | collective-permute-done | bytes 524320 | tf_op jit(solution)/shard_map/ppermute | solution.py:1134
  865.5 24.3 %attend_backward.3 = (f32[256,1024]{1,0:T(8,128)}, bf16[1024,2048]{1,0:T(8,128)(2,1)}, f32[1,1024]{1,0:T(1,128)}, bf16[256,1024]{1,0:T(8,128)(2,1)}, bf16[2,256,...) custom-call(s32[2]{0:T(128)} %pad_add_fusion.2.scal, ...), custom_call_target="tpu_custom_call" | custom-call | flops 28010655744 | bytes 19922944 | tf_op jit(solution)/shard_map/attend_backward/pallas_call | solution.py:1006
  940.3 11.8 %reduce-scatter.9.cloned.1.call-done.refs_2_ = bf16[3,384,1024]{2,1,0:T(8,128)(2,1)} async-done(((bf16[3,1536,1024]{2,1,0:T(8,128)(2,1)}), bf16[3,384,1024]{2,1,0:T(8,128)(2,1)}) %reduce-scatter.9.cloned.1.call-update) | async-done | bytes 2359312 | tf_op jit(solution)/shard_map/reduce_scatter | solution.py:1509
  1008.8 32.1 %collective-permute-done.131 = bf16[64,3200]{1,0:T(8,128)(2,1)} collective-permute-done((bf16[64,3200]{1,0:T(8,128)(2,1)S(1)}, bf16[64,3200]{1,0:T(8,128)(2,1)}, u32[]{:S(2)}, u32[]{:S(2)}) %collective-permute-start.131) | collective-permute-done | bytes 409632 | tf_op jit(solution)/shard_map/ppermute | solution.py:1134
  (566 shorter events, 607.7 us)
Async XLA Ops:
  7.2 267.6 %all-gather.4.cloned.1.call-start = ((), (), s32[]{:S(2)}) async-start(), calls=%async_computation.4 | async-start | bytes 15728640 | tf_op jit(solution)/shard_map/all_gather | solution.py:1287
  21.7 411.5 %all-gather.6.cloned.1.call-start = ((), (), s32[]{:S(2)}) async-start(), calls=%async_computation.5 | async-start | bytes 11796480 | tf_op jit(solution)/shard_map/all_gather | solution.py:1287
  45.7 45.5 %collective-permute-start.10 = (bf16[256,3200]{1,0:T(8,128)(2,1)S(1)}, bf16[256,3200]{1,0:T(8,128)(2,1)}, u32[]{:S(2)}, u32[]{:S(2)}) collective-permute-start(bf16[256,3200]{1,0:T(8,128)(2,1)S(1)} %pad_maximum_fusion.refs_0_), channel_id=1, source_target_pairs={{0,16},{1,17},{2,18},{3,19},{4,20},{5,21},{6,22},{7,23},{8,24},{9,... | collective-permute-start | bytes 4915208 | tf_op jit(solution)/shard_map/ppermute | solution.py:1213
  47.0 59.3 %collective-permute-start.13 = (bf16[256,3200]{1,0:T(8,128)(2,1)}, bf16[256,3200]{1,0:T(8,128)(2,1)}, u32[]{:S(2)}, u32[]{:S(2)}) collective-permute-start(bf16[256,3200]{1,0:T(8,128)(2,1)} %collective-permute-done.9.refs_3_), channel_id=1, source_target_pairs={{0,16},{1,17},{2,18},{3,19},{4,20},{5,21},{6,22},{7,23},{8,24},{9,... | collective-permute-start | bytes 4915208 | tf_op jit(solution)/shard_map/ppermute | solution.py:1213
  48.3 75.4 %collective-permute-start.12 = (bf16[256,3200]{1,0:T(8,128)(2,1)}, bf16[256,3200]{1,0:T(8,128)(2,1)}, u32[]{:S(2)}, u32[]{:S(2)}) collective-permute-start(bf16[256,3200]{1,0:T(8,128)(2,1)} %collective-permute-done.8.refs_2_), channel_id=1, source_target_pairs={{0,16},{1,17},{2,18},{3,19},{4,20},{5,21},{6,22},{7,23},{8,24},{9,... | collective-permute-start | bytes 4915208 | tf_op jit(solution)/shard_map/ppermute | solution.py:1213
  49.6 76.6 %collective-permute-start.11 = (bf16[256,3200]{1,0:T(8,128)(2,1)}, bf16[256,3200]{1,0:T(8,128)(2,1)}, u32[]{:S(2)}, u32[]{:S(2)}) collective-permute-start(bf16[256,3200]{1,0:T(8,128)(2,1)} %collective-permute-done.7.refs_1_), channel_id=1, source_target_pairs={{0,16},{1,17},{2,18},{3,19},{4,20},{5,21},{6,22},{7,23},{8,24},{9,... | collective-permute-start | bytes 4915208 | tf_op jit(solution)/shard_map/ppermute | solution.py:1213
  183.5 314.0 %all-gather.8.cloned.1.call-start = ((), (), s32[]{:S(2)}) async-start(), calls=%async_computation.6 | async-start | bytes 3932160 | tf_op jit(solution)/shard_map/all_gather | solution.py:1287
  183.5 49.9 %collective-permute-start.34 = (bf16[64,3200]{1,0:T(8,128)(2,1)S(1)}, bf16[64,3200]{1,0:T(8,128)(2,1)S(1)}, u32[]{:S(2)}, u32[]{:S(2)}) collective-permute-start(bf16[64,3200]{1,0:T(8,128)(2,1)S(1)} %concatenate.51), channel_id=1, source_target_pairs={{16,19},{17,18},{18,17},{19,16},{20,23},{21,22},{22,21},{23,20},{2... | collective-permute-start | bytes 1228808 | tf_op jit(solution)/shard_map/ppermute | solution.py:1134
  196.9 58.9 %collective-permute-start.19 = (bf16[272,1024]{1,0:T(8,128)(2,1)}, bf16[272,1024]{1,0:T(8,128)(2,1)}, u32[]{:S(2)}, u32[]{:S(2)}) collective-permute-start(bf16[272,1024]{1,0:T(8,128)(2,1)} %get-tuple-element.162.rest_0_), channel_id=1, source_target_pairs={{0,12},{4,8},{8,4},{12,0},{16,28},{20,24},{24,20},{28,16},{1,13},{... | collective-permute-start | bytes 1671176 | tf_op jit(solution)/shard_map/ppermute | solution.py:1134
  198.1 57.7 %collective-permute-start.18 = (bf16[272,1024]{1,0:T(8,128)(2,1)}, bf16[272,1024]{1,0:T(8,128)(2,1)}, u32[]{:S(2)}, u32[]{:S(2)}) collective-permute-start(bf16[272,1024]{1,0:T(8,128)(2,1)} %get-tuple-element.162.rest_0_), channel_id=1, source_target_pairs={{0,8},{4,12},{8,0},{12,4},{16,24},{20,28},{24,16},{28,20},{1,9},{5... | collective-permute-start | bytes 1671176 | tf_op jit(solution)/shard_map/ppermute | solution.py:1134
  198.8 57.5 %collective-permute-start.17 = (bf16[272,1024]{1,0:T(8,128)(2,1)}, bf16[272,1024]{1,0:T(8,128)(2,1)}, u32[]{:S(2)}, u32[]{:S(2)}) collective-permute-start(bf16[272,1024]{1,0:T(8,128)(2,1)} %get-tuple-element.162.rest_0_), channel_id=1, source_target_pairs={{0,4},{4,0},{8,12},{12,8},{16,20},{20,16},{24,28},{28,24},{1,5},{5... | collective-permute-start | bytes 1671176 | tf_op jit(solution)/shard_map/ppermute | solution.py:1134
  199.6 55.4 %collective-permute-start.33 = (bf16[64,3200]{1,0:T(8,128)(2,1)S(1)}, bf16[64,3200]{1,0:T(8,128)(2,1)S(1)}, u32[]{:S(2)}, u32[]{:S(2)}) collective-permute-start(bf16[64,3200]{1,0:T(8,128)(2,1)S(1)} %concatenate.51), channel_id=1, source_target_pairs={{16,18},{17,19},{18,16},{19,17},{20,22},{21,23},{22,20},{23,21},{2... | collective-permute-start | bytes 1228808 | tf_op jit(solution)/shard_map/ppermute | solution.py:1134
  259.7 40.3 %collective-permute-start.37 = (bf16[256,3200]{1,0:T(8,128)(2,1)}, bf16[256,3200]{1,0:T(8,128)(2,1)}, u32[]{:S(2)}, u32[]{:S(2)}) collective-permute-start(bf16[256,3200]{1,0:T(8,128)(2,1)} %pad_maximum_fusion.1.refs_0_), channel_id=1, source_target_pairs={{16,28},{20,24},{24,20},{28,16},{17,29},{21,25},{25,21},{29,17},{1... | collective-permute-start | bytes 4915208 | tf_op jit(solution)/shard_map/ppermute | solution.py:1134
  263.8 38.7 %collective-permute-start.36 = (bf16[256,3200]{1,0:T(8,128)(2,1)}, bf16[256,3200]{1,0:T(8,128)(2,1)}, u32[]{:S(2)}, u32[]{:S(2)}) collective-permute-start(bf16[256,3200]{1,0:T(8,128)(2,1)} %pad_maximum_fusion.1.refs_0_), channel_id=1, source_target_pairs={{16,24},{20,28},{24,16},{28,20},{17,25},{21,29},{25,17},{29,21},{1... | collective-permute-start | bytes 4915208 | tf_op jit(solution)/shard_map/ppermute | solution.py:1134
  265.9 39.1 %collective-permute-start.35 = (bf16[256,3200]{1,0:T(8,128)(2,1)}, bf16[256,3200]{1,0:T(8,128)(2,1)}, u32[]{:S(2)}, u32[]{:S(2)}) collective-permute-start(bf16[256,3200]{1,0:T(8,128)(2,1)} %pad_maximum_fusion.1.refs_0_), channel_id=1, source_target_pairs={{16,20},{20,16},{24,28},{28,24},{17,21},{21,17},{25,29},{29,25},{1... | collective-permute-start | bytes 4915208 | tf_op jit(solution)/shard_map/ppermute | solution.py:1134
  420.5 219.0 %reduce-scatter.5.cloned.1.call-start = ((), (), s32[]{:S(2)}) async-start(), calls=%async_computation.7 | async-start | bytes 3932160 | tf_op jit(solution)/shard_map/reduce_scatter | solution.py:1509
  564.2 279.5 %reduce-scatter.7.cloned.1.call-start = ((), (), s32[]{:S(2)}) async-start(), calls=%async_computation.8 | async-start | bytes 11796480 | tf_op jit(solution)/shard_map/reduce_scatter | solution.py:1509
  625.0 327.2 %reduce-scatter.9.cloned.1.call-start = ((), (), s32[]{:S(2)}) async-start(), calls=%async_computation.9 | async-start | bytes 11796480 | tf_op jit(solution)/shard_map/reduce_scatter | solution.py:1509
  788.7 259.2 %reduce-scatter.11.cloned.1.call-start = ((), (), s32[]{:S(2)}) async-start(), calls=%async_computation.10 | async-start | bytes 3932160 | tf_op jit(solution)/shard_map/reduce_scatter | solution.py:1509
  970.8 70.1 %collective-permute-start.131 = (bf16[64,3200]{1,0:T(8,128)(2,1)S(1)}, bf16[64,3200]{1,0:T(8,128)(2,1)}, u32[]{:S(2)}, u32[]{:S(2)}) collective-permute-start(bf16[64,3200]{1,0:T(8,128)(2,1)S(1)} %get-tuple-element.382), channel_id=1, source_target_pairs={{16,19},{17,18},{18,17},{19,16},{20,23},{21,22},{22,21},{23,20},{2... | collective-permute-start | bytes 1228808 | tf_op jit(solution)/shard_map/ppermute | solution.py:1134
  975.5 66.7 %collective-permute-start.124 = (bf16[64,3200]{1,0:T(8,128)(2,1)}, bf16[64,3200]{1,0:T(8,128)(2,1)}, u32[]{:S(2)}, u32[]{:S(2)}) collective-permute-start(bf16[64,3200]{1,0:T(8,128)(2,1)} %get-tuple-element.377), channel_id=1, source_target_pairs={{0,1},{1,0},{2,3},{3,2},{4,5},{5,4},{6,7},{7,6},{8,9},{9,8},{10,11... | collective-permute-start | bytes 1228808 | tf_op jit(solution)/shard_map/ppermute | solution.py:1134
  978.3 63.9 %collective-permute-start.125 = (bf16[64,3200]{1,0:T(8,128)(2,1)}, bf16[64,3200]{1,0:T(8,128)(2,1)}, u32[]{:S(2)}, u32[]{:S(2)}) collective-permute-start(bf16[64,3200]{1,0:T(8,128)(2,1)} %get-tuple-element.378), channel_id=1, source_target_pairs={{0,2},{1,3},{2,0},{3,1},{4,6},{5,7},{6,4},{7,5},{8,10},{9,11},{10,... | collective-permute-start | bytes 1228808 | tf_op jit(solution)/shard_map/ppermute | solution.py:1134
  992.2 50.0 %collective-permute-start.128 = (bf16[64,3200]{1,0:T(8,128)(2,1)S(1)}, bf16[64,3200]{1,0:T(8,128)(2,1)S(1)}, u32[]{:S(2)}, u32[]{:S(2)}) collective-permute-start(bf16[64,3200]{1,0:T(8,128)(2,1)S(1)} %get-tuple-element.299), channel_id=1, source_target_pairs={{0,3},{1,2},{2,1},{3,0},{4,7},{5,6},{6,5},{7,4},{8,11},{9,10},{10,... | collective-permute-start | bytes 1228808 | tf_op jit(solution)/shard_map/ppermute | solution.py:1134
  997.4 57.1 %collective-permute-start.120 = (f32[256,1024]{1,0:T(8,128)}, f32[256,1024]{1,0:T(8,128)}, u32[]{:S(2)}, u32[]{:S(2)}) collective-permute-start(f32[256,1024]{1,0:T(8,128)} %broadcast_select_fusion.1), channel_id=1, source_target_pairs={{0,16},{16,0},{1,17},{17,1},{2,18},{18,2},{3,19},{19,3},{4,20},{20... | collective-permute-start | bytes 3145736 | tf_op jit(solution)/shard_map/ppermute | solution.py:1138
  (192 other events, 2666.2 us)
Sparse Core Ops, SparseCore 0:
  21.9 243.2 all-gather.3
  267.3 165.8 all-gather.5
  435.4 62.0 all-gather.7
  564.3 59.5 reduce-scatter.4
  626.1 161.6 reduce-scatter.6
  790.0 162.1 reduce-scatter.8
  954.4 93.4 reduce-scatter.10

commit v6 on v5

--- a/solution.py
+++ b/solution.py
@@ -304,7 +304,7 @@
     if routed:
         rank, refs = refs[0], refs[1:]
         arrived, refs = refs[:routed], refs[routed:]
-    hidden, mixed_out, grad_out, message, refs = *refs[:4], refs[4:]
+    hidden, grad_out, message, refs = *refs[:3], refs[3:]
     rows, width = middle.shape
     mixed = terms[0][...].astype(F32)
     for term in terms[1:]:
@@ -318,7 +318,6 @@
         mixed = mixed + mm_tn(jnp.concatenate(hots, axis=0), given)
     output = middle[...] + mixed
     hidden[...] = output.astype(BF16)
-    mixed_out[...] = mixed
     grad = (output - goal[...].astype(F32)) * valid[...]
     grad_out[...] = grad
     error = 0.5 * jnp.sum(jnp.sum(grad * grad, axis=1, keepdims=True), axis=0, keepdims=True)
@@ -344,7 +343,6 @@
         name="finish",
         out_shape=[
             jax.ShapeDtypeStruct((rows, width), BF16),
-            jax.ShapeDtypeStruct((rows, width), F32),
             jax.ShapeDtypeStruct((rows, width), F32),
             jax.ShapeDtypeStruct((rows + EXT, width), BF16),
             *[jax.ShapeDtypeStruct((2, slots, width), BF16) for _ in range(messages)],
@@ -476,7 +474,7 @@
         outs, rest = rest[:sources], rest[sources:]
         held, w1, w2 = rest[:3]
     else:
-        rows_out, w1, w2 = rest
+        outs, (w1, w2) = rest[:sources], rest[sources:]
     width = w1.shape[0]
     step, part = pl.program_id(0), pl.program_id(1)
     portions = sources // (xs.shape[1] // slots)
@@ -508,7 +506,8 @@
             combine(rank, held, prior, outs, rest[3:], slots)
 
     else:
-        rows_out[0] = given
+        for j in range(sources):
+            outs[j][...] = given[j]
 
 
 def weight_specs(blocks, depth, base=0):
@@ -564,7 +563,7 @@
 def experts_forward(scal, xs, rank, gates, blocks, depth, slots, first, prior=(), combined=True):
     sources, local, rows = rank.shape
     width = xs.shape[2]
-    portions = max(1, sources // 8)
+    portions = max(1, sources // 8) if combined else 1
     count = sources * slots
     arrays, specs = weight_specs(blocks, depth)
     anywhere = pl.BlockSpec(memory_space=pl.ANY)
@@ -587,9 +586,7 @@
             *(
                 [anywhere] * sources
                 if combined
-                else [
-                    pl.BlockSpec((1, sources // portions, slots, width), lambda e, r: (e, r, 0, 0))
-                ]
+                else [resident((slots, width))] * sources
             ),
         ],
         out_shape=[
@@ -598,7 +595,7 @@
             *(
                 [jax.ShapeDtypeStruct((rows, width), BF16)] * sources
                 if combined
-                else [jax.ShapeDtypeStruct((local, sources, slots, width), BF16)]
+                else [jax.ShapeDtypeStruct((slots, width), BF16)] * sources
             ),
         ],
         scratch_shapes=[
@@ -1348,6 +1345,7 @@
             scal = jnp.stack([first + a, *[jnp.asarray(k) for k in range(depth)]]).astype(jnp.int32)
             by_rows = sparse and at == len(runs[layer]) - 1
             if by_rows:
+                terms = [added(terms)]
                 scal = after(scal, terms)
             run, outs = experts_forward(
                 scal,
@@ -1367,11 +1365,13 @@
         if layer == layers - 1:
             routed = [last_rank, [], slots] if sparse else []
             if sparse:
-                near, far = outs[0][0, :devices], swapped(outs[0][0, devices:])
-                routed[1] = [near[0], far[0]] + [
-                    exchanged(jnp.stack([near[k], far[k]]), "ctx", k) for k in range(1, devices)
-                ]
-            hidden_rows, mixed, grad_output, message, *row_messages = finish(
+                near = outs[:devices]
+                near = near[:1] + [exchanged(near[k], "ctx", k) for k in range(1, devices)]
+                far = [swapped(block) for block in outs[devices:]]
+                far = far[:1] + [exchanged(far[k], "ctx", k) for k in range(1, devices)]
+                routed[1] = [block for pair in zip(near, far) for block in pair]
+            mixed = None
+            hidden_rows, grad_output, message, *row_messages = finish(
                 terms, middle, my_targets, valid, *routed
             )
             hidden.append(hidden_rows)
@@ -1584,16 +1584,17 @@
         jnp.concatenate([outward_plane, inward_plane], axis=1), 0, sums if sums else None
     )
     second_terms = home_line(jnp.concatenate(planes, axis=1), 1)
+    input_out = placed_rows(after(input_grads, inward_plane))[None, :, None]
+    first_terms, second_terms = after((first_terms, second_terms), input_out)
     shared_grads = jnp.where(first_core, added(first_terms), added(second_terms))
     outward, inward = shared_grads[:, : 2 * width], shared_grads[:, 2 * width :]
-    input_out = placed_rows(after(input_grads, inward_plane))
     if sums:
         part = after(part, (first_terms, second_terms))
     up_sum, down_sum = placed(pieces + pieces_of(layer, at, part), last, sums)
     at = 2 * KW
     return (
         hidden_out[None, :, None],
-        input_out[None, :, None],
+        input_out,
         loss_value,
         inward[:, at + EXPERTS][None],
         outward[:, width:][None],

time: 1080 us -> 1080 us (level)
  waiting for transfers between devices: 416 us -> 392 us
  starting transfers between devices: 213 us -> 234 us
    ppermute x75 -> x78, waiting for transfers between devices: 288 us -> 273 us  [exchanged(): lax.ppermute(value, ('section', axis), pairs_within(axis, by, sections))]
    ppermute x4, starting transfers between devices: 12.1 us -> 23.6 us  [pieces_of(): arrived = lax.ppermute(part, 'section', [(1 - layer, layer)])]
    ppermute x75 -> x78, starting transfers between devices: 116 us -> 125 us  [exchanged(): lax.ppermute(value, ('section', axis), pairs_within(axis, by, sections))]
    ppermute x41 -> x44, starting transfers between devices: 50.9 us -> 51.1 us  [swapped(): return lax.ppermute(value, 'section', [(0, 1), (1, 0)])]
  transfers between devices with their start and end apart: 141 -> 147, of which waited for: 57 -> 58; matrix products, arithmetic and copies ran while one was open for 10% -> 10% of each run, Pallas kernels for 25% -> 25%
where the time goes in v6:
time: 1080 us; the launch traced here: 1070 us
  waiting for transfers between devices  392 us (36%)
  Pallas kernels  299 us (28%)
  starting transfers between devices  234 us (22%)
  other arithmetic  87.8 us (8%)
  local copies, waits for them, and re-layouts  33.1 us (3%)
  between operations  19.7 us (2%)
    ppermute x78, waiting for transfers between devices, exchanged(): lax.ppermute(value, ('section', axis), pairs_within(axis, by, sections))  273 us
    ppermute x78, starting transfers between devices, exchanged(): lax.ppermute(value, ('section', axis), pairs_within(axis, by, sections))  125 us
    pallas_call x4, Pallas kernels, experts_backward(): pl.pallas_call(kernel, name='experts_backward', grid=(local, portions), i...  74 us
    ppermute x8, waiting for transfers between devices, shared_of_plane(): lax.ppermute(own, 'section', [(layer, 1 - layer)])  72.3 us
    ppermute x44, starting transfers between devices, swapped(): return lax.ppermute(value, 'section', [(0, 1), (1, 0)])  51.1 us
    pallas_call x2, Pallas kernels, attend_backward(): pl.pallas_call(functools.partial(attend_back_kernel, devices, len(parts))...  48.4 us
    pallas_call x3, Pallas kernels, experts_forward(): pl.pallas_call(functools.partial(experts_kernel, sources, depth, slots, b...  45.9 us
    pallas_call x5, Pallas kernels, dispatch(): pl.pallas_call(functools.partial(dispatch_kernel, sources, slots, backwar...  29.3 us
  transfers between devices with their start and end apart: 147, of which 58 were waited for; matrix products, arithmetic and copies ran while one was open for 10% of the time, Pallas kernels for 25%

profile of v6, /device:TPU:9, one launch (start us, length us, event | category | flops | bytes accessed | tf_op | source)
XLA Modules:
  0.0 1067.6 jit_solution(14307330184367713544)
XLA Ops:
  53.9 37.3 %collective-permute-done.10.refs_4_ = bf16[256,3200]{1,0:T(8,128)(2,1)} collective-permute-done((bf16[256,3200]{1,0:T(8,128)(2,1)S(1)}, bf16[256,3200]{1,0:T(8,128)(2,1)}, u32[]{:S(2)}, u32[]{:S(2)}) %collective-permute-start.10) | collective-permute-done | bytes 1638432 | tf_op jit(solution)/shard_map/ppermute | solution.py:1210
  91.2 15.1 %collective-permute-done.13.refs_7_ = bf16[256,3200]{1,0:T(8,128)(2,1)} collective-permute-done((bf16[256,3200]{1,0:T(8,128)(2,1)}, bf16[256,3200]{1,0:T(8,128)(2,1)}, u32[]{:S(2)}, u32[]{:S(2)}) %collective-permute-start.13) | collective-permute-done | bytes 1638432 | tf_op jit(solution)/shard_map/ppermute | solution.py:1210
  106.2 17.5 %collective-permute-done.12.refs_6_ = bf16[256,3200]{1,0:T(8,128)(2,1)} collective-permute-done((bf16[256,3200]{1,0:T(8,128)(2,1)}, bf16[256,3200]{1,0:T(8,128)(2,1)}, u32[]{:S(2)}, u32[]{:S(2)}) %collective-permute-start.12) | collective-permute-done | bytes 1638432 | tf_op jit(solution)/shard_map/ppermute | solution.py:1210
  152.6 12.6 %collective-permute-done.15.rest_2_.rest_6_.rest_18_.rest_22_ = bf16[2,256,512]{2,1,0:T(8,128)(2,1)S(1)} collective-permute-done((bf16[2,256,512]{2,1,0:T(8,128)(2,1)}, bf16[2,256,512]{2,1,0:T(8,128)(2,1)S(1)}, u32[]{:S(2)}, u32[]{:S(2)}) %collective-permute-start.15) | collective-permute-done | bytes 524320 | tf_op jit(solution)/shard_map/ppermute | solution.py:1131
  166.1 14.0 %attend.2 = (bf16[256,1024]{1,0:T(8,128)(2,1)}, f32[4,2,512]{2,1,0:T(2,128)}, f32[256,1024]{1,0:T(8,128)}, bf16[272,1024]{1,0:T(8,128)(2,1)}) custom-call(s32[2]{0:T(128)} %pad_add_fusion.2.scal, bf16[256,1024]{1,0:T(8,128)(2,1)} %dynamic-slice_bitcast_fusion.1.x.rest_14_, bf16[256,1024]{1,0:T(8,128)(2,1)} %get-tuple-element.174.q.rest_10_, ...), custom_call_target="tpu_custom_call" | custom-call | flops 15790320640 | bytes 9437184 | tf_op jit(solution)/shard_map/attend/pallas_call | solution.py:215
  183.5 13.3 %collective-permute-start.34 = (bf16[64,3200]{1,0:T(8,128)(2,1)S(1)}, bf16[64,3200]{1,0:T(8,128)(2,1)S(1)}, u32[]{:S(2)}, u32[]{:S(2)}) collective-permute-start(bf16[64,3200]{1,0:T(8,128)(2,1)S(1)} %concatenate.51), channel_id=1, source_target_pairs={{16,19},{17,18},{18,17},{19,16},{20,23},{21,22},{22,21},{23,20},{2... | collective-permute-start | bytes 1228808 | tf_op jit(solution)/shard_map/ppermute | solution.py:1131
  205.5 27.9 %collective-permute-done.34 = bf16[64,3200]{1,0:T(8,128)(2,1)S(1)} collective-permute-done((bf16[64,3200]{1,0:T(8,128)(2,1)S(1)}, bf16[64,3200]{1,0:T(8,128)(2,1)S(1)}, u32[]{:S(2)}, u32[]{:S(2)}) %collective-permute-start.34) | collective-permute-done | bytes 409632 | tf_op jit(solution)/shard_map/ppermute | solution.py:1131
  235.3 19.7 %collective-permute-done.33 = bf16[64,3200]{1,0:T(8,128)(2,1)S(1)} collective-permute-done((bf16[64,3200]{1,0:T(8,128)(2,1)S(1)}, bf16[64,3200]{1,0:T(8,128)(2,1)S(1)}, u32[]{:S(2)}, u32[]{:S(2)}) %collective-permute-start.33) | collective-permute-done | bytes 409632 | tf_op jit(solution)/shard_map/ppermute | solution.py:1131
  274.8 21.6 %experts_forward.3 = (f32[4,640,1024]{2,1,0:T(8,128)}, bf16[4,640,1024]{2,1,0:T(8,128)(2,1)}, bf16[256,1024]{1,0:T(8,128)(2,1)}, bf16[256,1024]{1,0:T(8,128)(2,1...) custom-call(s32[5]{0:T(128)} %stack.168.scal.refs_0_, ...), custom_call_target="tpu_custom_call" | custom-call | flops 20937965568 | bytes 20971520 | tf_op jit(solution)/shard_map/experts_forward/pallas_call | solution.py:571
  330.3 11.4 %collective-permute-done.31 = bf16[256,1024]{1,0:T(8,128)(2,1)} collective-permute-done((bf16[256,1024]{1,0:T(8,128)(2,1)}, bf16[256,1024]{1,0:T(8,128)(2,1)}, u32[]{:S(2)}, u32[]{:S(2)}) %collective-permute-start.31) | collective-permute-done | bytes 524320 | tf_op jit(solution)/shard_map/ppermute | solution.py:1131
  363.3 13.0 %collective-permute-done.43.rest_2_.rest_6_.rest_18_.rest_22_ = bf16[2,256,512]{2,1,0:T(8,128)(2,1)} collective-permute-done((bf16[2,256,512]{2,1,0:T(8,128)(2,1)}, bf16[2,256,512]{2,1,0:T(8,128)(2,1)}, u32[]{:S(2)}, u32[]{:S(2)}) %collective-permute-start.43) | collective-permute-done | bytes 524320 | tf_op jit(solution)/shard_map/ppermute | solution.py:1131
  376.3 13.9 %attend.3 = (bf16[256,1024]{1,0:T(8,128)(2,1)}, f32[4,2,512]{2,1,0:T(2,128)}, f32[256,1024]{1,0:T(8,128)}, bf16[272,1024]{1,0:T(8,128)(2,1)}) custom-call(s32[2]{0:T(128)} %pad_add_fusion.2.scal, bf16[256,1024]{1,0:T(8,128)(2,1)} %get-tuple-element.385.x.rest_14_, bf16[256,1024]{1,0:T(8,128)(2,1)} %get-tuple-element.190.q.rest_10_, ...), custom_call_target="tpu_custom_call" | custom-call | flops 15790320640 | bytes 9437184 | tf_op jit(solution)/shard_map/attend/pallas_call | solution.py:215
  433.2 17.3 %experts_forward.4 = (f32[3,640,1024]{2,1,0:T(8,128)}, bf16[3,640,1024]{2,1,0:T(8,128)(2,1)}, bf16[256,1024]{1,0:T(8,128)(2,1)}, bf16[256,1024]{1,0:T(8,128)(2,1...) custom-call(s32[5]{0:T(128)} %stack.168.scal.refs_0_, ...), custom_call_target="tpu_custom_call" | custom-call | flops 19629342720 | bytes 15728640 | tf_op jit(solution)/shard_map/experts_forward/pallas_call | solution.py:571
  467.5 13.5 %collective-permute-done.56 = bf16[256,1024]{1,0:T(8,128)(2,1)S(1)} collective-permute-done((bf16[256,1024]{1,0:T(8,128)(2,1)S(1)}, bf16[256,1024]{1,0:T(8,128)(2,1)S(1)}, u32[]{:S(2)}, u32[]{:S(2)}) %collective-permute-start.56) | collective-permute-done | bytes 524320 | tf_op jit(solution)/shard_map/ppermute | solution.py:1131
  483.5 14.0 %all-gather.8.cloned.1.call-done.rest_3_.rest_4_.rest_5_.rest_6_.refs_15_.refs_16_.refs_17_.refs_18_ = bf16[1,1536,1024]{2,1,0:T(8,128)(2,1)} async-done(((bf16[1,384,1024]{2,1,0:T(8,128)(2,1)}), bf16[1,1536,1024]{2,1,0:T(8,128)(2,1)}) %all-gather.8.cloned.1.call-update) | async-done | bytes 3145744 | tf_op jit(solution)/shard_map/all_gather | solution.py:1284
  566.6 11.4 %collective-permute-done.79.rest_3_ = bf16[272,1024]{1,0:T(8,128)(2,1)S(1)} collective-permute-done((bf16[272,1024]{1,0:T(8,128)(2,1)S(1)}, bf16[272,1024]{1,0:T(8,128)(2,1)S(1)}, u32[]{:S(2)}, u32[]{:S(2)}) %collective-permute-start.79) | collective-permute-done | bytes 557088 | tf_op jit(solution)/shard_map/ppermute | solution.py:1131
  599.1 23.6 %experts_backward.5 = (bf16[3,1536,1024]{2,1,0:T(8,128)(2,1)}, f32[3,1,1024]{2,1,0:T(1,128)}, bf16[3,640,1024]{2,1,0:T(8,128)(2,1)}) custom-call(s32[5]{0:T(128)} %stack.168.scal.refs_0_, f32[8,3,256]{2,1,0:T(4,128)} %bitcast.182, f32[8,3,256]{2,1,0:T(4,128)} %bitcast.184, f32[8,2,256]{2,1,0:T(2,128)} %get-tuple-element.225.refs_3_, ...), custom_call_target="tpu_custom_call" | custom-call | flops 37544689664 | bytes 27525120 | tf_op jit(solution)/shard_map/experts_backward/pallas_call | solution.py:766
  646.2 12.4 %collective-permute-done.88.rest_3_ = bf16[256,1024]{1,0:T(8,128)(2,1)S(1)} collective-permute-done((bf16[256,1024]{1,0:T(8,128)(2,1)S(1)}, bf16[256,1024]{1,0:T(8,128)(2,1)S(1)}, u32[]{:S(2)}, u32[]{:S(2)}) %collective-permute-start.88) | collective-permute-done | bytes 524320 | tf_op jit(solution)/shard_map/ppermute | solution.py:1131
  659.5 24.1 %attend_backward.2 = (f32[256,1024]{1,0:T(8,128)}, bf16[1024,2048]{1,0:T(8,128)(2,1)}, f32[1,1024]{1,0:T(1,128)}, bf16[256,1024]{1,0:T(8,128)(2,1)}, bf16[2,256,...) custom-call(s32[2]{0:T(128)} %pad_add_fusion.2.scal, ...), custom_call_target="tpu_custom_call" | custom-call | flops 28010655744 | bytes 19922944 | tf_op jit(solution)/shard_map/attend_backward/pallas_call | solution.py:1003
  762.1 23.6 %experts_backward.6 = (bf16[3,1536,1024]{2,1,0:T(8,128)(2,1)}, f32[3,1,1024]{2,1,0:T(1,128)}, bf16[3,640,1024]{2,1,0:T(8,128)(2,1)}) custom-call(s32[5]{0:T(128)} %stack.168.scal.refs_0_, f32[8,3,256]{2,1,0:T(4,128)} %bitcast.173, f32[8,3,256]{2,1,0:T(4,128)} %bitcast.179, f32[8,2,256]{2,1,0:T(2,128)} %get-tuple-element.264.refs_3_, ...), custom_call_target="tpu_custom_call" | custom-call | flops 37544689664 | bytes 27525120 | tf_op jit(solution)/shard_map/experts_backward/pallas_call | solution.py:766
  811.5 16.2 %experts_backward.7 = (bf16[1,1536,1024]{2,1,0:T(8,128)(2,1)}, f32[1,1,1024]{2,1,0:T(1,128)}, bf16[256,1024]{1,0:T(8,128)(2,1)}, bf16[256,1024]{1,0:T(8,128)(2,1...) custom-call(s32[5]{0:T(128)} %concatenate.56.refs_0_, ...), custom_call_target="tpu_custom_call" | custom-call | flops 12514895872 | bytes 9175040 | tf_op jit(solution)/shard_map/experts_backward/pallas_call | solution.py:766
  862.4 24.3 %attend_backward.3 = (f32[256,1024]{1,0:T(8,128)}, bf16[1024,2048]{1,0:T(8,128)(2,1)}, f32[1,1024]{1,0:T(1,128)}, bf16[256,1024]{1,0:T(8,128)(2,1)}, bf16[2,256,...) custom-call(s32[2]{0:T(128)} %pad_add_fusion.2.scal, ...), custom_call_target="tpu_custom_call" | custom-call | flops 28010655744 | bytes 19922944 | tf_op jit(solution)/shard_map/attend_backward/pallas_call | solution.py:1003
  949.7 13.5 %collective-permute-start.133 = (bf16[3,384,1024]{2,1,0:T(8,128)(2,1)}, bf16[3,384,1024]{2,1,0:T(8,128)(2,1)}, u32[]{:S(2)}, u32[]{:S(2)}) collective-permute-start(bf16[3,384,1024]{2,1,0:T(8,128)(2,1)} %reduce-scatter.9.cloned.1.call-done.refs_2_), channel_id=1, source_target_pairs={{16,0},{17,1},{18,2},{19,3},{20,4},{21,5},{22,6},{23,7},{24,8},{25... | collective-permute-start | bytes 7077896 | tf_op jit(solution)/shard_map/ppermute | solution.py:1564
  1009.0 29.4 %collective-permute-done.136 = bf16[64,3200]{1,0:T(8,128)(2,1)} collective-permute-done((bf16[64,3200]{1,0:T(8,128)(2,1)}, bf16[64,3200]{1,0:T(8,128)(2,1)}, u32[]{:S(2)}, u32[]{:S(2)}) %collective-permute-start.136) | collective-permute-done | bytes 409632 | tf_op jit(solution)/shard_map/ppermute | solution.py:1131
  (571 shorter events, 607.7 us)
Async XLA Ops:
  7.2 267.6 %all-gather.4.cloned.1.call-start = ((), (), s32[]{:S(2)}) async-start(), calls=%async_computation.4 | async-start | bytes 15728640 | tf_op jit(solution)/shard_map/all_gather | solution.py:1284
  21.7 411.5 %all-gather.6.cloned.1.call-start = ((), (), s32[]{:S(2)}) async-start(), calls=%async_computation.5 | async-start | bytes 11796480 | tf_op jit(solution)/shard_map/all_gather | solution.py:1284
  45.6 45.5 %collective-permute-start.10 = (bf16[256,3200]{1,0:T(8,128)(2,1)S(1)}, bf16[256,3200]{1,0:T(8,128)(2,1)}, u32[]{:S(2)}, u32[]{:S(2)}) collective-permute-start(bf16[256,3200]{1,0:T(8,128)(2,1)S(1)} %pad_maximum_fusion.refs_0_), channel_id=1, source_target_pairs={{0,16},{1,17},{2,18},{3,19},{4,20},{5,21},{6,22},{7,23},{8,24},{9,... | collective-permute-start | bytes 4915208 | tf_op jit(solution)/shard_map/ppermute | solution.py:1210
  46.9 59.3 %collective-permute-start.13 = (bf16[256,3200]{1,0:T(8,128)(2,1)}, bf16[256,3200]{1,0:T(8,128)(2,1)}, u32[]{:S(2)}, u32[]{:S(2)}) collective-permute-start(bf16[256,3200]{1,0:T(8,128)(2,1)} %collective-permute-done.9.refs_3_), channel_id=1, source_target_pairs={{0,16},{1,17},{2,18},{3,19},{4,20},{5,21},{6,22},{7,23},{8,24},{9,... | collective-permute-start | bytes 4915208 | tf_op jit(solution)/shard_map/ppermute | solution.py:1210
  48.3 75.4 %collective-permute-start.12 = (bf16[256,3200]{1,0:T(8,128)(2,1)}, bf16[256,3200]{1,0:T(8,128)(2,1)}, u32[]{:S(2)}, u32[]{:S(2)}) collective-permute-start(bf16[256,3200]{1,0:T(8,128)(2,1)} %collective-permute-done.8.refs_2_), channel_id=1, source_target_pairs={{0,16},{1,17},{2,18},{3,19},{4,20},{5,21},{6,22},{7,23},{8,24},{9,... | collective-permute-start | bytes 4915208 | tf_op jit(solution)/shard_map/ppermute | solution.py:1210
  49.6 76.6 %collective-permute-start.11 = (bf16[256,3200]{1,0:T(8,128)(2,1)}, bf16[256,3200]{1,0:T(8,128)(2,1)}, u32[]{:S(2)}, u32[]{:S(2)}) collective-permute-start(bf16[256,3200]{1,0:T(8,128)(2,1)} %collective-permute-done.7.refs_1_), channel_id=1, source_target_pairs={{0,16},{1,17},{2,18},{3,19},{4,20},{5,21},{6,22},{7,23},{8,24},{9,... | collective-permute-start | bytes 4915208 | tf_op jit(solution)/shard_map/ppermute | solution.py:1210
  183.5 314.0 %all-gather.8.cloned.1.call-start = ((), (), s32[]{:S(2)}) async-start(), calls=%async_computation.6 | async-start | bytes 3932160 | tf_op jit(solution)/shard_map/all_gather | solution.py:1284
  183.5 49.9 %collective-permute-start.34 = (bf16[64,3200]{1,0:T(8,128)(2,1)S(1)}, bf16[64,3200]{1,0:T(8,128)(2,1)S(1)}, u32[]{:S(2)}, u32[]{:S(2)}) collective-permute-start(bf16[64,3200]{1,0:T(8,128)(2,1)S(1)} %concatenate.51), channel_id=1, source_target_pairs={{16,19},{17,18},{18,17},{19,16},{20,23},{21,22},{22,21},{23,20},{2... | collective-permute-start | bytes 1228808 | tf_op jit(solution)/shard_map/ppermute | solution.py:1131
  196.9 58.9 %collective-permute-start.19 = (bf16[272,1024]{1,0:T(8,128)(2,1)}, bf16[272,1024]{1,0:T(8,128)(2,1)}, u32[]{:S(2)}, u32[]{:S(2)}) collective-permute-start(bf16[272,1024]{1,0:T(8,128)(2,1)} %get-tuple-element.177.rest_0_), channel_id=1, source_target_pairs={{0,12},{4,8},{8,4},{12,0},{16,28},{20,24},{24,20},{28,16},{1,13},{... | collective-permute-start | bytes 1671176 | tf_op jit(solution)/shard_map/ppermute | solution.py:1131
  198.0 57.8 %collective-permute-start.18 = (bf16[272,1024]{1,0:T(8,128)(2,1)}, bf16[272,1024]{1,0:T(8,128)(2,1)}, u32[]{:S(2)}, u32[]{:S(2)}) collective-permute-start(bf16[272,1024]{1,0:T(8,128)(2,1)} %get-tuple-element.177.rest_0_), channel_id=1, source_target_pairs={{0,8},{4,12},{8,0},{12,4},{16,24},{20,28},{24,16},{28,20},{1,9},{5... | collective-permute-start | bytes 1671176 | tf_op jit(solution)/shard_map/ppermute | solution.py:1131
  198.9 57.4 %collective-permute-start.17 = (bf16[272,1024]{1,0:T(8,128)(2,1)}, bf16[272,1024]{1,0:T(8,128)(2,1)}, u32[]{:S(2)}, u32[]{:S(2)}) collective-permute-start(bf16[272,1024]{1,0:T(8,128)(2,1)} %get-tuple-element.177.rest_0_), channel_id=1, source_target_pairs={{0,4},{4,0},{8,12},{12,8},{16,20},{20,16},{24,28},{28,24},{1,5},{5... | collective-permute-start | bytes 1671176 | tf_op jit(solution)/shard_map/ppermute | solution.py:1131
  199.6 55.4 %collective-permute-start.33 = (bf16[64,3200]{1,0:T(8,128)(2,1)S(1)}, bf16[64,3200]{1,0:T(8,128)(2,1)S(1)}, u32[]{:S(2)}, u32[]{:S(2)}) collective-permute-start(bf16[64,3200]{1,0:T(8,128)(2,1)S(1)} %concatenate.51), channel_id=1, source_target_pairs={{16,18},{17,19},{18,16},{19,17},{20,22},{21,23},{22,20},{23,21},{2... | collective-permute-start | bytes 1228808 | tf_op jit(solution)/shard_map/ppermute | solution.py:1131
  259.7 40.3 %collective-permute-start.37 = (bf16[256,3200]{1,0:T(8,128)(2,1)}, bf16[256,3200]{1,0:T(8,128)(2,1)}, u32[]{:S(2)}, u32[]{:S(2)}) collective-permute-start(bf16[256,3200]{1,0:T(8,128)(2,1)} %pad_maximum_fusion.1.refs_0_), channel_id=1, source_target_pairs={{16,28},{20,24},{24,20},{28,16},{17,29},{21,25},{25,21},{29,17},{1... | collective-permute-start | bytes 4915208 | tf_op jit(solution)/shard_map/ppermute | solution.py:1131
  263.8 38.8 %collective-permute-start.36 = (bf16[256,3200]{1,0:T(8,128)(2,1)}, bf16[256,3200]{1,0:T(8,128)(2,1)}, u32[]{:S(2)}, u32[]{:S(2)}) collective-permute-start(bf16[256,3200]{1,0:T(8,128)(2,1)} %pad_maximum_fusion.1.refs_0_), channel_id=1, source_target_pairs={{16,24},{20,28},{24,16},{28,20},{17,25},{21,29},{25,17},{29,21},{1... | collective-permute-start | bytes 4915208 | tf_op jit(solution)/shard_map/ppermute | solution.py:1131
  265.9 39.1 %collective-permute-start.35 = (bf16[256,3200]{1,0:T(8,128)(2,1)}, bf16[256,3200]{1,0:T(8,128)(2,1)}, u32[]{:S(2)}, u32[]{:S(2)}) collective-permute-start(bf16[256,3200]{1,0:T(8,128)(2,1)} %pad_maximum_fusion.1.refs_0_), channel_id=1, source_target_pairs={{16,20},{20,16},{24,28},{28,24},{17,21},{21,17},{25,29},{29,25},{1... | collective-permute-start | bytes 4915208 | tf_op jit(solution)/shard_map/ppermute | solution.py:1131
  420.6 216.6 %reduce-scatter.5.cloned.1.call-start = ((), (), s32[]{:S(2)}) async-start(), calls=%async_computation.7 | async-start | bytes 3932160 | tf_op jit(solution)/shard_map/reduce_scatter | solution.py:1509
  561.9 279.4 %reduce-scatter.7.cloned.1.call-start = ((), (), s32[]{:S(2)}) async-start(), calls=%async_computation.8 | async-start | bytes 11796480 | tf_op jit(solution)/shard_map/reduce_scatter | solution.py:1509
  622.7 327.0 %reduce-scatter.9.cloned.1.call-start = ((), (), s32[]{:S(2)}) async-start(), calls=%async_computation.9 | async-start | bytes 11796480 | tf_op jit(solution)/shard_map/reduce_scatter | solution.py:1509
  785.7 257.0 %reduce-scatter.11.cloned.1.call-start = ((), (), s32[]{:S(2)}) async-start(), calls=%async_computation.10 | async-start | bytes 3932160 | tf_op jit(solution)/shard_map/reduce_scatter | solution.py:1509
  942.3 45.2 %collective-permute-start.132 = (bf16[3,384,1024]{2,1,0:T(8,128)(2,1)}, bf16[3,384,1024]{2,1,0:T(8,128)(2,1)}, u32[]{:S(2)}, u32[]{:S(2)}) collective-permute-start(bf16[3,384,1024]{2,1,0:T(8,128)(2,1)} %reduce-scatter.7.cloned.1.call-done.refs_0_), channel_id=1, source_target_pairs={{0,16},{1,17},{2,18},{3,19},{4,20},{5,21},{6,22},{7,23},{8,24},{9,... | collective-permute-start | bytes 7077896 | tf_op jit(solution)/shard_map/ppermute | solution.py:1564
  949.7 41.6 %collective-permute-start.133 = (bf16[3,384,1024]{2,1,0:T(8,128)(2,1)}, bf16[3,384,1024]{2,1,0:T(8,128)(2,1)}, u32[]{:S(2)}, u32[]{:S(2)}) collective-permute-start(bf16[3,384,1024]{2,1,0:T(8,128)(2,1)} %reduce-scatter.9.cloned.1.call-done.refs_2_), channel_id=1, source_target_pairs={{16,0},{17,1},{18,2},{19,3},{20,4},{21,5},{22,6},{23,7},{24,8},{25... | collective-permute-start | bytes 7077896 | tf_op jit(solution)/shard_map/ppermute | solution.py:1564
  987.5 50.9 %collective-permute-start.136 = (bf16[64,3200]{1,0:T(8,128)(2,1)}, bf16[64,3200]{1,0:T(8,128)(2,1)}, u32[]{:S(2)}, u32[]{:S(2)}) collective-permute-start(bf16[64,3200]{1,0:T(8,128)(2,1)} %get-tuple-element.407), channel_id=1, source_target_pairs={{16,18},{17,19},{18,16},{19,17},{20,22},{21,23},{22,20},{23,21},{2... | collective-permute-start | bytes 1228808 | tf_op jit(solution)/shard_map/ppermute | solution.py:1131
  991.4 47.0 %collective-permute-start.130 = (bf16[64,3200]{1,0:T(8,128)(2,1)}, bf16[64,3200]{1,0:T(8,128)(2,1)}, u32[]{:S(2)}, u32[]{:S(2)}) collective-permute-start(bf16[64,3200]{1,0:T(8,128)(2,1)} %get-tuple-element.410), channel_id=1, source_target_pairs={{0,1},{1,0},{2,3},{3,2},{4,5},{5,4},{6,7},{7,6},{8,9},{9,8},{10,11... | collective-permute-start | bytes 1228808 | tf_op jit(solution)/shard_map/ppermute | solution.py:1131
  1007.7 46.9 %collective-permute-start.138 = (bf16[1,384,1024]{2,1,0:T(8,128)(2,1)S(1)}, bf16[1,384,1024]{2,1,0:T(8,128)(2,1)S(1)}, u32[]{:S(2)}, u32[]{:S(2)}) collective-permute-start(bf16[1,384,1024]{2,1,0:T(8,128)(2,1)S(1)} %copy-done.9), channel_id=1, source_target_pairs={{0,16},{1,17},{2,18},{3,19},{4,20},{5,21},{6,22},{7,23},{8,24},{9,... | collective-permute-start | bytes 2359304 | tf_op jit(solution)/shard_map/ppermute | solution.py:1564
  (197 other events, 2492.9 us)
Sparse Core Ops, SparseCore 0:
  21.9 243.2 all-gather.3
  267.3 165.8 all-gather.5
  435.4 62.0 all-gather.7
  562.1 59.3 reduce-scatter.4
  623.7 161.6 reduce-scatter.6
  787.5 162.1 reduce-scatter.8
  952.0 90.6 reduce-scatter.10

commit v7 on v6

--- a/solution.py
+++ b/solution.py
@@ -1365,10 +1365,12 @@
         if layer == layers - 1:
             routed = [last_rank, [], slots] if sparse else []
             if sparse:
-                near = outs[:devices]
-                near = near[:1] + [exchanged(near[k], "ctx", k) for k in range(1, devices)]
-                far = [swapped(block) for block in outs[devices:]]
-                far = far[:1] + [exchanged(far[k], "ctx", k) for k in range(1, devices)]
+                near, far = outs[:devices], [swapped(block) for block in outs[devices:]]
+                near = after(near, far)
+                near, far = (
+                    blocks[:1] + [exchanged(blocks[k], "ctx", k) for k in range(1, devices)]
+                    for blocks in (near, far)
+                )
                 routed[1] = [block for pair in zip(near, far) for block in pair]
             mixed = None
             hidden_rows, grad_output, message, *row_messages = finish(

time: 1080 us -> 1080 us (level)
  transfers between devices with their start and end apart: 147 -> 147, of which waited for: 58 -> 56; matrix products, arithmetic and copies ran while one was open for 10% -> 10% of each run, Pallas kernels for 25% -> 25%
where the time goes in v7:
time: 1080 us; the launch traced here: 1070 us
  waiting for transfers between devices  390 us (36%)
  Pallas kernels  298 us (28%)
  starting transfers between devices  237 us (22%)
  other arithmetic  88.1 us (8%)
  local copies, waits for them, and re-layouts  33.1 us (3%)
  between operations  19.5 us (2%)
    ppermute x78, waiting for transfers between devices, exchanged(): lax.ppermute(value, ('section', axis), pairs_within(axis, by, sections))  271 us
    ppermute x78, starting transfers between devices, exchanged(): lax.ppermute(value, ('section', axis), pairs_within(axis, by, sections))  130 us
    pallas_call x4, Pallas kernels, experts_backward(): pl.pallas_call(kernel, name='experts_backward', grid=(local, portions), i...  74 us
    ppermute x8, waiting for transfers between devices, shared_of_plane(): lax.ppermute(own, 'section', [(layer, 1 - layer)])  72.3 us
    ppermute x44, starting transfers between devices, swapped(): return lax.ppermute(value, 'section', [(0, 1), (1, 0)])  49.2 us
    pallas_call x2, Pallas kernels, attend_backward(): pl.pallas_call(functools.partial(attend_back_kernel, devices, len(parts))...  48.7 us
    pallas_call x3, Pallas kernels, experts_forward(): pl.pallas_call(functools.partial(experts_kernel, sources, depth, slots, b...  45.6 us
    pallas_call x5, Pallas kernels, dispatch(): pl.pallas_call(functools.partial(dispatch_kernel, sources, slots, backwar...  29.3 us
  transfers between devices with their start and end apart: 147, of which 56 were waited for; matrix products, arithmetic and copies ran while one was open for 10% of the time, Pallas kernels for 25%

profile of v7, /device:TPU:9, one launch (start us, length us, event | category | flops | bytes accessed | tf_op | source)
XLA Modules:
  0.0 1068.0 jit_solution(10462758402823893780)
XLA Ops:
  53.9 37.3 %collective-permute-done.10.refs_4_ = bf16[256,3200]{1,0:T(8,128)(2,1)} collective-permute-done((bf16[256,3200]{1,0:T(8,128)(2,1)S(1)}, bf16[256,3200]{1,0:T(8,128)(2,1)}, u32[]{:S(2)}, u32[]{:S(2)}) %collective-permute-start.10) | collective-permute-done | bytes 1638432 | tf_op jit(solution)/shard_map/ppermute | solution.py:1210
  91.2 15.1 %collective-permute-done.13.refs_7_ = bf16[256,3200]{1,0:T(8,128)(2,1)} collective-permute-done((bf16[256,3200]{1,0:T(8,128)(2,1)}, bf16[256,3200]{1,0:T(8,128)(2,1)}, u32[]{:S(2)}, u32[]{:S(2)}) %collective-permute-start.13) | collective-permute-done | bytes 1638432 | tf_op jit(solution)/shard_map/ppermute | solution.py:1210
  106.2 17.5 %collective-permute-done.12.refs_6_ = bf16[256,3200]{1,0:T(8,128)(2,1)} collective-permute-done((bf16[256,3200]{1,0:T(8,128)(2,1)}, bf16[256,3200]{1,0:T(8,128)(2,1)}, u32[]{:S(2)}, u32[]{:S(2)}) %collective-permute-start.12) | collective-permute-done | bytes 1638432 | tf_op jit(solution)/shard_map/ppermute | solution.py:1210
  152.6 12.6 %collective-permute-done.15.rest_2_.rest_6_.rest_18_.rest_22_ = bf16[2,256,512]{2,1,0:T(8,128)(2,1)S(1)} collective-permute-done((bf16[2,256,512]{2,1,0:T(8,128)(2,1)}, bf16[2,256,512]{2,1,0:T(8,128)(2,1)S(1)}, u32[]{:S(2)}, u32[]{:S(2)}) %collective-permute-start.15) | collective-permute-done | bytes 524320 | tf_op jit(solution)/shard_map/ppermute | solution.py:1131
  166.1 14.0 %attend.2 = (bf16[256,1024]{1,0:T(8,128)(2,1)}, f32[4,2,512]{2,1,0:T(2,128)}, f32[256,1024]{1,0:T(8,128)}, bf16[272,1024]{1,0:T(8,128)(2,1)}) custom-call(s32[2]{0:T(128)} %pad_add_fusion.2.scal, bf16[256,1024]{1,0:T(8,128)(2,1)} %dynamic-slice_bitcast_fusion.1.x.rest_14_, bf16[256,1024]{1,0:T(8,128)(2,1)} %get-tuple-element.178.q.rest_10_, ...), custom_call_target="tpu_custom_call" | custom-call | flops 15790320640 | bytes 9437184 | tf_op jit(solution)/shard_map/attend/pallas_call | solution.py:215
  183.5 13.3 %collective-permute-start.34 = (bf16[64,3200]{1,0:T(8,128)(2,1)S(1)}, bf16[64,3200]{1,0:T(8,128)(2,1)S(1)}, u32[]{:S(2)}, u32[]{:S(2)}) collective-permute-start(bf16[64,3200]{1,0:T(8,128)(2,1)S(1)} %concatenate.51), channel_id=1, source_target_pairs={{16,19},{17,18},{18,17},{19,16},{20,23},{21,22},{22,21},{23,20},{2... | collective-permute-start | bytes 1228808 | tf_op jit(solution)/shard_map/ppermute | solution.py:1131
  205.5 27.8 %collective-permute-done.34 = bf16[64,3200]{1,0:T(8,128)(2,1)S(1)} collective-permute-done((bf16[64,3200]{1,0:T(8,128)(2,1)S(1)}, bf16[64,3200]{1,0:T(8,128)(2,1)S(1)}, u32[]{:S(2)}, u32[]{:S(2)}) %collective-permute-start.34) | collective-permute-done | bytes 409632 | tf_op jit(solution)/shard_map/ppermute | solution.py:1131
  235.3 19.7 %collective-permute-done.33 = bf16[64,3200]{1,0:T(8,128)(2,1)S(1)} collective-permute-done((bf16[64,3200]{1,0:T(8,128)(2,1)S(1)}, bf16[64,3200]{1,0:T(8,128)(2,1)S(1)}, u32[]{:S(2)}, u32[]{:S(2)}) %collective-permute-start.33) | collective-permute-done | bytes 409632 | tf_op jit(solution)/shard_map/ppermute | solution.py:1131
  275.1 21.6 %experts_forward.3 = (f32[4,640,1024]{2,1,0:T(8,128)}, bf16[4,640,1024]{2,1,0:T(8,128)(2,1)}, bf16[256,1024]{1,0:T(8,128)(2,1)}, bf16[256,1024]{1,0:T(8,128)(2,1...) custom-call(s32[5]{0:T(128)} %stack.168.scal.refs_0_, ...), custom_call_target="tpu_custom_call" | custom-call | flops 20937965568 | bytes 20971520 | tf_op jit(solution)/shard_map/experts_forward/pallas_call | solution.py:571
  363.7 13.0 %collective-permute-done.43.rest_2_.rest_6_.rest_18_.rest_22_ = bf16[2,256,512]{2,1,0:T(8,128)(2,1)} collective-permute-done((bf16[2,256,512]{2,1,0:T(8,128)(2,1)}, bf16[2,256,512]{2,1,0:T(8,128)(2,1)}, u32[]{:S(2)}, u32[]{:S(2)}) %collective-permute-start.43) | collective-permute-done | bytes 524320 | tf_op jit(solution)/shard_map/ppermute | solution.py:1131
  376.7 13.8 %attend.3 = (bf16[256,1024]{1,0:T(8,128)(2,1)}, f32[4,2,512]{2,1,0:T(2,128)}, f32[256,1024]{1,0:T(8,128)}, bf16[272,1024]{1,0:T(8,128)(2,1)}) custom-call(s32[2]{0:T(128)} %pad_add_fusion.2.scal, bf16[256,1024]{1,0:T(8,128)(2,1)} %get-tuple-element.393.x.rest_14_, bf16[256,1024]{1,0:T(8,128)(2,1)} %get-tuple-element.194.q.rest_10_, ...), custom_call_target="tpu_custom_call" | custom-call | flops 15790320640 | bytes 9437184 | tf_op jit(solution)/shard_map/attend/pallas_call | solution.py:215
  433.2 16.9 %experts_forward.4 = (f32[3,640,1024]{2,1,0:T(8,128)}, bf16[3,640,1024]{2,1,0:T(8,128)(2,1)}, bf16[256,1024]{1,0:T(8,128)(2,1)}, bf16[256,1024]{1,0:T(8,128)(2,1...) custom-call(s32[5]{0:T(128)} %stack.168.scal.refs_0_, ...), custom_call_target="tpu_custom_call" | custom-call | flops 19629342720 | bytes 15728640 | tf_op jit(solution)/shard_map/experts_forward/pallas_call | solution.py:571
  467.1 13.6 %collective-permute-done.56 = bf16[256,1024]{1,0:T(8,128)(2,1)S(1)} collective-permute-done((bf16[256,1024]{1,0:T(8,128)(2,1)S(1)}, bf16[256,1024]{1,0:T(8,128)(2,1)S(1)}, u32[]{:S(2)}, u32[]{:S(2)}) %collective-permute-start.56) | collective-permute-done | bytes 524320 | tf_op jit(solution)/shard_map/ppermute | solution.py:1131
  483.1 14.3 %all-gather.8.cloned.1.call-done.rest_3_.rest_4_.rest_5_.rest_6_.refs_15_.refs_16_.refs_17_.refs_18_ = bf16[1,1536,1024]{2,1,0:T(8,128)(2,1)} async-done(((bf16[1,384,1024]{2,1,0:T(8,128)(2,1)}), bf16[1,1536,1024]{2,1,0:T(8,128)(2,1)}) %all-gather.8.cloned.1.call-update) | async-done | bytes 3145744 | tf_op jit(solution)/shard_map/all_gather | solution.py:1284
  567.3 11.4 %collective-permute-done.79.rest_3_ = bf16[272,1024]{1,0:T(8,128)(2,1)S(1)} collective-permute-done((bf16[272,1024]{1,0:T(8,128)(2,1)S(1)}, bf16[272,1024]{1,0:T(8,128)(2,1)S(1)}, u32[]{:S(2)}, u32[]{:S(2)}) %collective-permute-start.79) | collective-permute-done | bytes 557088 | tf_op jit(solution)/shard_map/ppermute | solution.py:1131
  599.8 23.5 %experts_backward.5 = (bf16[3,1536,1024]{2,1,0:T(8,128)(2,1)}, f32[3,1,1024]{2,1,0:T(1,128)}, bf16[3,640,1024]{2,1,0:T(8,128)(2,1)}) custom-call(s32[5]{0:T(128)} %stack.168.scal.refs_0_, f32[8,3,256]{2,1,0:T(4,128)} %bitcast.182, f32[8,3,256]{2,1,0:T(4,128)} %bitcast.184, f32[8,2,256]{2,1,0:T(2,128)} %get-tuple-element.233.refs_3_, ...), custom_call_target="tpu_custom_call" | custom-call | flops 37544689664 | bytes 27525120 | tf_op jit(solution)/shard_map/experts_backward/pallas_call | solution.py:766
  647.1 12.9 %collective-permute-done.88.rest_3_ = bf16[256,1024]{1,0:T(8,128)(2,1)S(1)} collective-permute-done((bf16[256,1024]{1,0:T(8,128)(2,1)S(1)}, bf16[256,1024]{1,0:T(8,128)(2,1)S(1)}, u32[]{:S(2)}, u32[]{:S(2)}) %collective-permute-start.88) | collective-permute-done | bytes 524320 | tf_op jit(solution)/shard_map/ppermute | solution.py:1131
  660.9 24.2 %attend_backward.2 = (f32[256,1024]{1,0:T(8,128)}, bf16[1024,2048]{1,0:T(8,128)(2,1)}, f32[1,1024]{1,0:T(1,128)}, bf16[256,1024]{1,0:T(8,128)(2,1)}, bf16[2,256,...) custom-call(s32[2]{0:T(128)} %pad_add_fusion.2.scal, ...), custom_call_target="tpu_custom_call" | custom-call | flops 28010655744 | bytes 19922944 | tf_op jit(solution)/shard_map/attend_backward/pallas_call | solution.py:1003
  763.0 23.6 %experts_backward.6 = (bf16[3,1536,1024]{2,1,0:T(8,128)(2,1)}, f32[3,1,1024]{2,1,0:T(1,128)}, bf16[3,640,1024]{2,1,0:T(8,128)(2,1)}) custom-call(s32[5]{0:T(128)} %stack.168.scal.refs_0_, f32[8,3,256]{2,1,0:T(4,128)} %bitcast.173, f32[8,3,256]{2,1,0:T(4,128)} %bitcast.179, f32[8,2,256]{2,1,0:T(2,128)} %get-tuple-element.272.refs_3_, ...), custom_call_target="tpu_custom_call" | custom-call | flops 37544689664 | bytes 27525120 | tf_op jit(solution)/shard_map/experts_backward/pallas_call | solution.py:766
  812.6 16.2 %experts_backward.7 = (bf16[1,1536,1024]{2,1,0:T(8,128)(2,1)}, f32[1,1,1024]{2,1,0:T(1,128)}, bf16[256,1024]{1,0:T(8,128)(2,1)}, bf16[256,1024]{1,0:T(8,128)(2,1...) custom-call(s32[5]{0:T(128)} %concatenate.56.refs_0_, ...), custom_call_target="tpu_custom_call" | custom-call | flops 12514895872 | bytes 9175040 | tf_op jit(solution)/shard_map/experts_backward/pallas_call | solution.py:766
  850.7 12.6 %collective-permute-done.115.rest_3_ = bf16[256,1024]{1,0:T(8,128)(2,1)} collective-permute-done((bf16[256,1024]{1,0:T(8,128)(2,1)S(1)}, bf16[256,1024]{1,0:T(8,128)(2,1)}, u32[]{:S(2)}, u32[]{:S(2)}) %collective-permute-start.115) | collective-permute-done | bytes 524320 | tf_op jit(solution)/shard_map/ppermute | solution.py:1131
  864.1 24.5 %attend_backward.3 = (f32[256,1024]{1,0:T(8,128)}, bf16[1024,2048]{1,0:T(8,128)(2,1)}, f32[1,1024]{1,0:T(1,128)}, bf16[256,1024]{1,0:T(8,128)(2,1)}, bf16[2,256,...) custom-call(s32[2]{0:T(128)} %pad_add_fusion.2.scal, ...), custom_call_target="tpu_custom_call" | custom-call | flops 28010655744 | bytes 19922944 | tf_op jit(solution)/shard_map/attend_backward/pallas_call | solution.py:1003
  950.4 13.9 %collective-permute-start.133 = (bf16[3,384,1024]{2,1,0:T(8,128)(2,1)}, bf16[3,384,1024]{2,1,0:T(8,128)(2,1)}, u32[]{:S(2)}, u32[]{:S(2)}) collective-permute-start(bf16[3,384,1024]{2,1,0:T(8,128)(2,1)} %reduce-scatter.9.cloned.1.call-done.refs_2_), channel_id=1, source_target_pairs={{16,0},{17,1},{18,2},{19,3},{20,4},{21,5},{22,6},{23,7},{24,8},{25... | collective-permute-start | bytes 7077896 | tf_op jit(solution)/shard_map/ppermute | solution.py:1566
  1010.1 29.2 %collective-permute-done.136 = bf16[64,3200]{1,0:T(8,128)(2,1)} collective-permute-done((bf16[64,3200]{1,0:T(8,128)(2,1)}, bf16[64,3200]{1,0:T(8,128)(2,1)}, u32[]{:S(2)}, u32[]{:S(2)}) %collective-permute-start.136) | collective-permute-done | bytes 409632 | tf_op jit(solution)/shard_map/ppermute | solution.py:1131
  (571 shorter events, 606.0 us)
Async XLA Ops:
  7.2 267.9 %all-gather.4.cloned.1.call-start = ((), (), s32[]{:S(2)}) async-start(), calls=%async_computation.4 | async-start | bytes 15728640 | tf_op jit(solution)/shard_map/all_gather | solution.py:1284
  21.7 411.5 %all-gather.6.cloned.1.call-start = ((), (), s32[]{:S(2)}) async-start(), calls=%async_computation.5 | async-start | bytes 11796480 | tf_op jit(solution)/shard_map/all_gather | solution.py:1284
  45.6 45.5 %collective-permute-start.10 = (bf16[256,3200]{1,0:T(8,128)(2,1)S(1)}, bf16[256,3200]{1,0:T(8,128)(2,1)}, u32[]{:S(2)}, u32[]{:S(2)}) collective-permute-start(bf16[256,3200]{1,0:T(8,128)(2,1)S(1)} %pad_maximum_fusion.refs_0_), channel_id=1, source_target_pairs={{0,16},{1,17},{2,18},{3,19},{4,20},{5,21},{6,22},{7,23},{8,24},{9,... | collective-permute-start | bytes 4915208 | tf_op jit(solution)/shard_map/ppermute | solution.py:1210
  46.9 59.3 %collective-permute-start.13 = (bf16[256,3200]{1,0:T(8,128)(2,1)}, bf16[256,3200]{1,0:T(8,128)(2,1)}, u32[]{:S(2)}, u32[]{:S(2)}) collective-permute-start(bf16[256,3200]{1,0:T(8,128)(2,1)} %collective-permute-done.9.refs_3_), channel_id=1, source_target_pairs={{0,16},{1,17},{2,18},{3,19},{4,20},{5,21},{6,22},{7,23},{8,24},{9,... | collective-permute-start | bytes 4915208 | tf_op jit(solution)/shard_map/ppermute | solution.py:1210
  48.3 75.4 %collective-permute-start.12 = (bf16[256,3200]{1,0:T(8,128)(2,1)}, bf16[256,3200]{1,0:T(8,128)(2,1)}, u32[]{:S(2)}, u32[]{:S(2)}) collective-permute-start(bf16[256,3200]{1,0:T(8,128)(2,1)} %collective-permute-done.8.refs_2_), channel_id=1, source_target_pairs={{0,16},{1,17},{2,18},{3,19},{4,20},{5,21},{6,22},{7,23},{8,24},{9,... | collective-permute-start | bytes 4915208 | tf_op jit(solution)/shard_map/ppermute | solution.py:1210
  49.6 76.6 %collective-permute-start.11 = (bf16[256,3200]{1,0:T(8,128)(2,1)}, bf16[256,3200]{1,0:T(8,128)(2,1)}, u32[]{:S(2)}, u32[]{:S(2)}) collective-permute-start(bf16[256,3200]{1,0:T(8,128)(2,1)} %collective-permute-done.7.refs_1_), channel_id=1, source_target_pairs={{0,16},{1,17},{2,18},{3,19},{4,20},{5,21},{6,22},{7,23},{8,24},{9,... | collective-permute-start | bytes 4915208 | tf_op jit(solution)/shard_map/ppermute | solution.py:1210
  183.5 314.0 %all-gather.8.cloned.1.call-start = ((), (), s32[]{:S(2)}) async-start(), calls=%async_computation.6 | async-start | bytes 3932160 | tf_op jit(solution)/shard_map/all_gather | solution.py:1284
  183.5 49.9 %collective-permute-start.34 = (bf16[64,3200]{1,0:T(8,128)(2,1)S(1)}, bf16[64,3200]{1,0:T(8,128)(2,1)S(1)}, u32[]{:S(2)}, u32[]{:S(2)}) collective-permute-start(bf16[64,3200]{1,0:T(8,128)(2,1)S(1)} %concatenate.51), channel_id=1, source_target_pairs={{16,19},{17,18},{18,17},{19,16},{20,23},{21,22},{22,21},{23,20},{2... | collective-permute-start | bytes 1228808 | tf_op jit(solution)/shard_map/ppermute | solution.py:1131
  196.9 58.9 %collective-permute-start.19 = (bf16[272,1024]{1,0:T(8,128)(2,1)}, bf16[272,1024]{1,0:T(8,128)(2,1)}, u32[]{:S(2)}, u32[]{:S(2)}) collective-permute-start(bf16[272,1024]{1,0:T(8,128)(2,1)} %get-tuple-element.181.rest_0_), channel_id=1, source_target_pairs={{0,12},{4,8},{8,4},{12,0},{16,28},{20,24},{24,20},{28,16},{1,13},{... | collective-permute-start | bytes 1671176 | tf_op jit(solution)/shard_map/ppermute | solution.py:1131
  198.1 57.7 %collective-permute-start.18 = (bf16[272,1024]{1,0:T(8,128)(2,1)}, bf16[272,1024]{1,0:T(8,128)(2,1)}, u32[]{:S(2)}, u32[]{:S(2)}) collective-permute-start(bf16[272,1024]{1,0:T(8,128)(2,1)} %get-tuple-element.181.rest_0_), channel_id=1, source_target_pairs={{0,8},{4,12},{8,0},{12,4},{16,24},{20,28},{24,16},{28,20},{1,9},{5... | collective-permute-start | bytes 1671176 | tf_op jit(solution)/shard_map/ppermute | solution.py:1131
  198.9 57.4 %collective-permute-start.17 = (bf16[272,1024]{1,0:T(8,128)(2,1)}, bf16[272,1024]{1,0:T(8,128)(2,1)}, u32[]{:S(2)}, u32[]{:S(2)}) collective-permute-start(bf16[272,1024]{1,0:T(8,128)(2,1)} %get-tuple-element.181.rest_0_), channel_id=1, source_target_pairs={{0,4},{4,0},{8,12},{12,8},{16,20},{20,16},{24,28},{28,24},{1,5},{5... | collective-permute-start | bytes 1671176 | tf_op jit(solution)/shard_map/ppermute | solution.py:1131
  199.6 55.4 %collective-permute-start.33 = (bf16[64,3200]{1,0:T(8,128)(2,1)S(1)}, bf16[64,3200]{1,0:T(8,128)(2,1)S(1)}, u32[]{:S(2)}, u32[]{:S(2)}) collective-permute-start(bf16[64,3200]{1,0:T(8,128)(2,1)S(1)} %concatenate.51), channel_id=1, source_target_pairs={{16,18},{17,19},{18,16},{19,17},{20,22},{21,23},{22,20},{23,21},{2... | collective-permute-start | bytes 1228808 | tf_op jit(solution)/shard_map/ppermute | solution.py:1131
  259.7 40.7 %collective-permute-start.37 = (bf16[256,3200]{1,0:T(8,128)(2,1)}, bf16[256,3200]{1,0:T(8,128)(2,1)}, u32[]{:S(2)}, u32[]{:S(2)}) collective-permute-start(bf16[256,3200]{1,0:T(8,128)(2,1)} %pad_maximum_fusion.1.refs_0_), channel_id=1, source_target_pairs={{16,28},{20,24},{24,20},{28,16},{17,29},{21,25},{25,21},{29,17},{1... | collective-permute-start | bytes 4915208 | tf_op jit(solution)/shard_map/ppermute | solution.py:1131
  263.8 39.1 %collective-permute-start.36 = (bf16[256,3200]{1,0:T(8,128)(2,1)}, bf16[256,3200]{1,0:T(8,128)(2,1)}, u32[]{:S(2)}, u32[]{:S(2)}) collective-permute-start(bf16[256,3200]{1,0:T(8,128)(2,1)} %pad_maximum_fusion.1.refs_0_), channel_id=1, source_target_pairs={{16,24},{20,28},{24,16},{28,20},{17,25},{21,29},{25,17},{29,21},{1... | collective-permute-start | bytes 4915208 | tf_op jit(solution)/shard_map/ppermute | solution.py:1131
  265.9 39.5 %collective-permute-start.35 = (bf16[256,3200]{1,0:T(8,128)(2,1)}, bf16[256,3200]{1,0:T(8,128)(2,1)}, u32[]{:S(2)}, u32[]{:S(2)}) collective-permute-start(bf16[256,3200]{1,0:T(8,128)(2,1)} %pad_maximum_fusion.1.refs_0_), channel_id=1, source_target_pairs={{16,20},{20,16},{24,28},{28,24},{17,21},{21,17},{25,29},{29,25},{1... | collective-permute-start | bytes 4915208 | tf_op jit(solution)/shard_map/ppermute | solution.py:1131
  420.9 217.2 %reduce-scatter.5.cloned.1.call-start = ((), (), s32[]{:S(2)}) async-start(), calls=%async_computation.7 | async-start | bytes 3932160 | tf_op jit(solution)/shard_map/reduce_scatter | solution.py:1511
  562.6 279.8 %reduce-scatter.7.cloned.1.call-start = ((), (), s32[]{:S(2)}) async-start(), calls=%async_computation.8 | async-start | bytes 11796480 | tf_op jit(solution)/shard_map/reduce_scatter | solution.py:1511
  623.4 327.0 %reduce-scatter.9.cloned.1.call-start = ((), (), s32[]{:S(2)}) async-start(), calls=%async_computation.9 | async-start | bytes 11796480 | tf_op jit(solution)/shard_map/reduce_scatter | solution.py:1511
  786.6 256.5 %reduce-scatter.11.cloned.1.call-start = ((), (), s32[]{:S(2)}) async-start(), calls=%async_computation.10 | async-start | bytes 3932160 | tf_op jit(solution)/shard_map/reduce_scatter | solution.py:1511
  943.6 45.0 %collective-permute-start.132 = (bf16[3,384,1024]{2,1,0:T(8,128)(2,1)}, bf16[3,384,1024]{2,1,0:T(8,128)(2,1)}, u32[]{:S(2)}, u32[]{:S(2)}) collective-permute-start(bf16[3,384,1024]{2,1,0:T(8,128)(2,1)} %reduce-scatter.7.cloned.1.call-done.refs_0_), channel_id=1, source_target_pairs={{0,16},{1,17},{2,18},{3,19},{4,20},{5,21},{6,22},{7,23},{8,24},{9,... | collective-permute-start | bytes 7077896 | tf_op jit(solution)/shard_map/ppermute | solution.py:1566
  950.4 42.1 %collective-permute-start.133 = (bf16[3,384,1024]{2,1,0:T(8,128)(2,1)}, bf16[3,384,1024]{2,1,0:T(8,128)(2,1)}, u32[]{:S(2)}, u32[]{:S(2)}) collective-permute-start(bf16[3,384,1024]{2,1,0:T(8,128)(2,1)} %reduce-scatter.9.cloned.1.call-done.refs_2_), channel_id=1, source_target_pairs={{16,0},{17,1},{18,2},{19,3},{20,4},{21,5},{22,6},{23,7},{24,8},{25... | collective-permute-start | bytes 7077896 | tf_op jit(solution)/shard_map/ppermute | solution.py:1566
  988.6 50.7 %collective-permute-start.136 = (bf16[64,3200]{1,0:T(8,128)(2,1)}, bf16[64,3200]{1,0:T(8,128)(2,1)}, u32[]{:S(2)}, u32[]{:S(2)}) collective-permute-start(bf16[64,3200]{1,0:T(8,128)(2,1)} %get-tuple-element.415), channel_id=1, source_target_pairs={{16,18},{17,19},{18,16},{19,17},{20,22},{21,23},{22,20},{23,21},{2... | collective-permute-start | bytes 1228808 | tf_op jit(solution)/shard_map/ppermute | solution.py:1131
  992.5 46.8 %collective-permute-start.130 = (bf16[64,3200]{1,0:T(8,128)(2,1)}, bf16[64,3200]{1,0:T(8,128)(2,1)}, u32[]{:S(2)}, u32[]{:S(2)}) collective-permute-start(bf16[64,3200]{1,0:T(8,128)(2,1)} %get-tuple-element.418), channel_id=1, source_target_pairs={{0,1},{1,0},{2,3},{3,2},{4,5},{5,4},{6,7},{7,6},{8,9},{9,8},{10,11... | collective-permute-start | bytes 1228808 | tf_op jit(solution)/shard_map/ppermute | solution.py:1131
  1008.8 46.4 %collective-permute-start.138 = (bf16[1,384,1024]{2,1,0:T(8,128)(2,1)S(1)}, bf16[1,384,1024]{2,1,0:T(8,128)(2,1)S(1)}, u32[]{:S(2)}, u32[]{:S(2)}) collective-permute-start(bf16[1,384,1024]{2,1,0:T(8,128)(2,1)S(1)} %copy-done.9), channel_id=1, source_target_pairs={{0,16},{1,17},{2,18},{3,19},{4,20},{5,21},{6,22},{7,23},{8,24},{9,... | collective-permute-start | bytes 2359304 | tf_op jit(solution)/shard_map/ppermute | solution.py:1566
  (197 other events, 2501.2 us)
Sparse Core Ops, SparseCore 0:
  21.9 243.2 all-gather.3
  267.3 165.8 all-gather.5
  435.4 62.0 all-gather.7
  562.7 59.3 reduce-scatter.4
  624.3 161.6 reduce-scatter.6
  788.2 162.1 reduce-scatter.8
  952.7 90.4 reduce-scatter.10
